TPU v7x, 32 devices: a whole 2x2x4 slice. The times are simulated.
32 devices in a mesh: dp: 2 (over x), rep: 16 (over z, y, core).
Axes of the slice: x: 2, y: 2, z: 4, core: 2. Of those that a mesh axis runs over, the one named last changes fastest.
Arguments:
- block_in: bfloat16 [160, 196, 768], P(('dp', 'rep')), may hold values from -6 to 6
- tissue: int32 [160, 196], P(('dp', 'rep')), may hold values from 0 to 1, as said below
- text_emb: bfloat16 [160, 512], P(('dp', 'rep')), may hold values from -6 to 6
- text_order: int32 [160], replicated, may hold values from 0 to 159, each once
- owner_list: int32 [77], replicated, may hold values from 0 to 15, as said below
- master: float32 [16, 8, 128, 768], P('rep', None, 'dp'), as said below
- first_moment: float32 [16, 8, 128, 768], P('rep', None, 'dp'), as said below
- second_moment: float32 [16, 8, 128, 768], P('rep', None, 'dp'), as said below
Outputs:
- block_out: bfloat16 [160, 196, 768], P(('dp', 'rep'))
- input_grad: float32 [160, 196, 768], P(('dp', 'rep'))
- new_master: float32 [16, 8, 128, 768], P('rep', None, 'dp')
- new_first: float32 [16, 8, 128, 768], P('rep', None, 'dp')
- new_second: float32 [16, 8, 128, 768], P('rep', None, 'dp')
Inputs may be any that keep to these rules, and one draw needn't show every extreme that they name: owner_list[t] is the owner along rep of tile t of the weights' row view; no owner holds more than 8 tiles and some owner holds exactly 8. Every image has at least one twelfth of 196 tissue slots, rounded down, and never fewer than one; some image has all 196. `master`: slot s of owner r holds the tile that is the s-th of that owner's tiles in increasing tile order; slots that no tile takes hold values that are updated like the rest. `first_moment`: laid out as master. `second_moment`: laid out as master; positive.
All inputs are finite; a program needn't handle non-finite values.
Results may differ from a plain program's by a relative error of at most 0.011.
The roundings to bfloat16 on the way count: a program that leaves them out, or rounds other values in their place, can miss the bound.
Values may be sent and summed in bfloat16 or wider, within the bound.
No kernel may reach another device: no remote copies, remote signals or barrier semaphores. Data moves between devices by JAX's collectives and lax.ppermute only.
A program may use at most 192 MiB of HBM per device.

v0:
```python
import jax
import jax.numpy as jnp
from jax import lax
from jax.sharding import PartitionSpec as P

D = 768
HEADS = 12
HEAD = 64
FF = 3072
EMB = 512
PATCHES = 196
STEP = 10


logit_scale = 50.0
learn_rate = 0.03
beta_one = 0.9
beta_two = 0.999
adam_eps = 1e-08
decay_rate = 0.05
norm_eps = 1e-05
unit_eps = 1e-06


def matmul_plain(left_side, right_side):
    return jnp.dot(left_side, right_side, preferred_element_type=jnp.float32)


def matmul_right(left_side, right_side):
    return lax.dot_general(
        left_side, right_side, (((1,), (1,)), ((), ())), preferred_element_type=jnp.float32
    )


def matmul_left(left_side, right_side):
    return lax.dot_general(
        left_side, right_side, (((0,), (0,)), ((), ())), preferred_element_type=jnp.float32
    )


def layer_norm(tensor, gain_row, shift_row):
    center = tensor - jnp.mean(tensor, axis=-1, keepdims=True)
    spread = jnp.mean(center * center, axis=-1, keepdims=True)
    return center * lax.rsqrt(spread + norm_eps) * gain_row + shift_row


def unit_rows(tensor):
    return tensor * lax.rsqrt(jnp.sum(tensor * tensor, axis=-1, keepdims=True) + unit_eps)


def gelu_exact(tensor):
    return jax.nn.gelu(tensor, approximate=False)


def slot_place(owner_list, slot_count):
    tile_count = owner_list.shape[0]
    earlier = jnp.tril(jnp.ones((tile_count, tile_count), jnp.int32), -1)
    same_owner = (owner_list[:, None] == owner_list[None, :]).astype(jnp.int32)
    return owner_list * slot_count + jnp.sum(same_owner * earlier, axis=1)


def shards(block_in, tissue, text_emb, text_order, owner_list, master, first_moment, second_moment):
    n_dp = lax.axis_size("dp")
    n_rep = lax.axis_size("rep")
    count_img = block_in.shape[0]
    slot_count = master.shape[1]
    part_rows = master.shape[2]
    tile_rows = part_rows * n_dp
    tile_count = owner_list.shape[0]
    tokens = count_img * PATCHES
    image_total = text_order.shape[0]
    bf16 = jnp.bfloat16
    f32 = jnp.float32
    head_scale = HEAD ** (-0.5)
    placed = slot_place(owner_list, slot_count)
    gathered = lax.all_gather(master.astype(bf16), ("dp", "rep"), axis=0, tiled=True)
    gathered = gathered.reshape(n_dp, n_rep * slot_count, part_rows, D)
    weight_rows = jnp.transpose(jnp.take(gathered, placed, axis=1), (1, 0, 2, 3)).reshape(
        tile_count * tile_rows, D
    )
    vector_base = 4 * D + 2 * FF + EMB
    qkv_w = weight_rows[: 3 * D]
    out_w = weight_rows[3 * D : 4 * D]
    up_w = weight_rows[4 * D : 4 * D + FF]
    down_w = weight_rows[4 * D + FF : 4 * D + 2 * FF].reshape(D, FF)
    proj_w = weight_rows[4 * D + 2 * FF : vector_base]
    vector_rows = weight_rows[vector_base:].astype(f32)
    gain_one, shift_one, gain_two, shift_two = (
        vector_rows[0],
        vector_rows[1],
        vector_rows[2],
        vector_rows[3],
    )
    bias_q, bias_v, bias_o = (vector_rows[4], vector_rows[5], vector_rows[6])
    bias_up = vector_rows[7 : 7 + FF // D].reshape(FF)
    bias_down = vector_rows[7 + FF // D]
    inputs = block_in.reshape(tokens, D).astype(f32)
    valid_mask = tissue > 0
    normed, first_norm_back = jax.vjp(layer_norm, inputs, gain_one, shift_one)
    normed_b = normed.astype(bf16)
    merged_qkv = matmul_right(normed_b, qkv_w)
    head_shape = (count_img, PATCHES, HEADS, HEAD)
    queries = (merged_qkv[:, :D] + bias_q).astype(bf16).reshape(head_shape)
    key_heads = merged_qkv[:, D : 2 * D].astype(bf16).reshape(head_shape)
    value_heads = (merged_qkv[:, 2 * D :] + bias_v).astype(bf16).reshape(head_shape)
    raw_scores = (
        jnp.einsum("gqhd,gkhd->ghqk", queries, key_heads, preferred_element_type=f32) * head_scale
    )
    scores = jnp.where(valid_mask[:, None, None, :], raw_scores, -1000000000.0)
    top_score = jnp.max(scores, axis=-1, keepdims=True)
    expo = jnp.exp(scores - top_score)
    summed = jnp.sum(expo, axis=-1, keepdims=True)
    attention = expo / summed
    row_lse = top_score + jnp.log(summed)
    mixed_heads = jnp.einsum(
        "ghqk,gkhd->gqhd", attention.astype(bf16), value_heads, preferred_element_type=f32
    )
    attended = mixed_heads.reshape(tokens, D).astype(bf16)
    middle = inputs + (matmul_right(attended, out_w) + bias_o)
    normed_two, second_norm_back = jax.vjp(layer_norm, middle, gain_two, shift_two)
    normed_two_b = normed_two.astype(bf16)
    hidden_pre = matmul_right(normed_two_b, up_w) + bias_up
    hidden_act, gelu_back = jax.vjp(gelu_exact, hidden_pre)
    hidden_b = hidden_act.astype(bf16)
    block_out = (middle + (matmul_right(hidden_b, down_w) + bias_down)).astype(bf16)
    counts = jnp.sum(valid_mask.astype(f32), axis=1)
    pooled = (
        jnp.einsum(
            "gp,gpd->gd",
            valid_mask.astype(bf16),
            block_out.reshape(count_img, PATCHES, D),
            preferred_element_type=f32,
        )
        / counts[:, None]
    )
    pooled_b = pooled.astype(bf16)
    projected = matmul_right(pooled_b, proj_w)
    image_unit, unit_back = jax.vjp(unit_rows, projected)
    own_image = image_unit.astype(bf16)
    own_text = unit_rows(text_emb.astype(f32)).astype(bf16)
    all_image, all_text = (
        lax.all_gather(own_image, ("dp", "rep"), axis=0, tiled=True),
        lax.all_gather(own_text, ("dp", "rep"), axis=0, tiled=True),
    )

    def similarity(every_image, every_text):
        return (
            logit_scale * matmul_right(own_image, every_text),
            logit_scale * matmul_right(every_image, own_text),
        )

    rows_sim, cols_sim = similarity(all_image, all_text)
    rows_top = jnp.max(rows_sim, axis=1, keepdims=True)
    rows_lse = rows_top + jnp.log(jnp.sum(jnp.exp(rows_sim - rows_top), axis=1, keepdims=True))
    cols_top = jnp.max(cols_sim, axis=0, keepdims=True)
    cols_lse = cols_top + jnp.log(jnp.sum(jnp.exp(cols_sim - cols_top), axis=0, keepdims=True))
    all_image, all_text = (
        lax.all_gather(own_image, ("dp", "rep"), axis=0, tiled=True),
        lax.all_gather(own_text, ("dp", "rep"), axis=0, tiled=True),
    )
    rows_sim, cols_sim = similarity(all_image, all_text)
    first_image = lax.axis_index(("dp", "rep")) * count_img
    mine = lax.dynamic_slice_in_dim(text_order, first_image, count_img)
    row_hit = (mine[:, None] == jnp.arange(image_total, dtype=jnp.int32)[None, :]).astype(f32)
    col_hit = (
        text_order[:, None] == (first_image + jnp.arange(count_img, dtype=jnp.int32))[None, :]
    ).astype(f32)
    rows_grad = ((jnp.exp(rows_sim - rows_lse) - row_hit) / (2.0 * image_total)).astype(bf16)
    cols_grad = ((jnp.exp(cols_sim - cols_lse) - col_hit) / (2.0 * image_total)).astype(bf16)
    unit_grad = logit_scale * matmul_plain(rows_grad, all_text)
    unit_grad = unit_grad + lax.psum_scatter(
        logit_scale * matmul_plain(cols_grad, own_text),
        ("dp", "rep"),
        scatter_dimension=0,
        tiled=True,
    )
    proj_grad_b = unit_back(unit_grad)[0].astype(bf16)
    grad_proj = matmul_left(proj_grad_b, pooled_b)
    pooled_grad = matmul_plain(proj_grad_b, proj_w)
    share = valid_mask.astype(f32) / counts[:, None]
    out_grad = (share[:, :, None] * pooled_grad[:, None, :]).reshape(tokens, D)
    down_grad_b = out_grad.astype(bf16)
    grad_down = matmul_left(down_grad_b, hidden_b)
    grad_bias_down = jnp.sum(down_grad_b, axis=0, dtype=f32)
    pre_grad_b = gelu_back(matmul_plain(down_grad_b, down_w))[0].astype(bf16)
    grad_up = matmul_left(pre_grad_b, normed_two_b)
    grad_bias_up = jnp.sum(pre_grad_b, axis=0, dtype=f32)
    middle_part, grad_gain_two, grad_shift_two = second_norm_back(matmul_plain(pre_grad_b, up_w))
    middle_grad = out_grad + middle_part
    attn_grad_b = middle_grad.astype(bf16)
    grad_out = matmul_left(attn_grad_b, attended)
    grad_bias_o = jnp.sum(attn_grad_b, axis=0, dtype=f32)
    mixed_grad = matmul_plain(attn_grad_b, out_w).astype(bf16).reshape(head_shape)
    again_scores = jnp.where(
        valid_mask[:, None, None, :],
        jnp.einsum("gqhd,gkhd->ghqk", queries, key_heads, preferred_element_type=f32) * head_scale,
        -1000000000.0,
    )
    again_attention = jnp.exp(again_scores - row_lse)
    weight_grad = jnp.einsum("gqhd,gkhd->ghqk", mixed_grad, value_heads, preferred_element_type=f32)
    value_grad = jnp.einsum(
        "ghqk,gqhd->gkhd", again_attention.astype(bf16), mixed_grad, preferred_element_type=f32
    )
    score_grad = again_attention * (
        weight_grad - jnp.sum(again_attention * weight_grad, axis=-1, keepdims=True)
    )
    score_grad_b = score_grad.astype(bf16)
    query_grad = (
        jnp.einsum("ghqk,gkhd->gqhd", score_grad_b, key_heads, preferred_element_type=f32)
        * head_scale
    )
    key_grad = (
        jnp.einsum("ghqk,gqhd->gkhd", score_grad_b, queries, preferred_element_type=f32)
        * head_scale
    )
    query_grad_b = query_grad.reshape(tokens, D).astype(bf16)
    key_grad_b = key_grad.reshape(tokens, D).astype(bf16)
    value_grad_b = value_grad.reshape(tokens, D).astype(bf16)
    merged_grad_b = jnp.concatenate([query_grad_b, key_grad_b, value_grad_b], axis=1)
    grad_qkv = matmul_left(merged_grad_b, normed_b)
    grad_bias_q = jnp.sum(query_grad_b, axis=0, dtype=f32)
    grad_bias_v = jnp.sum(value_grad_b, axis=0, dtype=f32)
    input_part, grad_gain_one, grad_shift_one = first_norm_back(matmul_plain(merged_grad_b, qkv_w))
    input_grad = (middle_grad + input_part).reshape(count_img, PATCHES, D)
    vector_grad = jnp.concatenate(
        [
            jnp.stack(
                [
                    grad_gain_one,
                    grad_shift_one,
                    grad_gain_two,
                    grad_shift_two,
                    grad_bias_q,
                    grad_bias_v,
                    grad_bias_o,
                ]
            ),
            grad_bias_up.reshape(FF // D, D),
            grad_bias_down[None, :],
            jnp.zeros((tile_rows - 8 - FF // D, D), f32),
        ],
        axis=0,
    )
    grad_rows = jnp.concatenate(
        [grad_qkv, grad_out, grad_up, grad_down.reshape(FF, D), grad_proj, vector_grad], axis=0
    )
    by_tile = jnp.transpose(grad_rows.reshape(tile_count, n_dp, part_rows, D), (1, 0, 2, 3))
    buffer = jnp.zeros((n_dp, n_rep * slot_count, part_rows, D), f32).at[:, placed].set(by_tile)
    reduced = lax.psum_scatter(
        buffer.reshape(n_dp * n_rep, slot_count, part_rows, D),
        ("dp", "rep"),
        scatter_dimension=0,
        tiled=True,
    )
    new_first = beta_one * first_moment + (1.0 - beta_one) * reduced
    new_second = beta_two * second_moment + (1.0 - beta_two) * reduced * reduced
    step_dir = new_first / (1.0 - beta_one**STEP)
    step_norm = jnp.sqrt(new_second / (1.0 - beta_two**STEP)) + adam_eps
    new_master = master - learn_rate * (step_dir / step_norm + decay_rate * master)
    return (block_out.reshape(count_img, PATCHES, D), input_grad, new_master, new_first, new_second)


def solution(mesh):
    in_specs = (
        P(("dp", "rep"), None, None),
        P(("dp", "rep"), None),
        P(("dp", "rep"), None),
        P(),
        P(),
        P("rep", None, "dp", None),
        P("rep", None, "dp", None),
        P("rep", None, "dp", None),
    )
    out_specs = (
        P(("dp", "rep"), None, None),
        P(("dp", "rep"), None, None),
        P("rep", None, "dp", None),
        P("rep", None, "dp", None),
        P("rep", None, "dp", None),
    )
    return jax.shard_map(shards, mesh=mesh, in_specs=in_specs, out_specs=out_specs, check_vma=False)
```

profile of v0, /device:TPU:0, one launch (start us, length us, event | category | flops | bytes accessed | tf_op | source)
XLA Modules:
  0.0 1257.4 jit_solution(8139077843981678223)
XLA Ops:
  15.0 44.8 %all-gather = bf16[32,5,512]{2,1,0:T(8,128)(2,1)S(1)} all-gather(bf16[1,5,512]{2,1,0:T(8,128)(2,1)S(1)} %fusion.55), channel_id=1, replica_groups=mesh['dp'=2,'rep'=16] {'dp','rep'}, dimensions={0}, use_global_device_ids=true | all-gather | bytes 168960 | tf_op jit(solution)/shard_map/all_gather | solution.py:159
  61.9 107.7 %all-gather.4.cloned.1.call-done = bf16[32,8,64,768]{3,2,1,0:T(8,128)(2,1)} async-done(((bf16[1,8,64,768]{3,2,1,0:T(8,128)(2,1)}), bf16[32,8,64,768]{3,2,1,0:T(8,128)(2,1)}) %all-gather.4.cloned.1.call-update) | async-done | bytes 25165840 | tf_op jit(solution)/shard_map/all_gather | solution.py:76
  169.6 16.4 %gather_fusion = bf16[77,2,64,768]{3,2,1,0:T(8,128)(2,1)} fusion(bf16[2,128,64,768]{3,2,1,0:T(8,128)(2,1)} %bitcast.81, s32[1024]{0:T(1024)S(1)} %pad_clamp_fusion), kind=kCustom, calls=%fused_computation | custom fusion | bytes 30277940 | tf_op jit(solution)/shard_map/jit(_take)/gather | solution.py:78
  186.0 7.9 broadcast_select_fusion
  201.8 8.6 fusion.66
  213.0 8.6 reshape.290
  221.6 5.1 fusion.70
  228.6 5.7 reshape.329
  234.4 6.1 copy.68
  240.4 4.2 reshape.330
  244.7 5.4 copy.69
  250.1 4.2 reshape.328
  254.3 6.0 copy.70
  260.3 4.7 fusion.12
  265.1 3.8 fusion.6
  269.9 3.4 convert_bitcast_fusion
  274.8 3.7 convert_element_type.185
  278.5 4.4 fusion.67
  283.4 34.2 %multiply_convert_fusion.1 = (bf16[980,3072]{1,0:T(8,128)(2,1)S(1)}, f32[980,3072]{1,0:T(8,128)}, f32[980,3072]{1,0:T(8,128)}) fusion(f32[3072]{0:T(1024)S(1)} %copy-done.33, bf16[3072,768]{1,0:T(8,128)(2,1)} %bitcast.86, f32[980,768]{1,0:T(8,128)S(1)} %get-tuple-element.47, f32[768]{0:T(1024)S(1)} %copy-done.42, f32[768]{0:T(1024)S(1)} %get-tuple-element.13, ...), kind=kOutput, calls=%fused_computation.13 | convolution fusion | flops 4826680320 | bytes 37861024 | tf_op jit(solution)/shard_map/dot_general | solution.py:30
  320.2 6.0 add_convert_fusion.3
  326.2 3.2 reshape.291
  334.3 39.3 %all-gather.1 = bf16[32,5,512]{2,1,0:T(8,128)(2,1)S(1)} all-gather(bf16[1,5,512]{2,1,0:T(8,128)(2,1)S(1)} %fusion.52), channel_id=1, replica_groups=mesh['dp'=2,'rep'=16] {'dp','rep'}, dimensions={0}, use_global_device_ids=true | all-gather | bytes 168960 | tf_op jit(solution)/shard_map/all_gather | solution.py:158
  378.3 121.5 %all-reduce.3.cloned.1.call-done = f32[160,512]{1,0:T(8,128)} async-done(((f32[160,512]{1,0:T(8,128)}), f32[160,512]{1,0:T(8,128)}) %all-reduce.3.cloned.1.call-update) | async-done | bytes 327696
  505.1 3.4 convert_element_type.200
  508.5 17.1 %convert_reduce_fusion = (f32[3072]{0:T(1024)}, bf16[980,3072]{1,0:T(8,128)(2,1)S(1)}) fusion(f32[980,3072]{1,0:T(8,128)} %get-tuple-element.33, f32[980,3072]{1,0:T(8,128)} %get-tuple-element.48, f32[3072]{0:T(1024)S(1)} %copy-done.34, bf16[980,768]{1,0:T(8,128)(2,1)} %convert_element_type.200, bf16[768,3072]{1,0:T(8,128)(2,1)} %reshape.290), kind=kOutput, calls=%fused_computation.11 | convolution fusion | flops 4675396608 | bytes 36354048 | tf_op jit(solution)/shard_map/dot_general | solution.py:26
  525.6 8.3 multiply_reduce_fusion.2
  533.9 8.4 fusion.60
  543.9 3.0 fusion.64
  549.0 11.0 fusion.20
  565.9 4.2 reshape.331
  570.1 5.2 copy.74
  575.3 9.1 convert_reduce_fusion.1
  584.4 10.7 multiply_reduce_fusion
  595.1 7.3 multiply_convert_fusion
  602.4 3.4 fusion.18
  610.0 3.7 convert_element_type.214
  613.7 3.0 copy.78
  616.7 3.5 convert_element_type.207
  620.1 3.0 copy.81
  623.1 3.5 convert_element_type.210
  630.5 7.9 multiply_reduce_fusion.3
  638.4 6.6 fusion.21
  645.1 11.6 reshape.294
  656.9 76.2 %concatenate.7 = f32[9856,768]{1,0:T(8,128)} concatenate(f32[2304,768]{1,0:T(8,128)} %fusion.21, f32[768,768]{1,0:T(8,128)} %fusion.42, f32[3072,768]{1,0:T(8,128)} %fusion.60, f32[3072,768]{1,0:T(8,128)} %reshape.294, f32[512,768]{1,0:T(8,128)} %fusion.56, f32[1,768]{1,0:T(1,128)S(1)} %reshape.295, f32[1,768]{1,0:T(1,128)S(1)} %reshape.296, f32[1,768]{1,0:T(1,128)S(1)} %reshape.297, ...), dimensions={0} | concatenate | bytes 60555264 | tf_op jit(solution)/shard_map/concatenate | solution.py:244
  733.1 16.5 %broadcast_in_dim.97 = f32[2,128,64,768]{3,2,1,0:T(8,128)} broadcast(f32[]{:T(128)} %constant.62.clone.1), dimensions={} | broadcast | bytes 50331652 | tf_op jit(solution)/shard_map/broadcast_in_dim | solution.py:248
  749.5 62.5 %scatter_fusion = f32[2,128,64,768]{3,2,1,0:T(8,128)} fusion(f32[2,128,64,768]{3,2,1,0:T(8,128)} %broadcast_in_dim.97, s32[77]{0:T(128)S(1)} %copy-done.40, f32[77,2,64,768]{3,2,1,0:T(8,128)} %bitcast.79), kind=kCustom, calls=%fused_computation.1 | custom fusion | bytes 90833200 | tf_op jit(solution)/shard_map/scatter | solution.py:248
  818.3 426.5 %reduce-scatter.2.cloned.1.call-done = f32[1,8,64,768]{3,2,1,0:T(8,128)} async-done(((f32[32,8,64,768]{3,2,1,0:T(8,128)}), f32[1,8,64,768]{3,2,1,0:T(8,128)}) %reduce-scatter.2.cloned.1.call-update) | async-done | bytes 1572880 | tf_op jit(solution)/shard_map/reduce_scatter | solution.py:249
  1244.8 5.8 multiply_subtract_fusion
  (212 shorter events, 66.4 us)
Async XLA Ops:
  7.2 3.5 copy-start.2
  7.2 162.4 %all-gather.4.cloned.1.call-start = ((), (), s32[]{:S(2)}) async-start(), calls=%async_computation.1 | async-start | bytes 25952256 | tf_op jit(solution)/shard_map/all_gather | solution.py:76
  9.7 490.1 %all-reduce.3.cloned.1.call-start = ((), (), s32[]{:S(2)}) async-start(), calls=%async_computation.3 | async-start | bytes 655360
  9.9 2.9 copy-start.36
  10.0 3.5 copy-start.20
  10.7 4.2 copy-start.22
  12.6 48.0 %copy-start.50 = (s32[160]{0:T(256)S(1)}, s32[160]{0:T(256)}, u32[]{:S(2)}) copy-start(s32[160]{0:T(256)} %param.11) | copy-start | bytes 1924
  12.6 49.1 %copy-start.41 = (s32[77]{0:T(128)S(1)}, s32[77]{0:T(128)}, u32[]{:S(2)}) copy-start(s32[77]{0:T(128)} %param.12) | copy-start | bytes 928
  14.2 171.7 %copy-start.26 = (f32[980]{0:T(1024)}, f32[980]{0:T(1024)S(1)}, u32[]{:S(2)}) copy-start(f32[980]{0:T(1024)S(1)} %add.254) | copy-start | bytes 11764
  15.0 46.9 %copy-start.47 = (f32[5]{0:T(128)}, f32[5]{0:T(128)S(1)}, u32[]{:S(2)}) copy-start(f32[5]{0:T(128)S(1)} %add_rsqrt_fusion) | copy-start | bytes 64
  61.8 124.1 %copy-start.39 = (s32[77]{0:T(128)}, s32[77]{0:T(128)S(1)}, u32[]{:S(2)}) copy-start(s32[77]{0:T(128)S(1)} %get-tuple-element.35) | copy-start | bytes 928
  193.9 5.9 copy-start.1
  194.7 16.3 %copy-start.24 = (f32[768]{0:T(1024)}, f32[768]{0:T(1024)S(1)}, u32[]{:S(2)}) copy-start(f32[768]{0:T(1024)S(1)} %get-tuple-element.18) | copy-start | bytes 9220
  194.7 16.3 %copy-start.30 = (f32[768]{0:T(1024)}, f32[768]{0:T(1024)S(1)}, u32[]{:S(2)}) copy-start(f32[768]{0:T(1024)S(1)} %get-tuple-element.17) | copy-start | bytes 9220
  213.0 8.6 copy-start.15
  250.1 10.3 copy-start.3
  265.1 4.8 copy-start
  265.1 4.8 copy-start.11
  274.8 3.7 copy-start.45
  278.4 4.9 copy-start.33
  278.5 4.9 copy-start.42
  278.5 41.7 %slice-start.3 = ((s8[4718592]{0:T(1024)(128)(4,1)}), s8[4194304]{0:T(1024)(128)(4,1)S(1)}, s32[]{:S(2)}) async-start(s8[4718592]{0:T(1024)(128)(4,1)} %bitcast.84), calls=%async_computation.7 | async-start | bytes 8388608
  283.4 36.8 %slice-start.4 = ((s8[4718592]{0:T(1024)(128)(4,1)}), s8[524288]{0:T(1024)(128)(4,1)S(1)}, s32[]{:S(2)}) async-start(s8[4718592]{0:T(1024)(128)(4,1)} %bitcast.84), calls=%async_computation.8 | async-start | bytes 1048576
  283.4 36.8 %copy-start.44 = (f32[768]{0:T(1024)S(1)}, f32[768]{0:T(1024)}, u32[]{:S(2)}) copy-start(f32[768]{0:T(1024)} %get-tuple-element.11) | copy-start | bytes 9220
  326.2 5.0 copy-start.37
  326.2 7.2 copy-start.19
  326.2 48.1 %copy-start.23 = (bf16[5,512]{1,0:T(8,128)(2,1)S(1)}, bf16[5,512]{1,0:T(8,128)(2,1)}, u32[]{:S(2)}) copy-start(bf16[5,512]{1,0:T(8,128)(2,1)} %param.10) | copy-start | bytes 15364
  326.2 48.1 %copy-start.48 = (f32[5]{0:T(128)S(1)}, f32[5]{0:T(128)}, u32[]{:S(2)}) copy-start(f32[5]{0:T(128)} %copy-done.47) | copy-start | bytes 64
  326.2 49.5 %copy-start.51 = (s32[160]{0:T(256)S(1)}, s32[160]{0:T(256)}, u32[]{:S(2)}) copy-start(s32[160]{0:T(256)} %param.11) | copy-start | bytes 1924
  326.2 49.5 %copy-start.52 = (s32[5]{0:T(128)S(1)}, s32[5]{0:T(128)}, u32[]{:S(2)}) copy-start(s32[5]{0:T(128)} %iota_add_fusion) | copy-start | bytes 64
  329.5 174.1 %copy-start.21 = (f32[5,196]{1,0:T(8,128)S(1)}, f32[5,196]{1,0:T(8,128)}, u32[]{:S(2)}) copy-start(f32[5,196]{1,0:T(8,128)} %copy-done.20) | copy-start | bytes 11764
  333.4 44.9 %copy-start.49 = (f32[5]{0:T(128)}, f32[5]{0:T(128)S(1)}, u32[]{:S(2)}) copy-start(f32[5]{0:T(128)S(1)} %add_rsqrt_fusion.1) | copy-start | bytes 64
  376.8 131.7 %copy-start.34 = (f32[3072]{0:T(1024)S(1)}, f32[3072]{0:T(1024)}, u32[]{:S(2)}) copy-start(f32[3072]{0:T(1024)} %add.236) | copy-start | bytes 36868
  376.8 868.0 %reduce-scatter.2.cloned.1.call-start = ((), (), s32[]{:S(2)}) async-start(), calls=%async_computation.2 | async-start | bytes 51904512 | tf_op jit(solution)/shard_map/reduce_scatter | solution.py:249
  525.6 8.3 copy-start.43
  549.0 11.0 copy-start.8
  549.0 11.0 copy-start.9
  575.3 9.1 copy-start.12
  575.3 19.8 %slice-start = ((s8[12288000]{0:T(1024)(128)(4,1)}), s8[4194304]{0:T(1024)(128)(4,1)S(1)}, s32[]{:S(2)}) async-start(s8[12288000]{0:T(1024)(128)(4,1)} %bitcast.77), calls=%async_computation.4 | async-start | bytes 8388608
  575.3 19.8 %slice-start.1 = ((s8[12288000]{0:T(1024)(128)(4,1)}), s8[4194304]{0:T(1024)(128)(4,1)S(1)}, s32[]{:S(2)}) async-start(s8[12288000]{0:T(1024)(128)(4,1)} %bitcast.77), calls=%async_computation.5 | async-start | bytes 8388608
  584.4 10.7 slice-start.2
  595.1 7.3 copy-start.5
  602.4 3.5 copy-start.4
  630.5 7.9 copy-start.31
  638.4 6.6 copy-start.35
  638.4 6.6 copy-start.46
  733.1 16.5 %copy-start.40 = (s32[77]{0:T(128)S(1)}, s32[77]{0:T(128)}, u32[]{:S(2)}) copy-start(s32[77]{0:T(128)} %copy-done.39) | copy-start | bytes 928
  812.7 3.0 copy-start.7
  (15 other events, 28.2 us)
Sparse Core Ops, SparseCore 0:
  11.5 158.0 all-gather.3
  376.9 122.8 all-reduce.2
  812.2 432.5 reduce-scatter.1
where the time goes:
time: 1260 us
  waiting for transfers between devices  656 us (52%)
  local copies, waits for them, and re-layouts  301 us (24%)
  matrix products  158 us (13%)
  blocking collectives  84 us (7%)
  other arithmetic  44.3 us (4%)
  between operations  14.6 us (1%)
    reduce_scatter x1, waiting for transfers between devices, shards(): lax.psum_scatter(buffer.reshape(n_dp * n_rep, slot_count, part_rows, D),...  427 us
    unnamed x4, waiting for transfers between devices  122 us
    all_gather x1, waiting for transfers between devices, shards(): lax.all_gather(master.astype(bf16), ('dp', 'rep'), axis=0, tiled=True)  108 us
    concatenate x1, local copies, waits for them, and re-layouts, shards(): jnp.concatenate([grad_qkv, grad_out, grad_up, grad_down.reshape(FF, D), g...  76.2 us
    scatter x1, local copies, waits for them, and re-layouts, shards(): jnp.zeros((n_dp, n_rep * slot_count, part_rows, D), f32).at[:, placed]  62.5 us
    dot_general x7, matrix products, matmul_right(): lax.dot_general(left_side, right_side, (((1,), (1,)), ((), ())), preferre...  53.4 us
    all_gather x1, blocking collectives, shards(): lax.all_gather(own_text, ('dp', 'rep'), axis=0, tiled=True)  44.8 us
    all_gather x1, blocking collectives, shards(): lax.all_gather(own_image, ('dp', 'rep'), axis=0, tiled=True)  39.3 us
  transfers between devices with their start and end apart: 3, of which 3 were waited for; matrix products, arithmetic and copies ran while one was open for 1% of the time, Pallas kernels for 0%

commit v1 on v0

v1 whole, which is shorter than its diff:
```python
import functools

import jax
import jax.numpy as jnp
from jax import lax
from jax.experimental import pallas as pl
from jax.experimental.pallas import tpu as pltpu
from jax.sharding import PartitionSpec as P

D = 768
HEADS = 12
HEAD = 64
FF = 3072
EMB = 512
PATCHES = 196
STEP = 10
ROWS = 208
TR = 128

logit_scale = 50.0
learn_rate = 0.03
beta_one = 0.9
beta_two = 0.999
adam_eps = 1e-08
decay_rate = 0.05
norm_eps = 1e-05
unit_eps = 1e-06
masked_score = -1000000000.0

bf16 = jnp.bfloat16
f32 = jnp.float32
AXES = ("dp", "rep")
MIB = 1 << 20

X, Z, Y, CORE = range(4)
PIECES = [(x, z, y) for x in range(2) for z in range(4) for y in range(2)]

QKV_TILES = 3 * D // TR
OUT_TILES = D // TR
UP_TILES = FF // TR
DOWN_TILES = FF // TR
PROJ_TILES = EMB // TR
DOWN_FIRST = QKV_TILES + OUT_TILES + UP_TILES
PROJ_FIRST = DOWN_FIRST + DOWN_TILES
VEC_TILE = PROJ_FIRST + PROJ_TILES
PACK = (D + FF) // 3
CHUNK_TILES = (
    (QKV_TILES // 2, 0),
    (OUT_TILES // 2, QKV_TILES),
    (UP_TILES // 2, QKV_TILES + OUT_TILES),
    (DOWN_TILES // 2, DOWN_FIRST),
    (PROJ_TILES // 2, PROJ_FIRST),
)
CHUNK_AT = ((0, 0), (0, 9), (1, 0), (2, 0), (2, 12))
SAME_CORE = [[i * 2 + c for i in range(8)] for c in range(2)]


def nn(a, b):
    return lax.dot_general(a, b, (((1,), (0,)), ((), ())), preferred_element_type=f32)


def nt(a, b):
    return lax.dot_general(a, b, (((1,), (1,)), ((), ())), preferred_element_type=f32)


def tn(a, b):
    return lax.dot_general(a, b, (((0,), (0,)), ((), ())), preferred_element_type=f32)


def call(kernel, outs, ins, in_specs, out_specs, grid=None, scratch=(), flops=0, vmem=56, prefetch=0):
    moved = sum(a.size * a.dtype.itemsize for a in ins) + sum(o.size * o.dtype.itemsize for o in outs)
    params = pltpu.CompilerParams(
        vmem_limit_bytes=vmem * MIB,
        dimension_semantics=("arbitrary",) * len(grid or ()) or None,
    )
    return pl.pallas_call(
        kernel,
        out_shape=tuple(outs),
        grid_spec=pltpu.PrefetchScalarGridSpec(
            num_scalar_prefetch=prefetch,
            grid=grid or (1,),
            in_specs=in_specs,
            out_specs=tuple(out_specs),
            scratch_shapes=list(scratch),
        ),
        compiler_params=params,
        cost_estimate=pl.CostEstimate(flops=int(flops), bytes_accessed=int(moved), transcendentals=0),
    )(*ins)


def whole(shape):
    return pl.BlockSpec(shape, lambda *_: (0,) * len(shape))


def rows_at(rows, cols):
    return pl.BlockSpec((rows, cols), lambda i, *_: (i, 0))


def cols_at(rows, cols):
    return pl.BlockSpec((rows, cols), lambda i, *_: (0, i))


def sds(shape, dtype):
    return jax.ShapeDtypeStruct(shape, dtype)


class Weight:
    def __init__(self, arrays, tiles, first=0, quarters=False):
        self.arrays, self.tiles, self.first, self.quarters = tuple(arrays), tiles, first, quarters
        self.pieces = len(arrays) > 1
        self.specs = [pl.BlockSpec(memory_space=pl.ANY)] * len(arrays)
        shape = (tiles, TR // 4, FF) if quarters else (tiles, TR, D)
        self.scratch = [pltpu.VMEM(shape, bf16), pltpu.SemaphoreType.DMA((32 if self.pieces else 1,))]

    def copies(self, me, refs, out, sems):
        if not self.pieces:
            return [pltpu.make_async_copy(refs[0], out, sems.at[0])]
        copies = []
        half = self.tiles // 2
        for at, (c, x, y) in enumerate(sources(me)):
            for back in range(4):
                z = me[Z] ^ back
                if self.quarters:
                    row, col = x * 16, z * D + y * 384
                else:
                    row, col = x * 64 + z * 16, y * 384
                rows = pl.ds(pl.multiple_of(row, 16), 16)
                cols = pl.ds(pl.multiple_of(col, 128), 384)
                source = refs[at].at[back, pl.ds(self.first, half)]
                copies.append(
                    pltpu.make_async_copy(source, out.at[pl.ds(half * c, half), rows, cols], sems.at[len(copies)])
                )
        return copies

    def load(self, me, refs, out, sems):
        @pl.when(pl.program_id(0) == 0)
        def _():
            copies = self.copies(me, refs, out, sems)
            for copy in copies:
                copy.start()
            for copy in copies:
                copy.wait()


def normalized(x):
    center = x - jnp.mean(x, axis=-1, keepdims=True)
    spread = jnp.mean(center * center, axis=-1, keepdims=True)
    inverse = lax.rsqrt(spread + norm_eps)
    return center * inverse, inverse


def norm_back(grad, hat, inverse, gain):
    scaled = grad * gain
    first = jnp.mean(scaled, axis=-1, keepdims=True)
    second = jnp.mean(scaled * hat, axis=-1, keepdims=True)
    return inverse * (scaled - first - hat * second)


def column_sum(x):
    return jnp.sum(x, axis=0, keepdims=True)


def qkv_kernel(images, weight, me_ref, *refs):
    count = len(weight.arrays)
    pieces = refs[:count]
    x_ref, vec_in_ref, a_ref, qkv_ref, vec_ref, w_ref, sems, vec_half, vec_sems = refs[count:]
    j = pl.program_id(0)

    @pl.when(j == 0)
    def _():
        copies = weight.copies(me_ref, pieces, w_ref, sems)
        for copy in copies:
            copy.start()
        if weight.pieces:
            parts = []
            for at, (_, x, y) in list(enumerate(sources(me_ref)))[:4]:
                for back in range(4):
                    copy = pltpu.make_async_copy(pieces[at].at[back, 12], vec_half.at[y], vec_sems.at[len(parts)])
                    parts.append(((x == 0) & ((me_ref[Z] ^ back) == 0), copy))
            for here, copy in parts:
                pl.when(here)(copy.start)
            for here, copy in parts:
                pl.when(here)(copy.wait)
            vec_ref[...] = jnp.concatenate([vec_half[0], vec_half[1]], axis=1).astype(f32)
        else:
            vec_ref[...] = vec_in_ref[...]
        for i in range(images):
            hat, _ = normalized(x_ref[pl.ds(i * ROWS, ROWS), :].astype(f32))
            a_ref[pl.ds(i * ROWS, ROWS), :] = (hat * vec_ref[0:1, :] + vec_ref[1:2, :]).astype(bf16)
        for copy in copies:
            copy.wait()

    bias = jnp.where(j == 0, vec_ref[4:5, :], jnp.where(j == 2, vec_ref[5:6, :], 0.0))
    scale = jnp.where(j == 0, f32(HEAD**-0.5), f32(1.0))
    w = w_ref[pl.ds(6 * j, 6)].reshape(D, D)
    qkv_ref[...] = ((nt(a_ref[...], w) + bias) * scale).astype(bf16)


def qkv_forward(images, x, vec, weight, me):
    n = images * ROWS
    return call(
        functools.partial(qkv_kernel, images, weight),
        (sds((n, D), bf16), sds((n, 3 * D), bf16), sds((16, D), f32)),
        (me, *weight.arrays, x, vec),
        weight.specs + [whole((n, D)), whole((16, D))],
        [whole((n, D)), cols_at(n, D), whole((16, D))],
        grid=(3,),
        scratch=weight.scratch + [pltpu.VMEM((2, 16, 384), bf16), pltpu.SemaphoreType.DMA((16,))],
        flops=2 * n * D * 3 * D,
        prefetch=1,
    )


def attention_kernel(qkv_ref, mask_ref, o_ref, lse_ref):
    lane = lax.broadcasted_iota(jnp.int32, (ROWS, 2 * HEAD), 1)
    low_half = lane < HEAD
    valid = mask_ref[0] > 0.0
    lse_all = jnp.zeros((ROWS, 128), f32)
    for pair in range(HEADS // 2):
        at = pair * 2 * HEAD
        q = qkv_ref[:, at : at + 2 * HEAD]
        k = qkv_ref[:, D + at : D + at + 2 * HEAD]
        v = qkv_ref[:, 2 * D + at : 2 * D + at + 2 * HEAD]
        mixed = []
        for half in range(2):
            keep = low_half if half == 0 else jnp.logical_not(low_half)
            s = nt(q, jnp.where(keep, k, jnp.zeros_like(k)))
            s = jnp.where(valid, s, masked_score)
            top = jnp.max(s, axis=-1, keepdims=True)
            e = jnp.exp(s - top)
            total = jnp.sum(e, axis=-1, keepdims=True)
            p = e * (1.0 / total)
            mixed.append(nn(p.astype(bf16), v))
            lse_all = jnp.where(lane == 2 * pair + half, top + jnp.log(total), lse_all)
        o_ref[:, at : at + 2 * HEAD] = jnp.where(low_half, mixed[0], mixed[1]).astype(bf16)
    lse_ref[0] = jnp.transpose(lse_all)[0:16, :]


def attention_forward(images, qkv, mask_row):
    n = images * ROWS
    return call(
        attention_kernel,
        (sds((n, D), bf16), sds((images, 16, ROWS), f32)),
        (qkv, mask_row),
        [rows_at(ROWS, 3 * D), pl.BlockSpec((1, 1, ROWS), lambda i: (i, 0, 0))],
        [rows_at(ROWS, D), pl.BlockSpec((1, 16, ROWS), lambda i: (i, 0, 0))],
        grid=(images,),
        flops=4 * n * ROWS * D,
    )


def middle_kernel(weight, me_ref, *refs):
    count = len(weight.arrays)
    x_ref, o_ref, vec_ref, h_ref, m_ref, w_ref, sems = refs[count:]
    weight.load(me_ref, refs[:count], w_ref, sems)
    part = nt(o_ref[...], w_ref[...].reshape(D, D)) + vec_ref[6:7, :]
    middle = x_ref[...].astype(f32) + part
    h_ref[...] = middle
    hat, _ = normalized(middle)
    m_ref[...] = (hat * vec_ref[2:3, :] + vec_ref[3:4, :]).astype(bf16)


def middle_forward(images, x, o, vec, weight, me):
    n = images * ROWS
    return call(
        functools.partial(middle_kernel, weight),
        (sds((n, D), f32), sds((n, D), bf16)),
        (me, *weight.arrays, x, o, vec),
        weight.specs + [rows_at(ROWS, D), rows_at(ROWS, D), whole((16, D))],
        [rows_at(ROWS, D), rows_at(ROWS, D)],
        grid=(images,),
        scratch=weight.scratch,
        flops=2 * n * D * D,
        prefetch=1,
    )


def gelu_parts(u):
    r = jnp.abs(u) * 0.7071067811865476
    t = 1.0 / (1.0 + 0.3275911 * r)
    poly = t * (0.127414796 + t * (-0.142248368 + t * (0.7107068705 + t * (-0.7265760135 + t * 0.5307027145))))
    e = jnp.exp(-0.5 * u * u)
    tail = poly * e
    phi = jnp.where(u >= 0.0, 1.0 - tail, tail)
    return u * phi, phi + u * e * 0.3989422804014327


def up_kernel(images, weight, me_ref, *refs):
    count = len(weight.arrays)
    m_ref, bias_ref, sel_ref, act_ref, slope_ref, sum_ref, w_ref, sems = refs[count:]
    weight.load(me_ref, refs[:count], w_ref, sems)
    w = w_ref[pl.ds(6 * pl.program_id(0), 6)].reshape(D, D)
    total = jnp.zeros((16, D), f32)
    for i in range(images):
        at = pl.ds(i * ROWS, ROWS)
        u = nt(m_ref[at, :], w) + bias_ref[0]
        act, slope = gelu_parts(u)
        act = act.astype(bf16)
        act_ref[at, :] = act
        slope_ref[at, :] = slope.astype(bf16)
        total += nn(sel_ref[i], act)
    sum_ref[...] = total


def up_forward(images, m, weight, bias, sel, me):
    n = images * ROWS
    return call(
        functools.partial(up_kernel, images, weight),
        (sds((n, FF), bf16), sds((n, FF), bf16), sds((16, FF), f32)),
        (me, *weight.arrays, m, bias, sel),
        weight.specs
        + [whole((n, D)), pl.BlockSpec((1, 1, D), lambda j, *_: (j, 0, 0)), whole((images, 16, ROWS))],
        [cols_at(n, D), cols_at(n, D), cols_at(16, D)],
        grid=(FF // D,),
        scratch=weight.scratch,
        flops=2 * n * D * FF,
        prefetch=1,
    )


def down_kernel(weight, me_ref, *refs):
    count = len(weight.arrays)
    act_ref, h_ref, vec_ref, sel_ref, inv_ref, out_ref, pooled_ref, w_ref, sems, sum_ref = refs[count:]
    i = pl.program_id(0)
    weight.load(me_ref, refs[:count], w_ref, sems)
    y = nt(act_ref[...], w_ref[...].reshape(D, FF)) + vec_ref[11:12, :]
    out = (h_ref[...] + y).astype(bf16)
    out_ref[0] = out[0:PATCHES, :]
    part = nn(sel_ref[0], out)

    @pl.when(i == 0)
    def _():
        sum_ref[...] = part

    @pl.when(i > 0)
    def _():
        sum_ref[...] += part

    pooled_ref[...] = (sum_ref[...] * inv_ref[:, 0:1]).astype(bf16)


def down_forward(images, act, weight, h, vec, sel, inv_count, me):
    n = images * ROWS
    return call(
        functools.partial(down_kernel, weight),
        (sds((images, PATCHES, D), bf16), sds((16, D), bf16)),
        (me, *weight.arrays, act, h, vec, sel, inv_count),
        weight.specs
        + [
            rows_at(ROWS, FF),
            rows_at(ROWS, D),
            whole((16, D)),
            pl.BlockSpec((1, 16, ROWS), lambda i, *_: (i, 0, 0)),
            whole((16, 128)),
        ],
        [pl.BlockSpec((1, PATCHES, D), lambda i, *_: (i, 0, 0)), whole((16, D))],
        grid=(images,),
        scratch=weight.scratch + [pltpu.VMEM((16, D), f32)],
        flops=2 * n * D * FF,
        prefetch=1,
    )


def loss_kernel(total_images, proj, down, me_ref, first_ref, *refs):
    count = len(proj.arrays)
    pieces = refs[:count]
    if proj.pieces:
        down_pieces, rest = pieces, refs[count:]
    else:
        down_pieces, rest = refs[count : count + 1], refs[count + 1 :]
    text_ref, pooled_ref, order_ref, inv_ref, dz_ref, rank_ref, spread_ref, hidden_ref = rest[:8]
    proj_ref, proj_sems, down_ref, down_sems = rest[8:12]
    down_copies = down.copies(me_ref, down_pieces, down_ref, down_sems)
    proj_copies = proj.copies(me_ref, pieces, proj_ref, proj_sems)
    if proj.pieces:
        slab_ref, slab_sems = rest[12:]
        for at, (c, x, y) in enumerate(sources(me_ref)):
            for back in range(4):
                device = x * 16 + (me_ref[Z] ^ back) * 4 + y * 2 + c
                out = slab_ref.at[pl.ds(pl.multiple_of(device * 16, 16), 16)]
                proj_copies.append(pltpu.make_async_copy(pieces[at].at[back, 14], out, slab_sems.at[at * 4 + back]))
    for copy in proj_copies + down_copies:
        copy.start()
    for copy in proj_copies:
        copy.wait()
    if proj.pieces:
        images = total_images // 32
        shape = (total_images, 512)
        row = lax.broadcasted_iota(jnp.int32, shape, 0)
        col = lax.broadcasted_iota(jnp.int32, shape, 1)
        start = row // images * 16 + row % images
        held = slab_ref[...]
        left = nn(jnp.where(col == start, 1.0, 0.0).astype(bf16), held)
        right = nn(jnp.where(col == start + 8, 1.0, 0.0).astype(bf16), held[:, 0:128])
        text = jnp.concatenate([left, right], axis=1).astype(bf16)
    else:
        text = text_ref[...]
    proj_w = proj_ref[...].reshape(EMB, D)
    z = nt(pooled_ref[...], proj_w)
    square = jnp.sum(z * z, axis=-1, keepdims=True) + unit_eps
    inverse = lax.rsqrt(square)
    image = (z * inverse).astype(bf16)
    s = logit_scale * nt(image, text)
    shape = (total_images, total_images)
    hit = jnp.where(order_ref[:, 0:1] == lax.broadcasted_iota(jnp.int32, shape, 1), 1.0, 0.0)
    part = 1.0 / (2.0 * total_images)

    def grad_of(axis):
        top = jnp.max(s, axis=axis, keepdims=True)
        lse = top + jnp.log(jnp.sum(jnp.exp(s - top), axis=axis, keepdims=True))
        return ((jnp.exp(s - lse) - hit) * part).astype(bf16)

    de = logit_scale * (nn(grad_of(1), text) + nn(grad_of(0), text))
    dz = inverse * de - z * (inverse * inverse * inverse * jnp.sum(z * de, axis=-1, keepdims=True))
    dz = dz.astype(bf16)
    dz_ref[...] = dz
    pick = lax.broadcasted_iota(jnp.int32, (16, total_images), 1) == (
        first_ref[0] + lax.broadcasted_iota(jnp.int32, (16, total_images), 0)
    )
    own = nn(jnp.where(pick, 1.0, 0.0).astype(bf16), dz).astype(bf16)
    spread = nn(own, proj_w) * inv_ref[:, 0:1]
    spread_ref[...] = spread
    rank = spread.astype(bf16)
    rank_ref[...] = rank
    for copy in down_copies:
        copy.wait()
    hidden_ref[...] = nn(rank, down_ref[...].reshape(D, FF))


def loss_backward(me, first, pooled, text, order, proj, down, inv_count):
    total = pooled.shape[0]
    if proj.pieces:
        arrays, extra = proj.arrays, [pltpu.VMEM((512, 384), bf16), pltpu.SemaphoreType.DMA((32,))]
    else:
        arrays, extra = proj.arrays + down.arrays, []
    return call(
        functools.partial(loss_kernel, total, proj, down),
        (sds((total, EMB), bf16), sds((16, D), bf16), sds((16, D), f32), sds((16, FF), f32)),
        (me, first, *arrays, text, pooled, order, inv_count),
        [pl.BlockSpec(memory_space=pl.ANY)] * len(arrays)
        + [whole(text.shape), whole((total, D)), whole((total, 128)), whole((16, 128))],
        [whole((total, EMB)), whole((16, D)), whole((16, D)), whole((16, FF))],
        scratch=proj.scratch + down.scratch + extra,
        flops=6 * total * total * EMB + 2 * total * D * EMB + 32 * D * FF,
        prefetch=2,
    )


def weave(ref, value):
    for t in range(value.shape[0] // TR):
        for x, z, y in PIECES:
            row = t * TR + x * 64 + z * 16
            ref[x * 8 + z * 2 + y, pl.ds(t * 16, 16), :] = value[row : row + 16, y * 384 : y * 384 + 384]


def half_block(j, me):
    return (j // 2 + 1 - me[CORE]) % 2 * 2 + j % 2


def up_back_kernel(images, weight, me_ref, *refs):
    count = len(weight.arrays)
    slope_ref, m_ref, hidden_ref, col_ref, dm_ref, db_ref = refs[count : count + 6]
    w_ref, sems, du_ref = refs[-3:]
    j = pl.program_id(0)
    weight.load(me_ref, refs[:count], w_ref, sems)
    w = w_ref[pl.ds(6 * half_block(j, me_ref), 6)].reshape(D, D)
    for i in range(images):
        at = pl.ds(i * ROWS, ROWS)
        du = (slope_ref[at, :].astype(f32) * (col_ref[at, 0:1] * hidden_ref[i : i + 1, :])).astype(bf16)
        du_ref[at, :] = du
        part = nn(du, w)

        @pl.when(j == 0)
        def _():
            dm_ref[at, :] = part

        @pl.when(j > 0)
        def _():
            dm_ref[at, :] += part

    du = du_ref[...]
    db_ref[...] = nn(jnp.ones((16, images * ROWS), bf16), du)
    dw = tn(du, m_ref[...]).astype(bf16)
    if not weight.pieces:
        refs[count + 6][...] = dw
        return
    send_ref, keep_ref = refs[count + 6 : count + 8]

    @pl.when(j < 2)
    def _():
        weave(send_ref, dw)

    @pl.when(j >= 2)
    def _():
        weave(keep_ref, dw)


def up_backward(images, slope, m, weight, hidden, col, me):
    n = images * ROWS

    def cols(rows):
        return pl.BlockSpec((rows, D), lambda j, me: (0, half_block(j, me)))

    if weight.pieces:
        shapes = (sds((16, 192, 384), bf16),) * 2
        specs = [
            pl.BlockSpec((16, 96, 384), lambda j, me: (0, jnp.minimum(j, 1), 0)),
            pl.BlockSpec((16, 96, 384), lambda j, me: (0, jnp.maximum(j - 2, 0), 0)),
        ]
    else:
        shapes = (sds((FF, D), bf16),)
        specs = [pl.BlockSpec((D, D), lambda j, me: (half_block(j, me), 0))]
    return call(
        functools.partial(up_back_kernel, images, weight),
        (sds((n, D), f32), sds((16, FF), f32)) + shapes,
        (me, *weight.arrays, slope, m, hidden, col),
        weight.specs + [cols(n), whole((n, D)), cols(16), whole((n, 128))],
        [whole((n, D)), cols(16)] + specs,
        grid=(FF // D,),
        scratch=weight.scratch + [pltpu.VMEM((n, D), bf16)],
        flops=4 * n * D * FF,
        prefetch=1,
    )


def accumulate(i, ref, value):
    @pl.when(i == 0)
    def _():
        ref[...] = value

    @pl.when(i > 0)
    def _():
        ref[...] += value


def middle_back_kernel(images, weight, me_ref, *refs):
    count = len(weight.arrays)
    h_ref, dm_ref, col_ref, spread_ref, o_ref, vec_ref = refs[count : count + 6]
    dh_ref, do_ref, dw_ref, dvec_ref, w_ref, sems, acc_ref = refs[count + 6 :]
    i = pl.program_id(0)
    weight.load(me_ref, refs[:count], w_ref, sems)
    hat, inverse = normalized(h_ref[...])
    dm = dm_ref[...]
    part = norm_back(dm, hat, inverse, vec_ref[2:3, :])
    here = spread_ref[pl.ds(i, 1), :]
    dh = col_ref[:, 0:1] * here + part
    dh_ref[...] = dh
    dat = dh.astype(bf16)
    do_ref[...] = nn(dat, w_ref[...].reshape(D, D)).astype(bf16)
    accumulate(i, acc_ref, tn(dat, o_ref[...]))
    sums = jnp.concatenate(
        [
            column_sum(dm * hat),
            column_sum(dm),
            column_sum(dat.astype(f32)),
            column_sum(col_ref[:, 0:1]) * here.astype(bf16).astype(f32),
            jnp.zeros((4, D), f32),
        ],
        axis=0,
    )
    accumulate(i, dvec_ref, sums)

    @pl.when(i == images - 1)
    def _():
        dw = acc_ref[...].astype(bf16)
        if weight.pieces:
            for half in range(2):
                weave(dw_ref.at[half], dw[half * 384 : half * 384 + 384])
        else:
            dw_ref[...] = dw


def middle_backward(images, h, dm, col, spread, o, weight, vec, me):
    n = images * ROWS
    dw_shape = (2, 16, 48, 384) if weight.pieces else (D, D)
    return call(
        functools.partial(middle_back_kernel, images, weight),
        (sds((n, D), f32), sds((n, D), bf16), sds(dw_shape, bf16), sds((8, D), f32)),
        (me, *weight.arrays, h, dm, col, spread, o, vec),
        weight.specs
        + [
            rows_at(ROWS, D),
            rows_at(ROWS, D),
            rows_at(ROWS, 128),
            whole((16, D)),
            rows_at(ROWS, D),
            whole((16, D)),
        ],
        [rows_at(ROWS, D), rows_at(ROWS, D), whole(dw_shape), whole((8, D))],
        grid=(images,),
        scratch=weight.scratch + [pltpu.VMEM((D, D), f32)],
        flops=4 * n * D * D,
        prefetch=1,
    )


def attention_back_kernel(qkv_ref, do_ref, lse_ref, col_ref, dqkv_ref, db_ref):
    i = pl.program_id(0)
    low_half = lax.broadcasted_iota(jnp.int32, (ROWS, 2 * HEAD), 1) < HEAD
    valid = jnp.broadcast_to(col_ref[:, 0:1], (ROWS, ROWS)) > 0.0
    for pair in range(HEADS // 2):
        at = pair * 2 * HEAD
        q = qkv_ref[:, at : at + 2 * HEAD]
        k = qkv_ref[:, D + at : D + at + 2 * HEAD]
        v = qkv_ref[:, 2 * D + at : 2 * D + at + 2 * HEAD]
        do = do_ref[:, at : at + 2 * HEAD]
        dv, dk, dq = [], [], []
        for half in range(2):
            keep = low_half if half == 0 else jnp.logical_not(low_half)
            only_k = jnp.where(keep, k, jnp.zeros_like(k))
            only_v = jnp.where(keep, v, jnp.zeros_like(v))
            head = 2 * pair + half
            s = jnp.where(valid, nt(only_k, q), masked_score)
            p = jnp.exp(s - lse_ref[0, head : head + 1, :])
            dp = nt(only_v, do)
            share = jnp.sum(p * dp, axis=0, keepdims=True)
            ds = (p * (dp - share)).astype(bf16)
            dv.append(nn(p.astype(bf16), do))
            dk.append(nn(ds, q))
            dq.append(tn(ds, only_k))
        dqkv_ref[:, at : at + 2 * HEAD] = ((dq[0] + dq[1]) * (HEAD**-0.5)).astype(bf16)
        dqkv_ref[:, D + at : D + at + 2 * HEAD] = jnp.where(low_half, dk[0], dk[1]).astype(bf16)
        dqkv_ref[:, 2 * D + at : 2 * D + at + 2 * HEAD] = jnp.where(low_half, dv[0], dv[1]).astype(bf16)
    accumulate(i, db_ref, nn(jnp.ones((16, ROWS), bf16), dqkv_ref[...]))


def attention_backward(images, qkv, do, lse, col):
    n = images * ROWS
    return call(
        attention_back_kernel,
        (sds((n, 3 * D), bf16), sds((16, 3 * D), f32)),
        (qkv, do, lse, col),
        [
            rows_at(ROWS, 3 * D),
            rows_at(ROWS, D),
            pl.BlockSpec((1, 16, ROWS), lambda i: (i, 0, 0)),
            rows_at(ROWS, 128),
        ],
        [rows_at(ROWS, 3 * D), whole((16, 3 * D))],
        grid=(images,),
        flops=10 * n * ROWS * D,
    )


def qkv_grad_kernel(dqkv_ref, a_ref, dw_ref):
    dw_ref[...] = tn(dqkv_ref[...], a_ref[...]).astype(bf16)


def qkv_weight_grad(images, dqkv, a):
    n = images * ROWS
    return call(
        qkv_grad_kernel,
        (sds((3 * D, D), bf16),),
        (dqkv, a),
        [cols_at(n, D), whole((n, D))],
        [rows_at(D, D)],
        grid=(3,),
        flops=6 * n * D * D,
    )[0]


def qkv_grad_fast_kernel(_, dqkv_ref, a_ref, out_ref, pieces_ref):
    j = pl.program_id(0)

    @pl.when(j < 3)
    def _():
        weave(pieces_ref, tn(dqkv_ref[...], a_ref[...]).astype(bf16))

    @pl.when(j == 3)
    def _():
        pieces_ref[...] = out_ref[0]


def qkv_weight_grad_fast(images, dqkv, a, dw_out, me, other):
    n = images * ROWS

    def half(me):
        return 1 - me[CORE] if other else me[CORE]

    return call(
        qkv_grad_fast_kernel,
        (sds((16, 192, 384), bf16),),
        (me, dqkv, a, dw_out),
        [
            pl.BlockSpec((n, 384), lambda j, me: (0, half(me) * 3 + jnp.minimum(j, 2))),
            whole((n, D)),
            pl.BlockSpec((1, 16, 48, 384), lambda j, me: (half(me), 0, 0, 0)),
        ],
        [pl.BlockSpec((16, 48, 384), lambda j, me: (0, j, 0))],
        grid=(4,),
        flops=3 * n * D * D,
        prefetch=1,
    )[0]


def input_back_kernel(weight, me_ref, *refs):
    count = len(weight.arrays)
    x_ref, dqkv_ref, dh_ref, vec_ref, out_ref, dvec_ref, w_ref, sems = refs[count:]
    i = pl.program_id(0)
    weight.load(me_ref, refs[:count], w_ref, sems)
    da = nn(dqkv_ref[...], w_ref[...].reshape(3 * D, D))
    hat, inverse = normalized(x_ref[...].astype(f32))
    out = dh_ref[...] + norm_back(da, hat, inverse, vec_ref[0:1, :])
    out_ref[0] = out[0:PATCHES, :]
    sums = jnp.concatenate([column_sum(da * hat), column_sum(da), jnp.zeros((6, D), f32)], axis=0)
    accumulate(i, dvec_ref, sums)


def input_backward(images, x, dqkv, weight, dh, vec, me):
    n = images * ROWS
    return call(
        functools.partial(input_back_kernel, weight),
        (sds((images, PATCHES, D), f32), sds((8, D), f32)),
        (me, *weight.arrays, x, dqkv, dh, vec),
        weight.specs + [rows_at(ROWS, D), rows_at(ROWS, 3 * D), rows_at(ROWS, D), whole((16, D))],
        [pl.BlockSpec((1, PATCHES, D), lambda i, *_: (i, 0, 0)), whole((8, D))],
        grid=(images,),
        scratch=weight.scratch,
        flops=6 * n * D * D,
        prefetch=1,
    )


SUMMED, DOWN, PROJ, NONE, VEC = 0, 1, 2, 3, 4


def adam_kernel(part_rows, fast, kind_ref, row_ref, *refs):
    master_ref, first_ref, second_ref, summed_ref, down_ref, proj_ref, vec_ref = refs[:7]
    new_master_ref, new_first_ref, new_second_ref, grad_ref, woven_ref = refs[7:]
    kind = kind_ref[pl.program_id(0)]
    wide = FF // D

    @pl.when(kind == SUMMED)
    def _():
        if fast:
            for z in range(4):
                for y in range(2):
                    grad_ref[16 * z : 16 * z + 16, 384 * y : 384 * y + 384] = summed_ref[2 * z + y, 0].astype(f32)
        else:
            grad_ref[...] = summed_ref[0].astype(f32)

    @pl.when(kind == VEC)
    def _():
        grad_ref[...] = jnp.zeros_like(grad_ref)
        grad_ref[0 : vec_ref.shape[0], :] = vec_ref[...]

    @pl.when(kind == DOWN)
    def _():
        block = down_ref[...] if fast else down_ref[0]
        for c in range(D // 128):
            for b in range(wide):
                lanes = slice(b * D + c * 128, b * D + c * 128 + 128)
                woven_ref[c, pl.ds(b, part_rows // wide, stride=wide), :] = block[0 : part_rows // wide, lanes]
            grad_ref[:, c * 128 : (c + 1) * 128] = woven_ref[c]

    @pl.when(kind == PROJ)
    def _():
        grad_ref[...] = proj_ref[...]

    @pl.when(kind == NONE)
    def _():
        grad_ref[...] = jnp.zeros_like(grad_ref)

    grad = grad_ref[...]
    master = master_ref[0, 0]
    first = beta_one * first_ref[0, 0] + (1.0 - beta_one) * grad
    second = beta_two * second_ref[0, 0] + (1.0 - beta_two) * grad * grad
    new_first_ref[0, 0] = first
    new_second_ref[0, 0] = second
    direction = first / (1.0 - beta_one**STEP)
    size = jnp.sqrt(second / (1.0 - beta_two**STEP)) + adam_eps
    new_master_ref[0, 0] = master - learn_rate * (direction / size + decay_rate * master)


def adam(kind, row, master, first, second, summed, down, proj, vec, fast):
    slots, part_rows = master.shape[1:3]
    block = pl.BlockSpec((1, 1, part_rows, D), lambda s, *_: (0, s, 0, 0))
    each = part_rows * D // FF
    if fast:
        summed_spec = pl.BlockSpec((8, 1, 16, 384), lambda s, *_: (0, s, 0, 0))
        down_spec = pl.BlockSpec((each, FF), lambda s, kind, row: (jnp.where(kind[s] == DOWN, row[s] // each, 0), 0))
    else:
        summed_spec = pl.BlockSpec((1, part_rows, D), lambda s, *_: (s, 0, 0))
        down_spec = pl.BlockSpec((1,) + down.shape[1:], lambda s, *_: (s, 0, 0))
    return call(
        functools.partial(adam_kernel, part_rows, fast),
        (sds(master.shape, f32),) * 3,
        (kind, row, master, first, second, summed, down, proj, vec),
        [
            block,
            block,
            block,
            summed_spec,
            down_spec,
            pl.BlockSpec((part_rows, D), lambda s, kind, row: (jnp.where(kind[s] == PROJ, row[s] // part_rows, 0), 0)),
            whole(vec.shape),
        ],
        [block] * 3,
        grid=(slots,),
        scratch=[pltpu.VMEM((part_rows, D), f32), pltpu.VMEM((D // 128, part_rows, 128), f32)],
        flops=20 * slots * part_rows * D,
        prefetch=2,
    )


def rank_grad_kernel(images, *refs):
    dz_ref, pooled_ref, down_ref, proj_ref = refs[-4:]
    held = jnp.concatenate([ref[...].reshape(64, PACK) for ref in refs[:-4]], axis=0)
    shape = (512, 512)
    row = lax.broadcasted_iota(jnp.int32, shape, 0)
    col = lax.broadcasted_iota(jnp.int32, shape, 1)
    first = 0
    for segment in range(3):
        here = (row - col == segment * images) & (row // 16 == col // 16) & (col % 16 < images)
        rank = nn(jnp.where(here, 1.0, 0.0).astype(bf16), held[:, 0:D]).astype(bf16)
        part = held[:, D:PACK] if segment == 0 else held
        down_ref[:, first : first + part.shape[1]] = tn(rank, part)
        first += part.shape[1]
    proj_ref[...] = tn(dz_ref[...], pooled_ref[...])


def rank_grads(images, arrays, dz, pooled):
    return call(
        functools.partial(rank_grad_kernel, images),
        (sds((D, FF), f32), sds((EMB, D), f32)),
        (*arrays, dz, pooled),
        [whole(a.shape) for a in arrays] + [whole(dz.shape), whole(pooled.shape)],
        [whole((D, FF)), whole((EMB, D))],
        flops=1024 * D * FF,
    )


def slot_place(owner_list, slot_count):
    tile_count = owner_list.shape[0]
    earlier = jnp.tril(jnp.ones((tile_count, tile_count), jnp.int32), -1)
    same_owner = (owner_list[:, None] == owner_list[None, :]).astype(jnp.int32)
    return owner_list * slot_count + jnp.sum(same_owner * earlier, axis=1)


def gather_weights(master, placed):
    n_dp, n_rep = lax.axis_size("dp"), lax.axis_size("rep")
    slots, part_rows = master.shape[1:3]
    gathered = lax.all_gather(master.astype(bf16), AXES, axis=0, tiled=True)
    gathered = gathered.reshape(n_dp, n_rep * slots, part_rows, D)
    return jnp.transpose(jnp.take(gathered, placed, axis=1), (1, 0, 2, 3)).reshape(-1, D)


def scatter_grads(tiles, tile_of_slot, slots, part_rows):
    n_dp, n_rep = lax.axis_size("dp"), lax.axis_size("rep")
    count = tiles.shape[0]
    tiles = jnp.concatenate([tiles, jnp.zeros((1, TR, D), tiles.dtype)], axis=0)
    index = jnp.where(tile_of_slot < count, tile_of_slot, count)
    buffer = jnp.take(tiles, index, axis=0).reshape(n_rep * slots, n_dp, part_rows, D)
    buffer = jnp.transpose(buffer, (1, 0, 2, 3)).reshape(n_dp * n_rep, slots, part_rows, D)
    return lax.psum_scatter(buffer, AXES, scatter_dimension=0, tiled=True)[0]


def pairs(move):
    def number(x, z, y, c):
        return x * 16 + z * 4 + y * 2 + c

    return [(number(x, z, y, c), number(*move(x, z, y, c))) for x, z, y in PIECES for c in range(2)]


SWAP_CORE = pairs(lambda x, z, y, c: (x, z, y, 1 - c))
SWAP_X = pairs(lambda x, z, y, c: (1 - x, z, y, c))
SWAP_Y = pairs(lambda x, z, y, c: (x, z, 1 - y, c))
SWAP_XY = pairs(lambda x, z, y, c: (1 - x, z, 1 - y, c))
ACROSS_Z = [pairs(lambda x, z, y, c, k=k: (x, z ^ k, y, c)) for k in (1, 2, 3)]
CROSS_ONE = pairs(lambda x, z, y, c: (1 - x, z, y, c) if c == 0 else (x, z, 1 - y, c))
CROSS_TWO = pairs(lambda x, z, y, c: (x, z, 1 - y, c) if c == 0 else (1 - x, z, y, c))


def send(value, permutation):
    return lax.ppermute(value, AXES, permutation)


def add_kernel(count, _, *refs):
    out_ref = refs[-1]
    pieces = out_ref.shape[0]
    for p in range(pieces):
        total = refs[p * count][0].astype(f32)
        for k in range(1, count):
            total += refs[p * count + k][0].astype(f32)
        out_ref[p] = total.astype(bf16)


def add_pieces(sources, me, pieces, steps):
    rows = sources[0][0].shape[1]
    each = pieces // steps
    arrays, specs = [], []
    for p in range(each):
        for array, at in sources:
            arrays.append(array)
            specs.append(pl.BlockSpec((1, rows, 384), lambda i, me, p=p, at=at: (at(i * each + p, me), 0, 0)))
    return call(
        functools.partial(add_kernel, len(sources)),
        (sds((pieces, rows, 384), bf16),),
        (me, *arrays),
        specs,
        [pl.BlockSpec((each, rows, 384), lambda i, me: (i, 0, 0))],
        grid=(steps,),
        flops=pieces * rows * D,
        prefetch=1,
    )[0]


class PieceSum:
    def __init__(self, other, me):
        self.me = me
        self.one = send(other, SWAP_CORE)

    def first_send(self, i, me):
        return jnp.where(me[CORE] == 0, (1 - me[X]) * 8 + i, i * 2 + 1 - me[Y])

    def kept(self, i, me):
        return jnp.where(me[CORE] == 0, me[X] * 8 + i, i * 2 + me[Y])

    def second_send(self, i, me):
        return jnp.where(me[CORE] == 0, 2 * i + 1 - me[Y], (1 - me[X]) * 4 + i)

    def second_keep(self, i, me):
        return jnp.where(me[CORE] == 0, 2 * i + me[Y], me[X] * 4 + i)

    def cross_one(self):
        self.two = send(add_pieces([(self.mine, self.first_send), (self.one, self.first_send)], self.me, 8, 2), CROSS_ONE)

    def cross_two(self):
        def own(i, me):
            return self.kept(self.second_send(i, me), me)

        parts = [(self.mine, own), (self.one, own), (self.two, self.second_send)]
        self.three = send(add_pieces(parts, self.me, 4, 1), CROSS_TWO)

    def along_z(self, first):
        def z_at(i, me):
            return me[Z] ^ (first + i)

        def crossed(i, me):
            return self.second_keep(z_at(i, me), me)

        def own(i, me):
            return self.kept(crossed(i, me), me)

        return [(self.mine, own), (self.one, own), (self.two, crossed), (self.three, z_at)]

    def cross_z(self):
        parts = add_pieces(self.along_z(1), self.me, 3, 1)
        self.last = [send(parts[k], ACROSS_Z[k]) for k in range(3)]

    def total(self):
        arrived = [(part[None], lambda i, me: 0) for part in self.last]
        return add_pieces(self.along_z(0) + arrived, self.me, 1, 1)


def place_kernel(index_ref, mine_ref, theirs_ref, out_ref):
    for k in range(out_ref.shape[0]):
        at = index_ref[k]

        @pl.when(at < 24)
        def _():
            out_ref[k] = mine_ref[at]

        @pl.when((at >= 24) & (at < 48))
        def _():
            out_ref[k] = theirs_ref[at - 24]

        @pl.when(at >= 48)
        def _():
            out_ref[k] = jnp.zeros((16, 384), bf16)


def return_to_owners(sums, place):
    placed = call(
        place_kernel,
        (sds((64, 16, 384), bf16),),
        (place, sums, send(sums, SWAP_CORE)),
        [whole((24, 16, 384)), whole((24, 16, 384))],
        [whole((64, 16, 384))],
        prefetch=1,
    )[0]
    return lax.all_to_all(placed.reshape(8, 8, 16, 384), "rep", 0, 0, axis_index_groups=SAME_CORE)


def plan_kernel(owner_ref, me_ref, pick_ref, place_ref, kind_ref, row_ref, counts, placed, tile_of):
    x, c = me_ref[X], me_ref[CORE]
    rep = me_ref[Z] * 4 + me_ref[Y] * 2 + c

    @pl.loop(0, 16)
    def _(r):
        counts[r] = 0

    @pl.loop(0, 128)
    def _(k):
        tile_of[k] = 1 << 20

    @pl.loop(0, VEC_TILE + 1)
    def _(t):
        owner = owner_ref[t]
        at = owner * 8 + counts[owner]
        counts[owner] = counts[owner] + 1
        placed[t] = at
        tile_of[at] = t

    def slab(t):
        at = placed[t]
        owner = at // 8
        return jnp.where(owner % 2 == c, 0, 64) + owner // 2 * 8 + at % 8

    def fill(first, count, tile):
        @pl.loop(0, count)
        def _(k):
            pick_ref[first + k] = slab(tile + k)

    base = 0
    for tiles, tile in CHUNK_TILES:
        fill(base, tiles, tile + tiles * c)
        base += tiles
    pick_ref[base] = slab(VEC_TILE)

    @pl.loop(0, 64)
    def _(k):
        t = tile_of[k // 8 * 16 + c * 8 + k % 8]
        u = t - QKV_TILES
        v = u - OUT_TILES
        half = jnp.where(t < QKV_TILES, t // 9, jnp.where(u < OUT_TILES, u // 3, v // 12))
        place = jnp.where(t < QKV_TILES, t % 9, jnp.where(u < OUT_TILES, 9 + u % 3, 12 + v % 12))
        place_ref[k] = jnp.where(t < DOWN_FIRST, jnp.where(half == c, place, 24 + place), 48)

    @pl.loop(0, 8)
    def _(k):
        t = tile_of[rep * 8 + k]
        is_down = (t >= DOWN_FIRST) & (t < PROJ_FIRST)
        is_proj = (t >= PROJ_FIRST) & (t < VEC_TILE)
        kind = jnp.where(t < DOWN_FIRST, SUMMED, jnp.where(is_down, DOWN, jnp.where(is_proj, PROJ, NONE)))
        kind_ref[k] = jnp.where((t == VEC_TILE) & (x == 0), VEC, kind)
        row_ref[k] = jnp.where(
            is_down, ((t - DOWN_FIRST) * TR + x * 64) // 4, jnp.where(is_proj, (t - PROJ_FIRST) * TR + x * 64, 0)
        )


def plan(owner_list, me):
    smem = pl.BlockSpec(memory_space=pltpu.SMEM)
    sizes = (sum(tiles for tiles, _ in CHUNK_TILES) + 1, 64, 8, 8)
    return pl.pallas_call(
        plan_kernel,
        out_shape=tuple(sds((size,), jnp.int32) for size in sizes),
        in_specs=[smem, smem],
        out_specs=(smem,) * 4,
        scratch_shapes=[pltpu.SMEM((16,), jnp.int32), pltpu.SMEM((128,), jnp.int32), pltpu.SMEM((128,), jnp.int32)],
    )(owner_list, me)


def prepare_kernel(owner_ref, me_ref, master_ref, out_ref, lanes_ref, tile_ref):
    rep = me_ref[Z] * 4 + me_ref[Y] * 2 + me_ref[CORE]
    for s in range(9):
        tile_ref[s] = 0

    def note(t, held):
        here = owner_ref[t] == rep

        @pl.when(here)
        def _():
            tile_ref[held] = t

        return held + jnp.where(here, 1, 0)

    lax.fori_loop(DOWN_FIRST, PROJ_FIRST, note, lax.fori_loop(0, DOWN_FIRST, note, 0))
    for s in range(8):
        down = (tile_ref[s] >= DOWN_FIRST) & (tile_ref[s] < PROJ_FIRST)

        @pl.when(jnp.logical_not(down))
        def _():
            for z in range(4):
                for y in range(2):
                    out_ref[2 * z + y, s] = master_ref[0, s, 16 * z : 16 * z + 16, 384 * y : 384 * y + 384].astype(bf16)

        @pl.when(down)
        def _():
            for k in range(6):
                lanes_ref[k] = master_ref[0, s, :, 128 * k : 128 * k + 128]
            for z in range(4):
                for k in range(6):
                    part = lanes_ref[k, pl.ds(z, 16, stride=4), :]
                    out_ref[2 * z + k // 3, s, :, k % 3 * 128 : k % 3 * 128 + 128] = part.astype(bf16)


def pick_kernel(index_ref, mine_ref, theirs_ref, text_ref, one_ref, two_ref, three_ref):
    def slab(k, ref, j):
        at = index_ref[k]

        @pl.when(at < 64)
        def _():
            ref[j] = mine_ref[at]

        @pl.when(at >= 64)
        def _():
            ref[j] = theirs_ref[at - 64]

    k = 0
    for (tiles, _), (chunk, first) in zip(CHUNK_TILES, CHUNK_AT, strict=True):
        for j in range(tiles):
            slab(k, (one_ref, two_ref, three_ref)[chunk], first + j)
            k += 1
    slab(k, one_ref, 12)
    text = text_ref[...].astype(f32)
    count = text.shape[0]
    text = (text * lax.rsqrt(jnp.sum(text * text, axis=-1, keepdims=True) + unit_eps)).astype(bf16)
    three_ref[14] = jnp.zeros((16, 384), bf16)
    three_ref[14, 0:count, :] = text[:, 0:384]
    three_ref[14, 8 : 8 + count, 0:128] = text[:, 384:512]


class Spread:
    def __init__(self, block):
        self.parts = [block] + [send(block, move) for move in ACROSS_Z]

    def cross_one(self):
        self.ring = jnp.stack(self.parts)
        self.one = send(self.ring, CROSS_ONE)
        self.two = send(self.ring, CROSS_TWO)

    def cross_two(self):
        self.both = send(self.one, CROSS_TWO)
        self.near = [send(v, SWAP_CORE) for v in (self.ring, self.one, self.two)]

    def finish(self):
        self.near.append(send(self.both, SWAP_CORE))

    def arrays(self):
        return (self.ring, self.one, self.two, self.both, *self.near)


def meet(*values):
    return lax.optimization_barrier(values)


def sources(me):
    for other in range(2):
        c = me[CORE] if other == 0 else 1 - me[CORE]
        for crossed in range(4):
            one, two = crossed % 2, crossed // 2
            flip_x = jnp.where(c == 0, one, two)
            flip_y = jnp.where(c == 0, two, one)
            yield c, me[X] + flip_x - 2 * me[X] * flip_x, me[Y] + flip_y - 2 * me[Y] * flip_y


def pick_slabs(master, text_emb, owner_list, me):
    prepared = call(
        prepare_kernel,
        (sds((8, 8, 16, 384), bf16),),
        (owner_list, me, master),
        [whole(master.shape)],
        [whole((8, 8, 16, 384))],
        scratch=[pltpu.VMEM((6, 64, 128), f32), pltpu.SMEM((16,), jnp.int32)],
        prefetch=2,
    )[0]
    pick, place, kind, row = plan(owner_list, me)
    mine = lax.all_to_all(prepared, "rep", 0, 0, axis_index_groups=SAME_CORE).reshape(64, 16, 384)
    blocks = call(
        pick_kernel,
        tuple(sds((slabs, 16, 384), bf16) for slabs in (13, 12, 15)),
        (pick, mine, send(mine, SWAP_CORE), text_emb),
        [whole((64, 16, 384)), whole((64, 16, 384)), whole(text_emb.shape)],
        [whole((slabs, 16, 384)) for slabs in (13, 12, 15)],
        prefetch=1,
    )
    return blocks, place, kind, row


def shards(block_in, tissue, text_emb, text_order, owner_list, master, first_moment, second_moment):
    n_dp = lax.axis_size("dp")
    n_rep = lax.axis_size("rep")
    images = block_in.shape[0]
    slots, part_rows = master.shape[1:3]
    image_total = text_order.shape[0]
    n = images * ROWS
    dp_at, rep_at = lax.axis_index("dp"), lax.axis_index("rep")
    first_image = lax.axis_index(AXES) * images

    x = jnp.pad(block_in, ((0, 0), (0, ROWS - PATCHES), (0, 0))).reshape(n, D)
    valid = jnp.pad((tissue > 0).astype(f32), ((0, 0), (0, ROWS - PATCHES)))
    mask_row = valid[:, None, :]
    col = jnp.broadcast_to(valid.reshape(n, 1), (n, 128))
    numbers = jnp.arange(images, dtype=jnp.int32)
    sel = jnp.where(
        numbers[:, None, None] == jnp.arange(16, dtype=jnp.int32)[None, :, None], valid[:, None, :], 0.0
    ).astype(bf16)
    inv_count = jnp.pad(1.0 / jnp.sum(valid, axis=1), (0, 16 - images))
    inv_count = jnp.broadcast_to(inv_count[:, None], (16, 128))
    order = jnp.broadcast_to(text_order[:, None], (image_total, 128))
    first_image = first_image.astype(jnp.int32)[None]

    fast = (n_dp, n_rep, slots, part_rows) == (2, 16, 8, 64)
    if fast:
        me = jnp.stack([dp_at, rep_at // 4, rep_at // 2 % 2, rep_at % 2]).astype(jnp.int32)
        (block_one, block_two, block_three), place, kind, row = pick_slabs(master, text_emb, owner_list, me)
        x, col, sel, inv_count, order, first_image, block_one = lax.optimization_barrier(
            (x, col, sel, inv_count, order, first_image, block_one)
        )
        one = Spread(block_one)
        *one.parts, block_two, block_three = meet(*one.parts, block_two, block_three)
        two = Spread(block_two)
        one.cross_one()
        one.ring, one.one, one.two, *two.parts, block_three = meet(one.ring, one.one, one.two, *two.parts, block_three)
        one.cross_two()
        three = Spread(block_three)
        one.both, *one.near = meet(one.both, *one.near)
        one.finish()
        near, *two.parts = meet(one.near[3], *two.parts)
        one.near[3] = near
        two.cross_one()
        w_qkv = Weight(one.arrays(), QKV_TILES)
        w_out = Weight(one.arrays(), OUT_TILES, 9)
        a, qkv, vec = qkv_forward(images, x, jnp.zeros((16, D), f32), w_qkv, me)
        qkv, two.ring, two.one, two.two, *three.parts = meet(qkv, two.ring, two.one, two.two, *three.parts)
        two.cross_two()
        three.cross_one()
        o, lse = attention_forward(images, qkv, mask_row)
        o, two.both, *two.near = meet(o, two.both, *two.near)
        two.finish()
        w_up = Weight(two.arrays(), UP_TILES)
        h, m = middle_forward(images, x, o, vec, w_out, me)
        h, m, two.near[3], three.ring, three.one, three.two = meet(h, m, two.near[3], three.ring, three.one, three.two)
        three.cross_two()
        bias_up = vec[7 : 7 + FF // D].reshape(FF // D, 1, D)
        w_up = Weight(two.arrays(), UP_TILES)
        act, slope, act_sum = up_forward(images, m, w_up, bias_up, sel, me)
        act, three.both, *three.near = meet(act, three.both, *three.near)
        three.finish()
        w_down = Weight(three.arrays(), DOWN_TILES, quarters=True)
        w_proj = Weight(three.arrays(), PROJ_TILES, 12)
        all_text = jnp.zeros((16, 128), bf16)
    else:
        me = jnp.zeros((4,), jnp.int32)
        placed = slot_place(owner_list, slots)
        hits = placed[None, :] == jnp.arange(n_rep * slots, dtype=jnp.int32)[:, None]
        tile_ids = jnp.arange(owner_list.shape[0], dtype=jnp.int32)[None, :]
        tile_of_slot = jnp.where(jnp.any(hits, axis=1), jnp.sum(jnp.where(hits, tile_ids, 0), axis=1), 1 << 20)
        text = text_emb.astype(f32)
        own_text = (text * lax.rsqrt(jnp.sum(text * text, axis=-1, keepdims=True) + unit_eps)).astype(bf16)
        all_text = lax.all_gather(own_text, AXES, axis=0, tiled=True)
        tiles = gather_weights(master, placed).reshape(-1, TR, D)
        w_qkv = Weight([tiles[:QKV_TILES]], QKV_TILES)
        w_out = Weight([tiles[QKV_TILES : QKV_TILES + OUT_TILES]], OUT_TILES)
        w_up = Weight([tiles[QKV_TILES + OUT_TILES : DOWN_FIRST]], UP_TILES)
        w_down = Weight([tiles[DOWN_FIRST:PROJ_FIRST].reshape(DOWN_TILES, TR // 4, FF)], DOWN_TILES, quarters=True)
        w_proj = Weight([tiles[PROJ_FIRST:VEC_TILE]], PROJ_TILES)
        a, qkv, vec = qkv_forward(images, x, tiles[VEC_TILE, :16].astype(f32), w_qkv, me)
        bias_up = vec[7 : 7 + FF // D].reshape(FF // D, 1, D)
        o, lse = attention_forward(images, qkv, mask_row)
        h, m = middle_forward(images, x, o, vec, w_out, me)
        act, slope, act_sum = up_forward(images, m, w_up, bias_up, sel, me)
    block_out, pooled = down_forward(images, act, w_down, h, vec, sel, inv_count, me)

    pooled_all = lax.all_to_all(
        jnp.broadcast_to(pooled[None, :images], (n_dp * n_rep, images, D)), AXES, 0, 0
    ).reshape(image_total, D)
    dz_all, rank, spread, hidden = loss_backward(
        me, first_image, pooled_all, all_text, order, w_proj, w_down, inv_count
    )

    def vectors(g_one, g_two, g_bias, g_bias_up):
        parts = [
            g_one[0:2],
            g_two[0:2],
            g_bias[0:1, :D],
            g_bias[0:1, 2 * D :],
            g_two[2:3],
            g_bias_up[0].reshape(FF // D, D),
            g_two[3:4],
            jnp.zeros((16 - 8 - FF // D, D), f32),
        ]
        return jnp.concatenate(parts, axis=0)

    both = jnp.concatenate([rank[:images], act_sum[:images].astype(bf16)], axis=1)
    if fast:
        packed = jnp.concatenate([both[:, at * PACK : (at + 1) * PACK] for at in range(3)], axis=0)
        ranks = Spread(jnp.pad(packed, ((0, 16 - 3 * images), (0, 0))))
        dm, g_bias_up, other, mine = up_backward(images, slope, m, w_up, hidden, col, me)
        dm, other, mine, *ranks.parts = meet(dm, other, mine, *ranks.parts)
        up_sum = PieceSum(other, me)
        ranks.cross_one()
        dh, do, g_out, g_two = middle_backward(images, h, dm, col, spread, o, w_out, vec, me)
        dh, do, up_sum.mine, up_sum.one, ranks.ring, ranks.one, ranks.two = meet(
            dh, do, mine, up_sum.one, ranks.ring, ranks.one, ranks.two
        )
        up_sum.cross_one()
        ranks.cross_two()
        dqkv, g_bias = attention_backward(images, qkv, do, lse, col)
        dqkv, up_sum.two, ranks.both, *ranks.near = meet(dqkv, up_sum.two, ranks.both, *ranks.near)
        up_sum.cross_two()
        ranks.finish()
        other = qkv_weight_grad_fast(images, dqkv, a, g_out, me, True)
        other, dqkv, up_sum.three, ranks.near[3] = meet(other, dqkv, up_sum.three, ranks.near[3])
        qkv_sum = PieceSum(other, me)
        up_sum.cross_z()
        mine = qkv_weight_grad_fast(images, dqkv, a, g_out, me, False)
        dqkv, qkv_sum.mine, qkv_sum.one = meet(dqkv, mine, qkv_sum.one)
        qkv_sum.cross_one()
        input_grad, g_one = input_backward(images, x, dqkv, w_qkv, dh, vec, me)
        vec_sum = vectors(g_one, g_two, g_bias, g_bias_up)
        vec_sum, qkv_sum.two, *up_sum.last = meet(vec_sum, qkv_sum.two, *up_sum.last)
        qkv_sum.cross_two()
        vec_sum += send(vec_sum, SWAP_CORE)
        up_total = up_sum.total()
        vec_sum, up_total, qkv_sum.three = meet(vec_sum, up_total, qkv_sum.three)
        qkv_sum.cross_z()
        vec_sum += send(vec_sum, SWAP_X) + send(vec_sum, SWAP_Y) + send(vec_sum, SWAP_XY)
        g_down, g_proj = rank_grads(images, ranks.arrays(), dz_all, pooled_all)
        vec_sum, g_down, g_proj, *qkv_sum.last = meet(vec_sum, g_down, g_proj, *qkv_sum.last)
        sums = jnp.concatenate([qkv_sum.total()[0], up_total[0]], axis=0).reshape(24, 16, 384)
        vec_total = vec_sum + send(vec_sum, ACROSS_Z[0]) + send(vec_sum, ACROSS_Z[1]) + send(vec_sum, ACROSS_Z[2])
        summed = return_to_owners(sums, place)
    else:
        both_all = lax.all_gather(both, AXES, axis=0, tiled=True)
        dm, g_bias_up, g_up = up_backward(images, slope, m, w_up, hidden, col, me)
        dh, do, g_out, g_two = middle_backward(images, h, dm, col, spread, o, w_out, vec, me)
        dqkv, g_bias = attention_backward(images, qkv, do, lse, col)
        g_qkv = qkv_weight_grad(images, dqkv, a)
        input_grad, g_one = input_backward(images, x, dqkv, w_qkv, dh, vec, me)
        vec_total = vectors(g_one, g_two, g_bias, g_bias_up)
        mine = lax.dynamic_slice_in_dim(tile_of_slot, rep_at * slots, slots)
        first_row = dp_at * part_rows
        is_down = (mine >= DOWN_FIRST) & (mine < PROJ_FIRST)
        is_proj = (mine >= PROJ_FIRST) & (mine < VEC_TILE)
        kind = jnp.where(is_down, DOWN, jnp.where(is_proj, PROJ, jnp.where(mine <= VEC_TILE, SUMMED, NONE)))
        kind = kind.astype(jnp.int32)
        each = part_rows * D // FF
        row = jnp.where(is_proj, (mine - PROJ_FIRST) * TR + first_row, 0)
        down_rows = jnp.clip(((mine - DOWN_FIRST) * TR + first_row) * D // FF, 0, D - each)
        g_down = tn(both_all[:, :D], both_all[:, D:])
        g_down = jnp.stack([lax.dynamic_slice_in_dim(g_down, at, each) for at in down_rows])
        g_down = jnp.pad(g_down, ((0, 0), (0, max(0, 8 - each)), (0, 0)))
        g_proj = tn(dz_all, pooled_all)
        last = jnp.pad(vec_total, ((0, TR - 16), (0, 0))).astype(bf16)
        tiles = jnp.concatenate([g_qkv, g_out, g_up, last], axis=0).reshape(-1, TR, D)
        index = jnp.where(tile_of_slot == VEC_TILE, DOWN_FIRST, jnp.where(tile_of_slot < DOWN_FIRST, tile_of_slot, 1 << 20))
        summed = scatter_grads(tiles, index, slots, part_rows)
    new_master, new_first, new_second = adam(
        kind, row, master, first_moment, second_moment, summed, g_down, g_proj, vec_total, fast
    )
    return block_out, input_grad, new_master, new_first, new_second


def solution(mesh):
    in_specs = (
        P(("dp", "rep"), None, None),
        P(("dp", "rep"), None),
        P(("dp", "rep"), None),
        P(),
        P(),
        P("rep", None, "dp", None),
        P("rep", None, "dp", None),
        P("rep", None, "dp", None),
    )
    out_specs = (
        P(("dp", "rep"), None, None),
        P(("dp", "rep"), None, None),
        P("rep", None, "dp", None),
        P("rep", None, "dp", None),
        P("rep", None, "dp", None),
    )
    return jax.shard_map(shards, mesh=mesh, in_specs=in_specs, out_specs=out_specs, check_vma=False)
```

time: 1260 us -> 430 us (0.34)
  waiting for transfers between devices: 656 us -> 101 us
  local copies, waits for them, and re-layouts: 301 us -> 24.4 us
  Pallas kernels: 0 us -> 226 us
  matrix products: 158 us -> 0 us
  blocking collectives: 84 us -> 0 us
  starting transfers between devices: 0.12 us -> 67 us
  other arithmetic: 44.3 us -> 4.36 us
  between operations: 14.6 us -> 1.94 us
    reduce_scatter x1 -> x0, waiting for transfers between devices: 427 us -> none  [shards(): lax.psum_scatter(buffer.reshape(n_dp * n_rep, slot_count, part_rows, D),...]
    pallas_call x0 -> x26, Pallas kernels: none -> 226 us  [the longest x25 220 us: call(): pl.pallas_call(kernel, out_shape=tuple(outs), grid_spec=pltpu.PrefetchSca...]
    dot_general x26 -> x0, matrix products: 158 us -> none  [the longest x7 53.4 us: matmul_right(): lax.dot_general(left_side, right_side, (((1,), (1,)), ((), ())), preferre...]
    unnamed x4 -> x0, waiting for transfers between devices: 122 us -> none
    all_gather x1 -> x0, waiting for transfers between devices: 108 us -> none  [shards(): lax.all_gather(master.astype(bf16), ('dp', 'rep'), axis=0, tiled=True)]
    all_gather x2 -> x0, blocking collectives: 84 us -> none  [the longest x1 44.8 us: shards(): lax.all_gather(own_text, ('dp', 'rep'), axis=0, tiled=True)]
    concatenate x2 -> x1, local copies, waits for them, and re-layouts: 76.3 us -> 0.42 us  [vectors(): return jnp.concatenate(parts, axis=0)]
    ppermute x0 -> x61, waiting for transfers between devices: none -> 73.6 us  [send(): return lax.ppermute(value, AXES, permutation)]
  transfers between devices with their start and end apart: 3 -> 64, of which waited for: 3 -> 20; matrix products, arithmetic and copies ran while one was open for 1% -> 3% of each run, Pallas kernels for 0% -> 40%
where the time goes in v1:
time: 430 us; the launch traced here: 425 us
  Pallas kernels  226 us (53%)
  waiting for transfers between devices  101 us (23%)
  starting transfers between devices  67 us (16%)
  local copies, waits for them, and re-layouts  24.4 us (6%)
  other arithmetic  4.36 us (1%)
    pallas_call x25, Pallas kernels, call(): pl.pallas_call(kernel, out_shape=tuple(outs), grid_spec=pltpu.PrefetchSca...  220 us
    ppermute x61, waiting for transfers between devices, send(): return lax.ppermute(value, AXES, permutation)  73.6 us
    ppermute x61, starting transfers between devices, send(): return lax.ppermute(value, AXES, permutation)  52.8 us
    all_to_all x1, waiting for transfers between devices, pick_slabs(): lax.all_to_all(prepared, 'rep', 0, 0, axis_index_groups=SAME_CORE)  13.8 us
    all_to_all x1, waiting for transfers between devices, shards(): lax.all_to_all(jnp.broadcast_to(pooled[None, :images], (n_dp * n_rep, ima...  13 us
    unnamed x114, local copies, waits for them, and re-layouts  9.32 us
  transfers between devices with their start and end apart: 64, of which 20 were waited for; matrix products, arithmetic and copies ran while one was open for 3% of the time, Pallas kernels for 40%

profile of v1, /device:TPU:0, one launch (start us, length us, event | category | flops | bytes accessed | tf_op | source)
XLA Modules:
  0.0 424.7 jit_solution(5569298542844361676)
XLA Ops:
  1.3 3.3 shard_map.120
  4.6 7.3 %all-to-all-start = ((bf16[8,8,16,384]{3,2,1,0:T(8,128)(2,1)}), bf16[8,8,16,384]{3,2,1,0:T(8,128)(2,1)S(1)}, u32[]{:S(2)}, u32[]{:S(2)}) async-start(bf16[8,8,16,384]{3,2,1,0:T(8,128)(2,1)} %shard_map.120), calls=%async_computation | async-start | bytes 1572864 | tf_op jit(solution)/shard_map/all_to_all | solution.py:1159
  11.9 6.3 %shard_map.119 = (s32[39]{0:T(128)}, s32[64]{0:T(128)}, s32[8]{0:T(128)}, s32[8]{0:T(128)}) custom-call(s32[77]{0:T(128)} %owner_ref.3, s32[4]{0:T(128)} %pad_add_fusion.me_ref._), custom_call_target="tpu_custom_call" | custom-call | tf_op jit(solution)/shard_map/pallas_call | solution.py:1045
  18.2 13.8 %all-to-all-done = bf16[8,8,16,384]{3,2,1,0:T(8,128)(2,1)S(1)} async-done(((bf16[8,8,16,384]{3,2,1,0:T(8,128)(2,1)}), bf16[8,8,16,384]{3,2,1,0:T(8,128)(2,1)S(1)}, u32[]{:S(2)}, u32[]{:S(2)}) %all-to-all-start) | async-done | bytes 786464 | tf_op jit(solution)/shard_map/all_to_all | solution.py:1159
  35.2 3.3 shard_map.121
  42.6 2.6 collective-permute-start.1
  45.3 4.7 %collective-permute-done.3 = bf16[13,16,384]{2,1,0:T(8,128)(2,1)S(1)} collective-permute-done((bf16[13,16,384]{2,1,0:T(8,128)(2,1)}, bf16[13,16,384]{2,1,0:T(8,128)(2,1)S(1)}, u32[]{:S(2)}, u32[]{:S(2)}) %collective-permute-start.3) | collective-permute-done | bytes 159776 | tf_op jit(solution)/shard_map/ppermute | solution.py:875
  49.9 7.7 %collective-permute-done.2 = bf16[13,16,384]{2,1,0:T(8,128)(2,1)S(1)} collective-permute-done((bf16[13,16,384]{2,1,0:T(8,128)(2,1)}, bf16[13,16,384]{2,1,0:T(8,128)(2,1)S(1)}, u32[]{:S(2)}, u32[]{:S(2)}) %collective-permute-start.2) | collective-permute-done | bytes 159776 | tf_op jit(solution)/shard_map/ppermute | solution.py:875
  60.3 2.1 collective-permute-start.8
  62.4 2.3 collective-permute-start.6
  64.7 4.2 %collective-permute-done.8 = bf16[12,16,384]{2,1,0:T(8,128)(2,1)S(1)} collective-permute-done((bf16[12,16,384]{2,1,0:T(8,128)(2,1)S(1)}, bf16[12,16,384]{2,1,0:T(8,128)(2,1)S(1)}, u32[]{:S(2)}, u32[]{:S(2)}) %collective-permute-start.8) | collective-permute-done | bytes 147488 | tf_op jit(solution)/shard_map/ppermute | solution.py:875
  68.9 5.1 %collective-permute-done.7 = bf16[12,16,384]{2,1,0:T(8,128)(2,1)S(1)} collective-permute-done((bf16[12,16,384]{2,1,0:T(8,128)(2,1)S(1)}, bf16[12,16,384]{2,1,0:T(8,128)(2,1)S(1)}, u32[]{:S(2)}, u32[]{:S(2)}) %collective-permute-start.7) | collective-permute-done | bytes 147488 | tf_op jit(solution)/shard_map/ppermute | solution.py:875
  79.9 7.1 %collective-permute-done.9.refs_3_ = bf16[4,13,16,384]{3,2,1,0:T(8,128)(2,1)S(1)} collective-permute-done((bf16[4,13,16,384]{3,2,1,0:T(8,128)(2,1)S(1)}, bf16[4,13,16,384]{3,2,1,0:T(8,128)(2,1)S(1)}, u32[]{:S(2)}, u32[]{:S(2)}) %collective-permute-start.9) | collective-permute-done | bytes 639008 | tf_op jit(solution)/shard_map/ppermute | solution.py:875
  92.0 2.6 collective-permute-start.16
  95.2 11.8 %shard_map.122 = (bf16[1040,768]{1,0:T(8,128)(2,1)}, bf16[1040,2304]{1,0:T(8,128)(2,1)}, f32[16,768]{1,0:T(8,128)}) custom-call(s32[4]{0:T(128)} %pad_add_fusion.me_ref._, bf16[4,13,16,384]{3,2,1,0:T(8,128)(2,1)} %copy-done.4, bf16[4,13,16,384]{3,2,1,0:T(8,128)(2,1)} %copy-done.8, bf16[4,13,16,384]{3,2,1,0:T(8,128)(2,1)} %copy-done.7, ...), custom_call_target="tpu_custom_call" | custom-call | flops 3680501760 | bytes 13197328 | tf_op jit(solution)/shard_map/pallas_call | solution.py:76
  111.9 10.9 %shard_map.123 = (bf16[1040,768]{1,0:T(8,128)(2,1)}, f32[5,16,208]{2,1,0:T(8,128)}) custom-call(bf16[1040,2304]{1,0:T(8,128)(2,1)} %get-tuple-element.170.qkv_ref, f32[5,1,208]{2,1,0:T(1,128)} %broadcast_in_dim.90.mask_ref), custom_call_target="tpu_custom_call" | custom-call | flops 664535040 | bytes 6460480 | tf_op jit(solution)/shard_map/pallas_call | solution.py:76
  123.0 8.8 %shard_map.124 = (f32[1040,768]{1,0:T(8,128)}, bf16[1040,768]{1,0:T(8,128)(2,1)}) custom-call(s32[4]{0:T(128)} %pad_add_fusion.me_ref._, bf16[4,13,16,384]{3,2,1,0:T(8,128)(2,1)} %copy-done.4, bf16[4,13,16,384]{3,2,1,0:T(8,128)(2,1)} %copy-done.8, bf16[4,13,16,384]{3,2,1,0:T(8,128)(2,1)} %copy-done.7, bf16[4,13,16,384]{3,2,1,0:T(8,128)(2,1)} %copy-done.12, ...), custom_call_target="tpu_custom_call" | custom-call | flops 1226833920 | bytes 13148176 | tf_op jit(solution)/shard_map/pallas_call | solution.py:76
  137.2 23.5 %shard_map.125 = (bf16[1040,3072]{1,0:T(8,128)(2,1)}, bf16[1040,3072]{1,0:T(8,128)(2,1)}, f32[16,3072]{1,0:T(8,128)}) custom-call(s32[4]{0:T(128)} %pad_add_fusion.me_ref._, bf16[4,12,16,384]{3,2,1,0:T(8,128)(2,1)} %copy-done.28, bf16[4,12,16,384]{3,2,1,0:T(8,128)(2,1)} %copy-done.44, bf16[4,12,16,384]{3,2,1,0:T(8,128)(2,1)} %copy-done.43, ...), custom_call_target="tpu_custom_call" | custom-call | flops 4907335680 | bytes 19337744 | tf_op jit(solution)/shard_map/pallas_call | solution.py:76
  161.0 2.2 collective-permute-done.30.refs_7_
  164.1 15.0 %shard_map.126 = (bf16[5,196,768]{2,1,0:T(8,128)(2,1)}, bf16[16,768]{1,0:T(8,128)(2,1)}) custom-call(s32[4]{0:T(128)} %pad_add_fusion.me_ref._, bf16[4,15,16,384]{3,2,1,0:T(8,128)(2,1)} %copy-done.16, bf16[4,15,16,384]{3,2,1,0:T(8,128)(2,1)} %copy-done.21, bf16[4,15,16,384]{3,2,1,0:T(8,128)(2,1)} %copy-done.20, bf16[4,15,16,384]{3,2,1,0:T(8,128)(2,1)} %copy-done.25, ...), custom_call_target="tpu_custom_call" | custom-call | flops 4907335680 | bytes 17103376 | tf_op jit(solution)/shard_map/pallas_call | solution.py:76
  180.5 3.3 all-to-all-start.1
  183.9 13.0 %all-to-all-done.1 = bf16[32,5,768]{2,1,0:T(8,128)(2,1)S(1)} async-done(((bf16[32,5,768]{2,1,0:T(8,128)(2,1)}), bf16[32,5,768]{2,1,0:T(8,128)(2,1)S(1)}, u32[]{:S(2)}, u32[]{:S(2)}) %all-to-all-start.1) | async-done | bytes 245792 | tf_op jit(solution)/shard_map/all_to_all | solution.py:1256
  198.3 6.8 %shard_map.127 = (bf16[160,512]{1,0:T(8,128)(2,1)}, bf16[16,768]{1,0:T(8,128)(2,1)}, f32[16,768]{1,0:T(8,128)}, f32[16,3072]{1,0:T(8,128)}) custom-call(s32[4]{0:T(128)} %pad_add_fusion.me_ref._, s32[1]{0:T(128)} %bitcast.5.first_ref, bf16[4,15,16,384]{3,2,1,0:T(8,128)(2,1)} %copy-done.16, bf16[4,15,16,384]{3,2,1,0:T(8,128)(2,1)} %copy-done.21, ...), custom_call_target="tpu_custom_call" | custom-call | flops 279969792 | bytes 6672404 | tf_op jit(solution)/shard_map/pallas_call | solution.py:76
  210.3 28.9 %shard_map.128 = (f32[1040,768]{1,0:T(8,128)}, f32[16,3072]{1,0:T(8,128)}, bf16[16,192,384]{2,1,0:T(8,128)(2,1)}, bf16[16,192,384]{2,1,0:T(8,128)(2,1)}) custom-call(s32[4]{0:T(128)} %pad_add_fusion.me_ref._, bf16[4,12,16,384]{3,2,1,0:T(8,128)(2,1)} %copy-done.28, bf16[4,12,16,384]{3,2,1,0:T(8,128)(2,1)} %copy-done.44, bf16[4,12,16,384]{3,2,1,0:T(8,128)(2,1)} %copy-done.43, ...), custom_call_target="tpu_custom_call" | custom-call | flops 9814671360 | bytes 21544976 | tf_op jit(solution)/shard_map/pallas_call | solution.py:76
  241.5 13.5 %shard_map.129 = (f32[1040,768]{1,0:T(8,128)}, bf16[1040,768]{1,0:T(8,128)(2,1)}, bf16[2,16,48,384]{3,2,1,0:T(8,128)(2,1)}, f32[8,768]{1,0:T(8,128)}) custom-call(s32[4]{0:T(128)} %pad_add_fusion.me_ref._, bf16[4,13,16,384]{3,2,1,0:T(8,128)(2,1)} %copy-done.4, bf16[4,13,16,384]{3,2,1,0:T(8,128)(2,1)} %copy-done.8, bf16[4,13,16,384]{3,2,1,0:T(8,128)(2,1)} %copy-done.7, ...), custom_call_target="tpu_custom_call" | custom-call | flops 2453667840 | bytes 19726352 | tf_op jit(solution)/shard_map/pallas_call | solution.py:76
  256.5 3.4 shard_map.131
  262.6 21.3 %shard_map.130 = (bf16[1040,2304]{1,0:T(8,128)(2,1)}, f32[16,2304]{1,0:T(8,128)}) custom-call(bf16[1040,2304]{1,0:T(8,128)(2,1)} %get-tuple-element.170.qkv_ref, bf16[1040,768]{1,0:T(8,128)(2,1)} %get-tuple-element.223.do_ref, f32[5,16,208]{2,1,0:T(8,128)} %get-tuple-element.224.lse_ref, f32[1040,128]{1,0:T(8,128)} %broadcast_in_dim.82.refs_11_.refs_10_.col_ref), custom_call_target="tpu_custom_call" | custom-call | flops 1661337600 | bytes 11928576 | tf_op jit(solution)/shard_map/pallas_call | solution.py:76
  285.1 3.2 shard_map.133
  289.9 6.9 %shard_map.132 = bf16[16,192,384]{2,1,0:T(8,128)(2,1)} custom-call(s32[4]{0:T(128)} %pad_add_fusion.me_ref._, bf16[1040,2304]{1,0:T(8,128)(2,1)} %get-tuple-element.238.dqkv_ref.refs_9_, bf16[1040,768]{1,0:T(8,128)(2,1)} %get-tuple-element.232.a_ref, bf16[2,16,48,384]{3,2,1,0:T(8,128)(2,1)} %get-tuple-element.233.out_ref), custom_call_target="tpu_custom_call" | custom-call | flops 1840250880 | bytes 9928720 | tf_op jit(solution)/shard_map/pallas_call | solution.py:76
  298.5 7.0 %shard_map.134.refs_0_.refs_2_.refs_4_.refs_6_.refs_3_.refs_9_.refs_8_ = bf16[16,192,384]{2,1,0:T(8,128)(2,1)} custom-call(s32[4]{0:T(128)} %pad_add_fusion.me_ref._, bf16[1040,2304]{1,0:T(8,128)(2,1)} %get-tuple-element.238.dqkv_ref.refs_9_, bf16[1040,768]{1,0:T(8,128)(2,1)} %get-tuple-element.232.a_ref, bf16[2,16,48,384]{3,2,1,0:T(8,128)(2,1)} %get-tuple-element.233.out_ref), custom_call_target="tpu_custom_call" | custom-call | flops 1840250880 | bytes 9928720 | tf_op jit(solution)/shard_map/pallas_call | solution.py:76
  306.9 3.4 shard_map.136
  313.0 3.2 shard_map.137
  318.9 2.9 collective-permute-start.46
  321.8 12.3 %shard_map.135 = (f32[5,196,768]{2,1,0:T(8,128)}, f32[8,768]{1,0:T(8,128)}) custom-call(s32[4]{0:T(128)} %pad_add_fusion.me_ref._, bf16[4,13,16,384]{3,2,1,0:T(8,128)(2,1)} %copy-done.4, bf16[4,13,16,384]{3,2,1,0:T(8,128)(2,1)} %copy-done.8, bf16[4,13,16,384]{3,2,1,0:T(8,128)(2,1)} %copy-done.7, bf16[4,13,16,384]{3,2,1,0:T(8,128)(2,1)} %copy-done.12, ...), custom_call_target="tpu_custom_call" | custom-call | flops 3680501760 | bytes 17780752 | tf_op jit(solution)/shard_map/pallas_call | solution.py:76
  336.4 3.3 shard_map.139
  340.8 9.8 %shard_map.140 = (f32[768,3072]{1,0:T(8,128)}, f32[512,768]{1,0:T(8,128)}) custom-call(bf16[4,16,1280]{2,1,0:T(8,128)(2,1)} %copy-done.32, bf16[4,16,1280]{2,1,0:T(8,128)(2,1)} %copy-done.51, bf16[4,16,1280]{2,1,0:T(8,128)(2,1)} %copy-done.50, bf16[4,16,1280]{2,1,0:T(8,128)(2,1)} %copy-done.55, bf16[4,16,1280]{2,1,0:T(8,128)(2,1)} %copy-done.52, ...), custom_call_target="tpu_custom_call" | custom-call | flops 2415919104 | bytes 12730368 | tf_op jit(solution)/shard_map/pallas_call | solution.py:76
  350.5 2.7 shard_map.138
  356.9 3.2 shard_map.141
  362.7 2.9 collective-permute-start.54
  365.6 4.2 collective-permute-done.56
  369.9 5.7 %collective-permute-done.55 = bf16[192,384]{1,0:T(8,128)(2,1)S(1)} collective-permute-done((bf16[192,384]{1,0:T(8,128)(2,1)S(1)}, bf16[192,384]{1,0:T(8,128)(2,1)S(1)}, u32[]{:S(2)}, u32[]{:S(2)}) %collective-permute-start.55) | collective-permute-done | bytes 147488 | tf_op jit(solution)/shard_map/ppermute | solution.py:875
  376.3 2.9 shard_map.142
  382.5 3.6 shard_map.143
  386.1 3.5 all-to-all-start.2
  389.6 3.8 collective-permute-start.60
  394.1 14.8 %collective-permute-done.60 = f32[16,768]{1,0:T(8,128)S(1)} collective-permute-done((f32[16,768]{1,0:T(8,128)S(1)}, f32[16,768]{1,0:T(8,128)S(1)}, u32[]{:S(2)}, u32[]{:S(2)}) %collective-permute-start.60) | collective-permute-done | bytes 49184 | tf_op jit(solution)/shard_map/ppermute | solution.py:875
  408.9 5.6 %collective-permute-done.59 = f32[16,768]{1,0:T(8,128)S(1)} collective-permute-done((f32[16,768]{1,0:T(8,128)S(1)}, f32[16,768]{1,0:T(8,128)S(1)}, u32[]{:S(2)}, u32[]{:S(2)}) %collective-permute-start.59) | collective-permute-done | bytes 49184 | tf_op jit(solution)/shard_map/ppermute | solution.py:875
  416.0 8.4 %shard_map.144 = (f32[1,8,64,768]{3,2,1,0:T(8,128)}, f32[1,8,64,768]{3,2,1,0:T(8,128)}, f32[1,8,64,768]{3,2,1,0:T(8,128)}) custom-call(s32[8]{0:T(128)} %get-tuple-element.241.kind_ref, s32[8]{0:T(128)} %get-tuple-element.242.row_ref, f32[1,8,64,768]{3,2,1,0:T(8,128)} %refs_0_.1, f32[1,8,64,768]{3,2,1,0:T(8,128)} %refs_1_.1, f32[1,8,64,768]{3,2,1,0:T(8,128)} %refs_2_.1, ...), custom_call_target="tpu_custom_call" | custom-call | flops 7864320 | bytes 21282880 | tf_op jit(solution)/shard_map/pallas_call | solution.py:76
  (263 shorter events, 74.8 us)
Async XLA Ops:
  4.6 27.5 %all-to-all-start = ((bf16[8,8,16,384]{3,2,1,0:T(8,128)(2,1)}), bf16[8,8,16,384]{3,2,1,0:T(8,128)(2,1)S(1)}, u32[]{:S(2)}, u32[]{:S(2)}) async-start(bf16[8,8,16,384]{3,2,1,0:T(8,128)(2,1)} %shard_map.120), calls=%async_computation | async-start | bytes 1572864 | tf_op jit(solution)/shard_map/all_to_all | solution.py:1159
  41.9 15.7 %collective-permute-start.2 = (bf16[13,16,384]{2,1,0:T(8,128)(2,1)}, bf16[13,16,384]{2,1,0:T(8,128)(2,1)S(1)}, u32[]{:S(2)}, u32[]{:S(2)}) collective-permute-start(bf16[13,16,384]{2,1,0:T(8,128)(2,1)} %get-tuple-element.145), channel_id=1, source_target_pairs={{0,8},{1,9},{2,10},{3,11},{4,12},{5,13},{6,14},{7,15},{8,0},{9,1},... | collective-permute-start | bytes 479240 | tf_op jit(solution)/shard_map/ppermute | solution.py:875
  42.6 15.0 %collective-permute-start.1 = (bf16[13,16,384]{2,1,0:T(8,128)(2,1)}, bf16[13,16,384]{2,1,0:T(8,128)(2,1)S(1)}, u32[]{:S(2)}, u32[]{:S(2)}) collective-permute-start(bf16[13,16,384]{2,1,0:T(8,128)(2,1)} %get-tuple-element.145), channel_id=1, source_target_pairs={{0,4},{1,5},{2,6},{3,7},{4,0},{5,1},{6,2},{7,3},{8,12},{9,13},{10,... | collective-permute-start | bytes 479240 | tf_op jit(solution)/shard_map/ppermute | solution.py:875
  58.6 17.3 %collective-permute-start.5 = (bf16[4,13,16,384]{3,2,1,0:T(8,128)(2,1)S(1)}, bf16[4,13,16,384]{3,2,1,0:T(8,128)(2,1)S(1)}, u32[]{:S(2)}, u32[]{:S(2)}) collective-permute-start(bf16[4,13,16,384]{3,2,1,0:T(8,128)(2,1)S(1)} %pad_maximum_fusion.1.refs_0_), channel_id=1, source_target_pairs={{0,2},{1,17},{2,0},{3,19},{4,6},{5,21},{6,4},{7,23},{8,10},{9,25},... | collective-permute-start | bytes 1916936 | tf_op jit(solution)/shard_map/ppermute | solution.py:875
  58.7 17.2 %collective-permute-start.4 = (bf16[4,13,16,384]{3,2,1,0:T(8,128)(2,1)S(1)}, bf16[4,13,16,384]{3,2,1,0:T(8,128)(2,1)S(1)}, u32[]{:S(2)}, u32[]{:S(2)}) collective-permute-start(bf16[4,13,16,384]{3,2,1,0:T(8,128)(2,1)S(1)} %pad_maximum_fusion.1.refs_0_), channel_id=1, source_target_pairs={{0,16},{1,3},{2,18},{3,1},{4,20},{5,7},{6,22},{7,5},{8,24},{9,11},... | collective-permute-start | bytes 1916936 | tf_op jit(solution)/shard_map/ppermute | solution.py:875
  62.4 11.6 %collective-permute-start.7 = (bf16[12,16,384]{2,1,0:T(8,128)(2,1)S(1)}, bf16[12,16,384]{2,1,0:T(8,128)(2,1)S(1)}, u32[]{:S(2)}, u32[]{:S(2)}) collective-permute-start(bf16[12,16,384]{2,1,0:T(8,128)(2,1)S(1)} %copy-done.39), channel_id=1, source_target_pairs={{0,8},{1,9},{2,10},{3,11},{4,12},{5,13},{6,14},{7,15},{8,0},{9,1},... | collective-permute-start | bytes 442376 | tf_op jit(solution)/shard_map/ppermute | solution.py:875
  62.4 11.6 %collective-permute-start.6 = (bf16[12,16,384]{2,1,0:T(8,128)(2,1)S(1)}, bf16[12,16,384]{2,1,0:T(8,128)(2,1)S(1)}, u32[]{:S(2)}, u32[]{:S(2)}) collective-permute-start(bf16[12,16,384]{2,1,0:T(8,128)(2,1)S(1)} %copy-done.39), channel_id=1, source_target_pairs={{0,4},{1,5},{2,6},{3,7},{4,0},{5,1},{6,2},{7,3},{8,12},{9,13},{10,... | collective-permute-start | bytes 442376 | tf_op jit(solution)/shard_map/ppermute | solution.py:875
  76.6 10.4 %collective-permute-start.9 = (bf16[4,13,16,384]{3,2,1,0:T(8,128)(2,1)S(1)}, bf16[4,13,16,384]{3,2,1,0:T(8,128)(2,1)S(1)}, u32[]{:S(2)}, u32[]{:S(2)}) collective-permute-start(bf16[4,13,16,384]{3,2,1,0:T(8,128)(2,1)S(1)} %collective-permute-done.4.refs_1_), channel_id=1, source_target_pairs={{0,2},{1,17},{2,0},{3,19},{4,6},{5,21},{6,4},{7,23},{8,10},{9,25},... | collective-permute-start | bytes 1916936 | tf_op jit(solution)/shard_map/ppermute | solution.py:875
  89.2 17.9 %collective-permute-start.15 = (bf16[4,12,16,384]{3,2,1,0:T(8,128)(2,1)S(1)}, bf16[4,12,16,384]{3,2,1,0:T(8,128)(2,1)S(1)}, u32[]{:S(2)}, u32[]{:S(2)}) collective-permute-start(bf16[4,12,16,384]{3,2,1,0:T(8,128)(2,1)S(1)} %pad_maximum_fusion.2.refs_0_), channel_id=1, source_target_pairs={{0,2},{1,17},{2,0},{3,19},{4,6},{5,21},{6,4},{7,23},{8,10},{9,25},... | collective-permute-start | bytes 1769480 | tf_op jit(solution)/shard_map/ppermute | solution.py:875
  89.3 17.8 %collective-permute-start.14 = (bf16[4,12,16,384]{3,2,1,0:T(8,128)(2,1)S(1)}, bf16[4,12,16,384]{3,2,1,0:T(8,128)(2,1)S(1)}, u32[]{:S(2)}, u32[]{:S(2)}) collective-permute-start(bf16[4,12,16,384]{3,2,1,0:T(8,128)(2,1)S(1)} %pad_maximum_fusion.2.refs_0_), channel_id=1, source_target_pairs={{0,16},{1,3},{2,18},{3,1},{4,20},{5,7},{6,22},{7,5},{8,24},{9,11},... | collective-permute-start | bytes 1769480 | tf_op jit(solution)/shard_map/ppermute | solution.py:875
  90.1 16.9 %collective-permute-start.18 = (bf16[15,16,384]{2,1,0:T(8,128)(2,1)S(1)}, bf16[15,16,384]{2,1,0:T(8,128)(2,1)S(1)}, u32[]{:S(2)}, u32[]{:S(2)}) collective-permute-start(bf16[15,16,384]{2,1,0:T(8,128)(2,1)S(1)} %copy-done.31), channel_id=1, source_target_pairs={{0,12},{1,13},{2,14},{3,15},{4,8},{5,9},{6,10},{7,11},{8,4},{9,5},... | collective-permute-start | bytes 552968 | tf_op jit(solution)/shard_map/ppermute | solution.py:875
  91.9 15.1 %collective-permute-start.17 = (bf16[15,16,384]{2,1,0:T(8,128)(2,1)S(1)}, bf16[15,16,384]{2,1,0:T(8,128)(2,1)S(1)}, u32[]{:S(2)}, u32[]{:S(2)}) collective-permute-start(bf16[15,16,384]{2,1,0:T(8,128)(2,1)S(1)} %copy-done.31), channel_id=1, source_target_pairs={{0,8},{1,9},{2,10},{3,11},{4,12},{5,13},{6,14},{7,15},{8,0},{9,1},... | collective-permute-start | bytes 552968 | tf_op jit(solution)/shard_map/ppermute | solution.py:875
  92.0 15.1 %collective-permute-start.16 = (bf16[15,16,384]{2,1,0:T(8,128)(2,1)S(1)}, bf16[15,16,384]{2,1,0:T(8,128)(2,1)S(1)}, u32[]{:S(2)}, u32[]{:S(2)}) collective-permute-start(bf16[15,16,384]{2,1,0:T(8,128)(2,1)S(1)} %copy-done.31), channel_id=1, source_target_pairs={{0,4},{1,5},{2,6},{3,7},{4,0},{5,1},{6,2},{7,3},{8,12},{9,13},{10,... | collective-permute-start | bytes 552968 | tf_op jit(solution)/shard_map/ppermute | solution.py:875
  107.2 15.7 %collective-permute-start.22 = (bf16[4,12,16,384]{3,2,1,0:T(8,128)(2,1)S(1)}, bf16[4,12,16,384]{3,2,1,0:T(8,128)(2,1)S(1)}, u32[]{:S(2)}, u32[]{:S(2)}) collective-permute-start(bf16[4,12,16,384]{3,2,1,0:T(8,128)(2,1)S(1)} %collective-permute-done.15.refs_2_), channel_id=1, source_target_pairs={{0,1},{1,0},{2,3},{3,2},{4,5},{5,4},{6,7},{7,6},{8,9},{9,8},{10,11... | collective-permute-start | bytes 1769480 | tf_op jit(solution)/shard_map/ppermute | solution.py:875
  107.7 15.2 %collective-permute-start.21 = (bf16[4,12,16,384]{3,2,1,0:T(8,128)(2,1)S(1)}, bf16[4,12,16,384]{3,2,1,0:T(8,128)(2,1)S(1)}, u32[]{:S(2)}, u32[]{:S(2)}) collective-permute-start(bf16[4,12,16,384]{3,2,1,0:T(8,128)(2,1)S(1)} %collective-permute-done.14.refs_1_), channel_id=1, source_target_pairs={{0,1},{1,0},{2,3},{3,2},{4,5},{5,4},{6,7},{7,6},{8,9},{9,8},{10,11... | collective-permute-start | bytes 1769480 | tf_op jit(solution)/shard_map/ppermute | solution.py:875
  107.8 15.1 %collective-permute-start.19 = (bf16[4,12,16,384]{3,2,1,0:T(8,128)(2,1)S(1)}, bf16[4,12,16,384]{3,2,1,0:T(8,128)(2,1)S(1)}, u32[]{:S(2)}, u32[]{:S(2)}) collective-permute-start(bf16[4,12,16,384]{3,2,1,0:T(8,128)(2,1)S(1)} %collective-permute-done.14.refs_1_), channel_id=1, source_target_pairs={{0,2},{1,17},{2,0},{3,19},{4,6},{5,21},{6,4},{7,23},{8,10},{9,25},... | collective-permute-start | bytes 1769480 | tf_op jit(solution)/shard_map/ppermute | solution.py:875
  109.6 23.9 %collective-permute-start.25 = (bf16[4,15,16,384]{3,2,1,0:T(8,128)(2,1)S(1)}, bf16[4,15,16,384]{3,2,1,0:T(8,128)(2,1)S(1)}, u32[]{:S(2)}, u32[]{:S(2)}) collective-permute-start(bf16[4,15,16,384]{3,2,1,0:T(8,128)(2,1)S(1)} %pad_maximum_fusion.refs_0_), channel_id=1, source_target_pairs={{0,2},{1,17},{2,0},{3,19},{4,6},{5,21},{6,4},{7,23},{8,10},{9,25},... | collective-permute-start | bytes 2211848 | tf_op jit(solution)/shard_map/ppermute | solution.py:875
  110.0 23.5 %collective-permute-start.24 = (bf16[4,15,16,384]{3,2,1,0:T(8,128)(2,1)S(1)}, bf16[4,15,16,384]{3,2,1,0:T(8,128)(2,1)S(1)}, u32[]{:S(2)}, u32[]{:S(2)}) collective-permute-start(bf16[4,15,16,384]{3,2,1,0:T(8,128)(2,1)S(1)} %pad_maximum_fusion.refs_0_), channel_id=1, source_target_pairs={{0,16},{1,3},{2,18},{3,1},{4,20},{5,7},{6,22},{7,5},{8,24},{9,11},... | collective-permute-start | bytes 2211848 | tf_op jit(solution)/shard_map/ppermute | solution.py:875
  122.9 10.6 %collective-permute-start.23 = (bf16[4,12,16,384]{3,2,1,0:T(8,128)(2,1)S(1)}, bf16[4,12,16,384]{3,2,1,0:T(8,128)(2,1)S(1)}, u32[]{:S(2)}, u32[]{:S(2)}) collective-permute-start(bf16[4,12,16,384]{3,2,1,0:T(8,128)(2,1)S(1)} %collective-permute-done.19.refs_3_), channel_id=1, source_target_pairs={{0,1},{1,0},{2,3},{3,2},{4,5},{5,4},{6,7},{7,6},{8,9},{9,8},{10,11... | collective-permute-start | bytes 1769480 | tf_op jit(solution)/shard_map/ppermute | solution.py:875
  133.5 27.3 %collective-permute-start.27 = (bf16[4,15,16,384]{3,2,1,0:T(8,128)(2,1)S(1)}, bf16[4,15,16,384]{3,2,1,0:T(8,128)(2,1)S(1)}, u32[]{:S(2)}, u32[]{:S(2)}) collective-permute-start(bf16[4,15,16,384]{3,2,1,0:T(8,128)(2,1)S(1)} %pad_maximum_fusion.refs_0_), channel_id=1, source_target_pairs={{0,1},{1,0},{2,3},{3,2},{4,5},{5,4},{6,7},{7,6},{8,9},{9,8},{10,11... | collective-permute-start | bytes 2211848 | tf_op jit(solution)/shard_map/ppermute | solution.py:875
  133.5 27.3 %collective-permute-start.29 = (bf16[4,15,16,384]{3,2,1,0:T(8,128)(2,1)S(1)}, bf16[4,15,16,384]{3,2,1,0:T(8,128)(2,1)S(1)}, u32[]{:S(2)}, u32[]{:S(2)}) collective-permute-start(bf16[4,15,16,384]{3,2,1,0:T(8,128)(2,1)S(1)} %collective-permute-done.25.refs_2_), channel_id=1, source_target_pairs={{0,1},{1,0},{2,3},{3,2},{4,5},{5,4},{6,7},{7,6},{8,9},{9,8},{10,11... | collective-permute-start | bytes 2211848 | tf_op jit(solution)/shard_map/ppermute | solution.py:875
  134.0 26.8 %collective-permute-start.28 = (bf16[4,15,16,384]{3,2,1,0:T(8,128)(2,1)S(1)}, bf16[4,15,16,384]{3,2,1,0:T(8,128)(2,1)S(1)}, u32[]{:S(2)}, u32[]{:S(2)}) collective-permute-start(bf16[4,15,16,384]{3,2,1,0:T(8,128)(2,1)S(1)} %collective-permute-done.24.refs_1_), channel_id=1, source_target_pairs={{0,1},{1,0},{2,3},{3,2},{4,5},{5,4},{6,7},{7,6},{8,9},{9,8},{10,11... | collective-permute-start | bytes 2211848 | tf_op jit(solution)/shard_map/ppermute | solution.py:875
  134.1 26.7 %collective-permute-start.26 = (bf16[4,15,16,384]{3,2,1,0:T(8,128)(2,1)S(1)}, bf16[4,15,16,384]{3,2,1,0:T(8,128)(2,1)S(1)}, u32[]{:S(2)}, u32[]{:S(2)}) collective-permute-start(bf16[4,15,16,384]{3,2,1,0:T(8,128)(2,1)S(1)} %collective-permute-done.24.refs_1_), channel_id=1, source_target_pairs={{0,2},{1,17},{2,0},{3,19},{4,6},{5,21},{6,4},{7,23},{8,10},{9,25},... | collective-permute-start | bytes 2211848 | tf_op jit(solution)/shard_map/ppermute | solution.py:875
  180.5 16.4 %all-to-all-start.1 = ((bf16[32,5,768]{2,1,0:T(8,128)(2,1)}), bf16[32,5,768]{2,1,0:T(8,128)(2,1)S(1)}, u32[]{:S(2)}, u32[]{:S(2)}) async-start(bf16[32,5,768]{2,1,0:T(8,128)(2,1)} %broadcast_in_dim.92), calls=%async_computation.1 | async-start | bytes 786432 | tf_op jit(solution)/shard_map/all_to_all | solution.py:1256
  205.9 33.4 %collective-permute-start.33 = (bf16[16,1280]{1,0:T(8,128)(2,1)S(1)}, bf16[16,1280]{1,0:T(8,128)(2,1)S(1)}, u32[]{:S(2)}, u32[]{:S(2)}) collective-permute-start(bf16[16,1280]{1,0:T(8,128)(2,1)S(1)} %fusion.6), channel_id=1, source_target_pairs={{0,12},{1,13},{2,14},{3,15},{4,8},{5,9},{6,10},{7,11},{8,4},{9,5},... | collective-permute-start | bytes 122888 | tf_op jit(solution)/shard_map/ppermute | solution.py:875
  207.9 31.4 %collective-permute-start.32 = (bf16[16,1280]{1,0:T(8,128)(2,1)S(1)}, bf16[16,1280]{1,0:T(8,128)(2,1)S(1)}, u32[]{:S(2)}, u32[]{:S(2)}) collective-permute-start(bf16[16,1280]{1,0:T(8,128)(2,1)S(1)} %fusion.6), channel_id=1, source_target_pairs={{0,8},{1,9},{2,10},{3,11},{4,12},{5,13},{6,14},{7,15},{8,0},{9,1},... | collective-permute-start | bytes 122888 | tf_op jit(solution)/shard_map/ppermute | solution.py:875
  208.3 31.0 %collective-permute-start.31 = (bf16[16,1280]{1,0:T(8,128)(2,1)S(1)}, bf16[16,1280]{1,0:T(8,128)(2,1)S(1)}, u32[]{:S(2)}, u32[]{:S(2)}) collective-permute-start(bf16[16,1280]{1,0:T(8,128)(2,1)S(1)} %fusion.6), channel_id=1, source_target_pairs={{0,4},{1,5},{2,6},{3,7},{4,0},{5,1},{6,2},{7,3},{8,12},{9,13},{10,... | collective-permute-start | bytes 122888 | tf_op jit(solution)/shard_map/ppermute | solution.py:875
  239.3 15.8 %collective-permute-start.34 = (bf16[16,192,384]{2,1,0:T(8,128)(2,1)}, bf16[16,192,384]{2,1,0:T(8,128)(2,1)S(1)}, u32[]{:S(2)}, u32[]{:S(2)}) collective-permute-start(bf16[16,192,384]{2,1,0:T(8,128)(2,1)} %get-tuple-element.218), channel_id=1, source_target_pairs={{0,1},{1,0},{2,3},{3,2},{4,5},{5,4},{6,7},{7,6},{8,9},{9,8},{10,11... | collective-permute-start | bytes 7077896 | tf_op jit(solution)/shard_map/ppermute | solution.py:875
  239.4 15.6 %collective-permute-start.36 = (bf16[4,16,1280]{2,1,0:T(8,128)(2,1)S(1)}, bf16[4,16,1280]{2,1,0:T(8,128)(2,1)S(1)}, u32[]{:S(2)}, u32[]{:S(2)}) collective-permute-start(bf16[4,16,1280]{2,1,0:T(8,128)(2,1)S(1)} %pad_maximum_fusion.4.refs_0_), channel_id=1, source_target_pairs={{0,2},{1,17},{2,0},{3,19},{4,6},{5,21},{6,4},{7,23},{8,10},{9,25},... | collective-permute-start | bytes 491528 | tf_op jit(solution)/shard_map/ppermute | solution.py:875
  240.9 14.1 %collective-permute-start.35 = (bf16[4,16,1280]{2,1,0:T(8,128)(2,1)S(1)}, bf16[4,16,1280]{2,1,0:T(8,128)(2,1)S(1)}, u32[]{:S(2)}, u32[]{:S(2)}) collective-permute-start(bf16[4,16,1280]{2,1,0:T(8,128)(2,1)S(1)} %pad_maximum_fusion.4.refs_0_), channel_id=1, source_target_pairs={{0,16},{1,3},{2,18},{3,1},{4,20},{5,7},{6,22},{7,5},{8,24},{9,11},... | collective-permute-start | bytes 491528 | tf_op jit(solution)/shard_map/ppermute | solution.py:875
  260.0 24.0 %collective-permute-start.37 = (bf16[8,192,384]{2,1,0:T(8,128)(2,1)}, bf16[8,192,384]{2,1,0:T(8,128)(2,1)S(1)}, u32[]{:S(2)}, u32[]{:S(2)}) collective-permute-start(bf16[8,192,384]{2,1,0:T(8,128)(2,1)} %shard_map.131), channel_id=1, source_target_pairs={{0,16},{1,3},{2,18},{3,1},{4,20},{5,7},{6,22},{7,5},{8,24},{9,11},... | collective-permute-start | bytes 3538952 | tf_op jit(solution)/shard_map/ppermute | solution.py:875
  261.4 22.5 %collective-permute-start.39 = (bf16[4,16,1280]{2,1,0:T(8,128)(2,1)S(1)}, bf16[4,16,1280]{2,1,0:T(8,128)(2,1)S(1)}, u32[]{:S(2)}, u32[]{:S(2)}) collective-permute-start(bf16[4,16,1280]{2,1,0:T(8,128)(2,1)S(1)} %pad_maximum_fusion.4.refs_0_), channel_id=1, source_target_pairs={{0,1},{1,0},{2,3},{3,2},{4,5},{5,4},{6,7},{7,6},{8,9},{9,8},{10,11... | collective-permute-start | bytes 491528 | tf_op jit(solution)/shard_map/ppermute | solution.py:875
  261.4 22.5 %collective-permute-start.41 = (bf16[4,16,1280]{2,1,0:T(8,128)(2,1)S(1)}, bf16[4,16,1280]{2,1,0:T(8,128)(2,1)S(1)}, u32[]{:S(2)}, u32[]{:S(2)}) collective-permute-start(bf16[4,16,1280]{2,1,0:T(8,128)(2,1)S(1)} %collective-permute-done.36.refs_2_), channel_id=1, source_target_pairs={{0,1},{1,0},{2,3},{3,2},{4,5},{5,4},{6,7},{7,6},{8,9},{9,8},{10,11... | collective-permute-start | bytes 491528 | tf_op jit(solution)/shard_map/ppermute | solution.py:875
  261.9 22.0 %collective-permute-start.40 = (bf16[4,16,1280]{2,1,0:T(8,128)(2,1)S(1)}, bf16[4,16,1280]{2,1,0:T(8,128)(2,1)S(1)}, u32[]{:S(2)}, u32[]{:S(2)}) collective-permute-start(bf16[4,16,1280]{2,1,0:T(8,128)(2,1)S(1)} %collective-permute-done.35.refs_1_), channel_id=1, source_target_pairs={{0,1},{1,0},{2,3},{3,2},{4,5},{5,4},{6,7},{7,6},{8,9},{9,8},{10,11... | collective-permute-start | bytes 491528 | tf_op jit(solution)/shard_map/ppermute | solution.py:875
  262.0 21.9 %collective-permute-start.38 = (bf16[4,16,1280]{2,1,0:T(8,128)(2,1)S(1)}, bf16[4,16,1280]{2,1,0:T(8,128)(2,1)S(1)}, u32[]{:S(2)}, u32[]{:S(2)}) collective-permute-start(bf16[4,16,1280]{2,1,0:T(8,128)(2,1)S(1)} %collective-permute-done.35.refs_1_), channel_id=1, source_target_pairs={{0,2},{1,17},{2,0},{3,19},{4,6},{5,21},{6,4},{7,23},{8,10},{9,25},... | collective-permute-start | bytes 491528 | tf_op jit(solution)/shard_map/ppermute | solution.py:875
  310.3 25.0 %collective-permute-start.45 = (bf16[8,192,384]{2,1,0:T(8,128)(2,1)}, bf16[8,192,384]{2,1,0:T(8,128)(2,1)S(1)}, u32[]{:S(2)}, u32[]{:S(2)}) collective-permute-start(bf16[8,192,384]{2,1,0:T(8,128)(2,1)} %shard_map.136), channel_id=1, source_target_pairs={{0,16},{1,3},{2,18},{3,1},{4,20},{5,7},{6,22},{7,5},{8,24},{9,11},... | collective-permute-start | bytes 3538952 | tf_op jit(solution)/shard_map/ppermute | solution.py:875
  317.3 17.9 %collective-permute-start.48 = (bf16[192,384]{1,0:T(8,128)(2,1)S(1)}, bf16[192,384]{1,0:T(8,128)(2,1)S(1)}, u32[]{:S(2)}, u32[]{:S(2)}) collective-permute-start(bf16[192,384]{1,0:T(8,128)(2,1)S(1)} %get-tuple-element.278), channel_id=1, source_target_pairs={{0,12},{1,13},{2,14},{3,15},{4,8},{5,9},{6,10},{7,11},{8,4},{9,5},... | collective-permute-start | bytes 442376 | tf_op jit(solution)/shard_map/ppermute | solution.py:875
  318.9 16.4 %collective-permute-start.47 = (bf16[192,384]{1,0:T(8,128)(2,1)S(1)}, bf16[192,384]{1,0:T(8,128)(2,1)S(1)}, u32[]{:S(2)}, u32[]{:S(2)}) collective-permute-start(bf16[192,384]{1,0:T(8,128)(2,1)S(1)} %get-tuple-element.279), channel_id=1, source_target_pairs={{0,8},{1,9},{2,10},{3,11},{4,12},{5,13},{6,14},{7,15},{8,0},{9,1},... | collective-permute-start | bytes 442376 | tf_op jit(solution)/shard_map/ppermute | solution.py:875
  318.9 16.4 %collective-permute-start.46 = (bf16[192,384]{1,0:T(8,128)(2,1)S(1)}, bf16[192,384]{1,0:T(8,128)(2,1)S(1)}, u32[]{:S(2)}, u32[]{:S(2)}) collective-permute-start(bf16[192,384]{1,0:T(8,128)(2,1)S(1)} %get-tuple-element.280), channel_id=1, source_target_pairs={{0,4},{1,5},{2,6},{3,7},{4,0},{5,1},{6,2},{7,3},{8,12},{9,13},{10,... | collective-permute-start | bytes 442376 | tf_op jit(solution)/shard_map/ppermute | solution.py:875
  339.7 13.6 %collective-permute-start.50 = (bf16[4,192,384]{2,1,0:T(8,128)(2,1)}, bf16[4,192,384]{2,1,0:T(8,128)(2,1)S(1)}, u32[]{:S(2)}, u32[]{:S(2)}) collective-permute-start(bf16[4,192,384]{2,1,0:T(8,128)(2,1)} %shard_map.139), channel_id=1, source_target_pairs={{0,2},{1,17},{2,0},{3,19},{4,6},{5,21},{6,4},{7,23},{8,10},{9,25},... | collective-permute-start | bytes 1769480 | tf_op jit(solution)/shard_map/ppermute | solution.py:875
  340.8 12.5 %collective-permute-start.49 = (f32[16,768]{1,0:T(8,128)S(1)}, f32[16,768]{1,0:T(8,128)S(1)}, u32[]{:S(2)}, u32[]{:S(2)}) collective-permute-start(f32[16,768]{1,0:T(8,128)S(1)} %concatenate.14), channel_id=1, source_target_pairs={{0,1},{1,0},{2,3},{3,2},{4,5},{5,4},{6,7},{7,6},{8,9},{9,8},{10,11... | collective-permute-start | bytes 147464 | tf_op jit(solution)/shard_map/ppermute | solution.py:875
  354.8 10.8 %collective-permute-start.52 = (f32[16,768]{1,0:T(8,128)S(1)}, f32[16,768]{1,0:T(8,128)S(1)}, u32[]{:S(2)}, u32[]{:S(2)}) collective-permute-start(f32[16,768]{1,0:T(8,128)S(1)} %add.42), channel_id=1, source_target_pairs={{0,2},{1,3},{2,0},{3,1},{4,6},{5,7},{6,4},{7,5},{8,10},{9,11},{10,... | collective-permute-start | bytes 147464 | tf_op jit(solution)/shard_map/ppermute | solution.py:875
  362.7 12.9 %collective-permute-start.55 = (bf16[192,384]{1,0:T(8,128)(2,1)S(1)}, bf16[192,384]{1,0:T(8,128)(2,1)S(1)}, u32[]{:S(2)}, u32[]{:S(2)}) collective-permute-start(bf16[192,384]{1,0:T(8,128)(2,1)S(1)} %get-tuple-element.276), channel_id=1, source_target_pairs={{0,8},{1,9},{2,10},{3,11},{4,12},{5,13},{6,14},{7,15},{8,0},{9,1},... | collective-permute-start | bytes 442376 | tf_op jit(solution)/shard_map/ppermute | solution.py:875
  362.7 12.9 %collective-permute-start.54 = (bf16[192,384]{1,0:T(8,128)(2,1)S(1)}, bf16[192,384]{1,0:T(8,128)(2,1)S(1)}, u32[]{:S(2)}, u32[]{:S(2)}) collective-permute-start(bf16[192,384]{1,0:T(8,128)(2,1)S(1)} %get-tuple-element.277), channel_id=1, source_target_pairs={{0,4},{1,5},{2,6},{3,7},{4,0},{5,1},{6,2},{7,3},{8,12},{9,13},{10,... | collective-permute-start | bytes 442376 | tf_op jit(solution)/shard_map/ppermute | solution.py:875
  386.1 29.0 %all-to-all-start.2 = ((bf16[8,8,16,384]{3,2,1,0:T(8,128)(2,1)}), bf16[8,8,16,384]{3,2,1,0:T(8,128)(2,1)S(1)}, u32[]{:S(2)}, u32[]{:S(2)}) async-start(bf16[8,8,16,384]{3,2,1,0:T(8,128)(2,1)} %bitcast.50), calls=%async_computation.2 | async-start | bytes 1572864 | tf_op jit(solution)/shard_map/all_to_all | solution.py:982
  389.6 19.3 %collective-permute-start.60 = (f32[16,768]{1,0:T(8,128)S(1)}, f32[16,768]{1,0:T(8,128)S(1)}, u32[]{:S(2)}, u32[]{:S(2)}) collective-permute-start(f32[16,768]{1,0:T(8,128)S(1)} %add_add_fusion.1), channel_id=1, source_target_pairs={{0,12},{1,13},{2,14},{3,15},{4,8},{5,9},{6,10},{7,11},{8,4},{9,5},... | collective-permute-start | bytes 147464 | tf_op jit(solution)/shard_map/ppermute | solution.py:875
  393.4 21.1 %collective-permute-start.59 = (f32[16,768]{1,0:T(8,128)S(1)}, f32[16,768]{1,0:T(8,128)S(1)}, u32[]{:S(2)}, u32[]{:S(2)}) collective-permute-start(f32[16,768]{1,0:T(8,128)S(1)} %add_add_fusion.1), channel_id=1, source_target_pairs={{0,8},{1,9},{2,10},{3,11},{4,12},{5,13},{6,14},{7,15},{8,0},{9,1},... | collective-permute-start | bytes 147464 | tf_op jit(solution)/shard_map/ppermute | solution.py:875
  393.4 21.1 %collective-permute-start.58 = (f32[16,768]{1,0:T(8,128)S(1)}, f32[16,768]{1,0:T(8,128)S(1)}, u32[]{:S(2)}, u32[]{:S(2)}) collective-permute-start(f32[16,768]{1,0:T(8,128)S(1)} %add_add_fusion.1), channel_id=1, source_target_pairs={{0,4},{1,5},{2,6},{3,7},{4,0},{5,1},{6,2},{7,3},{8,12},{9,13},{10,... | collective-permute-start | bytes 147464 | tf_op jit(solution)/shard_map/ppermute | solution.py:875
  (73 other events, 687.2 us)

commit v2 on v1

--- a/solution.py
+++ b/solution.py
@@ -67,7 +67,11 @@
     return lax.dot_general(a, b, (((0,), (0,)), ((), ())), preferred_element_type=f32)
 
 
-def call(kernel, outs, ins, in_specs, out_specs, grid=None, scratch=(), flops=0, vmem=56, prefetch=0):
+def call(kernel, outs, ins, in_specs, out_specs, grid=None, scratch=(), flops=0, vmem=24, prefetch=0, in_hbm=()):
+    ins = [
+        pltpu.with_memory_space_constraint(a, pltpu.HBM) if k >= prefetch and (s.memory_space is pltpu.HBM or k in in_hbm) else a
+        for k, (a, s) in enumerate(zip(ins, [None] * prefetch + list(in_specs), strict=True))
+    ]
     moved = sum(a.size * a.dtype.itemsize for a in ins) + sum(o.size * o.dtype.itemsize for o in outs)
     params = pltpu.CompilerParams(
         vmem_limit_bytes=vmem * MIB,
@@ -108,13 +112,13 @@
     def __init__(self, arrays, tiles, first=0, quarters=False):
         self.arrays, self.tiles, self.first, self.quarters = tuple(arrays), tiles, first, quarters
         self.pieces = len(arrays) > 1
-        self.specs = [pl.BlockSpec(memory_space=pl.ANY)] * len(arrays)
+        self.specs = [pl.BlockSpec(memory_space=pltpu.HBM)] * len(arrays)
         shape = (tiles, TR // 4, FF) if quarters else (tiles, TR, D)
         self.scratch = [pltpu.VMEM(shape, bf16), pltpu.SemaphoreType.DMA((32 if self.pieces else 1,))]
 
     def copies(self, me, refs, out, sems):
         if not self.pieces:
-            return [pltpu.make_async_copy(refs[0], out, sems.at[0])]
+            return [lambda: pltpu.make_async_copy(refs[0], out, sems.at[0])]
         copies = []
         half = self.tiles // 2
         for at, (c, x, y) in enumerate(sources(me)):
@@ -127,19 +131,28 @@
                 rows = pl.ds(pl.multiple_of(row, 16), 16)
                 cols = pl.ds(pl.multiple_of(col, 128), 384)
                 source = refs[at].at[back, pl.ds(self.first, half)]
-                copies.append(
-                    pltpu.make_async_copy(source, out.at[pl.ds(half * c, half), rows, cols], sems.at[len(copies)])
-                )
+                place = out.at[pl.ds(half * c, half), rows, cols]
+                copies.append(functools.partial(pltpu.make_async_copy, source, place, sems.at[len(copies)]))
         return copies
+
+    def start(self, me, refs, out, sems):
+        for copy in self.copies(me, refs, out, sems):
+            copy().start()
+
+    def wait(self, me, refs, out, sems, part=None, parts=1):
+        copies = self.copies(me, refs, out, sems)
+        if part is not None and not self.pieces:
+            copies = copies if part == 0 else []
+        elif part is not None:
+            copies = copies[16 * part : 16 * part + 16] if parts == 2 else copies[part::4]
+        for copy in copies:
+            copy().wait()
 
     def load(self, me, refs, out, sems):
         @pl.when(pl.program_id(0) == 0)
         def _():
-            copies = self.copies(me, refs, out, sems)
-            for copy in copies:
-                copy.start()
-            for copy in copies:
-                copy.wait()
+            self.start(me, refs, out, sems)
+            self.wait(me, refs, out, sems)
 
 
 def normalized(x):
@@ -156,8 +169,22 @@
     return inverse * (scaled - first - hat * second)
 
 
+def accumulate(i, ref, value):
+    @pl.when(i == 0)
+    def _():
+        ref[...] = value
+
+    @pl.when(i > 0)
+    def _():
+        ref[...] += value
+
+
 def column_sum(x):
     return jnp.sum(x, axis=0, keepdims=True)
+
+
+def qkv_block(j, me):
+    return jnp.where(me[CORE] == 0, j, 2 - j)
 
 
 def qkv_kernel(images, weight, me_ref, *refs):
@@ -168,9 +195,7 @@
 
     @pl.when(j == 0)
     def _():
-        copies = weight.copies(me_ref, pieces, w_ref, sems)
-        for copy in copies:
-            copy.start()
+        weight.start(me_ref, pieces, w_ref, sems)
         if weight.pieces:
             parts = []
             for at, (_, x, y) in list(enumerate(sources(me_ref)))[:4]:
@@ -187,9 +212,13 @@
         for i in range(images):
             hat, _ = normalized(x_ref[pl.ds(i * ROWS, ROWS), :].astype(f32))
             a_ref[pl.ds(i * ROWS, ROWS), :] = (hat * vec_ref[0:1, :] + vec_ref[1:2, :]).astype(bf16)
-        for copy in copies:
-            copy.wait()
-
+        weight.wait(me_ref, pieces, w_ref, sems, 0, 2)
+
+    @pl.when(j == 1)
+    def _():
+        weight.wait(me_ref, pieces, w_ref, sems, 1, 2)
+
+    j = qkv_block(j, me_ref)
     bias = jnp.where(j == 0, vec_ref[4:5, :], jnp.where(j == 2, vec_ref[5:6, :], 0.0))
     scale = jnp.where(j == 0, f32(HEAD**-0.5), f32(1.0))
     w = w_ref[pl.ds(6 * j, 6)].reshape(D, D)
@@ -203,7 +232,7 @@
         (sds((n, D), bf16), sds((n, 3 * D), bf16), sds((16, D), f32)),
         (me, *weight.arrays, x, vec),
         weight.specs + [whole((n, D)), whole((16, D))],
-        [whole((n, D)), cols_at(n, D), whole((16, D))],
+        [whole((n, D)), pl.BlockSpec((n, D), lambda j, me: (0, qkv_block(j, me))), whole((16, D))],
         grid=(3,),
         scratch=weight.scratch + [pltpu.VMEM((2, 16, 384), bf16), pltpu.SemaphoreType.DMA((16,))],
         flops=2 * n * D * 3 * D,
@@ -276,41 +305,50 @@
 
 
 def gelu_parts(u):
-    r = jnp.abs(u) * 0.7071067811865476
-    t = 1.0 / (1.0 + 0.3275911 * r)
+    size = jnp.abs(u)
+    t = 1.0 / (1.0 + 0.23164189 * size)
     poly = t * (0.127414796 + t * (-0.142248368 + t * (0.7107068705 + t * (-0.7265760135 + t * 0.5307027145))))
-    e = jnp.exp(-0.5 * u * u)
-    tail = poly * e
-    phi = jnp.where(u >= 0.0, 1.0 - tail, tail)
-    return u * phi, phi + u * e * 0.3989422804014327
+    e = jnp.exp2(u * u * -0.7213475204444817)
+    act = jnp.maximum(u, 0.0) - size * (poly * e)
+    w = e * (poly - 0.3989422804014327 * size)
+    return act, jnp.where(u >= 0.0, 1.0 - w, w)
+
+
+def own_block(j, me):
+    return (j // 2 + me[CORE]) % 2 * 2 + j % 2
 
 
 def up_kernel(images, weight, me_ref, *refs):
     count = len(weight.arrays)
-    m_ref, bias_ref, sel_ref, act_ref, slope_ref, sum_ref, w_ref, sems = refs[count:]
-    weight.load(me_ref, refs[:count], w_ref, sems)
-    w = w_ref[pl.ds(6 * pl.program_id(0), 6)].reshape(D, D)
-    total = jnp.zeros((16, D), f32)
+    m_ref, bias_ref, act_ref, slope_ref, w_ref, sems = refs[count:]
+    j = pl.program_id(0)
+
+    @pl.when(j == 0)
+    def _():
+        weight.start(me_ref, refs[:count], w_ref, sems)
+        weight.wait(me_ref, refs[:count], w_ref, sems, 0, 2)
+
+    @pl.when(j == 2)
+    def _():
+        weight.wait(me_ref, refs[:count], w_ref, sems, 1, 2)
+
+    w = w_ref[pl.ds(6 * own_block(j, me_ref), 6)].reshape(D, D)
     for i in range(images):
         at = pl.ds(i * ROWS, ROWS)
-        u = nt(m_ref[at, :], w) + bias_ref[0]
-        act, slope = gelu_parts(u)
-        act = act.astype(bf16)
-        act_ref[at, :] = act
+        act, slope = gelu_parts(nt(m_ref[at, :], w) + bias_ref[0])
+        act_ref[at, :] = act.astype(bf16)
         slope_ref[at, :] = slope.astype(bf16)
-        total += nn(sel_ref[i], act)
-    sum_ref[...] = total
-
-
-def up_forward(images, m, weight, bias, sel, me):
+
+
+def up_forward(images, m, weight, bias, me):
     n = images * ROWS
+    cols = pl.BlockSpec((n, D), lambda j, me: (0, own_block(j, me)))
     return call(
         functools.partial(up_kernel, images, weight),
-        (sds((n, FF), bf16), sds((n, FF), bf16), sds((16, FF), f32)),
-        (me, *weight.arrays, m, bias, sel),
-        weight.specs
-        + [whole((n, D)), pl.BlockSpec((1, 1, D), lambda j, *_: (j, 0, 0)), whole((images, 16, ROWS))],
-        [cols_at(n, D), cols_at(n, D), cols_at(16, D)],
+        (sds((n, FF), bf16), sds((n, FF), bf16)),
+        (me, *weight.arrays, m, bias),
+        weight.specs + [whole((n, D)), pl.BlockSpec((1, 1, D), lambda j, me: (own_block(j, me), 0, 0))],
+        [cols, cols],
         grid=(FF // D,),
         scratch=weight.scratch,
         flops=2 * n * D * FF,
@@ -318,44 +356,79 @@
     )
 
 
-def down_kernel(weight, me_ref, *refs):
+def act_sum_kernel(images, act_ref, sel_ref, sum_ref):
+    total = jnp.zeros(sum_ref.shape, f32)
+    for i in range(images):
+        total += nn(sel_ref[i], act_ref[pl.ds(i * ROWS, ROWS), :])
+    sum_ref[...] = total.astype(bf16)
+
+
+def act_sums(images, act, sel):
+    n = images * ROWS
+    return call(
+        functools.partial(act_sum_kernel, images),
+        (sds((16, FF), bf16),),
+        (act, sel),
+        [cols_at(n, D), whole((images, 16, ROWS))],
+        [cols_at(16, D)],
+        grid=(FF // D,),
+        flops=32 * n * FF,
+    )[0]
+
+
+def down_kernel(images, weight, me_ref, *refs):
     count = len(weight.arrays)
-    act_ref, h_ref, vec_ref, sel_ref, inv_ref, out_ref, pooled_ref, w_ref, sems, sum_ref = refs[count:]
-    i = pl.program_id(0)
-    weight.load(me_ref, refs[:count], w_ref, sems)
-    y = nt(act_ref[...], w_ref[...].reshape(D, FF)) + vec_ref[11:12, :]
-    out = (h_ref[...] + y).astype(bf16)
-    out_ref[0] = out[0:PATCHES, :]
-    part = nn(sel_ref[0], out)
-
-    @pl.when(i == 0)
-    def _():
-        sum_ref[...] = part
-
-    @pl.when(i > 0)
-    def _():
-        sum_ref[...] += part
-
-    pooled_ref[...] = (sum_ref[...] * inv_ref[:, 0:1]).astype(bf16)
+    act_ref, h_ref, vec_ref, sel_ref, inv_ref, out_ref, pooled_ref, w_ref, sems, sum_ref, y_ref = refs[count:]
+    k = pl.program_id(0)
+    quarters = FF // D
+
+    @pl.when(k == 0)
+    def _():
+        weight.start(me_ref, refs[:count], w_ref, sems)
+
+    for part in range(quarters):
+
+        @pl.when(k == part)
+        def _():
+            weight.wait(me_ref, refs[:count], w_ref, sems, part, quarters)
+
+    @pl.when(k < quarters)
+    def _():
+        cols = pl.ds(pl.multiple_of((me_ref[Z] ^ k) * D, 128), D)
+        accumulate(k, y_ref, nt(act_ref[...], w_ref[:, :, cols].reshape(D, D)))
+
+    @pl.when(k >= quarters)
+    def _():
+        i = k - quarters
+        y = y_ref[pl.ds(pl.multiple_of(i * ROWS, 16), ROWS), :] + vec_ref[11:12, :]
+        out = (h_ref[...] + y).astype(bf16)
+        out_ref[0] = out[0:PATCHES, :]
+        accumulate(i, sum_ref, nn(sel_ref[0], out))
+        pooled_ref[...] = (sum_ref[...] * inv_ref[:, 0:1]).astype(bf16)
 
 
 def down_forward(images, act, weight, h, vec, sel, inv_count, me):
     n = images * ROWS
+    quarters = FF // D
+
+    def image(k):
+        return jnp.maximum(k - quarters, 0)
+
     return call(
-        functools.partial(down_kernel, weight),
+        functools.partial(down_kernel, images, weight),
         (sds((images, PATCHES, D), bf16), sds((16, D), bf16)),
         (me, *weight.arrays, act, h, vec, sel, inv_count),
         weight.specs
         + [
-            rows_at(ROWS, FF),
-            rows_at(ROWS, D),
+            pl.BlockSpec((n, D), lambda k, me: (0, me[Z] ^ jnp.minimum(k, quarters - 1))),
+            pl.BlockSpec((ROWS, D), lambda k, me: (image(k), 0)),
             whole((16, D)),
-            pl.BlockSpec((1, 16, ROWS), lambda i, *_: (i, 0, 0)),
+            pl.BlockSpec((1, 16, ROWS), lambda k, me: (image(k), 0, 0)),
             whole((16, 128)),
         ],
-        [pl.BlockSpec((1, PATCHES, D), lambda i, *_: (i, 0, 0)), whole((16, D))],
-        grid=(images,),
-        scratch=weight.scratch + [pltpu.VMEM((16, D), f32)],
+        [pl.BlockSpec((1, PATCHES, D), lambda k, me: (image(k), 0, 0)), whole((16, D))],
+        grid=(quarters + images,),
+        scratch=weight.scratch + [pltpu.VMEM((16, D), f32), pltpu.VMEM((n, D), f32)],
         flops=2 * n * D * FF,
         prefetch=1,
     )
@@ -368,21 +441,24 @@
         down_pieces, rest = pieces, refs[count:]
     else:
         down_pieces, rest = refs[count : count + 1], refs[count + 1 :]
-    text_ref, pooled_ref, order_ref, inv_ref, dz_ref, rank_ref, spread_ref, hidden_ref = rest[:8]
-    proj_ref, proj_sems, down_ref, down_sems = rest[8:12]
+    text_ref, pooled_ref, order_ref, inv_ref, dz_ref, rank_ref, spread_ref, hidden_ref, all_ref = rest[:9]
+    proj_ref, proj_sems, down_ref, down_sems, rows_ref = rest[9:14]
     down_copies = down.copies(me_ref, down_pieces, down_ref, down_sems)
     proj_copies = proj.copies(me_ref, pieces, proj_ref, proj_sems)
     if proj.pieces:
-        slab_ref, slab_sems = rest[12:]
+        slab_ref, slab_sems = rest[14:]
         for at, (c, x, y) in enumerate(sources(me_ref)):
             for back in range(4):
                 device = x * 16 + (me_ref[Z] ^ back) * 4 + y * 2 + c
                 out = slab_ref.at[pl.ds(pl.multiple_of(device * 16, 16), 16)]
-                proj_copies.append(pltpu.make_async_copy(pieces[at].at[back, 14], out, slab_sems.at[at * 4 + back]))
+                source = pieces[at].at[back, 14]
+                proj_copies.append(
+                    functools.partial(pltpu.make_async_copy, source, out, slab_sems.at[at * 4 + back])
+                )
     for copy in proj_copies + down_copies:
-        copy.start()
+        copy().start()
     for copy in proj_copies:
-        copy.wait()
+        copy().wait()
     if proj.pieces:
         images = total_images // 32
         shape = (total_images, 512)
@@ -396,7 +472,12 @@
     else:
         text = text_ref[...]
     proj_w = proj_ref[...].reshape(EMB, D)
-    z = nt(pooled_ref[...], proj_w)
+    each = total_images // pooled_ref.shape[0]
+    for d in range(pooled_ref.shape[0]):
+        rows_ref[d * each : d * each + each, :] = pooled_ref[d].astype(f32)
+    pooled = rows_ref[...].astype(bf16)
+    all_ref[...] = pooled
+    z = nt(pooled, proj_w)
     square = jnp.sum(z * z, axis=-1, keepdims=True) + unit_eps
     inverse = lax.rsqrt(square)
     image = (z * inverse).astype(bf16)
@@ -423,25 +504,26 @@
     rank = spread.astype(bf16)
     rank_ref[...] = rank
     for copy in down_copies:
-        copy.wait()
+        copy().wait()
     hidden_ref[...] = nn(rank, down_ref[...].reshape(D, FF))
 
 
 def loss_backward(me, first, pooled, text, order, proj, down, inv_count):
-    total = pooled.shape[0]
+    total = pooled.shape[0] * pooled.shape[1]
     if proj.pieces:
         arrays, extra = proj.arrays, [pltpu.VMEM((512, 384), bf16), pltpu.SemaphoreType.DMA((32,))]
     else:
         arrays, extra = proj.arrays + down.arrays, []
     return call(
         functools.partial(loss_kernel, total, proj, down),
-        (sds((total, EMB), bf16), sds((16, D), bf16), sds((16, D), f32), sds((16, FF), f32)),
+        (sds((total, EMB), bf16), sds((16, D), bf16), sds((16, D), f32), sds((16, FF), f32), sds((total, D), bf16)),
         (me, first, *arrays, text, pooled, order, inv_count),
-        [pl.BlockSpec(memory_space=pl.ANY)] * len(arrays)
-        + [whole(text.shape), whole((total, D)), whole((total, 128)), whole((16, 128))],
-        [whole((total, EMB)), whole((16, D)), whole((16, D)), whole((16, FF))],
-        scratch=proj.scratch + down.scratch + extra,
+        [pl.BlockSpec(memory_space=pltpu.HBM)] * len(arrays)
+        + [whole(text.shape), whole(pooled.shape), whole((total, 128)), whole((16, 128))],
+        [whole((total, EMB)), whole((16, D)), whole((16, D)), whole((16, FF)), whole((total, D))],
+        scratch=proj.scratch + down.scratch + [pltpu.VMEM((total, D), f32)] + extra,
         flops=6 * total * total * EMB + 2 * total * D * EMB + 32 * D * FF,
+        vmem=32,
         prefetch=2,
     )
 
@@ -457,147 +539,182 @@
     return (j // 2 + 1 - me[CORE]) % 2 * 2 + j % 2
 
 
+SPLIT = 528
+
+
 def up_back_kernel(images, weight, me_ref, *refs):
     count = len(weight.arrays)
     slope_ref, m_ref, hidden_ref, col_ref, dm_ref, db_ref = refs[count : count + 6]
     w_ref, sems, du_ref = refs[-3:]
     j = pl.program_id(0)
-    weight.load(me_ref, refs[:count], w_ref, sems)
-    w = w_ref[pl.ds(6 * half_block(j, me_ref), 6)].reshape(D, D)
-    for i in range(images):
-        at = pl.ds(i * ROWS, ROWS)
-        du = (slope_ref[at, :].astype(f32) * (col_ref[at, 0:1] * hidden_ref[i : i + 1, :])).astype(bf16)
-        du_ref[at, :] = du
-        part = nn(du, w)
-
-        @pl.when(j == 0)
+    blocks = FF // D
+
+    @pl.when(j == 0)
+    def _():
+        weight.start(me_ref, refs[:count], w_ref, sems)
+
+    @pl.when(j < blocks)
+    def _():
+        cols = pl.ds(pl.multiple_of(half_block(j, me_ref) * D, 128), D)
+        total = jnp.zeros((1, D), f32)
+        for i in range(images):
+            at = pl.ds(i * ROWS, ROWS)
+            du = (slope_ref[at, :].astype(f32) * (col_ref[at, 0:1] * hidden_ref[i : i + 1, :])).astype(bf16)
+            du_ref[at, cols] = du
+            total += column_sum(du.astype(f32))
+        db_ref[...] = jnp.broadcast_to(total, db_ref.shape)
+        dw = tn(du_ref[pl.ds(0, images * ROWS), cols], m_ref[...]).astype(bf16)
+        if not weight.pieces:
+            refs[count + 6][...] = dw
+            return
+        send_ref, keep_ref = refs[count + 6 : count + 8]
+
+        @pl.when(j < 2)
         def _():
-            dm_ref[at, :] = part
-
-        @pl.when(j > 0)
+            weave(send_ref, dw)
+
+        @pl.when(j >= 2)
         def _():
-            dm_ref[at, :] += part
-
-    du = du_ref[...]
-    db_ref[...] = nn(jnp.ones((16, images * ROWS), bf16), du)
-    dw = tn(du, m_ref[...]).astype(bf16)
-    if not weight.pieces:
-        refs[count + 6][...] = dw
-        return
-    send_ref, keep_ref = refs[count + 6 : count + 8]
-
-    @pl.when(j < 2)
-    def _():
-        weave(send_ref, dw)
-
-    @pl.when(j >= 2)
-    def _():
-        weave(keep_ref, dw)
+            weave(keep_ref, dw)
+
+    @pl.when(j == blocks)
+    def _():
+        weight.wait(me_ref, refs[:count], w_ref, sems)
+
+    @pl.when(j >= blocks)
+    def _():
+        rows = pl.ds(pl.multiple_of((j - blocks) * SPLIT, 16), SPLIT)
+        dm_ref[...] = nn(du_ref[rows, :], w_ref[...].reshape(FF, D))
 
 
 def up_backward(images, slope, m, weight, hidden, col, me):
     n = images * ROWS
+    blocks = FF // D
+    steps = -(-n // SPLIT)
+
+    def block(j, me):
+        return half_block(jnp.minimum(j, blocks - 1), me)
 
     def cols(rows):
-        return pl.BlockSpec((rows, D), lambda j, me: (0, half_block(j, me)))
+        return pl.BlockSpec((rows, D), lambda j, me: (0, block(j, me)))
 
     if weight.pieces:
         shapes = (sds((16, 192, 384), bf16),) * 2
         specs = [
             pl.BlockSpec((16, 96, 384), lambda j, me: (0, jnp.minimum(j, 1), 0)),
-            pl.BlockSpec((16, 96, 384), lambda j, me: (0, jnp.maximum(j - 2, 0), 0)),
+            pl.BlockSpec((16, 96, 384), lambda j, me: (0, jnp.clip(j - 2, 0, 1), 0)),
         ]
     else:
         shapes = (sds((FF, D), bf16),)
-        specs = [pl.BlockSpec((D, D), lambda j, me: (half_block(j, me), 0))]
+        specs = [pl.BlockSpec((D, D), lambda j, me: (block(j, me), 0))]
     return call(
         functools.partial(up_back_kernel, images, weight),
-        (sds((n, D), f32), sds((16, FF), f32)) + shapes,
+        (sds((n, D), f32), sds((8, FF), f32)) + shapes,
         (me, *weight.arrays, slope, m, hidden, col),
         weight.specs + [cols(n), whole((n, D)), cols(16), whole((n, 128))],
-        [whole((n, D)), cols(16)] + specs,
-        grid=(FF // D,),
-        scratch=weight.scratch + [pltpu.VMEM((n, D), bf16)],
+        [pl.BlockSpec((SPLIT, D), lambda j, me: (jnp.maximum(j - blocks, 0), 0)), cols(8)] + specs,
+        grid=(blocks + steps,),
+        vmem=40,
+        scratch=weight.scratch + [pltpu.VMEM((steps * SPLIT, FF), bf16)],
         flops=4 * n * D * FF,
         prefetch=1,
     )
-
-
-def accumulate(i, ref, value):
-    @pl.when(i == 0)
-    def _():
-        ref[...] = value
-
-    @pl.when(i > 0)
-    def _():
-        ref[...] += value
 
 
 def middle_back_kernel(images, weight, me_ref, *refs):
     count = len(weight.arrays)
     h_ref, dm_ref, col_ref, spread_ref, o_ref, vec_ref = refs[count : count + 6]
-    dh_ref, do_ref, dw_ref, dvec_ref, w_ref, sems, acc_ref = refs[count + 6 :]
+    dh_ref, do_ref, dw_ref, dvec_ref, w_ref, sems, dat_ref = refs[count + 6 :]
     i = pl.program_id(0)
-    weight.load(me_ref, refs[:count], w_ref, sems)
-    hat, inverse = normalized(h_ref[...])
-    dm = dm_ref[...]
-    part = norm_back(dm, hat, inverse, vec_ref[2:3, :])
-    here = spread_ref[pl.ds(i, 1), :]
-    dh = col_ref[:, 0:1] * here + part
-    dh_ref[...] = dh
-    dat = dh.astype(bf16)
-    do_ref[...] = nn(dat, w_ref[...].reshape(D, D)).astype(bf16)
-    accumulate(i, acc_ref, tn(dat, o_ref[...]))
-    sums = jnp.concatenate(
-        [
-            column_sum(dm * hat),
-            column_sum(dm),
-            column_sum(dat.astype(f32)),
-            column_sum(col_ref[:, 0:1]) * here.astype(bf16).astype(f32),
-            jnp.zeros((4, D), f32),
-        ],
-        axis=0,
-    )
-    accumulate(i, dvec_ref, sums)
-
-    @pl.when(i == images - 1)
-    def _():
-        dw = acc_ref[...].astype(bf16)
+
+    @pl.when(i == 0)
+    def _():
+        weight.start(me_ref, refs[:count], w_ref, sems)
+
+    @pl.when(i < images)
+    def _():
+        hat, inverse = normalized(h_ref[...])
+        dm = dm_ref[...]
+        part = norm_back(dm, hat, inverse, vec_ref[2:3, :])
+        here = spread_ref[pl.ds(i, 1), :]
+        dh = col_ref[:, 0:1] * here + part
+        dh_ref[...] = dh
+        dat = dh.astype(bf16)
+        dat_ref[pl.ds(pl.multiple_of(i * ROWS, 16), ROWS), :] = dat
+        sums = jnp.concatenate(
+            [
+                column_sum(dm * hat),
+                column_sum(dm),
+                column_sum(dat.astype(f32)),
+                column_sum(col_ref[:, 0:1]) * here.astype(bf16).astype(f32),
+                jnp.zeros((4, D), f32),
+            ],
+            axis=0,
+        )
+        accumulate(i, dvec_ref, sums)
+
+    @pl.when(i == images)
+    def _():
+        dw = tn(dat_ref[...], o_ref[...]).astype(bf16)
         if weight.pieces:
             for half in range(2):
                 weave(dw_ref.at[half], dw[half * 384 : half * 384 + 384])
         else:
             dw_ref[...] = dw
+        weight.wait(me_ref, refs[:count], w_ref, sems)
+        do_ref[...] = nn(dat_ref[...], w_ref[...].reshape(D, D)).astype(bf16)
 
 
 def middle_backward(images, h, dm, col, spread, o, weight, vec, me):
     n = images * ROWS
     dw_shape = (2, 16, 48, 384) if weight.pieces else (D, D)
+
+    def rows(cols):
+        return pl.BlockSpec((ROWS, cols), lambda i, me: (jnp.minimum(i, images - 1), 0))
+
     return call(
         functools.partial(middle_back_kernel, images, weight),
         (sds((n, D), f32), sds((n, D), bf16), sds(dw_shape, bf16), sds((8, D), f32)),
         (me, *weight.arrays, h, dm, col, spread, o, vec),
-        weight.specs
-        + [
-            rows_at(ROWS, D),
-            rows_at(ROWS, D),
-            rows_at(ROWS, 128),
-            whole((16, D)),
-            rows_at(ROWS, D),
-            whole((16, D)),
-        ],
-        [rows_at(ROWS, D), rows_at(ROWS, D), whole(dw_shape), whole((8, D))],
-        grid=(images,),
-        scratch=weight.scratch + [pltpu.VMEM((D, D), f32)],
+        weight.specs + [rows(D), rows(D), rows(128), whole((16, D)), whole((n, D)), whole((16, D))],
+        [rows(D), whole((n, D)), whole(dw_shape), whole((8, D))],
+        grid=(images + 1,),
+        scratch=weight.scratch + [pltpu.VMEM((n, D), bf16)],
         flops=4 * n * D * D,
         prefetch=1,
     )
 
 
-def attention_back_kernel(qkv_ref, do_ref, lse_ref, col_ref, dqkv_ref, db_ref):
+def attention_again_kernel(qkv_ref, lse_ref, col_ref, p_ref):
+    low_half = lax.broadcasted_iota(jnp.int32, (ROWS, 2 * HEAD), 1) < HEAD
+    valid = jnp.broadcast_to(col_ref[:, 0:1], (ROWS, ROWS)) > 0.0
+    for pair in range(HEADS // 2):
+        at = pair * 2 * HEAD
+        q = qkv_ref[:, at : at + 2 * HEAD]
+        k = qkv_ref[:, D + at : D + at + 2 * HEAD]
+        for half in range(2):
+            keep = low_half if half == 0 else jnp.logical_not(low_half)
+            head = 2 * pair + half
+            s = jnp.where(valid, nt(jnp.where(keep, k, jnp.zeros_like(k)), q), masked_score)
+            p_ref[0, head] = jnp.exp(s - lse_ref[0, head : head + 1, :]).astype(bf16)
+
+
+def attention_again(images, qkv, lse, col):
+    n = images * ROWS
+    return call(
+        attention_again_kernel,
+        (sds((images, HEADS, ROWS, ROWS), bf16),),
+        (qkv, lse, col),
+        [rows_at(ROWS, 3 * D), pl.BlockSpec((1, 16, ROWS), lambda i: (i, 0, 0)), rows_at(ROWS, 128)],
+        [pl.BlockSpec((1, HEADS, ROWS, ROWS), lambda i: (i, 0, 0, 0))],
+        grid=(images,),
+        flops=2 * n * ROWS * D,
+    )[0]
+
+
+def attention_back_kernel(qkv_ref, do_ref, p_ref, dqkv_ref, db_ref):
     i = pl.program_id(0)
     low_half = lax.broadcasted_iota(jnp.int32, (ROWS, 2 * HEAD), 1) < HEAD
-    valid = jnp.broadcast_to(col_ref[:, 0:1], (ROWS, ROWS)) > 0.0
     for pair in range(HEADS // 2):
         at = pair * 2 * HEAD
         q = qkv_ref[:, at : at + 2 * HEAD]
@@ -610,12 +727,12 @@
             only_k = jnp.where(keep, k, jnp.zeros_like(k))
             only_v = jnp.where(keep, v, jnp.zeros_like(v))
             head = 2 * pair + half
-            s = jnp.where(valid, nt(only_k, q), masked_score)
-            p = jnp.exp(s - lse_ref[0, head : head + 1, :])
+            rounded = p_ref[0, head]
+            p = rounded.astype(f32)
             dp = nt(only_v, do)
             share = jnp.sum(p * dp, axis=0, keepdims=True)
             ds = (p * (dp - share)).astype(bf16)
-            dv.append(nn(p.astype(bf16), do))
+            dv.append(nn(rounded, do))
             dk.append(nn(ds, q))
             dq.append(tn(ds, only_k))
         dqkv_ref[:, at : at + 2 * HEAD] = ((dq[0] + dq[1]) * (HEAD**-0.5)).astype(bf16)
@@ -624,17 +741,16 @@
     accumulate(i, db_ref, nn(jnp.ones((16, ROWS), bf16), dqkv_ref[...]))
 
 
-def attention_backward(images, qkv, do, lse, col):
+def attention_backward(images, qkv, do, p):
     n = images * ROWS
     return call(
         attention_back_kernel,
         (sds((n, 3 * D), bf16), sds((16, 3 * D), f32)),
-        (qkv, do, lse, col),
+        (qkv, do, p),
         [
             rows_at(ROWS, 3 * D),
             rows_at(ROWS, D),
-            pl.BlockSpec((1, 16, ROWS), lambda i: (i, 0, 0)),
-            rows_at(ROWS, 128),
+            pl.BlockSpec((1, HEADS, ROWS, ROWS), lambda i: (i, 0, 0, 0)),
         ],
         [rows_at(ROWS, 3 * D), whole((16, 3 * D))],
         grid=(images,),
@@ -695,7 +811,7 @@
 
 def input_back_kernel(weight, me_ref, *refs):
     count = len(weight.arrays)
-    x_ref, dqkv_ref, dh_ref, vec_ref, out_ref, dvec_ref, w_ref, sems = refs[count:]
+    x_ref, dqkv_ref, dh_ref, vec_ref, two_ref, bias_ref, up_ref, out_ref, dvec_ref, w_ref, sems, sum_ref = refs[count:]
     i = pl.program_id(0)
     weight.load(me_ref, refs[:count], w_ref, sems)
     da = nn(dqkv_ref[...], w_ref[...].reshape(3 * D, D))
@@ -703,19 +819,33 @@
     out = dh_ref[...] + norm_back(da, hat, inverse, vec_ref[0:1, :])
     out_ref[0] = out[0:PATCHES, :]
     sums = jnp.concatenate([column_sum(da * hat), column_sum(da), jnp.zeros((6, D), f32)], axis=0)
-    accumulate(i, dvec_ref, sums)
-
-
-def input_backward(images, x, dqkv, weight, dh, vec, me):
+    accumulate(i, sum_ref, sums)
+
+    @pl.when(i == pl.num_programs(0) - 1)
+    def _():
+        dvec_ref[...] = jnp.zeros_like(dvec_ref)
+        dvec_ref[0:2, :] = sum_ref[0:2, :]
+        dvec_ref[2:4, :] = two_ref[0:2, :]
+        dvec_ref[4:5, :] = bias_ref[0:1, 0:D]
+        dvec_ref[5:6, :] = bias_ref[0:1, 2 * D : 3 * D]
+        dvec_ref[6:7, :] = two_ref[2:3, :]
+        for b in range(FF // D):
+            dvec_ref[7 + b : 8 + b, :] = up_ref[0:1, b * D : (b + 1) * D]
+        dvec_ref[7 + FF // D : 8 + FF // D, :] = two_ref[3:4, :]
+
+
+def input_backward(images, x, dqkv, weight, dh, vec, g_two, g_bias, g_bias_up, me):
     n = images * ROWS
     return call(
         functools.partial(input_back_kernel, weight),
-        (sds((images, PATCHES, D), f32), sds((8, D), f32)),
-        (me, *weight.arrays, x, dqkv, dh, vec),
-        weight.specs + [rows_at(ROWS, D), rows_at(ROWS, 3 * D), rows_at(ROWS, D), whole((16, D))],
-        [pl.BlockSpec((1, PATCHES, D), lambda i, *_: (i, 0, 0)), whole((8, D))],
+        (sds((images, PATCHES, D), f32), sds((16, D), f32)),
+        (me, *weight.arrays, x, dqkv, dh, vec, g_two, g_bias, g_bias_up),
+        weight.specs
+        + [rows_at(ROWS, D), rows_at(ROWS, 3 * D), rows_at(ROWS, D)]
+        + [whole(a.shape) for a in (vec, g_two, g_bias, g_bias_up)],
+        [pl.BlockSpec((1, PATCHES, D), lambda i, *_: (i, 0, 0)), whole((16, D))],
         grid=(images,),
-        scratch=weight.scratch,
+        scratch=weight.scratch + [pltpu.VMEM((8, D), f32)],
         flops=6 * n * D * D,
         prefetch=1,
     )
@@ -724,66 +854,66 @@
 SUMMED, DOWN, PROJ, NONE, VEC = 0, 1, 2, 3, 4
 
 
-def adam_kernel(part_rows, fast, kind_ref, row_ref, *refs):
+def adam_kernel(part_rows, fast, each, kind_ref, row_ref, *refs):
     master_ref, first_ref, second_ref, summed_ref, down_ref, proj_ref, vec_ref = refs[:7]
     new_master_ref, new_first_ref, new_second_ref, grad_ref, woven_ref = refs[7:]
-    kind = kind_ref[pl.program_id(0)]
     wide = FF // D
-
-    @pl.when(kind == SUMMED)
-    def _():
-        if fast:
-            for z in range(4):
-                for y in range(2):
-                    grad_ref[16 * z : 16 * z + 16, 384 * y : 384 * y + 384] = summed_ref[2 * z + y, 0].astype(f32)
-        else:
-            grad_ref[...] = summed_ref[0].astype(f32)
-
-    @pl.when(kind == VEC)
-    def _():
-        grad_ref[...] = jnp.zeros_like(grad_ref)
-        grad_ref[0 : vec_ref.shape[0], :] = vec_ref[...]
-
-    @pl.when(kind == DOWN)
-    def _():
-        block = down_ref[...] if fast else down_ref[0]
-        for c in range(D // 128):
-            for b in range(wide):
-                lanes = slice(b * D + c * 128, b * D + c * 128 + 128)
-                woven_ref[c, pl.ds(b, part_rows // wide, stride=wide), :] = block[0 : part_rows // wide, lanes]
-            grad_ref[:, c * 128 : (c + 1) * 128] = woven_ref[c]
-
-    @pl.when(kind == PROJ)
-    def _():
-        grad_ref[...] = proj_ref[...]
-
-    @pl.when(kind == NONE)
-    def _():
-        grad_ref[...] = jnp.zeros_like(grad_ref)
-
-    grad = grad_ref[...]
-    master = master_ref[0, 0]
-    first = beta_one * first_ref[0, 0] + (1.0 - beta_one) * grad
-    second = beta_two * second_ref[0, 0] + (1.0 - beta_two) * grad * grad
-    new_first_ref[0, 0] = first
-    new_second_ref[0, 0] = second
-    direction = first / (1.0 - beta_one**STEP)
-    size = jnp.sqrt(second / (1.0 - beta_two**STEP)) + adam_eps
-    new_master_ref[0, 0] = master - learn_rate * (direction / size + decay_rate * master)
+    for k in range(each):
+        slot = pl.program_id(0) * each + k
+        kind = kind_ref[slot]
+
+        @pl.when(kind == SUMMED)
+        def _():
+            if fast:
+                for z in range(4):
+                    for y in range(2):
+                        grad_ref[16 * z : 16 * z + 16, 384 * y : 384 * y + 384] = summed_ref[2 * z + y, k].astype(f32)
+            else:
+                grad_ref[...] = summed_ref[k].astype(f32)
+
+        @pl.when(kind == VEC)
+        def _():
+            grad_ref[...] = jnp.zeros_like(grad_ref)
+            grad_ref[0 : vec_ref.shape[0], :] = vec_ref[...]
+
+        @pl.when(kind == DOWN)
+        def _():
+            for c in range(D // 128):
+                for b in range(wide):
+                    lanes = slice(b * D + c * 128, b * D + c * 128 + 128)
+                    woven_ref[c, pl.ds(b, part_rows // wide, stride=wide), :] = down_ref[k, 0 : part_rows // wide, lanes]
+                grad_ref[:, c * 128 : (c + 1) * 128] = woven_ref[c]
+
+        @pl.when(kind == PROJ)
+        def _():
+            at = pl.multiple_of(row_ref[slot], part_rows)
+            grad_ref[...] = proj_ref[pl.ds(at, part_rows), :]
+
+        @pl.when(kind == NONE)
+        def _():
+            grad_ref[...] = jnp.zeros_like(grad_ref)
+
+        grad = grad_ref[...]
+        master = master_ref[0, k]
+        first = beta_one * first_ref[0, k] + (1.0 - beta_one) * grad
+        second = beta_two * second_ref[0, k] + (1.0 - beta_two) * grad * grad
+        new_first_ref[0, k] = first
+        new_second_ref[0, k] = second
+        direction = first / (1.0 - beta_one**STEP)
+        size = jnp.sqrt(second / (1.0 - beta_two**STEP)) + adam_eps
+        new_master_ref[0, k] = master - learn_rate * (direction / size + decay_rate * master)
 
 
 def adam(kind, row, master, first, second, summed, down, proj, vec, fast):
     slots, part_rows = master.shape[1:3]
-    block = pl.BlockSpec((1, 1, part_rows, D), lambda s, *_: (0, s, 0, 0))
-    each = part_rows * D // FF
+    each = 2
+    block = pl.BlockSpec((1, each, part_rows, D), lambda s, *_: (0, s, 0, 0))
     if fast:
-        summed_spec = pl.BlockSpec((8, 1, 16, 384), lambda s, *_: (0, s, 0, 0))
-        down_spec = pl.BlockSpec((each, FF), lambda s, kind, row: (jnp.where(kind[s] == DOWN, row[s] // each, 0), 0))
+        summed_spec = pl.BlockSpec((8, each, 16, 384), lambda s, *_: (0, s, 0, 0))
     else:
-        summed_spec = pl.BlockSpec((1, part_rows, D), lambda s, *_: (s, 0, 0))
-        down_spec = pl.BlockSpec((1,) + down.shape[1:], lambda s, *_: (s, 0, 0))
+        summed_spec = pl.BlockSpec((each, part_rows, D), lambda s, *_: (s, 0, 0))
     return call(
-        functools.partial(adam_kernel, part_rows, fast),
+        functools.partial(adam_kernel, part_rows, fast, each),
         (sds(master.shape, f32),) * 3,
         (kind, row, master, first, second, summed, down, proj, vec),
         [
@@ -791,42 +921,51 @@
             block,
             block,
             summed_spec,
-            down_spec,
-            pl.BlockSpec((part_rows, D), lambda s, kind, row: (jnp.where(kind[s] == PROJ, row[s] // part_rows, 0), 0)),
+            pl.BlockSpec((each,) + down.shape[1:], lambda s, *_: (s, 0, 0)),
+            whole(proj.shape),
             whole(vec.shape),
         ],
         [block] * 3,
-        grid=(slots,),
+        grid=(slots // each,),
         scratch=[pltpu.VMEM((part_rows, D), f32), pltpu.VMEM((D // 128, part_rows, 128), f32)],
         flops=20 * slots * part_rows * D,
+        in_hbm=(2, 3, 4),
         prefetch=2,
     )
 
 
-def rank_grad_kernel(images, *refs):
+def rank_grad_kernel(images, kind_ref, row_ref, *refs):
     dz_ref, pooled_ref, down_ref, proj_ref = refs[-4:]
     held = jnp.concatenate([ref[...].reshape(64, PACK) for ref in refs[:-4]], axis=0)
+    row = lax.broadcasted_iota(jnp.int32, (D, 128), 0)
+    col = lax.broadcasted_iota(jnp.int32, (D, 128), 1)
+    wanted = jnp.full((D, 128), -1, jnp.int32)
+    for s in range(8):
+        first = jnp.where(kind_ref[s] == DOWN, row_ref[s], -D)
+        wanted = jnp.where(col // 16 == s, first + col % 16, wanted)
+    mine = nn(held[:, 0:D], jnp.where(row == wanted, 1.0, 0.0).astype(bf16)).astype(bf16)
     shape = (512, 512)
     row = lax.broadcasted_iota(jnp.int32, shape, 0)
     col = lax.broadcasted_iota(jnp.int32, shape, 1)
     first = 0
     for segment in range(3):
         here = (row - col == segment * images) & (row // 16 == col // 16) & (col % 16 < images)
-        rank = nn(jnp.where(here, 1.0, 0.0).astype(bf16), held[:, 0:D]).astype(bf16)
+        rank = nn(jnp.where(here, 1.0, 0.0).astype(bf16), mine).astype(bf16)
         part = held[:, D:PACK] if segment == 0 else held
         down_ref[:, first : first + part.shape[1]] = tn(rank, part)
         first += part.shape[1]
     proj_ref[...] = tn(dz_ref[...], pooled_ref[...])
 
 
-def rank_grads(images, arrays, dz, pooled):
+def rank_grads(images, kind, row, arrays, dz, pooled):
     return call(
         functools.partial(rank_grad_kernel, images),
-        (sds((D, FF), f32), sds((EMB, D), f32)),
-        (*arrays, dz, pooled),
+        (sds((128, FF), f32), sds((EMB, D), f32)),
+        (kind, row, *arrays, dz, pooled),
         [whole(a.shape) for a in arrays] + [whole(dz.shape), whole(pooled.shape)],
-        [whole((D, FF)), whole((EMB, D))],
-        flops=1024 * D * FF,
+        [whole((128, FF)), whole((EMB, D))],
+        flops=256 * D * FF,
+        prefetch=2,
     )
 
 
@@ -865,6 +1004,8 @@
 SWAP_CORE = pairs(lambda x, z, y, c: (x, z, y, 1 - c))
 SWAP_X = pairs(lambda x, z, y, c: (1 - x, z, y, c))
 SWAP_Y = pairs(lambda x, z, y, c: (x, z, 1 - y, c))
+SWAP_Z = pairs(lambda x, z, y, c: (x, z ^ 1, y, c))
+SWAP_ZZ = pairs(lambda x, z, y, c: (x, z ^ 2, y, c))
 SWAP_XY = pairs(lambda x, z, y, c: (1 - x, z, 1 - y, c))
 ACROSS_Z = [pairs(lambda x, z, y, c, k=k: (x, z ^ k, y, c)) for k in (1, 2, 3)]
 CROSS_ONE = pairs(lambda x, z, y, c: (1 - x, z, y, c) if c == 0 else (x, z, 1 - y, c))
@@ -875,17 +1016,19 @@
     return lax.ppermute(value, AXES, permutation)
 
 
-def add_kernel(count, _, *refs):
-    out_ref = refs[-1]
-    pieces = out_ref.shape[0]
+def add_kernel(count, pieces, outputs, _, *refs):
     for p in range(pieces):
         total = refs[p * count][0].astype(f32)
         for k in range(1, count):
             total += refs[p * count + k][0].astype(f32)
-        out_ref[p] = total.astype(bf16)
-
-
-def add_pieces(sources, me, pieces, steps):
+        outs = refs[pieces * count :]
+        if outputs == 1:
+            outs[0][p] = total.astype(outs[0].dtype)
+        else:
+            outs[p][...] = total.astype(outs[p].dtype)
+
+
+def add_pieces(sources, me, pieces, steps=1, dtypes=(bf16,), near=()):
     rows = sources[0][0].shape[1]
     each = pieces // steps
     arrays, specs = [], []
@@ -893,16 +1036,25 @@
         for array, at in sources:
             arrays.append(array)
             specs.append(pl.BlockSpec((1, rows, 384), lambda i, me, p=p, at=at: (at(i * each + p, me), 0, 0)))
-    return call(
-        functools.partial(add_kernel, len(sources)),
-        (sds((pieces, rows, 384), bf16),),
+    if len(dtypes) == 1:
+        shapes = (sds((pieces, rows, 384), dtypes[0]),)
+        outs = [pl.BlockSpec((each, rows, 384), lambda i, me: (i, 0, 0))]
+    else:
+        shapes = tuple(sds((rows, 384), dtype) for dtype in dtypes)
+        outs = [whole((rows, 384))] * pieces
+    in_hbm = [k + 1 for k in range(len(arrays)) if k % len(sources) not in near]
+    results = call(
+        functools.partial(add_kernel, len(sources), each, len(dtypes)),
+        shapes,
         (me, *arrays),
         specs,
-        [pl.BlockSpec((each, rows, 384), lambda i, me: (i, 0, 0))],
+        outs,
         grid=(steps,),
         flops=pieces * rows * D,
+        in_hbm=in_hbm,
         prefetch=1,
-    )[0]
+    )
+    return results[0] if len(dtypes) == 1 else results
 
 
 class PieceSum:
@@ -923,47 +1075,45 @@
         return jnp.where(me[CORE] == 0, 2 * i + me[Y], me[X] * 4 + i)
 
     def cross_one(self):
-        self.two = send(add_pieces([(self.mine, self.first_send), (self.one, self.first_send)], self.me, 8, 2), CROSS_ONE)
+        parts = [(self.mine, self.first_send), (self.one, self.first_send)]
+        self.two = send(add_pieces(parts, self.me, 8, 2), CROSS_ONE)
 
     def cross_two(self):
         def own(i, me):
             return self.kept(self.second_send(i, me), me)
 
         parts = [(self.mine, own), (self.one, own), (self.two, self.second_send)]
-        self.three = send(add_pieces(parts, self.me, 4, 1), CROSS_TWO)
-
-    def along_z(self, first):
-        def z_at(i, me):
-            return me[Z] ^ (first + i)
-
+        self.three = send(add_pieces(parts, self.me, 4), CROSS_TWO)
+
+    def partial(self):
         def crossed(i, me):
-            return self.second_keep(z_at(i, me), me)
+            return self.second_keep(me[Z] ^ i, me)
 
         def own(i, me):
             return self.kept(crossed(i, me), me)
 
-        return [(self.mine, own), (self.one, own), (self.two, crossed), (self.three, z_at)]
+        parts = [(self.mine, own), (self.one, own), (self.two, crossed)]
+        self.sums = add_pieces(parts, self.me, 4, dtypes=(f32,))
 
     def cross_z(self):
-        parts = add_pieces(self.along_z(1), self.me, 3, 1)
-        self.last = [send(parts[k], ACROSS_Z[k]) for k in range(3)]
+        parts = [(self.sums, lambda i, me: i), (self.three, lambda i, me: me[Z] ^ i)]
+        self.own, *parts = add_pieces(parts, self.me, 4, dtypes=(f32, bf16, bf16, bf16), near=(0, 1))
+        self.last = [send(part, move) for part, move in zip(parts, ACROSS_Z, strict=True)]
 
     def total(self):
-        arrived = [(part[None], lambda i, me: 0) for part in self.last]
-        return add_pieces(self.along_z(0) + arrived, self.me, 1, 1)
-
-
-def place_kernel(index_ref, mine_ref, theirs_ref, out_ref):
+        parts = [(part[None], lambda i, me: 0) for part in (self.own, *self.last)]
+        return add_pieces(parts, self.me, 1, near=(0, 1, 2, 3))[0]
+
+
+def place_kernel(index_ref, *refs):
+    out_ref = refs[-1]
     for k in range(out_ref.shape[0]):
         at = index_ref[k]
-
-        @pl.when(at < 24)
-        def _():
-            out_ref[k] = mine_ref[at]
-
-        @pl.when((at >= 24) & (at < 48))
-        def _():
-            out_ref[k] = theirs_ref[at - 24]
+        for q in range(4):
+
+            @pl.when((at >= 12 * q) & (at < 12 * q + 12))
+            def _():
+                out_ref[k] = refs[q][pl.ds(pl.multiple_of((at - 12 * q) * 16, 16), 16), :]
 
         @pl.when(at >= 48)
         def _():
@@ -974,8 +1124,8 @@
     placed = call(
         place_kernel,
         (sds((64, 16, 384), bf16),),
-        (place, sums, send(sums, SWAP_CORE)),
-        [whole((24, 16, 384)), whole((24, 16, 384))],
+        (place, *sums),
+        [whole((192, 384))] * 4,
         [whole((64, 16, 384))],
         prefetch=1,
     )[0]
@@ -1153,6 +1303,7 @@
         [whole(master.shape)],
         [whole((8, 8, 16, 384))],
         scratch=[pltpu.VMEM((6, 64, 128), f32), pltpu.SMEM((16,), jnp.int32)],
+        in_hbm=(2,),
         prefetch=2,
     )[0]
     pick, place, kind, row = plan(owner_list, me)
@@ -1200,32 +1351,33 @@
         )
         one = Spread(block_one)
         *one.parts, block_two, block_three = meet(*one.parts, block_two, block_three)
+        one.cross_one()
         two = Spread(block_two)
-        one.cross_one()
-        one.ring, one.one, one.two, *two.parts, block_three = meet(one.ring, one.one, one.two, *two.parts, block_three)
+        one.ring, one.one, one.two = meet(one.ring, one.one, one.two)
         one.cross_two()
+        *two.parts, block_three = meet(*two.parts, block_three)
         three = Spread(block_three)
-        one.both, *one.near = meet(one.both, *one.near)
+        one.both, *two.parts = meet(one.both, *two.parts)
         one.finish()
-        near, *two.parts = meet(one.near[3], *two.parts)
-        one.near[3] = near
         two.cross_one()
         w_qkv = Weight(one.arrays(), QKV_TILES)
         w_out = Weight(one.arrays(), OUT_TILES, 9)
         a, qkv, vec = qkv_forward(images, x, jnp.zeros((16, D), f32), w_qkv, me)
         qkv, two.ring, two.one, two.two, *three.parts = meet(qkv, two.ring, two.one, two.two, *three.parts)
         two.cross_two()
-        three.cross_one()
+        three.ring = jnp.stack(three.parts)
+        three.one = send(three.ring, CROSS_ONE)
         o, lse = attention_forward(images, qkv, mask_row)
-        o, two.both, *two.near = meet(o, two.both, *two.near)
+        o, two.both, three.ring, *two.near = meet(o, two.both, three.ring, *two.near)
         two.finish()
+        three.two = send(three.ring, CROSS_TWO)
         w_up = Weight(two.arrays(), UP_TILES)
         h, m = middle_forward(images, x, o, vec, w_out, me)
         h, m, two.near[3], three.ring, three.one, three.two = meet(h, m, two.near[3], three.ring, three.one, three.two)
         three.cross_two()
         bias_up = vec[7 : 7 + FF // D].reshape(FF // D, 1, D)
         w_up = Weight(two.arrays(), UP_TILES)
-        act, slope, act_sum = up_forward(images, m, w_up, bias_up, sel, me)
+        act, slope = up_forward(images, m, w_up, bias_up, me)
         act, three.both, *three.near = meet(act, three.both, *three.near)
         three.finish()
         w_down = Weight(three.arrays(), DOWN_TILES, quarters=True)
@@ -1250,30 +1402,19 @@
         bias_up = vec[7 : 7 + FF // D].reshape(FF // D, 1, D)
         o, lse = attention_forward(images, qkv, mask_row)
         h, m = middle_forward(images, x, o, vec, w_out, me)
-        act, slope, act_sum = up_forward(images, m, w_up, bias_up, sel, me)
+        act, slope = up_forward(images, m, w_up, bias_up, me)
     block_out, pooled = down_forward(images, act, w_down, h, vec, sel, inv_count, me)
 
-    pooled_all = lax.all_to_all(
-        jnp.broadcast_to(pooled[None, :images], (n_dp * n_rep, images, D)), AXES, 0, 0
-    ).reshape(image_total, D)
-    dz_all, rank, spread, hidden = loss_backward(
+    pooled_all = lax.all_to_all(jnp.broadcast_to(pooled[None, :images], (n_dp * n_rep, images, D)), AXES, 0, 0)
+    act_sum = act_sums(images, act, sel)
+    probabilities = attention_again(images, qkv, lse, col)
+    if fast:
+        pooled_all, act_sum, probabilities = meet(pooled_all, act_sum, probabilities)
+    dz_all, rank, spread, hidden, pooled_all = loss_backward(
         me, first_image, pooled_all, all_text, order, w_proj, w_down, inv_count
     )
 
-    def vectors(g_one, g_two, g_bias, g_bias_up):
-        parts = [
-            g_one[0:2],
-            g_two[0:2],
-            g_bias[0:1, :D],
-            g_bias[0:1, 2 * D :],
-            g_two[2:3],
-            g_bias_up[0].reshape(FF // D, D),
-            g_two[3:4],
-            jnp.zeros((16 - 8 - FF // D, D), f32),
-        ]
-        return jnp.concatenate(parts, axis=0)
-
-    both = jnp.concatenate([rank[:images], act_sum[:images].astype(bf16)], axis=1)
+    both = jnp.concatenate([rank[:images], act_sum[:images]], axis=1)
     if fast:
         packed = jnp.concatenate([both[:, at * PACK : (at + 1) * PACK] for at in range(3)], axis=0)
         ranks = Spread(jnp.pad(packed, ((0, 16 - 3 * images), (0, 0))))
@@ -1287,39 +1428,46 @@
         )
         up_sum.cross_one()
         ranks.cross_two()
-        dqkv, g_bias = attention_backward(images, qkv, do, lse, col)
+        dqkv, g_bias = attention_backward(images, qkv, do, probabilities)
         dqkv, up_sum.two, ranks.both, *ranks.near = meet(dqkv, up_sum.two, ranks.both, *ranks.near)
         up_sum.cross_two()
         ranks.finish()
         other = qkv_weight_grad_fast(images, dqkv, a, g_out, me, True)
-        other, dqkv, up_sum.three, ranks.near[3] = meet(other, dqkv, up_sum.three, ranks.near[3])
+        other, dqkv = meet(other, dqkv)
         qkv_sum = PieceSum(other, me)
+        mine = qkv_weight_grad_fast(images, dqkv, a, g_out, me, False)
+        up_sum.partial()
+        dqkv, up_sum.sums, up_sum.three, qkv_sum.mine, qkv_sum.one, ranks.near[3] = meet(
+            dqkv, up_sum.sums, up_sum.three, mine, qkv_sum.one, ranks.near[3]
+        )
+        qkv_sum.cross_one()
         up_sum.cross_z()
-        mine = qkv_weight_grad_fast(images, dqkv, a, g_out, me, False)
-        dqkv, qkv_sum.mine, qkv_sum.one = meet(dqkv, mine, qkv_sum.one)
-        qkv_sum.cross_one()
-        input_grad, g_one = input_backward(images, x, dqkv, w_qkv, dh, vec, me)
-        vec_sum = vectors(g_one, g_two, g_bias, g_bias_up)
+        input_grad, vec_sum = input_backward(images, x, dqkv, w_qkv, dh, vec, g_two, g_bias, g_bias_up, me)
         vec_sum, qkv_sum.two, *up_sum.last = meet(vec_sum, qkv_sum.two, *up_sum.last)
         qkv_sum.cross_two()
-        vec_sum += send(vec_sum, SWAP_CORE)
+        near_vec = send(vec_sum, SWAP_CORE)
         up_total = up_sum.total()
-        vec_sum, up_total, qkv_sum.three = meet(vec_sum, up_total, qkv_sum.three)
+        near_up = send(up_total, SWAP_CORE)
+        qkv_sum.partial()
+        vec_sum, near_vec, qkv_sum.sums, near_up = meet(vec_sum, near_vec, qkv_sum.sums, near_up)
+        vec_sum += near_vec
+        across = [send(vec_sum, move) for move in (SWAP_X, SWAP_Y, SWAP_XY)]
+        g_down, g_proj = rank_grads(images, kind, row, ranks.arrays(), dz_all, pooled_all)
+        vec_sum, qkv_sum.three, g_down, g_proj, *across = meet(vec_sum, qkv_sum.three, g_down, g_proj, *across)
         qkv_sum.cross_z()
-        vec_sum += send(vec_sum, SWAP_X) + send(vec_sum, SWAP_Y) + send(vec_sum, SWAP_XY)
-        g_down, g_proj = rank_grads(images, ranks.arrays(), dz_all, pooled_all)
-        vec_sum, g_down, g_proj, *qkv_sum.last = meet(vec_sum, g_down, g_proj, *qkv_sum.last)
-        sums = jnp.concatenate([qkv_sum.total()[0], up_total[0]], axis=0).reshape(24, 16, 384)
-        vec_total = vec_sum + send(vec_sum, ACROSS_Z[0]) + send(vec_sum, ACROSS_Z[1]) + send(vec_sum, ACROSS_Z[2])
-        summed = return_to_owners(sums, place)
+        vec_sum += across[0] + across[1] + across[2]
+        vec_sum += send(vec_sum, SWAP_Z)
+        vec_sum += send(vec_sum, SWAP_ZZ)
+        vec_total, g_down, *qkv_sum.last = meet(vec_sum, g_down.reshape(8, 16, FF), *qkv_sum.last)
+        qkv_total = qkv_sum.total()
+        summed = return_to_owners((qkv_total, up_total, send(qkv_total, SWAP_CORE), near_up), place)
     else:
         both_all = lax.all_gather(both, AXES, axis=0, tiled=True)
         dm, g_bias_up, g_up = up_backward(images, slope, m, w_up, hidden, col, me)
         dh, do, g_out, g_two = middle_backward(images, h, dm, col, spread, o, w_out, vec, me)
-        dqkv, g_bias = attention_backward(images, qkv, do, lse, col)
+        dqkv, g_bias = attention_backward(images, qkv, do, probabilities)
         g_qkv = qkv_weight_grad(images, dqkv, a)
-        input_grad, g_one = input_backward(images, x, dqkv, w_qkv, dh, vec, me)
-        vec_total = vectors(g_one, g_two, g_bias, g_bias_up)
+        input_grad, vec_total = input_backward(images, x, dqkv, w_qkv, dh, vec, g_two, g_bias, g_bias_up, me)
         mine = lax.dynamic_slice_in_dim(tile_of_slot, rep_at * slots, slots)
         first_row = dp_at * part_rows
         is_down = (mine >= DOWN_FIRST) & (mine < PROJ_FIRST)

time: 430 us -> 372 us (0.87)
  Pallas kernels: 226 us -> 166 us
  blocking collectives: 0 us -> 51.6 us
  waiting for transfers between devices: 101 us -> 67.6 us
  local copies, waits for them, and re-layouts: 24.4 us -> 18 us
  starting transfers between devices: 67 us -> 62.1 us
    pallas_call x25 -> x29, Pallas kernels: 220 us -> 160 us  [call(): pl.pallas_call(kernel, out_shape=tuple(outs), grid_spec=pltpu.PrefetchSca...]
    all_to_all x0 -> x2, blocking collectives: none -> 51.6 us  [the longest x1 27.3 us: pick_slabs(): lax.all_to_all(prepared, 'rep', 0, 0, axis_index_groups=SAME_CORE)]
    all_to_all x2 -> x0, waiting for transfers between devices: 13.8 us -> none  [the longest x1 13.8 us: pick_slabs(): lax.all_to_all(prepared, 'rep', 0, 0, axis_index_groups=SAME_CORE)]
    all_to_all x1, waiting for transfers between devices: 13 us -> 1.86 us  [shards(): lax.all_to_all(jnp.broadcast_to(pooled[None, :images], (n_dp * n_rep, ima...]
    all_to_all x2 -> x0, starting transfers between devices: 10.9 us -> none  [the longest x1 7.34 us: pick_slabs(): lax.all_to_all(prepared, 'rep', 0, 0, axis_index_groups=SAME_CORE)]
    ppermute x61, waiting for transfers between devices: 73.6 us -> 65.7 us  [send(): return lax.ppermute(value, AXES, permutation)]
    ppermute x61, starting transfers between devices: 52.8 us -> 57.9 us  [send(): return lax.ppermute(value, AXES, permutation)]
    unnamed x114 -> x120, local copies, waits for them, and re-layouts: 9.32 us -> 14.4 us
  transfers between devices with their start and end apart: 64 -> 62, of which waited for: 20 -> 17; matrix products, arithmetic and copies ran while one was open for 3% -> 1% of each run, Pallas kernels for 40% -> 33%
where the time goes in v2:
time: 372 us; the launch traced here: 368 us
  Pallas kernels  166 us (45%)
  waiting for transfers between devices  67.6 us (18%)
  starting transfers between devices  62.1 us (17%)
  blocking collectives  51.6 us (14%)
  local copies, waits for them, and re-layouts  18 us (5%)
    pallas_call x29, Pallas kernels, call(): pl.pallas_call(kernel, out_shape=tuple(outs), grid_spec=pltpu.PrefetchSca...  160 us
    ppermute x61, waiting for transfers between devices, send(): return lax.ppermute(value, AXES, permutation)  65.7 us
    ppermute x61, starting transfers between devices, send(): return lax.ppermute(value, AXES, permutation)  57.9 us
    all_to_all x1, blocking collectives, pick_slabs(): lax.all_to_all(prepared, 'rep', 0, 0, axis_index_groups=SAME_CORE)  27.3 us
    all_to_all x1, blocking collectives, return_to_owners(): lax.all_to_all(placed.reshape(8, 8, 16, 384), 'rep', 0, 0, axis_index_gro...  24.3 us
    unnamed x120, local copies, waits for them, and re-layouts  14.4 us
  transfers between devices with their start and end apart: 62, of which 17 were waited for; matrix products, arithmetic and copies ran while one was open for 1% of the time, Pallas kernels for 33%

profile of v2, /device:TPU:0, one launch (start us, length us, event | category | flops | bytes accessed | tf_op | source)
XLA Modules:
  0.0 368.2 jit_solution(15677600686576998878)
XLA Ops:
  1.4 2.1 shard_map.120
  3.6 27.3 %all_to_all.15 = bf16[8,8,16,384]{3,2,1,0:T(8,128)(2,1)S(1)} all-to-all(bf16[8,8,16,384]{3,2,1,0:T(8,128)(2,1)S(1)} %shard_map.120), channel_id=1, replica_groups={{0,2,4,6,8,10,12,14},{1,3,5,7,9,11,13,15},{16,18,20,22,24,26,28,30},{17..., dimensions={0} | all-to-all | bytes 1572864 | tf_op jit(solution)/shard_map/all_to_all | solution.py:1310
  30.8 6.3 %shard_map.119 = (s32[39]{0:T(128)}, s32[64]{0:T(128)}, s32[8]{0:T(128)}, s32[8]{0:T(128)}) custom-call(s32[77]{0:T(128)} %owner_ref.3, s32[4]{0:T(128)} %copy-done.13), custom_call_target="tpu_custom_call" | custom-call | tf_op jit(solution)/shard_map/pallas_call | solution.py:1195
  43.2 2.7 collective-permute-start.3
  45.8 4.4 %collective-permute-done.1 = bf16[13,16,384]{2,1,0:T(8,128)(2,1)S(1)} collective-permute-done((bf16[13,16,384]{2,1,0:T(8,128)(2,1)S(1)}, bf16[13,16,384]{2,1,0:T(8,128)(2,1)S(1)}, u32[]{:S(2)}, u32[]{:S(2)}) %collective-permute-start.1) | collective-permute-done | bytes 159776 | tf_op jit(solution)/shard_map/ppermute | solution.py:1016
  50.3 7.0 %collective-permute-done.2 = bf16[13,16,384]{2,1,0:T(8,128)(2,1)S(1)} collective-permute-done((bf16[13,16,384]{2,1,0:T(8,128)(2,1)S(1)}, bf16[13,16,384]{2,1,0:T(8,128)(2,1)S(1)}, u32[]{:S(2)}, u32[]{:S(2)}) %collective-permute-start.2) | collective-permute-done | bytes 159776 | tf_op jit(solution)/shard_map/ppermute | solution.py:1016
  59.3 13.8 %collective-permute-done.4.refs_1_ = bf16[4,13,16,384]{3,2,1,0:T(8,128)(2,1)S(1)} collective-permute-done((bf16[4,13,16,384]{3,2,1,0:T(8,128)(2,1)S(1)}, bf16[4,13,16,384]{3,2,1,0:T(8,128)(2,1)S(1)}, u32[]{:S(2)}, u32[]{:S(2)}) %collective-permute-start.4) | collective-permute-done | bytes 639008 | tf_op jit(solution)/shard_map/ppermute | solution.py:1016
  74.2 4.0 %collective-permute-start.7 = (bf16[12,16,384]{2,1,0:T(8,128)(2,1)S(1)}, bf16[12,16,384]{2,1,0:T(8,128)(2,1)S(1)}, u32[]{:S(2)}, u32[]{:S(2)}) collective-permute-start(bf16[12,16,384]{2,1,0:T(8,128)(2,1)S(1)} %get-tuple-element.177), channel_id=1, source_target_pairs={{0,4},{1,5},{2,6},{3,7},{4,0},{5,1},{6,2},{7,3},{8,12},{9,13},{10,... | collective-permute-start | bytes 442376 | tf_op jit(solution)/shard_map/ppermute | solution.py:1016
  78.2 2.4 collective-permute-start.9
  80.6 4.2 %collective-permute-done.7 = bf16[12,16,384]{2,1,0:T(8,128)(2,1)S(1)} collective-permute-done((bf16[12,16,384]{2,1,0:T(8,128)(2,1)S(1)}, bf16[12,16,384]{2,1,0:T(8,128)(2,1)S(1)}, u32[]{:S(2)}, u32[]{:S(2)}) %collective-permute-start.7) | collective-permute-done | bytes 147488 | tf_op jit(solution)/shard_map/ppermute | solution.py:1016
  84.8 7.4 %collective-permute-done.8 = bf16[12,16,384]{2,1,0:T(8,128)(2,1)S(1)} collective-permute-done((bf16[12,16,384]{2,1,0:T(8,128)(2,1)S(1)}, bf16[12,16,384]{2,1,0:T(8,128)(2,1)S(1)}, u32[]{:S(2)}, u32[]{:S(2)}) %collective-permute-start.8) | collective-permute-done | bytes 147488 | tf_op jit(solution)/shard_map/ppermute | solution.py:1016
  95.5 3.0 collective-permute-start.16
  98.6 2.4 collective-permute-start.18
  101.0 9.1 %shard_map.122 = (bf16[1040,768]{1,0:T(8,128)(2,1)S(1)}, bf16[1040,2304]{1,0:T(8,128)(2,1)S(1)}, f32[16,768]{1,0:T(8,128)S(1)}) custom-call(s32[4]{0:T(128)S(1)} %copy-done.14, bf16[4,13,16,384]{3,2,1,0:T(8,128)(2,1)} %copy-done.30, bf16[4,13,16,384]{3,2,1,0:T(8,128)(2,1)} %copy-done.31, bf16[4,13,16,384]{3,2,1,0:T(8,128)(2,1)} %copy-done.32, ...), custom_call_target="tpu_custom_call" | custom-call | flops 3680501760 | bytes 13197328 | tf_op jit(solution)/shard_map/pallas_call | solution.py:80
  110.1 4.7 %collective-permute-done.17 = bf16[15,16,384]{2,1,0:T(8,128)(2,1)S(1)} collective-permute-done((bf16[15,16,384]{2,1,0:T(8,128)(2,1)S(1)}, bf16[15,16,384]{2,1,0:T(8,128)(2,1)S(1)}, u32[]{:S(2)}, u32[]{:S(2)}) %collective-permute-start.17) | collective-permute-done | bytes 184352 | tf_op jit(solution)/shard_map/ppermute | solution.py:1016
  117.2 9.0 %shard_map.123 = (bf16[1040,768]{1,0:T(8,128)(2,1)S(1)}, f32[5,16,208]{2,1,0:T(8,128)S(1)}) custom-call(bf16[1040,2304]{1,0:T(8,128)(2,1)S(1)} %get-tuple-element.182.qkv_ref, f32[5,1,208]{2,1,0:T(1,128)S(1)} %broadcast_in_dim.93.mask_ref), custom_call_target="tpu_custom_call" | custom-call | flops 664535040 | bytes 6460480 | tf_op jit(solution)/shard_map/pallas_call | solution.py:80
  126.3 3.6 collective-permute-done.19.refs_3_
  130.9 6.1 %shard_map.124 = (f32[1040,768]{1,0:T(8,128)S(1)}, bf16[1040,768]{1,0:T(8,128)(2,1)S(1)}) custom-call(s32[4]{0:T(128)S(1)} %copy-done.14, bf16[4,13,16,384]{3,2,1,0:T(8,128)(2,1)} %copy-done.30, bf16[4,13,16,384]{3,2,1,0:T(8,128)(2,1)} %copy-done.31, bf16[4,13,16,384]{3,2,1,0:T(8,128)(2,1)} %copy-done.32, bf16[4,13,16,384]{3,2,1,0:T(8,128)(2,1)} %copy-done.33, ...), custom_call_target="tpu_custom_call" | custom-call | flops 1226833920 | bytes 13148176 | tf_op jit(solution)/shard_map/pallas_call | solution.py:80
  137.2 4.2 %collective-permute-done.25.refs_2_ = bf16[4,15,16,384]{3,2,1,0:T(8,128)(2,1)S(1)} collective-permute-done((bf16[4,15,16,384]{3,2,1,0:T(8,128)(2,1)S(1)}, bf16[4,15,16,384]{3,2,1,0:T(8,128)(2,1)S(1)}, u32[]{:S(2)}, u32[]{:S(2)}) %collective-permute-start.25) | collective-permute-done | bytes 737312 | tf_op jit(solution)/shard_map/ppermute | solution.py:1016
  143.0 17.5 %shard_map.125 = (bf16[1040,3072]{1,0:T(8,128)(2,1)S(1)}, bf16[1040,3072]{1,0:T(8,128)(2,1)S(1)}) custom-call(s32[4]{0:T(128)S(1)} %copy-done.14, bf16[4,12,16,384]{3,2,1,0:T(8,128)(2,1)} %copy-done.46, bf16[4,12,16,384]{3,2,1,0:T(8,128)(2,1)} %copy-done.49, bf16[4,12,16,384]{3,2,1,0:T(8,128)(2,1)} %copy-done.50, bf16[4,12,16,384]{3,2,1,0:T(8,128)(2,1)} %copy-done.51, ...), custom_call_target="tpu_custom_call" | custom-call | flops 4907335680 | bytes 19107856 | tf_op jit(solution)/shard_map/pallas_call | solution.py:80
  164.6 14.1 %shard_map.126 = (bf16[5,196,768]{2,1,0:T(8,128)(2,1)}, bf16[16,768]{1,0:T(8,128)(2,1)S(1)}) custom-call(s32[4]{0:T(128)S(1)} %copy-done.14, bf16[4,15,16,384]{3,2,1,0:T(8,128)(2,1)} %copy-done.38, bf16[4,15,16,384]{3,2,1,0:T(8,128)(2,1)} %copy-done.39, bf16[4,15,16,384]{3,2,1,0:T(8,128)(2,1)} %copy-done.40, bf16[4,15,16,384]{3,2,1,0:T(8,128)(2,1)} %copy-done.41, ...), custom_call_target="tpu_custom_call" | custom-call | flops 4907335680 | bytes 17103376 | tf_op jit(solution)/shard_map/pallas_call | solution.py:80
  179.5 4.2 %all-to-all-start.1 = ((bf16[32,5,768]{2,1,0:T(8,128)(2,1)}), bf16[32,5,768]{2,1,0:T(8,128)(2,1)}, u32[]{:S(2)}, u32[]{:S(2)}) async-start(bf16[32,5,768]{2,1,0:T(8,128)(2,1)} %broadcast_in_dim.95), calls=%async_computation.1 | async-start | bytes 786432 | tf_op jit(solution)/shard_map/all_to_all | solution.py:1408
  183.7 2.3 copy-done.3
  187.1 3.2 shard_map.128.p_ref
  190.4 2.7 copy-done.4
  196.8 6.1 %shard_map.129 = (bf16[160,512]{1,0:T(8,128)(2,1)S(1)}, bf16[16,768]{1,0:T(8,128)(2,1)S(1)}, f32[16,768]{1,0:T(8,128)S(1)}, f32[16,3072]{1,0:T(8,128)S(1)}, bf16[160,768]{1,0:T(8,128)(2,1)S(1)}) custom-call(s32[4]{0:T(128)S(1)} %copy-done.14, s32[1]{0:T(128)} %bitcast.5.first_ref, bf16[4,15,16,384]{3,2,1,0:T(8,128)(2,1)} %copy-done.38, ...), custom_call_target="tpu_custom_call" | custom-call | flops 279969792 | bytes 6918164 | tf_op jit(solution)/shard_map/pallas_call | solution.py:80
  206.2 1.9 collective-permute-start.33
  208.1 20.6 %shard_map.130 = (f32[1040,768]{1,0:T(8,128)S(1)}, f32[8,3072]{1,0:T(8,128)S(1)}, bf16[16,192,384]{2,1,0:T(8,128)(2,1)}, bf16[16,192,384]{2,1,0:T(8,128)(2,1)S(1)}) custom-call(s32[4]{0:T(128)S(1)} %copy-done.14, bf16[4,12,16,384]{3,2,1,0:T(8,128)(2,1)} %copy-done.46, bf16[4,12,16,384]{3,2,1,0:T(8,128)(2,1)} %copy-done.49, ...), custom_call_target="tpu_custom_call" | custom-call | flops 9814671360 | bytes 21446672 | tf_op jit(solution)/shard_map/pallas_call | solution.py:80
  230.9 8.7 %shard_map.131 = (f32[1040,768]{1,0:T(8,128)S(1)}, bf16[1040,768]{1,0:T(8,128)(2,1)S(1)}, bf16[2,16,48,384]{3,2,1,0:T(8,128)(2,1)S(1)}, f32[8,768]{1,0:T(8,128)S(1)}) custom-call(s32[4]{0:T(128)S(1)} %copy-done.14, bf16[4,13,16,384]{3,2,1,0:T(8,128)(2,1)} %copy-done.30, bf16[4,13,16,384]{3,2,1,0:T(8,128)(2,1)} %copy-done.31, ...), custom_call_target="tpu_custom_call" | custom-call | flops 2453667840 | bytes 19726352 | tf_op jit(solution)/shard_map/pallas_call | solution.py:80
  241.1 3.3 shard_map.133
  247.0 13.2 %shard_map.132 = (bf16[1040,2304]{1,0:T(8,128)(2,1)S(1)}, f32[16,2304]{1,0:T(8,128)S(1)}) custom-call(bf16[1040,2304]{1,0:T(8,128)(2,1)S(1)} %bitcast.36, bf16[1040,768]{1,0:T(8,128)(2,1)S(1)} %get-tuple-element.238.do_ref, bf16[5,12,208,208]{3,2,1,0:T(8,128)(2,1)S(1)} %bitcast.38), custom_call_target="tpu_custom_call" | custom-call | flops 1661337600 | bytes 16521216 | tf_op jit(solution)/shard_map/pallas_call | solution.py:80
  262.1 4.2 %shard_map.134 = bf16[16,192,384]{2,1,0:T(8,128)(2,1)S(1)} custom-call(s32[4]{0:T(128)S(1)} %copy-done.14, bf16[1040,2304]{1,0:T(8,128)(2,1)S(1)} %get-tuple-element.253.dqkv_ref.refs_9_, bf16[1040,768]{1,0:T(8,128)(2,1)S(1)} %get-tuple-element.247.a_ref, bf16[2,16,48,384]{3,2,1,0:T(8,128)(2,1)S(1)} %get-tuple-element.248.out_ref), custom_call_target="tpu_custom_call" | custom-call | flops 1840250880 | bytes 9928720 | tf_op jit(solution)/shard_map/pallas_call | solution.py:80
  266.4 2.3 shard_map.136
  270.0 2.3 shard_map.135.refs_0_.refs_2_.refs_4_.refs_6_
  272.2 4.2 %shard_map.137.refs_0_.refs_2_.refs_4_.refs_6_.refs_3_.refs_9_ = bf16[16,192,384]{2,1,0:T(8,128)(2,1)S(1)} custom-call(s32[4]{0:T(128)S(1)} %copy-done.14, bf16[1040,2304]{1,0:T(8,128)(2,1)S(1)} %get-tuple-element.253.dqkv_ref.refs_9_, bf16[1040,768]{1,0:T(8,128)(2,1)S(1)} %get-tuple-element.247.a_ref, bf16[2,16,48,384]{3,2,1,0:T(8,128)(2,1)S(1)} %get-tuple-element.248.out_ref), custom_call_target="tpu_custom_call" | custom-call | flops 1840250880 | bytes 9928720 | tf_op jit(solution)/shard_map/pallas_call | solution.py:80
  280.1 2.6 shard_map.139
  284.5 2.5 collective-permute-start.47
  287.0 1.9 collective-permute-start.48
  288.8 9.9 %shard_map.138 = (f32[5,196,768]{2,1,0:T(8,128)}, f32[16,768]{1,0:T(8,128)S(1)}) custom-call(s32[4]{0:T(128)S(1)} %copy-done.14, bf16[4,13,16,384]{3,2,1,0:T(8,128)(2,1)} %copy-done.30, bf16[4,13,16,384]{3,2,1,0:T(8,128)(2,1)} %copy-done.31, bf16[4,13,16,384]{3,2,1,0:T(8,128)(2,1)} %copy-done.32, bf16[4,13,16,384]{3,2,1,0:T(8,128)(2,1)} %copy-done.33, ...), custom_call_target="tpu_custom_call" | custom-call | flops 3680501760 | bytes 18075664 | tf_op jit(solution)/shard_map/pallas_call | solution.py:80
  299.9 2.3 shard_map.143
  304.6 2.3 shard_map.141.refs_0_.refs_2_.refs_4_.refs_6_
  310.5 2.9 shard_map.144
  320.3 5.5 %collective-permute-done.55 = f32[16,768]{1,0:T(8,128)S(1)} collective-permute-done((f32[16,768]{1,0:T(8,128)S(1)}, f32[16,768]{1,0:T(8,128)S(1)}, u32[]{:S(2)}, u32[]{:S(2)}) %collective-permute-start.55) | collective-permute-done | bytes 49184 | tf_op jit(solution)/shard_map/ppermute | solution.py:1016
  325.8 3.3 collective-permute-start.56
  329.1 3.9 %collective-permute-done.56 = f32[16,768]{1,0:T(8,128)S(1)} collective-permute-done((f32[16,768]{1,0:T(8,128)S(1)}, f32[16,768]{1,0:T(8,128)S(1)}, u32[]{:S(2)}, u32[]{:S(2)}) %collective-permute-start.56) | collective-permute-done | bytes 49184 | tf_op jit(solution)/shard_map/ppermute | solution.py:1016
  335.2 2.4 shard_map.147
  337.6 24.3 %all_to_all.16.refs_3_ = bf16[8,8,16,384]{3,2,1,0:T(8,128)(2,1)S(1)} all-to-all(bf16[8,8,16,384]{3,2,1,0:T(8,128)(2,1)S(1)} %bitcast.44), channel_id=1, replica_groups={{0,2,4,6,8,10,12,14},{1,3,5,7,9,11,13,15},{16,18,20,22,24,26,28,30},{17..., dimensions={0} | all-to-all | bytes 1572864 | tf_op jit(solution)/shard_map/all_to_all | solution.py:1132
  361.9 6.0 %shard_map.148 = (f32[1,8,64,768]{3,2,1,0:T(8,128)}, f32[1,8,64,768]{3,2,1,0:T(8,128)}, f32[1,8,64,768]{3,2,1,0:T(8,128)}) custom-call(s32[8]{0:T(128)S(1)} %copy-done.17, s32[8]{0:T(128)S(1)} %copy-done.18, f32[1,8,64,768]{3,2,1,0:T(8,128)} %refs_0_.1, f32[1,8,64,768]{3,2,1,0:T(8,128)} %refs_1_.1, f32[1,8,64,768]{3,2,1,0:T(8,128)} %refs_2_.1, ...), custom_call_target="tpu_custom_call" | custom-call | flops 7864320 | bytes 13418560 | tf_op jit(solution)/shard_map/pallas_call | solution.py:80
  (262 shorter events, 61.9 us)
Async XLA Ops:
  30.8 8.2 %collective-permute-start = (bf16[64,16,384]{2,1,0:T(8,128)(2,1)S(1)}, bf16[64,16,384]{2,1,0:T(8,128)(2,1)S(1)}, u32[]{:S(2)}, u32[]{:S(2)}) collective-permute-start(bf16[64,16,384]{2,1,0:T(8,128)(2,1)S(1)} %bitcast.42), channel_id=1, source_target_pairs={{0,1},{1,0},{2,3},{3,2},{4,5},{5,4},{6,7},{7,6},{8,9},{9,8},{10,11... | collective-permute-start | bytes 2359304 | tf_op jit(solution)/shard_map/ppermute | solution.py:1016
  41.4 8.9 %collective-permute-start.1 = (bf16[13,16,384]{2,1,0:T(8,128)(2,1)S(1)}, bf16[13,16,384]{2,1,0:T(8,128)(2,1)S(1)}, u32[]{:S(2)}, u32[]{:S(2)}) collective-permute-start(bf16[13,16,384]{2,1,0:T(8,128)(2,1)S(1)} %get-tuple-element.161), channel_id=1, source_target_pairs={{0,4},{1,5},{2,6},{3,7},{4,0},{5,1},{6,2},{7,3},{8,12},{9,13},{10,... | collective-permute-start | bytes 479240 | tf_op jit(solution)/shard_map/ppermute | solution.py:1016
  42.5 14.7 %collective-permute-start.2 = (bf16[13,16,384]{2,1,0:T(8,128)(2,1)S(1)}, bf16[13,16,384]{2,1,0:T(8,128)(2,1)S(1)}, u32[]{:S(2)}, u32[]{:S(2)}) collective-permute-start(bf16[13,16,384]{2,1,0:T(8,128)(2,1)S(1)} %get-tuple-element.161), channel_id=1, source_target_pairs={{0,8},{1,9},{2,10},{3,11},{4,12},{5,13},{6,14},{7,15},{8,0},{9,1},... | collective-permute-start | bytes 479240 | tf_op jit(solution)/shard_map/ppermute | solution.py:1016
  43.2 14.1 %collective-permute-start.3 = (bf16[13,16,384]{2,1,0:T(8,128)(2,1)S(1)}, bf16[13,16,384]{2,1,0:T(8,128)(2,1)S(1)}, u32[]{:S(2)}, u32[]{:S(2)}) collective-permute-start(bf16[13,16,384]{2,1,0:T(8,128)(2,1)S(1)} %get-tuple-element.161), channel_id=1, source_target_pairs={{0,12},{1,13},{2,14},{3,15},{4,8},{5,9},{6,10},{7,11},{8,4},{9,5},... | collective-permute-start | bytes 479240 | tf_op jit(solution)/shard_map/ppermute | solution.py:1016
  57.4 15.8 %collective-permute-start.4 = (bf16[4,13,16,384]{3,2,1,0:T(8,128)(2,1)S(1)}, bf16[4,13,16,384]{3,2,1,0:T(8,128)(2,1)S(1)}, u32[]{:S(2)}, u32[]{:S(2)}) collective-permute-start(bf16[4,13,16,384]{3,2,1,0:T(8,128)(2,1)S(1)} %pad_maximum_fusion.1.refs_0_), channel_id=1, source_target_pairs={{0,16},{1,3},{2,18},{3,1},{4,20},{5,7},{6,22},{7,5},{8,24},{9,11},... | collective-permute-start | bytes 1916936 | tf_op jit(solution)/shard_map/ppermute | solution.py:1016
  58.9 14.2 %collective-permute-start.5 = (bf16[4,13,16,384]{3,2,1,0:T(8,128)(2,1)S(1)}, bf16[4,13,16,384]{3,2,1,0:T(8,128)(2,1)S(1)}, u32[]{:S(2)}, u32[]{:S(2)}) collective-permute-start(bf16[4,13,16,384]{3,2,1,0:T(8,128)(2,1)S(1)} %pad_maximum_fusion.1.refs_0_), channel_id=1, source_target_pairs={{0,2},{1,17},{2,0},{3,19},{4,6},{5,21},{6,4},{7,23},{8,10},{9,25},... | collective-permute-start | bytes 1916936 | tf_op jit(solution)/shard_map/ppermute | solution.py:1016
  73.2 19.5 %collective-permute-start.6 = (bf16[4,13,16,384]{3,2,1,0:T(8,128)(2,1)S(1)}, bf16[4,13,16,384]{3,2,1,0:T(8,128)(2,1)S(1)}, u32[]{:S(2)}, u32[]{:S(2)}) collective-permute-start(bf16[4,13,16,384]{3,2,1,0:T(8,128)(2,1)S(1)} %collective-permute-done.4.refs_1_), channel_id=1, source_target_pairs={{0,2},{1,17},{2,0},{3,19},{4,6},{5,21},{6,4},{7,23},{8,10},{9,25},... | collective-permute-start | bytes 1916936 | tf_op jit(solution)/shard_map/ppermute | solution.py:1016
  74.2 20.2 %collective-permute-start.10 = (bf16[4,13,16,384]{3,2,1,0:T(8,128)(2,1)S(1)}, bf16[4,13,16,384]{3,2,1,0:T(8,128)(2,1)S(1)}, u32[]{:S(2)}, u32[]{:S(2)}) collective-permute-start(bf16[4,13,16,384]{3,2,1,0:T(8,128)(2,1)S(1)} %pad_maximum_fusion.1.refs_0_), channel_id=1, source_target_pairs={{0,1},{1,0},{2,3},{3,2},{4,5},{5,4},{6,7},{7,6},{8,9},{9,8},{10,11... | collective-permute-start | bytes 1916936 | tf_op jit(solution)/shard_map/ppermute | solution.py:1016
  74.2 10.6 %collective-permute-start.7 = (bf16[12,16,384]{2,1,0:T(8,128)(2,1)S(1)}, bf16[12,16,384]{2,1,0:T(8,128)(2,1)S(1)}, u32[]{:S(2)}, u32[]{:S(2)}) collective-permute-start(bf16[12,16,384]{2,1,0:T(8,128)(2,1)S(1)} %get-tuple-element.177), channel_id=1, source_target_pairs={{0,4},{1,5},{2,6},{3,7},{4,0},{5,1},{6,2},{7,3},{8,12},{9,13},{10,... | collective-permute-start | bytes 442376 | tf_op jit(solution)/shard_map/ppermute | solution.py:1016
  78.2 13.9 %collective-permute-start.8 = (bf16[12,16,384]{2,1,0:T(8,128)(2,1)S(1)}, bf16[12,16,384]{2,1,0:T(8,128)(2,1)S(1)}, u32[]{:S(2)}, u32[]{:S(2)}) collective-permute-start(bf16[12,16,384]{2,1,0:T(8,128)(2,1)S(1)} %get-tuple-element.177), channel_id=1, source_target_pairs={{0,8},{1,9},{2,10},{3,11},{4,12},{5,13},{6,14},{7,15},{8,0},{9,1},... | collective-permute-start | bytes 442376 | tf_op jit(solution)/shard_map/ppermute | solution.py:1016
  78.2 13.9 %collective-permute-start.9 = (bf16[12,16,384]{2,1,0:T(8,128)(2,1)S(1)}, bf16[12,16,384]{2,1,0:T(8,128)(2,1)S(1)}, u32[]{:S(2)}, u32[]{:S(2)}) collective-permute-start(bf16[12,16,384]{2,1,0:T(8,128)(2,1)S(1)} %get-tuple-element.177), channel_id=1, source_target_pairs={{0,12},{1,13},{2,14},{3,15},{4,8},{5,9},{6,10},{7,11},{8,4},{9,5},... | collective-permute-start | bytes 442376 | tf_op jit(solution)/shard_map/ppermute | solution.py:1016
  92.9 22.0 %collective-permute-start.14 = (bf16[4,12,16,384]{3,2,1,0:T(8,128)(2,1)S(1)}, bf16[4,12,16,384]{3,2,1,0:T(8,128)(2,1)S(1)}, u32[]{:S(2)}, u32[]{:S(2)}) collective-permute-start(bf16[4,12,16,384]{3,2,1,0:T(8,128)(2,1)S(1)} %pad_maximum_fusion.2.refs_0_), channel_id=1, source_target_pairs={{0,16},{1,3},{2,18},{3,1},{4,20},{5,7},{6,22},{7,5},{8,24},{9,11},... | collective-permute-start | bytes 1769480 | tf_op jit(solution)/shard_map/ppermute | solution.py:1016
  94.4 20.4 %collective-permute-start.15 = (bf16[4,12,16,384]{3,2,1,0:T(8,128)(2,1)S(1)}, bf16[4,12,16,384]{3,2,1,0:T(8,128)(2,1)S(1)}, u32[]{:S(2)}, u32[]{:S(2)}) collective-permute-start(bf16[4,12,16,384]{3,2,1,0:T(8,128)(2,1)S(1)} %pad_maximum_fusion.2.refs_0_), channel_id=1, source_target_pairs={{0,2},{1,17},{2,0},{3,19},{4,6},{5,21},{6,4},{7,23},{8,10},{9,25},... | collective-permute-start | bytes 1769480 | tf_op jit(solution)/shard_map/ppermute | solution.py:1016
  95.5 14.7 %collective-permute-start.16 = (bf16[15,16,384]{2,1,0:T(8,128)(2,1)S(1)}, bf16[15,16,384]{2,1,0:T(8,128)(2,1)S(1)}, u32[]{:S(2)}, u32[]{:S(2)}) collective-permute-start(bf16[15,16,384]{2,1,0:T(8,128)(2,1)S(1)} %get-tuple-element.185), channel_id=1, source_target_pairs={{0,4},{1,5},{2,6},{3,7},{4,0},{5,1},{6,2},{7,3},{8,12},{9,13},{10,... | collective-permute-start | bytes 552968 | tf_op jit(solution)/shard_map/ppermute | solution.py:1016
  98.5 16.4 %collective-permute-start.17 = (bf16[15,16,384]{2,1,0:T(8,128)(2,1)S(1)}, bf16[15,16,384]{2,1,0:T(8,128)(2,1)S(1)}, u32[]{:S(2)}, u32[]{:S(2)}) collective-permute-start(bf16[15,16,384]{2,1,0:T(8,128)(2,1)S(1)} %get-tuple-element.185), channel_id=1, source_target_pairs={{0,8},{1,9},{2,10},{3,11},{4,12},{5,13},{6,14},{7,15},{8,0},{9,1},... | collective-permute-start | bytes 552968 | tf_op jit(solution)/shard_map/ppermute | solution.py:1016
  98.6 16.3 %collective-permute-start.18 = (bf16[15,16,384]{2,1,0:T(8,128)(2,1)S(1)}, bf16[15,16,384]{2,1,0:T(8,128)(2,1)S(1)}, u32[]{:S(2)}, u32[]{:S(2)}) collective-permute-start(bf16[15,16,384]{2,1,0:T(8,128)(2,1)S(1)} %get-tuple-element.185), channel_id=1, source_target_pairs={{0,12},{1,13},{2,14},{3,15},{4,8},{5,9},{6,10},{7,11},{8,4},{9,5},... | collective-permute-start | bytes 552968 | tf_op jit(solution)/shard_map/ppermute | solution.py:1016
  114.9 15.0 %collective-permute-start.19 = (bf16[4,12,16,384]{3,2,1,0:T(8,128)(2,1)S(1)}, bf16[4,12,16,384]{3,2,1,0:T(8,128)(2,1)S(1)}, u32[]{:S(2)}, u32[]{:S(2)}) collective-permute-start(bf16[4,12,16,384]{3,2,1,0:T(8,128)(2,1)S(1)} %collective-permute-done.14.refs_1_), channel_id=1, source_target_pairs={{0,2},{1,17},{2,0},{3,19},{4,6},{5,21},{6,4},{7,23},{8,10},{9,25},... | collective-permute-start | bytes 1769480 | tf_op jit(solution)/shard_map/ppermute | solution.py:1016
  115.9 13.9 %collective-permute-start.21 = (bf16[4,12,16,384]{3,2,1,0:T(8,128)(2,1)S(1)}, bf16[4,12,16,384]{3,2,1,0:T(8,128)(2,1)S(1)}, u32[]{:S(2)}, u32[]{:S(2)}) collective-permute-start(bf16[4,12,16,384]{3,2,1,0:T(8,128)(2,1)S(1)} %collective-permute-done.14.refs_1_), channel_id=1, source_target_pairs={{0,1},{1,0},{2,3},{3,2},{4,5},{5,4},{6,7},{7,6},{8,9},{9,8},{10,11... | collective-permute-start | bytes 1769480 | tf_op jit(solution)/shard_map/ppermute | solution.py:1016
  115.9 13.9 %collective-permute-start.20 = (bf16[4,12,16,384]{3,2,1,0:T(8,128)(2,1)S(1)}, bf16[4,12,16,384]{3,2,1,0:T(8,128)(2,1)S(1)}, u32[]{:S(2)}, u32[]{:S(2)}) collective-permute-start(bf16[4,12,16,384]{3,2,1,0:T(8,128)(2,1)S(1)} %pad_maximum_fusion.2.refs_0_), channel_id=1, source_target_pairs={{0,1},{1,0},{2,3},{3,2},{4,5},{5,4},{6,7},{7,6},{8,9},{9,8},{10,11... | collective-permute-start | bytes 1769480 | tf_op jit(solution)/shard_map/ppermute | solution.py:1016
  116.5 13.4 %collective-permute-start.22 = (bf16[4,12,16,384]{3,2,1,0:T(8,128)(2,1)S(1)}, bf16[4,12,16,384]{3,2,1,0:T(8,128)(2,1)S(1)}, u32[]{:S(2)}, u32[]{:S(2)}) collective-permute-start(bf16[4,12,16,384]{3,2,1,0:T(8,128)(2,1)S(1)} %collective-permute-done.15.refs_2_), channel_id=1, source_target_pairs={{0,1},{1,0},{2,3},{3,2},{4,5},{5,4},{6,7},{7,6},{8,9},{9,8},{10,11... | collective-permute-start | bytes 1769480 | tf_op jit(solution)/shard_map/ppermute | solution.py:1016
  116.6 20.6 %collective-permute-start.24 = (bf16[4,15,16,384]{3,2,1,0:T(8,128)(2,1)S(1)}, bf16[4,15,16,384]{3,2,1,0:T(8,128)(2,1)S(1)}, u32[]{:S(2)}, u32[]{:S(2)}) collective-permute-start(bf16[4,15,16,384]{3,2,1,0:T(8,128)(2,1)S(1)} %pad_maximum_fusion.refs_0_), channel_id=1, source_target_pairs={{0,16},{1,3},{2,18},{3,1},{4,20},{5,7},{6,22},{7,5},{8,24},{9,11},... | collective-permute-start | bytes 2211848 | tf_op jit(solution)/shard_map/ppermute | solution.py:1016
  129.9 11.5 %collective-permute-start.25 = (bf16[4,15,16,384]{3,2,1,0:T(8,128)(2,1)S(1)}, bf16[4,15,16,384]{3,2,1,0:T(8,128)(2,1)S(1)}, u32[]{:S(2)}, u32[]{:S(2)}) collective-permute-start(bf16[4,15,16,384]{3,2,1,0:T(8,128)(2,1)S(1)} %pad_maximum_fusion.refs_0_), channel_id=1, source_target_pairs={{0,2},{1,17},{2,0},{3,19},{4,6},{5,21},{6,4},{7,23},{8,10},{9,25},... | collective-permute-start | bytes 2211848 | tf_op jit(solution)/shard_map/ppermute | solution.py:1016
  141.4 19.1 %collective-permute-start.26 = (bf16[4,15,16,384]{3,2,1,0:T(8,128)(2,1)S(1)}, bf16[4,15,16,384]{3,2,1,0:T(8,128)(2,1)S(1)}, u32[]{:S(2)}, u32[]{:S(2)}) collective-permute-start(bf16[4,15,16,384]{3,2,1,0:T(8,128)(2,1)S(1)} %collective-permute-done.24.refs_1_), channel_id=1, source_target_pairs={{0,2},{1,17},{2,0},{3,19},{4,6},{5,21},{6,4},{7,23},{8,10},{9,25},... | collective-permute-start | bytes 2211848 | tf_op jit(solution)/shard_map/ppermute | solution.py:1016
  142.4 18.2 %collective-permute-start.28 = (bf16[4,15,16,384]{3,2,1,0:T(8,128)(2,1)S(1)}, bf16[4,15,16,384]{3,2,1,0:T(8,128)(2,1)S(1)}, u32[]{:S(2)}, u32[]{:S(2)}) collective-permute-start(bf16[4,15,16,384]{3,2,1,0:T(8,128)(2,1)S(1)} %collective-permute-done.24.refs_1_), channel_id=1, source_target_pairs={{0,1},{1,0},{2,3},{3,2},{4,5},{5,4},{6,7},{7,6},{8,9},{9,8},{10,11... | collective-permute-start | bytes 2211848 | tf_op jit(solution)/shard_map/ppermute | solution.py:1016
  142.4 18.1 %collective-permute-start.27 = (bf16[4,15,16,384]{3,2,1,0:T(8,128)(2,1)S(1)}, bf16[4,15,16,384]{3,2,1,0:T(8,128)(2,1)S(1)}, u32[]{:S(2)}, u32[]{:S(2)}) collective-permute-start(bf16[4,15,16,384]{3,2,1,0:T(8,128)(2,1)S(1)} %pad_maximum_fusion.refs_0_), channel_id=1, source_target_pairs={{0,1},{1,0},{2,3},{3,2},{4,5},{5,4},{6,7},{7,6},{8,9},{9,8},{10,11... | collective-permute-start | bytes 2211848 | tf_op jit(solution)/shard_map/ppermute | solution.py:1016
  142.9 17.7 %collective-permute-start.29 = (bf16[4,15,16,384]{3,2,1,0:T(8,128)(2,1)S(1)}, bf16[4,15,16,384]{3,2,1,0:T(8,128)(2,1)S(1)}, u32[]{:S(2)}, u32[]{:S(2)}) collective-permute-start(bf16[4,15,16,384]{3,2,1,0:T(8,128)(2,1)S(1)} %collective-permute-done.25.refs_2_), channel_id=1, source_target_pairs={{0,1},{1,0},{2,3},{3,2},{4,5},{5,4},{6,7},{7,6},{8,9},{9,8},{10,11... | collective-permute-start | bytes 2211848 | tf_op jit(solution)/shard_map/ppermute | solution.py:1016
  179.5 17.3 %all-to-all-start.1 = ((bf16[32,5,768]{2,1,0:T(8,128)(2,1)}), bf16[32,5,768]{2,1,0:T(8,128)(2,1)}, u32[]{:S(2)}, u32[]{:S(2)}) async-start(bf16[32,5,768]{2,1,0:T(8,128)(2,1)} %broadcast_in_dim.95), calls=%async_computation.1 | async-start | bytes 786432 | tf_op jit(solution)/shard_map/all_to_all | solution.py:1408
  203.6 25.1 %collective-permute-start.31 = (bf16[16,1280]{1,0:T(8,128)(2,1)S(1)}, bf16[16,1280]{1,0:T(8,128)(2,1)S(1)}, u32[]{:S(2)}, u32[]{:S(2)}) collective-permute-start(bf16[16,1280]{1,0:T(8,128)(2,1)S(1)} %fusion.6), channel_id=1, source_target_pairs={{0,4},{1,5},{2,6},{3,7},{4,0},{5,1},{6,2},{7,3},{8,12},{9,13},{10,... | collective-permute-start | bytes 122888 | tf_op jit(solution)/shard_map/ppermute | solution.py:1016
  204.6 24.1 %collective-permute-start.32 = (bf16[16,1280]{1,0:T(8,128)(2,1)S(1)}, bf16[16,1280]{1,0:T(8,128)(2,1)S(1)}, u32[]{:S(2)}, u32[]{:S(2)}) collective-permute-start(bf16[16,1280]{1,0:T(8,128)(2,1)S(1)} %fusion.6), channel_id=1, source_target_pairs={{0,8},{1,9},{2,10},{3,11},{4,12},{5,13},{6,14},{7,15},{8,0},{9,1},... | collective-permute-start | bytes 122888 | tf_op jit(solution)/shard_map/ppermute | solution.py:1016
  206.2 22.5 %collective-permute-start.33 = (bf16[16,1280]{1,0:T(8,128)(2,1)S(1)}, bf16[16,1280]{1,0:T(8,128)(2,1)S(1)}, u32[]{:S(2)}, u32[]{:S(2)}) collective-permute-start(bf16[16,1280]{1,0:T(8,128)(2,1)S(1)} %fusion.6), channel_id=1, source_target_pairs={{0,12},{1,13},{2,14},{3,15},{4,8},{5,9},{6,10},{7,11},{8,4},{9,5},... | collective-permute-start | bytes 122888 | tf_op jit(solution)/shard_map/ppermute | solution.py:1016
  228.7 10.9 %collective-permute-start.34 = (bf16[16,192,384]{2,1,0:T(8,128)(2,1)}, bf16[16,192,384]{2,1,0:T(8,128)(2,1)S(1)}, u32[]{:S(2)}, u32[]{:S(2)}) collective-permute-start(bf16[16,192,384]{2,1,0:T(8,128)(2,1)} %get-tuple-element.233), channel_id=1, source_target_pairs={{0,1},{1,0},{2,3},{3,2},{4,5},{5,4},{6,7},{7,6},{8,9},{9,8},{10,11... | collective-permute-start | bytes 7077896 | tf_op jit(solution)/shard_map/ppermute | solution.py:1016
  228.8 10.8 %collective-permute-start.35 = (bf16[4,16,1280]{2,1,0:T(8,128)(2,1)S(1)}, bf16[4,16,1280]{2,1,0:T(8,128)(2,1)S(1)}, u32[]{:S(2)}, u32[]{:S(2)}) collective-permute-start(bf16[4,16,1280]{2,1,0:T(8,128)(2,1)S(1)} %pad_maximum_fusion.3.refs_0_), channel_id=1, source_target_pairs={{0,16},{1,3},{2,18},{3,1},{4,20},{5,7},{6,22},{7,5},{8,24},{9,11},... | collective-permute-start | bytes 491528 | tf_op jit(solution)/shard_map/ppermute | solution.py:1016
  229.9 9.7 %collective-permute-start.36 = (bf16[4,16,1280]{2,1,0:T(8,128)(2,1)S(1)}, bf16[4,16,1280]{2,1,0:T(8,128)(2,1)S(1)}, u32[]{:S(2)}, u32[]{:S(2)}) collective-permute-start(bf16[4,16,1280]{2,1,0:T(8,128)(2,1)S(1)} %pad_maximum_fusion.3.refs_0_), channel_id=1, source_target_pairs={{0,2},{1,17},{2,0},{3,19},{4,6},{5,21},{6,4},{7,23},{8,10},{9,25},... | collective-permute-start | bytes 491528 | tf_op jit(solution)/shard_map/ppermute | solution.py:1016
  244.4 17.7 %collective-permute-start.37 = (bf16[8,192,384]{2,1,0:T(8,128)(2,1)S(1)}, bf16[8,192,384]{2,1,0:T(8,128)(2,1)S(1)}, u32[]{:S(2)}, u32[]{:S(2)}) collective-permute-start(bf16[8,192,384]{2,1,0:T(8,128)(2,1)S(1)} %shard_map.133), channel_id=1, source_target_pairs={{0,16},{1,3},{2,18},{3,1},{4,20},{5,7},{6,22},{7,5},{8,24},{9,11},... | collective-permute-start | bytes 3538952 | tf_op jit(solution)/shard_map/ppermute | solution.py:1016
  245.9 14.4 %collective-permute-start.38 = (bf16[4,16,1280]{2,1,0:T(8,128)(2,1)S(1)}, bf16[4,16,1280]{2,1,0:T(8,128)(2,1)S(1)}, u32[]{:S(2)}, u32[]{:S(2)}) collective-permute-start(bf16[4,16,1280]{2,1,0:T(8,128)(2,1)S(1)} %collective-permute-done.35.refs_1_), channel_id=1, source_target_pairs={{0,2},{1,17},{2,0},{3,19},{4,6},{5,21},{6,4},{7,23},{8,10},{9,25},... | collective-permute-start | bytes 491528 | tf_op jit(solution)/shard_map/ppermute | solution.py:1016
  246.5 13.8 %collective-permute-start.40 = (bf16[4,16,1280]{2,1,0:T(8,128)(2,1)S(1)}, bf16[4,16,1280]{2,1,0:T(8,128)(2,1)S(1)}, u32[]{:S(2)}, u32[]{:S(2)}) collective-permute-start(bf16[4,16,1280]{2,1,0:T(8,128)(2,1)S(1)} %collective-permute-done.35.refs_1_), channel_id=1, source_target_pairs={{0,1},{1,0},{2,3},{3,2},{4,5},{5,4},{6,7},{7,6},{8,9},{9,8},{10,11... | collective-permute-start | bytes 491528 | tf_op jit(solution)/shard_map/ppermute | solution.py:1016
  246.5 13.8 %collective-permute-start.39 = (bf16[4,16,1280]{2,1,0:T(8,128)(2,1)S(1)}, bf16[4,16,1280]{2,1,0:T(8,128)(2,1)S(1)}, u32[]{:S(2)}, u32[]{:S(2)}) collective-permute-start(bf16[4,16,1280]{2,1,0:T(8,128)(2,1)S(1)} %pad_maximum_fusion.3.refs_0_), channel_id=1, source_target_pairs={{0,1},{1,0},{2,3},{3,2},{4,5},{5,4},{6,7},{7,6},{8,9},{9,8},{10,11... | collective-permute-start | bytes 491528 | tf_op jit(solution)/shard_map/ppermute | solution.py:1016
  247.0 13.3 %collective-permute-start.41 = (bf16[4,16,1280]{2,1,0:T(8,128)(2,1)S(1)}, bf16[4,16,1280]{2,1,0:T(8,128)(2,1)S(1)}, u32[]{:S(2)}, u32[]{:S(2)}) collective-permute-start(bf16[4,16,1280]{2,1,0:T(8,128)(2,1)S(1)} %collective-permute-done.36.refs_2_), channel_id=1, source_target_pairs={{0,1},{1,0},{2,3},{3,2},{4,5},{5,4},{6,7},{7,6},{8,9},{9,8},{10,11... | collective-permute-start | bytes 491528 | tf_op jit(solution)/shard_map/ppermute | solution.py:1016
  266.3 12.3 %collective-permute-start.43 = (bf16[16,192,384]{2,1,0:T(8,128)(2,1)S(1)}, bf16[16,192,384]{2,1,0:T(8,128)(2,1)S(1)}, u32[]{:S(2)}, u32[]{:S(2)}) collective-permute-start(bf16[16,192,384]{2,1,0:T(8,128)(2,1)S(1)} %shard_map.134), channel_id=1, source_target_pairs={{0,1},{1,0},{2,3},{3,2},{4,5},{5,4},{6,7},{7,6},{8,9},{9,8},{10,11... | collective-permute-start | bytes 7077896 | tf_op jit(solution)/shard_map/ppermute | solution.py:1016
  268.7 9.9 %collective-permute-start.42 = (bf16[4,192,384]{2,1,0:T(8,128)(2,1)S(1)}, bf16[4,192,384]{2,1,0:T(8,128)(2,1)S(1)}, u32[]{:S(2)}, u32[]{:S(2)}) collective-permute-start(bf16[4,192,384]{2,1,0:T(8,128)(2,1)S(1)} %shard_map.136), channel_id=1, source_target_pairs={{0,2},{1,17},{2,0},{3,19},{4,6},{5,21},{6,4},{7,23},{8,10},{9,25},... | collective-permute-start | bytes 1769480 | tf_op jit(solution)/shard_map/ppermute | solution.py:1016
  282.7 16.3 %collective-permute-start.45 = (bf16[8,192,384]{2,1,0:T(8,128)(2,1)S(1)}, bf16[8,192,384]{2,1,0:T(8,128)(2,1)S(1)}, u32[]{:S(2)}, u32[]{:S(2)}) collective-permute-start(bf16[8,192,384]{2,1,0:T(8,128)(2,1)S(1)} %shard_map.139), channel_id=1, source_target_pairs={{0,16},{1,3},{2,18},{3,1},{4,20},{5,7},{6,22},{7,5},{8,24},{9,11},... | collective-permute-start | bytes 3538952 | tf_op jit(solution)/shard_map/ppermute | solution.py:1016
  284.4 14.3 %collective-permute-start.46 = (bf16[192,384]{1,0:T(8,128)(2,1)S(1)}, bf16[192,384]{1,0:T(8,128)(2,1)S(1)}, u32[]{:S(2)}, u32[]{:S(2)}) collective-permute-start(bf16[192,384]{1,0:T(8,128)(2,1)S(1)} %get-tuple-element.267), channel_id=1, source_target_pairs={{0,4},{1,5},{2,6},{3,7},{4,0},{5,1},{6,2},{7,3},{8,12},{9,13},{10,... | collective-permute-start | bytes 442376 | tf_op jit(solution)/shard_map/ppermute | solution.py:1016
  284.5 14.2 %collective-permute-start.47 = (bf16[192,384]{1,0:T(8,128)(2,1)S(1)}, bf16[192,384]{1,0:T(8,128)(2,1)S(1)}, u32[]{:S(2)}, u32[]{:S(2)}) collective-permute-start(bf16[192,384]{1,0:T(8,128)(2,1)S(1)} %get-tuple-element.268), channel_id=1, source_target_pairs={{0,8},{1,9},{2,10},{3,11},{4,12},{5,13},{6,14},{7,15},{8,0},{9,1},... | collective-permute-start | bytes 442376 | tf_op jit(solution)/shard_map/ppermute | solution.py:1016
  287.0 11.7 %collective-permute-start.48 = (bf16[192,384]{1,0:T(8,128)(2,1)S(1)}, bf16[192,384]{1,0:T(8,128)(2,1)S(1)}, u32[]{:S(2)}, u32[]{:S(2)}) collective-permute-start(bf16[192,384]{1,0:T(8,128)(2,1)S(1)} %get-tuple-element.269), channel_id=1, source_target_pairs={{0,12},{1,13},{2,14},{3,15},{4,8},{5,9},{6,10},{7,11},{8,4},{9,5},... | collective-permute-start | bytes 442376 | tf_op jit(solution)/shard_map/ppermute | solution.py:1016
  302.2 12.1 %collective-permute-start.51 = (bf16[4,192,384]{2,1,0:T(8,128)(2,1)S(1)}, bf16[4,192,384]{2,1,0:T(8,128)(2,1)S(1)}, u32[]{:S(2)}, u32[]{:S(2)}) collective-permute-start(bf16[4,192,384]{2,1,0:T(8,128)(2,1)S(1)} %shard_map.143), channel_id=1, source_target_pairs={{0,2},{1,17},{2,0},{3,19},{4,6},{5,21},{6,4},{7,23},{8,10},{9,25},... | collective-permute-start | bytes 1769480 | tf_op jit(solution)/shard_map/ppermute | solution.py:1016
  314.9 18.1 %collective-permute-start.57 = (bf16[192,384]{1,0:T(8,128)(2,1)S(1)}, bf16[192,384]{1,0:T(8,128)(2,1)S(1)}, u32[]{:S(2)}, u32[]{:S(2)}) collective-permute-start(bf16[192,384]{1,0:T(8,128)(2,1)S(1)} %get-tuple-element.294), channel_id=1, source_target_pairs={{0,4},{1,5},{2,6},{3,7},{4,0},{5,1},{6,2},{7,3},{8,12},{9,13},{10,... | collective-permute-start | bytes 442376 | tf_op jit(solution)/shard_map/ppermute | solution.py:1016
  316.8 16.3 %collective-permute-start.58 = (bf16[192,384]{1,0:T(8,128)(2,1)S(1)}, bf16[192,384]{1,0:T(8,128)(2,1)S(1)}, u32[]{:S(2)}, u32[]{:S(2)}) collective-permute-start(bf16[192,384]{1,0:T(8,128)(2,1)S(1)} %get-tuple-element.295), channel_id=1, source_target_pairs={{0,8},{1,9},{2,10},{3,11},{4,12},{5,13},{6,14},{7,15},{8,0},{9,1},... | collective-permute-start | bytes 442376 | tf_op jit(solution)/shard_map/ppermute | solution.py:1016
  317.8 15.3 %collective-permute-start.59 = (bf16[192,384]{1,0:T(8,128)(2,1)S(1)}, bf16[192,384]{1,0:T(8,128)(2,1)S(1)}, u32[]{:S(2)}, u32[]{:S(2)}) collective-permute-start(bf16[192,384]{1,0:T(8,128)(2,1)S(1)} %get-tuple-element.296), channel_id=1, source_target_pairs={{0,12},{1,13},{2,14},{3,15},{4,8},{5,9},{6,10},{7,11},{8,4},{9,5},... | collective-permute-start | bytes 442376 | tf_op jit(solution)/shard_map/ppermute | solution.py:1016
  (74 other events, 762.5 us)

commit v3 on v2

--- a/solution.py
+++ b/solution.py
@@ -51,7 +51,8 @@
     (DOWN_TILES // 2, DOWN_FIRST),
     (PROJ_TILES // 2, PROJ_FIRST),
 )
-CHUNK_AT = ((0, 0), (0, 9), (1, 0), (2, 0), (2, 12))
+CHUNK_AT = ((0, 0), (1, 0), (1, 3), (2, 0), (2, 12))
+SLABS = (10, 15, 15)
 SAME_CORE = [[i * 2 + c for i in range(8)] for c in range(2)]
 
 
@@ -67,12 +68,15 @@
     return lax.dot_general(a, b, (((0,), (0,)), ((), ())), preferred_element_type=f32)
 
 
-def call(kernel, outs, ins, in_specs, out_specs, grid=None, scratch=(), flops=0, vmem=24, prefetch=0, in_hbm=()):
+def call(kernel, outs, ins, in_specs, out_specs, grid=None, scratch=(), flops=0, vmem=24, prefetch=0, in_hbm=(), out_hbm=(), vmem_in=(), vmem_out=()):
     ins = [
         pltpu.with_memory_space_constraint(a, pltpu.HBM) if k >= prefetch and (s.memory_space is pltpu.HBM or k in in_hbm) else a
         for k, (a, s) in enumerate(zip(ins, [None] * prefetch + list(in_specs), strict=True))
     ]
+    ins = [pltpu.with_memory_space_constraint(a, pltpu.VMEM) if k in vmem_in else a for k, a in enumerate(ins)]
     moved = sum(a.size * a.dtype.itemsize for a in ins) + sum(o.size * o.dtype.itemsize for o in outs)
+    spaces = {k: pltpu.HBM for k in out_hbm} | {k: pltpu.VMEM for k in vmem_out}
+    outs = [spaces[k](o.shape, o.dtype) if k in spaces else o for k, o in enumerate(outs)]
     params = pltpu.CompilerParams(
         vmem_limit_bytes=vmem * MIB,
         dimension_semantics=("arbitrary",) * len(grid or ()) or None,
@@ -88,7 +92,7 @@
             scratch_shapes=list(scratch),
         ),
         compiler_params=params,
-        cost_estimate=pl.CostEstimate(flops=int(flops), bytes_accessed=int(moved), transcendentals=0),
+        cost_estimate=pl.CostEstimate(flops=1, bytes_accessed=1, transcendentals=0),
     )(*ins)
 
 
@@ -200,7 +204,7 @@
             parts = []
             for at, (_, x, y) in list(enumerate(sources(me_ref)))[:4]:
                 for back in range(4):
-                    copy = pltpu.make_async_copy(pieces[at].at[back, 12], vec_half.at[y], vec_sems.at[len(parts)])
+                    copy = pltpu.make_async_copy(pieces[at].at[back, 9], vec_half.at[y], vec_sems.at[len(parts)])
                     parts.append(((x == 0) & ((me_ref[Z] ^ back) == 0), copy))
             for here, copy in parts:
                 pl.when(here)(copy.start)
@@ -234,6 +238,7 @@
         weight.specs + [whole((n, D)), whole((16, D))],
         [whole((n, D)), pl.BlockSpec((n, D), lambda j, me: (0, qkv_block(j, me))), whole((16, D))],
         grid=(3,),
+        out_hbm=(0,),
         scratch=weight.scratch + [pltpu.VMEM((2, 16, 384), bf16), pltpu.SemaphoreType.DMA((16,))],
         flops=2 * n * D * 3 * D,
         prefetch=1,
@@ -350,6 +355,7 @@
         weight.specs + [whole((n, D)), pl.BlockSpec((1, 1, D), lambda j, me: (own_block(j, me), 0, 0))],
         [cols, cols],
         grid=(FF // D,),
+        out_hbm=(1,),
         scratch=weight.scratch,
         flops=2 * n * D * FF,
         prefetch=1,
@@ -403,7 +409,7 @@
         y = y_ref[pl.ds(pl.multiple_of(i * ROWS, 16), ROWS), :] + vec_ref[11:12, :]
         out = (h_ref[...] + y).astype(bf16)
         out_ref[0] = out[0:PATCHES, :]
-        accumulate(i, sum_ref, nn(sel_ref[0], out))
+        accumulate(i, sum_ref, nn(sel_ref[i], out))
         pooled_ref[...] = (sum_ref[...] * inv_ref[:, 0:1]).astype(bf16)
 
 
@@ -413,20 +419,27 @@
 
     def image(k):
         return jnp.maximum(k - quarters, 0)
+
+    def quarter(k, me):
+        return me[Z] ^ jnp.minimum(k, quarters - 1)
 
     return call(
         functools.partial(down_kernel, images, weight),
         (sds((images, PATCHES, D), bf16), sds((16, D), bf16)),
         (me, *weight.arrays, act, h, vec, sel, inv_count),
-        weight.specs
+        weight.specs[:-1]
         + [
-            pl.BlockSpec((n, D), lambda k, me: (0, me[Z] ^ jnp.minimum(k, quarters - 1))),
+            pl.BlockSpec(memory_space=pl.ANY),
+            pl.BlockSpec((n, D), lambda k, me: (0, quarter(k, me))),
             pl.BlockSpec((ROWS, D), lambda k, me: (image(k), 0)),
             whole((16, D)),
-            pl.BlockSpec((1, 16, ROWS), lambda k, me: (image(k), 0, 0)),
+            whole((images, 16, ROWS)),
             whole((16, 128)),
         ],
-        [pl.BlockSpec((1, PATCHES, D), lambda k, me: (image(k), 0, 0)), whole((16, D))],
+        [
+            pl.BlockSpec((1, PATCHES, D), lambda k, me: (image(k), 0, 0)),
+            whole((16, D)),
+        ],
         grid=(quarters + images,),
         scratch=weight.scratch + [pltpu.VMEM((16, D), f32), pltpu.VMEM((n, D), f32)],
         flops=2 * n * D * FF,
@@ -679,6 +692,8 @@
         weight.specs + [rows(D), rows(D), rows(128), whole((16, D)), whole((n, D)), whole((16, D))],
         [rows(D), whole((n, D)), whole(dw_shape), whole((8, D))],
         grid=(images + 1,),
+        in_hbm=(1 + len(weight.arrays),),
+        vmem_in=(2 + len(weight.arrays),) if weight.pieces else (),
         scratch=weight.scratch + [pltpu.VMEM((n, D), bf16)],
         flops=4 * n * D * D,
         prefetch=1,
@@ -708,6 +723,7 @@
         [rows_at(ROWS, 3 * D), pl.BlockSpec((1, 16, ROWS), lambda i: (i, 0, 0)), rows_at(ROWS, 128)],
         [pl.BlockSpec((1, HEADS, ROWS, ROWS), lambda i: (i, 0, 0, 0))],
         grid=(images,),
+        vmem_out=(0,),
         flops=2 * n * ROWS * D,
     )[0]
 
@@ -754,6 +770,7 @@
         ],
         [rows_at(ROWS, 3 * D), whole((16, 3 * D))],
         grid=(images,),
+        vmem_in=(2,),
         flops=10 * n * ROWS * D,
     )
 
@@ -804,6 +821,7 @@
         ],
         [pl.BlockSpec((16, 48, 384), lambda j, me: (0, j, 0))],
         grid=(4,),
+        out_hbm=(0,),
         flops=3 * n * D * D,
         prefetch=1,
     )[0]
@@ -906,7 +924,7 @@
 
 def adam(kind, row, master, first, second, summed, down, proj, vec, fast):
     slots, part_rows = master.shape[1:3]
-    each = 2
+    each = slots // 2
     block = pl.BlockSpec((1, each, part_rows, D), lambda s, *_: (0, s, 0, 0))
     if fast:
         summed_spec = pl.BlockSpec((8, each, 16, 384), lambda s, *_: (0, s, 0, 0))
@@ -929,7 +947,7 @@
         grid=(slots // each,),
         scratch=[pltpu.VMEM((part_rows, D), f32), pltpu.VMEM((D // 128, part_rows, 128), f32)],
         flops=20 * slots * part_rows * D,
-        in_hbm=(2, 3, 4),
+        in_hbm=(2, 3, 4, 6, 7),
         prefetch=2,
     )
 
@@ -964,6 +982,7 @@
         (kind, row, *arrays, dz, pooled),
         [whole(a.shape) for a in arrays] + [whole(dz.shape), whole(pooled.shape)],
         [whole((128, FF)), whole((EMB, D))],
+        out_hbm=(0, 1),
         flops=256 * D * FF,
         prefetch=2,
     )
@@ -1076,14 +1095,14 @@
 
     def cross_one(self):
         parts = [(self.mine, self.first_send), (self.one, self.first_send)]
-        self.two = send(add_pieces(parts, self.me, 8, 2), CROSS_ONE)
+        self.two = send(add_pieces(parts, self.me, 8, 2, near=(1,)), CROSS_ONE)
 
     def cross_two(self):
         def own(i, me):
             return self.kept(self.second_send(i, me), me)
 
         parts = [(self.mine, own), (self.one, own), (self.two, self.second_send)]
-        self.three = send(add_pieces(parts, self.me, 4), CROSS_TWO)
+        self.three = send(add_pieces(parts, self.me, 4, near=(2,)), CROSS_TWO)
 
     def partial(self):
         def crossed(i, me):
@@ -1252,7 +1271,7 @@
         for j in range(tiles):
             slab(k, (one_ref, two_ref, three_ref)[chunk], first + j)
             k += 1
-    slab(k, one_ref, 12)
+    slab(k, one_ref, 9)
     text = text_ref[...].astype(f32)
     count = text.shape[0]
     text = (text * lax.rsqrt(jnp.sum(text * text, axis=-1, keepdims=True) + unit_eps)).astype(bf16)
@@ -1268,14 +1287,20 @@
     def cross_one(self):
         self.ring = jnp.stack(self.parts)
         self.one = send(self.ring, CROSS_ONE)
-        self.two = send(self.ring, CROSS_TWO)
+        self.two = None
+        self.near = []
 
     def cross_two(self):
+        if self.two is None:
+            self.two = send(self.ring, CROSS_TWO)
         self.both = send(self.one, CROSS_TWO)
-        self.near = [send(v, SWAP_CORE) for v in (self.ring, self.one, self.two)]
+
+    def send_near(self, *which):
+        for k in which:
+            self.near.append(send(getattr(self, ("ring", "one", "two", "both")[k]), SWAP_CORE))
 
     def finish(self):
-        self.near.append(send(self.both, SWAP_CORE))
+        self.send_near(*range(len(self.near), 4))
 
     def arrays(self):
         return (self.ring, self.one, self.two, self.both, *self.near)
@@ -1295,7 +1320,7 @@
             yield c, me[X] + flip_x - 2 * me[X] * flip_x, me[Y] + flip_y - 2 * me[Y] * flip_y
 
 
-def pick_slabs(master, text_emb, owner_list, me):
+def pick_slabs(master, text_emb, owner_list, me, *others):
     prepared = call(
         prepare_kernel,
         (sds((8, 8, 16, 384), bf16),),
@@ -1308,15 +1333,16 @@
     )[0]
     pick, place, kind, row = plan(owner_list, me)
     mine = lax.all_to_all(prepared, "rep", 0, 0, axis_index_groups=SAME_CORE).reshape(64, 16, 384)
+    mine, pick, *others = meet(mine, pick, *others)
     blocks = call(
         pick_kernel,
-        tuple(sds((slabs, 16, 384), bf16) for slabs in (13, 12, 15)),
+        tuple(sds((slabs, 16, 384), bf16) for slabs in SLABS),
         (pick, mine, send(mine, SWAP_CORE), text_emb),
         [whole((64, 16, 384)), whole((64, 16, 384)), whole(text_emb.shape)],
-        [whole((slabs, 16, 384)) for slabs in (13, 12, 15)],
+        [whole((slabs, 16, 384)) for slabs in SLABS],
         prefetch=1,
     )
-    return blocks, place, kind, row
+    return blocks, (place, kind, row), others
 
 
 def shards(block_in, tissue, text_emb, text_order, owner_list, master, first_moment, second_moment):
@@ -1345,40 +1371,42 @@
     fast = (n_dp, n_rep, slots, part_rows) == (2, 16, 8, 64)
     if fast:
         me = jnp.stack([dp_at, rep_at // 4, rep_at // 2 % 2, rep_at % 2]).astype(jnp.int32)
-        (block_one, block_two, block_three), place, kind, row = pick_slabs(master, text_emb, owner_list, me)
-        x, col, sel, inv_count, order, first_image, block_one = lax.optimization_barrier(
-            (x, col, sel, inv_count, order, first_image, block_one)
+        (block_one, block_two, block_three), (place, kind, row), others = pick_slabs(
+            master, text_emb, owner_list, me, x, mask_row, col, sel, inv_count, order, first_image
         )
+        x, mask_row, col, sel, inv_count, order, first_image = others
         one = Spread(block_one)
-        *one.parts, block_two, block_three = meet(*one.parts, block_two, block_three)
+        *one.parts, block_two = meet(*one.parts, block_two)
         one.cross_one()
+        one.two = send(one.ring, CROSS_TWO)
         two = Spread(block_two)
         one.ring, one.one, one.two = meet(one.ring, one.one, one.two)
         one.cross_two()
-        *two.parts, block_three = meet(*two.parts, block_three)
-        three = Spread(block_three)
-        one.both, *two.parts = meet(one.both, *two.parts)
+        one.send_near(0, 1)
+        one.two, *two.parts = meet(one.two, *two.parts)
+        one.send_near(2)
+        one.both, block_three = meet(one.both, block_three)
         one.finish()
         two.cross_one()
+        two.send_near(0)
         w_qkv = Weight(one.arrays(), QKV_TILES)
-        w_out = Weight(one.arrays(), OUT_TILES, 9)
         a, qkv, vec = qkv_forward(images, x, jnp.zeros((16, D), f32), w_qkv, me)
-        qkv, two.ring, two.one, two.two, *three.parts = meet(qkv, two.ring, two.one, two.two, *three.parts)
+        qkv, two.ring, two.one, two.near[0], block_three = meet(qkv, two.ring, two.one, two.near[0], block_three)
         two.cross_two()
-        three.ring = jnp.stack(three.parts)
-        three.one = send(three.ring, CROSS_ONE)
+        three = Spread(block_three)
         o, lse = attention_forward(images, qkv, mask_row)
-        o, two.both, three.ring, *two.near = meet(o, two.both, three.ring, *two.near)
+        o, two.two, two.both, *three.parts = meet(o, two.two, two.both, *three.parts)
         two.finish()
-        three.two = send(three.ring, CROSS_TWO)
-        w_up = Weight(two.arrays(), UP_TILES)
+        three.cross_one()
+        w_out = Weight(two.arrays(), OUT_TILES)
         h, m = middle_forward(images, x, o, vec, w_out, me)
-        h, m, two.near[3], three.ring, three.one, three.two = meet(h, m, two.near[3], three.ring, three.one, three.two)
+        h, m, three.ring, three.one = meet(h, m, three.ring, three.one)
         three.cross_two()
+        three.send_near(0, 1)
         bias_up = vec[7 : 7 + FF // D].reshape(FF // D, 1, D)
-        w_up = Weight(two.arrays(), UP_TILES)
+        w_up = Weight(two.arrays(), UP_TILES, 3)
         act, slope = up_forward(images, m, w_up, bias_up, me)
-        act, three.both, *three.near = meet(act, three.both, *three.near)
+        act, three.two, three.both, *three.near = meet(act, three.two, three.both, *three.near)
         three.finish()
         w_down = Weight(three.arrays(), DOWN_TILES, quarters=True)
         w_proj = Weight(three.arrays(), PROJ_TILES, 12)
@@ -1422,16 +1450,18 @@
         dm, other, mine, *ranks.parts = meet(dm, other, mine, *ranks.parts)
         up_sum = PieceSum(other, me)
         ranks.cross_one()
+        ranks.two = send(ranks.ring, CROSS_TWO)
         dh, do, g_out, g_two = middle_backward(images, h, dm, col, spread, o, w_out, vec, me)
         dh, do, up_sum.mine, up_sum.one, ranks.ring, ranks.one, ranks.two = meet(
             dh, do, mine, up_sum.one, ranks.ring, ranks.one, ranks.two
         )
         up_sum.cross_one()
         ranks.cross_two()
+        ranks.send_near(0, 1, 2)
         dqkv, g_bias = attention_backward(images, qkv, do, probabilities)
         dqkv, up_sum.two, ranks.both, *ranks.near = meet(dqkv, up_sum.two, ranks.both, *ranks.near)
+        ranks.finish()
         up_sum.cross_two()
-        ranks.finish()
         other = qkv_weight_grad_fast(images, dqkv, a, g_out, me, True)
         other, dqkv = meet(other, dqkv)
         qkv_sum = PieceSum(other, me)
@@ -1447,20 +1477,23 @@
         qkv_sum.cross_two()
         near_vec = send(vec_sum, SWAP_CORE)
         up_total = up_sum.total()
+        vec_sum, near_vec, up_total = meet(vec_sum, near_vec, up_total)
+        vec_sum += near_vec
+        vec_sum += send(vec_sum, SWAP_ZZ)
+        qkv_sum.partial()
+        vec_sum, qkv_sum.sums, qkv_sum.three, up_total = meet(vec_sum, qkv_sum.sums, qkv_sum.three, up_total)
+        qkv_sum.cross_z()
         near_up = send(up_total, SWAP_CORE)
-        qkv_sum.partial()
-        vec_sum, near_vec, qkv_sum.sums, near_up = meet(vec_sum, near_vec, qkv_sum.sums, near_up)
-        vec_sum += near_vec
-        across = [send(vec_sum, move) for move in (SWAP_X, SWAP_Y, SWAP_XY)]
+        vec_sum += send(vec_sum, SWAP_Y)
+        vec_sum += send(vec_sum, SWAP_Z)
+        near_up, vec_sum, *qkv_sum.last = meet(near_up, vec_sum, *qkv_sum.last)
+        qkv_total = qkv_sum.total()
+        near_qkv = send(qkv_total, SWAP_CORE)
+        near_qkv, vec_sum = meet(near_qkv, vec_sum)
+        summed = return_to_owners((qkv_total, up_total, near_qkv, near_up), place)
+        vec_total = vec_sum + send(vec_sum, SWAP_X)
         g_down, g_proj = rank_grads(images, kind, row, ranks.arrays(), dz_all, pooled_all)
-        vec_sum, qkv_sum.three, g_down, g_proj, *across = meet(vec_sum, qkv_sum.three, g_down, g_proj, *across)
-        qkv_sum.cross_z()
-        vec_sum += across[0] + across[1] + across[2]
-        vec_sum += send(vec_sum, SWAP_Z)
-        vec_sum += send(vec_sum, SWAP_ZZ)
-        vec_total, g_down, *qkv_sum.last = meet(vec_sum, g_down.reshape(8, 16, FF), *qkv_sum.last)
-        qkv_total = qkv_sum.total()
-        summed = return_to_owners((qkv_total, up_total, send(qkv_total, SWAP_CORE), near_up), place)
+        summed, g_down, g_proj, vec_total = meet(summed, g_down.reshape(8, 16, FF), g_proj, vec_total)
     else:
         both_all = lax.all_gather(both, AXES, axis=0, tiled=True)
         dm, g_bias_up, g_up = up_backward(images, slope, m, w_up, hidden, col, me)

time: 372 us -> 343 us (0.922)
  blocking collectives: 51.6 us -> 0 us
  waiting for transfers between devices: 67.6 us -> 84.6 us
  starting transfers between devices: 62.1 us -> 69.8 us
  local copies, waits for them, and re-layouts: 18 us -> 10.9 us
  Pallas kernels: 166 us -> 171 us
    all_to_all x2 -> x0, blocking collectives: 51.6 us -> none  [the longest x1 27.3 us: pick_slabs(): lax.all_to_all(prepared, 'rep', 0, 0, axis_index_groups=SAME_CORE)]
    all_to_all x0 -> x2, waiting for transfers between devices: none -> 26.7 us  [the longest x1 14.8 us: return_to_owners(): lax.all_to_all(placed.reshape(8, 8, 16, 384), 'rep', 0, 0, axis_index_gro...]
    all_to_all x0 -> x2, starting transfers between devices: none -> 12 us  [the longest x1 7.28 us: pick_slabs(): lax.all_to_all(prepared, 'rep', 0, 0, axis_index_groups=SAME_CORE)]
    ppermute x61 -> x60, waiting for transfers between devices: 65.7 us -> 54.8 us  [send(): return lax.ppermute(value, AXES, permutation)]
    unnamed x120 -> x112, local copies, waits for them, and re-layouts: 14.4 us -> 8.09 us
    pallas_call x29, Pallas kernels: 160 us -> 165 us  [call(): pl.pallas_call(kernel, out_shape=tuple(outs), grid_spec=pltpu.PrefetchSca...]
    ppermute x61 -> x60, starting transfers between devices: 57.9 us -> 53.7 us  [send(): return lax.ppermute(value, AXES, permutation)]
  transfers between devices with their start and end apart: 62 -> 63, of which waited for: 17 -> 26; matrix products, arithmetic and copies ran while one was open for 1% -> 1% of each run, Pallas kernels for 33% -> 37%
where the time goes in v3:
time: 343 us; the launch traced here: 339 us
  Pallas kernels  171 us (50%)
  waiting for transfers between devices  84.6 us (25%)
  starting transfers between devices  69.8 us (20%)
  local copies, waits for them, and re-layouts  10.9 us (3%)
    pallas_call x29, Pallas kernels, call(): pl.pallas_call(kernel, out_shape=tuple(outs), grid_spec=pltpu.PrefetchSca...  165 us
    ppermute x60, waiting for transfers between devices, send(): return lax.ppermute(value, AXES, permutation)  54.8 us
    ppermute x60, starting transfers between devices, send(): return lax.ppermute(value, AXES, permutation)  53.7 us
    all_to_all x1, waiting for transfers between devices, return_to_owners(): lax.all_to_all(placed.reshape(8, 8, 16, 384), 'rep', 0, 0, axis_index_gro...  14.8 us
    all_to_all x1, waiting for transfers between devices, pick_slabs(): lax.all_to_all(prepared, 'rep', 0, 0, axis_index_groups=SAME_CORE)  12 us
    unnamed x112, local copies, waits for them, and re-layouts  8.09 us
    all_to_all x1, starting transfers between devices, pick_slabs(): lax.all_to_all(prepared, 'rep', 0, 0, axis_index_groups=SAME_CORE)  7.28 us
  transfers between devices with their start and end apart: 63, of which 26 were waited for; matrix products, arithmetic and copies ran while one was open for 1% of the time, Pallas kernels for 37%

profile of v3, /device:TPU:0, one launch (start us, length us, event | category | flops | bytes accessed | tf_op | source)
XLA Modules:
  0.0 339.1 jit_solution(14413819114518217604)
XLA Ops:
  1.4 3.0 shard_map.119
  4.4 7.3 %all-to-all-start = ((bf16[8,8,16,384]{3,2,1,0:T(8,128)(2,1)}), bf16[8,8,16,384]{3,2,1,0:T(8,128)(2,1)S(1)}, u32[]{:S(2)}, u32[]{:S(2)}) async-start(bf16[8,8,16,384]{3,2,1,0:T(8,128)(2,1)} %shard_map.119), calls=%async_computation | async-start | bytes 1572864 | tf_op jit(solution)/shard_map/all_to_all | solution.py:1335
  11.7 6.3 %shard_map.120 = (s32[39]{0:T(128)}, s32[64]{0:T(128)}, s32[8]{0:T(128)}, s32[8]{0:T(128)}) custom-call(s32[77]{0:T(128)} %owner_ref.3, s32[4]{0:T(128)} %copy-done.17), custom_call_target="tpu_custom_call" | custom-call | tf_op jit(solution)/shard_map/pallas_call | solution.py:1214
  19.9 12.0 %all-to-all-done = bf16[8,8,16,384]{3,2,1,0:T(8,128)(2,1)S(1)} async-done(((bf16[8,8,16,384]{3,2,1,0:T(8,128)(2,1)}), bf16[8,8,16,384]{3,2,1,0:T(8,128)(2,1)S(1)}, u32[]{:S(2)}, u32[]{:S(2)}) %all-to-all-start) | async-done | bytes 786464 | tf_op jit(solution)/shard_map/all_to_all | solution.py:1335
  32.3 2.3 collective-permute-done.theirs_ref
  37.5 2.7 collective-permute-start.3
  40.1 2.2 collective-permute-done.1
  42.3 6.1 %collective-permute-done.2 = bf16[10,16,384]{2,1,0:T(8,128)(2,1)S(1)} collective-permute-done((bf16[10,16,384]{2,1,0:T(8,128)(2,1)S(1)}, bf16[10,16,384]{2,1,0:T(8,128)(2,1)S(1)}, u32[]{:S(2)}, u32[]{:S(2)}) %collective-permute-start.2) | collective-permute-done | bytes 122912 | tf_op jit(solution)/shard_map/ppermute | solution.py:1035
  51.3 2.4 collective-permute-start.6
  53.7 2.4 collective-permute-start.8
  56.0 5.1 %collective-permute-done.4.refs_1_ = bf16[4,10,16,384]{3,2,1,0:T(8,128)(2,1)S(1)} collective-permute-done((bf16[4,10,16,384]{3,2,1,0:T(8,128)(2,1)S(1)}, bf16[4,10,16,384]{3,2,1,0:T(8,128)(2,1)S(1)}, u32[]{:S(2)}, u32[]{:S(2)}) %collective-permute-start.4) | collective-permute-done | bytes 491552 | tf_op jit(solution)/shard_map/ppermute | solution.py:1035
  61.6 7.5 %collective-permute-done.7 = bf16[15,16,384]{2,1,0:T(8,128)(2,1)S(1)} collective-permute-done((bf16[15,16,384]{2,1,0:T(8,128)(2,1)S(1)}, bf16[15,16,384]{2,1,0:T(8,128)(2,1)S(1)}, u32[]{:S(2)}, u32[]{:S(2)}) %collective-permute-start.7) | collective-permute-done | bytes 184352 | tf_op jit(solution)/shard_map/ppermute | solution.py:1035
  70.3 3.1 collective-permute-done.9.refs_3_
  76.7 9.4 %shard_map.122 = (bf16[1040,768]{1,0:T(8,128)(2,1)}, bf16[1040,2304]{1,0:T(8,128)(2,1)S(1)}, f32[16,768]{1,0:T(8,128)S(1)}) custom-call(s32[4]{0:T(128)S(1)} %copy-done.18, bf16[4,10,16,384]{3,2,1,0:T(8,128)(2,1)} %copy-done.36, bf16[4,10,16,384]{3,2,1,0:T(8,128)(2,1)} %copy-done.43, bf16[4,10,16,384]{3,2,1,0:T(8,128)(2,1)} %copy-done.44, ...), custom_call_target="tpu_custom_call" | custom-call | flops 1 | bytes 1 | tf_op jit(solution)/shard_map/pallas_call | solution.py:84
  89.5 3.3 collective-permute-start.20
  92.7 9.0 %shard_map.123 = (bf16[1040,768]{1,0:T(8,128)(2,1)S(1)}, f32[5,16,208]{2,1,0:T(8,128)S(1)}) custom-call(bf16[1040,2304]{1,0:T(8,128)(2,1)S(1)} %get-tuple-element.177.qkv_ref, f32[5,1,208]{2,1,0:T(1,128)S(1)} %broadcast_in_dim.84.mask_ref), custom_call_target="tpu_custom_call" | custom-call | flops 1 | bytes 1 | tf_op jit(solution)/shard_map/pallas_call | solution.py:84
  101.9 3.8 %collective-permute-done.19 = bf16[15,16,384]{2,1,0:T(8,128)(2,1)S(1)} collective-permute-done((bf16[15,16,384]{2,1,0:T(8,128)(2,1)S(1)}, bf16[15,16,384]{2,1,0:T(8,128)(2,1)S(1)}, u32[]{:S(2)}, u32[]{:S(2)}) %collective-permute-start.19) | collective-permute-done | bytes 184352 | tf_op jit(solution)/shard_map/ppermute | solution.py:1035
  106.4 2.5 collective-permute-start.24
  110.3 6.1 %shard_map.124 = (f32[1040,768]{1,0:T(8,128)S(1)}, bf16[1040,768]{1,0:T(8,128)(2,1)S(1)}) custom-call(s32[4]{0:T(128)S(1)} %copy-done.18, bf16[4,15,16,384]{3,2,1,0:T(8,128)(2,1)} %copy-done.27, bf16[4,15,16,384]{3,2,1,0:T(8,128)(2,1)} %copy-done.28, bf16[4,15,16,384]{3,2,1,0:T(8,128)(2,1)} %copy-done.30, bf16[4,15,16,384]{3,2,1,0:T(8,128)(2,1)} %copy-done.31, ...), custom_call_target="tpu_custom_call" | custom-call | flops 1 | bytes 1 | tf_op jit(solution)/shard_map/pallas_call | solution.py:84
  120.9 18.3 %shard_map.125 = (bf16[1040,3072]{1,0:T(8,128)(2,1)S(1)}, bf16[1040,3072]{1,0:T(8,128)(2,1)}) custom-call(s32[4]{0:T(128)S(1)} %copy-done.18, bf16[4,15,16,384]{3,2,1,0:T(8,128)(2,1)} %copy-done.27, bf16[4,15,16,384]{3,2,1,0:T(8,128)(2,1)} %copy-done.28, bf16[4,15,16,384]{3,2,1,0:T(8,128)(2,1)} %copy-done.30, bf16[4,15,16,384]{3,2,1,0:T(8,128)(2,1)} %copy-done.31, ...), custom_call_target="tpu_custom_call" | custom-call | flops 1 | bytes 1 | tf_op jit(solution)/shard_map/pallas_call | solution.py:84
  143.0 13.8 %shard_map.126 = (bf16[5,196,768]{2,1,0:T(8,128)(2,1)}, bf16[16,768]{1,0:T(8,128)(2,1)S(1)}) custom-call(s32[4]{0:T(128)S(1)} %copy-done.18, bf16[4,15,16,384]{3,2,1,0:T(8,128)(2,1)} %copy-done.35, bf16[4,15,16,384]{3,2,1,0:T(8,128)(2,1)} %copy-done.37, bf16[4,15,16,384]{3,2,1,0:T(8,128)(2,1)} %copy-done.38, bf16[4,15,16,384]{3,2,1,0:T(8,128)(2,1)} %copy-done.39, ...), custom_call_target="tpu_custom_call" | custom-call | flops 1 | bytes 1 | tf_op jit(solution)/shard_map/pallas_call | solution.py:84
  157.7 4.1 %all-to-all-start.1 = ((bf16[32,5,768]{2,1,0:T(8,128)(2,1)}), bf16[32,5,768]{2,1,0:T(8,128)(2,1)S(1)}, u32[]{:S(2)}, u32[]{:S(2)}) async-start(bf16[32,5,768]{2,1,0:T(8,128)(2,1)} %broadcast_in_dim.95), calls=%async_computation.1 | async-start | bytes 786432 | tf_op jit(solution)/shard_map/all_to_all | solution.py:1436
  161.8 2.3 copy-done.6
  164.1 3.2 shard_map.128.p_ref
  167.3 2.6 copy-done.7
  171.8 3.0 all-to-all-done.1.refs_9_
  174.9 5.1 %shard_map.129 = (bf16[160,512]{1,0:T(8,128)(2,1)S(1)}, bf16[16,768]{1,0:T(8,128)(2,1)S(1)}, f32[16,768]{1,0:T(8,128)S(1)}, f32[16,3072]{1,0:T(8,128)S(1)}, bf16[160,768]{1,0:T(8,128)(2,1)S(1)}) custom-call(s32[4]{0:T(128)S(1)} %copy-done.18, s32[1]{0:T(128)} %bitcast.6.first_ref, bf16[4,15,16,384]{3,2,1,0:T(8,128)(2,1)} %copy-done.35, ...), custom_call_target="tpu_custom_call" | custom-call | flops 1 | bytes 1 | tf_op jit(solution)/shard_map/pallas_call | solution.py:84
  184.4 19.7 %shard_map.130 = (f32[1040,768]{1,0:T(8,128)S(1)}, f32[8,3072]{1,0:T(8,128)S(1)}, bf16[16,192,384]{2,1,0:T(8,128)(2,1)S(1)}, bf16[16,192,384]{2,1,0:T(8,128)(2,1)S(1)}) custom-call(s32[4]{0:T(128)S(1)} %copy-done.18, bf16[4,15,16,384]{3,2,1,0:T(8,128)(2,1)} %copy-done.27, bf16[4,15,16,384]{3,2,1,0:T(8,128)(2,1)} %copy-done.28, ...), custom_call_target="tpu_custom_call" | custom-call | flops 1 | bytes 1 | tf_op jit(solution)/shard_map/pallas_call | solution.py:84
  206.4 10.4 %shard_map.131 = (f32[1040,768]{1,0:T(8,128)S(1)}, bf16[1040,768]{1,0:T(8,128)(2,1)S(1)}, bf16[2,16,48,384]{3,2,1,0:T(8,128)(2,1)S(1)}, f32[8,768]{1,0:T(8,128)S(1)}) custom-call(s32[4]{0:T(128)S(1)} %copy-done.18, bf16[4,15,16,384]{3,2,1,0:T(8,128)(2,1)} %copy-done.27, bf16[4,15,16,384]{3,2,1,0:T(8,128)(2,1)} %copy-done.28, ...), custom_call_target="tpu_custom_call" | custom-call | flops 1 | bytes 1 | tf_op jit(solution)/shard_map/pallas_call | solution.py:84
  216.9 3.3 shard_map.133
  222.8 13.3 %shard_map.132 = (bf16[1040,2304]{1,0:T(8,128)(2,1)S(1)}, f32[16,2304]{1,0:T(8,128)S(1)}) custom-call(bf16[1040,2304]{1,0:T(8,128)(2,1)S(1)} %bitcast.36, bf16[1040,768]{1,0:T(8,128)(2,1)S(1)} %get-tuple-element.228.do_ref, bf16[5,12,208,208]{3,2,1,0:T(8,128)(2,1)S(1)} %bitcast.41), custom_call_target="tpu_custom_call" | custom-call | flops 1 | bytes 1 | tf_op jit(solution)/shard_map/pallas_call | solution.py:84
  237.9 4.9 %shard_map.134 = bf16[16,192,384]{2,1,0:T(8,128)(2,1)} custom-call(s32[4]{0:T(128)S(1)} %copy-done.18, bf16[1040,2304]{1,0:T(8,128)(2,1)S(1)} %get-tuple-element.243.dqkv_ref.refs_9_, bf16[1040,768]{1,0:T(8,128)(2,1)S(1)} %copy-done.11, bf16[2,16,48,384]{3,2,1,0:T(8,128)(2,1)S(1)} %get-tuple-element.238.out_ref), custom_call_target="tpu_custom_call" | custom-call | flops 1 | bytes 1 | tf_op jit(solution)/shard_map/pallas_call | solution.py:84
  242.8 2.1 shard_map.136
  246.2 2.3 shard_map.135.refs_0_.refs_2_.refs_4_.refs_6_
  248.5 5.0 %shard_map.137.refs_0_.refs_2_.refs_4_.refs_6_.refs_3_.refs_9_ = bf16[16,192,384]{2,1,0:T(8,128)(2,1)} custom-call(s32[4]{0:T(128)S(1)} %copy-done.18, bf16[1040,2304]{1,0:T(8,128)(2,1)S(1)} %get-tuple-element.243.dqkv_ref.refs_9_, bf16[1040,768]{1,0:T(8,128)(2,1)S(1)} %copy-done.11, bf16[2,16,48,384]{3,2,1,0:T(8,128)(2,1)S(1)} %get-tuple-element.238.out_ref), custom_call_target="tpu_custom_call" | custom-call | flops 1 | bytes 1 | tf_op jit(solution)/shard_map/pallas_call | solution.py:84
  254.9 2.4 shard_map.139
  259.0 2.4 collective-permute-start.47
  263.4 10.0 %shard_map.138 = (f32[5,196,768]{2,1,0:T(8,128)}, f32[16,768]{1,0:T(8,128)S(1)}) custom-call(s32[4]{0:T(128)S(1)} %copy-done.18, bf16[4,10,16,384]{3,2,1,0:T(8,128)(2,1)} %copy-done.36, bf16[4,10,16,384]{3,2,1,0:T(8,128)(2,1)} %copy-done.43, bf16[4,10,16,384]{3,2,1,0:T(8,128)(2,1)} %copy-done.44, bf16[4,10,16,384]{3,2,1,0:T(8,128)(2,1)} %copy-done.45, ...), custom_call_target="tpu_custom_call" | custom-call | flops 1 | bytes 1 | tf_op jit(solution)/shard_map/pallas_call | solution.py:84
  273.5 2.2 shard_map.143
  279.8 2.3 shard_map.142.refs_0_.refs_2_.refs_4_.refs_6_
  282.1 2.3 collective-permute-done.50
  292.0 2.8 collective-permute-done.53
  295.8 5.9 %collective-permute-done.54 = f32[16,768]{1,0:T(8,128)S(1)} collective-permute-done((f32[16,768]{1,0:T(8,128)S(1)}, f32[16,768]{1,0:T(8,128)S(1)}, u32[]{:S(2)}, u32[]{:S(2)}) %collective-permute-start.54) | collective-permute-done | bytes 49184 | tf_op jit(solution)/shard_map/ppermute | solution.py:1035
  304.2 3.3 shard_map.146
  307.5 4.8 %all-to-all-start.2 = ((bf16[8,8,16,384]{3,2,1,0:T(8,128)(2,1)}), bf16[8,8,16,384]{3,2,1,0:T(8,128)(2,1)S(1)}, u32[]{:S(2)}, u32[]{:S(2)}) async-start(bf16[8,8,16,384]{3,2,1,0:T(8,128)(2,1)} %bitcast.33), calls=%async_computation.2 | async-start | bytes 1572864 | tf_op jit(solution)/shard_map/all_to_all | solution.py:1151
  313.6 4.3 %shard_map.147 = (f32[128,3072]{1,0:T(8,128)}, f32[512,768]{1,0:T(8,128)}) custom-call(s32[8]{0:T(128)S(1)} %copy-done.22, s32[8]{0:T(128)S(1)} %copy-done.23, bf16[4,16,1280]{2,1,0:T(8,128)(2,1)S(1)} %pad_maximum_fusion.3.refs_0_, bf16[4,16,1280]{2,1,0:T(8,128)(2,1)S(1)} %collective-permute-done.35.refs_1_, ...), custom_call_target="tpu_custom_call" | custom-call | flops 1 | bytes 1 | tf_op jit(solution)/shard_map/pallas_call | solution.py:84
  317.9 14.8 %all-to-all-done.2.refs_3_ = bf16[8,8,16,384]{3,2,1,0:T(8,128)(2,1)S(1)} async-done(((bf16[8,8,16,384]{3,2,1,0:T(8,128)(2,1)}), bf16[8,8,16,384]{3,2,1,0:T(8,128)(2,1)S(1)}, u32[]{:S(2)}, u32[]{:S(2)}) %all-to-all-start.2) | async-done | bytes 786464 | tf_op jit(solution)/shard_map/all_to_all | solution.py:1151
  332.7 6.2 %shard_map.148 = (f32[1,8,64,768]{3,2,1,0:T(8,128)}, f32[1,8,64,768]{3,2,1,0:T(8,128)}, f32[1,8,64,768]{3,2,1,0:T(8,128)}) custom-call(s32[8]{0:T(128)S(1)} %copy-done.22, s32[8]{0:T(128)S(1)} %copy-done.23, f32[1,8,64,768]{3,2,1,0:T(8,128)} %refs_0_.1, f32[1,8,64,768]{3,2,1,0:T(8,128)} %refs_1_.1, f32[1,8,64,768]{3,2,1,0:T(8,128)} %refs_2_.1, ...), custom_call_target="tpu_custom_call" | custom-call | flops 1 | bytes 1 | tf_op jit(solution)/shard_map/pallas_call | solution.py:84
  (255 shorter events, 63.9 us)
Async XLA Ops:
  4.4 27.5 %all-to-all-start = ((bf16[8,8,16,384]{3,2,1,0:T(8,128)(2,1)}), bf16[8,8,16,384]{3,2,1,0:T(8,128)(2,1)S(1)}, u32[]{:S(2)}, u32[]{:S(2)}) async-start(bf16[8,8,16,384]{3,2,1,0:T(8,128)(2,1)} %shard_map.119), calls=%async_computation | async-start | bytes 1572864 | tf_op jit(solution)/shard_map/all_to_all | solution.py:1335
  36.1 12.4 %collective-permute-start.2 = (bf16[10,16,384]{2,1,0:T(8,128)(2,1)S(1)}, bf16[10,16,384]{2,1,0:T(8,128)(2,1)S(1)}, u32[]{:S(2)}, u32[]{:S(2)}) collective-permute-start(bf16[10,16,384]{2,1,0:T(8,128)(2,1)S(1)} %get-tuple-element.157), channel_id=1, source_target_pairs={{0,8},{1,9},{2,10},{3,11},{4,12},{5,13},{6,14},{7,15},{8,0},{9,1},... | collective-permute-start | bytes 368648 | tf_op jit(solution)/shard_map/ppermute | solution.py:1035
  37.5 11.0 %collective-permute-start.3 = (bf16[10,16,384]{2,1,0:T(8,128)(2,1)S(1)}, bf16[10,16,384]{2,1,0:T(8,128)(2,1)S(1)}, u32[]{:S(2)}, u32[]{:S(2)}) collective-permute-start(bf16[10,16,384]{2,1,0:T(8,128)(2,1)S(1)} %get-tuple-element.157), channel_id=1, source_target_pairs={{0,12},{1,13},{2,14},{3,15},{4,8},{5,9},{6,10},{7,11},{8,4},{9,5},... | collective-permute-start | bytes 368648 | tf_op jit(solution)/shard_map/ppermute | solution.py:1035
  48.6 12.6 %collective-permute-start.4 = (bf16[4,10,16,384]{3,2,1,0:T(8,128)(2,1)S(1)}, bf16[4,10,16,384]{3,2,1,0:T(8,128)(2,1)S(1)}, u32[]{:S(2)}, u32[]{:S(2)}) collective-permute-start(bf16[4,10,16,384]{3,2,1,0:T(8,128)(2,1)S(1)} %pad_maximum_fusion.2.refs_0_), channel_id=1, source_target_pairs={{0,16},{1,3},{2,18},{3,1},{4,20},{5,7},{6,22},{7,5},{8,24},{9,11},... | collective-permute-start | bytes 1474568 | tf_op jit(solution)/shard_map/ppermute | solution.py:1035
  50.1 11.0 %collective-permute-start.5 = (bf16[4,10,16,384]{3,2,1,0:T(8,128)(2,1)S(1)}, bf16[4,10,16,384]{3,2,1,0:T(8,128)(2,1)S(1)}, u32[]{:S(2)}, u32[]{:S(2)}) collective-permute-start(bf16[4,10,16,384]{3,2,1,0:T(8,128)(2,1)S(1)} %pad_maximum_fusion.2.refs_0_), channel_id=1, source_target_pairs={{0,2},{1,17},{2,0},{3,19},{4,6},{5,21},{6,4},{7,23},{8,10},{9,25},... | collective-permute-start | bytes 1474568 | tf_op jit(solution)/shard_map/ppermute | solution.py:1035
  51.3 10.3 %collective-permute-start.6 = (bf16[15,16,384]{2,1,0:T(8,128)(2,1)S(1)}, bf16[15,16,384]{2,1,0:T(8,128)(2,1)S(1)}, u32[]{:S(2)}, u32[]{:S(2)}) collective-permute-start(bf16[15,16,384]{2,1,0:T(8,128)(2,1)S(1)} %get-tuple-element.170), channel_id=1, source_target_pairs={{0,4},{1,5},{2,6},{3,7},{4,0},{5,1},{6,2},{7,3},{8,12},{9,13},{10,... | collective-permute-start | bytes 552968 | tf_op jit(solution)/shard_map/ppermute | solution.py:1035
  53.7 15.4 %collective-permute-start.7 = (bf16[15,16,384]{2,1,0:T(8,128)(2,1)S(1)}, bf16[15,16,384]{2,1,0:T(8,128)(2,1)S(1)}, u32[]{:S(2)}, u32[]{:S(2)}) collective-permute-start(bf16[15,16,384]{2,1,0:T(8,128)(2,1)S(1)} %get-tuple-element.170), channel_id=1, source_target_pairs={{0,8},{1,9},{2,10},{3,11},{4,12},{5,13},{6,14},{7,15},{8,0},{9,1},... | collective-permute-start | bytes 552968 | tf_op jit(solution)/shard_map/ppermute | solution.py:1035
  53.7 15.4 %collective-permute-start.8 = (bf16[15,16,384]{2,1,0:T(8,128)(2,1)S(1)}, bf16[15,16,384]{2,1,0:T(8,128)(2,1)S(1)}, u32[]{:S(2)}, u32[]{:S(2)}) collective-permute-start(bf16[15,16,384]{2,1,0:T(8,128)(2,1)S(1)} %get-tuple-element.170), channel_id=1, source_target_pairs={{0,12},{1,13},{2,14},{3,15},{4,8},{5,9},{6,10},{7,11},{8,4},{9,5},... | collective-permute-start | bytes 552968 | tf_op jit(solution)/shard_map/ppermute | solution.py:1035
  61.2 12.2 %collective-permute-start.9 = (bf16[4,10,16,384]{3,2,1,0:T(8,128)(2,1)S(1)}, bf16[4,10,16,384]{3,2,1,0:T(8,128)(2,1)S(1)}, u32[]{:S(2)}, u32[]{:S(2)}) collective-permute-start(bf16[4,10,16,384]{3,2,1,0:T(8,128)(2,1)S(1)} %collective-permute-done.4.refs_1_), channel_id=1, source_target_pairs={{0,2},{1,17},{2,0},{3,19},{4,6},{5,21},{6,4},{7,23},{8,10},{9,25},... | collective-permute-start | bytes 1474568 | tf_op jit(solution)/shard_map/ppermute | solution.py:1035
  61.6 11.8 %collective-permute-start.10 = (bf16[4,10,16,384]{3,2,1,0:T(8,128)(2,1)S(1)}, bf16[4,10,16,384]{3,2,1,0:T(8,128)(2,1)S(1)}, u32[]{:S(2)}, u32[]{:S(2)}) collective-permute-start(bf16[4,10,16,384]{3,2,1,0:T(8,128)(2,1)S(1)} %pad_maximum_fusion.2.refs_0_), channel_id=1, source_target_pairs={{0,1},{1,0},{2,3},{3,2},{4,5},{5,4},{6,7},{7,6},{8,9},{9,8},{10,11... | collective-permute-start | bytes 1474568 | tf_op jit(solution)/shard_map/ppermute | solution.py:1035
  69.2 17.0 %collective-permute-start.14 = (bf16[4,15,16,384]{3,2,1,0:T(8,128)(2,1)S(1)}, bf16[4,15,16,384]{3,2,1,0:T(8,128)(2,1)S(1)}, u32[]{:S(2)}, u32[]{:S(2)}) collective-permute-start(bf16[4,15,16,384]{3,2,1,0:T(8,128)(2,1)S(1)} %pad_maximum_fusion.refs_0_), channel_id=1, source_target_pairs={{0,16},{1,3},{2,18},{3,1},{4,20},{5,7},{6,22},{7,5},{8,24},{9,11},... | collective-permute-start | bytes 2211848 | tf_op jit(solution)/shard_map/ppermute | solution.py:1035
  69.8 16.5 %collective-permute-start.15 = (bf16[4,15,16,384]{3,2,1,0:T(8,128)(2,1)S(1)}, bf16[4,15,16,384]{3,2,1,0:T(8,128)(2,1)S(1)}, u32[]{:S(2)}, u32[]{:S(2)}) collective-permute-start(bf16[4,15,16,384]{3,2,1,0:T(8,128)(2,1)S(1)} %pad_maximum_fusion.refs_0_), channel_id=1, source_target_pairs={{0,1},{1,0},{2,3},{3,2},{4,5},{5,4},{6,7},{7,6},{8,9},{9,8},{10,11... | collective-permute-start | bytes 2211848 | tf_op jit(solution)/shard_map/ppermute | solution.py:1035
  86.3 19.4 %collective-permute-start.16 = (bf16[4,15,16,384]{3,2,1,0:T(8,128)(2,1)S(1)}, bf16[4,15,16,384]{3,2,1,0:T(8,128)(2,1)S(1)}, u32[]{:S(2)}, u32[]{:S(2)}) collective-permute-start(bf16[4,15,16,384]{3,2,1,0:T(8,128)(2,1)S(1)} %pad_maximum_fusion.refs_0_), channel_id=1, source_target_pairs={{0,2},{1,17},{2,0},{3,19},{4,6},{5,21},{6,4},{7,23},{8,10},{9,25},... | collective-permute-start | bytes 2211848 | tf_op jit(solution)/shard_map/ppermute | solution.py:1035
  86.5 19.2 %collective-permute-start.17 = (bf16[4,15,16,384]{3,2,1,0:T(8,128)(2,1)S(1)}, bf16[4,15,16,384]{3,2,1,0:T(8,128)(2,1)S(1)}, u32[]{:S(2)}, u32[]{:S(2)}) collective-permute-start(bf16[4,15,16,384]{3,2,1,0:T(8,128)(2,1)S(1)} %collective-permute-done.14.refs_1_), channel_id=1, source_target_pairs={{0,2},{1,17},{2,0},{3,19},{4,6},{5,21},{6,4},{7,23},{8,10},{9,25},... | collective-permute-start | bytes 2211848 | tf_op jit(solution)/shard_map/ppermute | solution.py:1035
  88.4 13.4 %collective-permute-start.18 = (bf16[15,16,384]{2,1,0:T(8,128)(2,1)S(1)}, bf16[15,16,384]{2,1,0:T(8,128)(2,1)S(1)}, u32[]{:S(2)}, u32[]{:S(2)}) collective-permute-start(bf16[15,16,384]{2,1,0:T(8,128)(2,1)S(1)} %get-tuple-element.188), channel_id=1, source_target_pairs={{0,4},{1,5},{2,6},{3,7},{4,0},{5,1},{6,2},{7,3},{8,12},{9,13},{10,... | collective-permute-start | bytes 552968 | tf_op jit(solution)/shard_map/ppermute | solution.py:1035
  89.4 16.2 %collective-permute-start.19 = (bf16[15,16,384]{2,1,0:T(8,128)(2,1)S(1)}, bf16[15,16,384]{2,1,0:T(8,128)(2,1)S(1)}, u32[]{:S(2)}, u32[]{:S(2)}) collective-permute-start(bf16[15,16,384]{2,1,0:T(8,128)(2,1)S(1)} %get-tuple-element.188), channel_id=1, source_target_pairs={{0,8},{1,9},{2,10},{3,11},{4,12},{5,13},{6,14},{7,15},{8,0},{9,1},... | collective-permute-start | bytes 552968 | tf_op jit(solution)/shard_map/ppermute | solution.py:1035
  89.5 16.2 %collective-permute-start.20 = (bf16[15,16,384]{2,1,0:T(8,128)(2,1)S(1)}, bf16[15,16,384]{2,1,0:T(8,128)(2,1)S(1)}, u32[]{:S(2)}, u32[]{:S(2)}) collective-permute-start(bf16[15,16,384]{2,1,0:T(8,128)(2,1)S(1)} %get-tuple-element.188), channel_id=1, source_target_pairs={{0,12},{1,13},{2,14},{3,15},{4,8},{5,9},{6,10},{7,11},{8,4},{9,5},... | collective-permute-start | bytes 552968 | tf_op jit(solution)/shard_map/ppermute | solution.py:1035
  101.8 7.2 %collective-permute-start.21 = (bf16[4,15,16,384]{3,2,1,0:T(8,128)(2,1)S(1)}, bf16[4,15,16,384]{3,2,1,0:T(8,128)(2,1)S(1)}, u32[]{:S(2)}, u32[]{:S(2)}) collective-permute-start(bf16[4,15,16,384]{3,2,1,0:T(8,128)(2,1)S(1)} %collective-permute-done.14.refs_1_), channel_id=1, source_target_pairs={{0,1},{1,0},{2,3},{3,2},{4,5},{5,4},{6,7},{7,6},{8,9},{9,8},{10,11... | collective-permute-start | bytes 2211848 | tf_op jit(solution)/shard_map/ppermute | solution.py:1035
  106.4 12.0 %collective-permute-start.24 = (bf16[4,15,16,384]{3,2,1,0:T(8,128)(2,1)S(1)}, bf16[4,15,16,384]{3,2,1,0:T(8,128)(2,1)S(1)}, u32[]{:S(2)}, u32[]{:S(2)}) collective-permute-start(bf16[4,15,16,384]{3,2,1,0:T(8,128)(2,1)S(1)} %pad_maximum_fusion.1.refs_0_), channel_id=1, source_target_pairs={{0,16},{1,3},{2,18},{3,1},{4,20},{5,7},{6,22},{7,5},{8,24},{9,11},... | collective-permute-start | bytes 2211848 | tf_op jit(solution)/shard_map/ppermute | solution.py:1035
  118.4 20.9 %collective-permute-start.25 = (bf16[4,15,16,384]{3,2,1,0:T(8,128)(2,1)S(1)}, bf16[4,15,16,384]{3,2,1,0:T(8,128)(2,1)S(1)}, u32[]{:S(2)}, u32[]{:S(2)}) collective-permute-start(bf16[4,15,16,384]{3,2,1,0:T(8,128)(2,1)S(1)} %pad_maximum_fusion.1.refs_0_), channel_id=1, source_target_pairs={{0,2},{1,17},{2,0},{3,19},{4,6},{5,21},{6,4},{7,23},{8,10},{9,25},... | collective-permute-start | bytes 2211848 | tf_op jit(solution)/shard_map/ppermute | solution.py:1035
  118.4 21.0 %collective-permute-start.26 = (bf16[4,15,16,384]{3,2,1,0:T(8,128)(2,1)S(1)}, bf16[4,15,16,384]{3,2,1,0:T(8,128)(2,1)S(1)}, u32[]{:S(2)}, u32[]{:S(2)}) collective-permute-start(bf16[4,15,16,384]{3,2,1,0:T(8,128)(2,1)S(1)} %collective-permute-done.24.refs_1_), channel_id=1, source_target_pairs={{0,2},{1,17},{2,0},{3,19},{4,6},{5,21},{6,4},{7,23},{8,10},{9,25},... | collective-permute-start | bytes 2211848 | tf_op jit(solution)/shard_map/ppermute | solution.py:1035
  120.4 19.0 %collective-permute-start.27 = (bf16[4,15,16,384]{3,2,1,0:T(8,128)(2,1)S(1)}, bf16[4,15,16,384]{3,2,1,0:T(8,128)(2,1)S(1)}, u32[]{:S(2)}, u32[]{:S(2)}) collective-permute-start(bf16[4,15,16,384]{3,2,1,0:T(8,128)(2,1)S(1)} %pad_maximum_fusion.1.refs_0_), channel_id=1, source_target_pairs={{0,1},{1,0},{2,3},{3,2},{4,5},{5,4},{6,7},{7,6},{8,9},{9,8},{10,11... | collective-permute-start | bytes 2211848 | tf_op jit(solution)/shard_map/ppermute | solution.py:1035
  120.4 19.0 %collective-permute-start.28 = (bf16[4,15,16,384]{3,2,1,0:T(8,128)(2,1)S(1)}, bf16[4,15,16,384]{3,2,1,0:T(8,128)(2,1)S(1)}, u32[]{:S(2)}, u32[]{:S(2)}) collective-permute-start(bf16[4,15,16,384]{3,2,1,0:T(8,128)(2,1)S(1)} %collective-permute-done.24.refs_1_), channel_id=1, source_target_pairs={{0,1},{1,0},{2,3},{3,2},{4,5},{5,4},{6,7},{7,6},{8,9},{9,8},{10,11... | collective-permute-start | bytes 2211848 | tf_op jit(solution)/shard_map/ppermute | solution.py:1035
  157.7 17.2 %all-to-all-start.1 = ((bf16[32,5,768]{2,1,0:T(8,128)(2,1)}), bf16[32,5,768]{2,1,0:T(8,128)(2,1)S(1)}, u32[]{:S(2)}, u32[]{:S(2)}) async-start(bf16[32,5,768]{2,1,0:T(8,128)(2,1)} %broadcast_in_dim.95), calls=%async_computation.1 | async-start | bytes 786432 | tf_op jit(solution)/shard_map/all_to_all | solution.py:1436
  180.0 24.2 %collective-permute-start.31 = (bf16[16,1280]{1,0:T(8,128)(2,1)S(1)}, bf16[16,1280]{1,0:T(8,128)(2,1)S(1)}, u32[]{:S(2)}, u32[]{:S(2)}) collective-permute-start(bf16[16,1280]{1,0:T(8,128)(2,1)S(1)} %fusion.6), channel_id=1, source_target_pairs={{0,4},{1,5},{2,6},{3,7},{4,0},{5,1},{6,2},{7,3},{8,12},{9,13},{10,... | collective-permute-start | bytes 122888 | tf_op jit(solution)/shard_map/ppermute | solution.py:1035
  181.0 23.2 %collective-permute-start.32 = (bf16[16,1280]{1,0:T(8,128)(2,1)S(1)}, bf16[16,1280]{1,0:T(8,128)(2,1)S(1)}, u32[]{:S(2)}, u32[]{:S(2)}) collective-permute-start(bf16[16,1280]{1,0:T(8,128)(2,1)S(1)} %fusion.6), channel_id=1, source_target_pairs={{0,8},{1,9},{2,10},{3,11},{4,12},{5,13},{6,14},{7,15},{8,0},{9,1},... | collective-permute-start | bytes 122888 | tf_op jit(solution)/shard_map/ppermute | solution.py:1035
  182.6 21.6 %collective-permute-start.33 = (bf16[16,1280]{1,0:T(8,128)(2,1)S(1)}, bf16[16,1280]{1,0:T(8,128)(2,1)S(1)}, u32[]{:S(2)}, u32[]{:S(2)}) collective-permute-start(bf16[16,1280]{1,0:T(8,128)(2,1)S(1)} %fusion.6), channel_id=1, source_target_pairs={{0,12},{1,13},{2,14},{3,15},{4,8},{5,9},{6,10},{7,11},{8,4},{9,5},... | collective-permute-start | bytes 122888 | tf_op jit(solution)/shard_map/ppermute | solution.py:1035
  204.2 12.7 %collective-permute-start.34 = (bf16[16,192,384]{2,1,0:T(8,128)(2,1)S(1)}, bf16[16,192,384]{2,1,0:T(8,128)(2,1)S(1)}, u32[]{:S(2)}, u32[]{:S(2)}) collective-permute-start(bf16[16,192,384]{2,1,0:T(8,128)(2,1)S(1)} %get-tuple-element.223), channel_id=1, source_target_pairs={{0,1},{1,0},{2,3},{3,2},{4,5},{5,4},{6,7},{7,6},{8,9},{9,8},{10,11... | collective-permute-start | bytes 7077896 | tf_op jit(solution)/shard_map/ppermute | solution.py:1035
  204.3 12.5 %collective-permute-start.35 = (bf16[4,16,1280]{2,1,0:T(8,128)(2,1)S(1)}, bf16[4,16,1280]{2,1,0:T(8,128)(2,1)S(1)}, u32[]{:S(2)}, u32[]{:S(2)}) collective-permute-start(bf16[4,16,1280]{2,1,0:T(8,128)(2,1)S(1)} %pad_maximum_fusion.3.refs_0_), channel_id=1, source_target_pairs={{0,16},{1,3},{2,18},{3,1},{4,20},{5,7},{6,22},{7,5},{8,24},{9,11},... | collective-permute-start | bytes 491528 | tf_op jit(solution)/shard_map/ppermute | solution.py:1035
  205.4 11.5 %collective-permute-start.36 = (bf16[4,16,1280]{2,1,0:T(8,128)(2,1)S(1)}, bf16[4,16,1280]{2,1,0:T(8,128)(2,1)S(1)}, u32[]{:S(2)}, u32[]{:S(2)}) collective-permute-start(bf16[4,16,1280]{2,1,0:T(8,128)(2,1)S(1)} %pad_maximum_fusion.3.refs_0_), channel_id=1, source_target_pairs={{0,2},{1,17},{2,0},{3,19},{4,6},{5,21},{6,4},{7,23},{8,10},{9,25},... | collective-permute-start | bytes 491528 | tf_op jit(solution)/shard_map/ppermute | solution.py:1035
  220.2 17.7 %collective-permute-start.37 = (bf16[8,192,384]{2,1,0:T(8,128)(2,1)S(1)}, bf16[8,192,384]{2,1,0:T(8,128)(2,1)S(1)}, u32[]{:S(2)}, u32[]{:S(2)}) collective-permute-start(bf16[8,192,384]{2,1,0:T(8,128)(2,1)S(1)} %shard_map.133), channel_id=1, source_target_pairs={{0,16},{1,3},{2,18},{3,1},{4,20},{5,7},{6,22},{7,5},{8,24},{9,11},... | collective-permute-start | bytes 3538952 | tf_op jit(solution)/shard_map/ppermute | solution.py:1035
  221.7 14.4 %collective-permute-start.38 = (bf16[4,16,1280]{2,1,0:T(8,128)(2,1)S(1)}, bf16[4,16,1280]{2,1,0:T(8,128)(2,1)S(1)}, u32[]{:S(2)}, u32[]{:S(2)}) collective-permute-start(bf16[4,16,1280]{2,1,0:T(8,128)(2,1)S(1)} %collective-permute-done.35.refs_1_), channel_id=1, source_target_pairs={{0,2},{1,17},{2,0},{3,19},{4,6},{5,21},{6,4},{7,23},{8,10},{9,25},... | collective-permute-start | bytes 491528 | tf_op jit(solution)/shard_map/ppermute | solution.py:1035
  222.3 13.9 %collective-permute-start.40 = (bf16[4,16,1280]{2,1,0:T(8,128)(2,1)S(1)}, bf16[4,16,1280]{2,1,0:T(8,128)(2,1)S(1)}, u32[]{:S(2)}, u32[]{:S(2)}) collective-permute-start(bf16[4,16,1280]{2,1,0:T(8,128)(2,1)S(1)} %collective-permute-done.35.refs_1_), channel_id=1, source_target_pairs={{0,1},{1,0},{2,3},{3,2},{4,5},{5,4},{6,7},{7,6},{8,9},{9,8},{10,11... | collective-permute-start | bytes 491528 | tf_op jit(solution)/shard_map/ppermute | solution.py:1035
  222.3 13.8 %collective-permute-start.39 = (bf16[4,16,1280]{2,1,0:T(8,128)(2,1)S(1)}, bf16[4,16,1280]{2,1,0:T(8,128)(2,1)S(1)}, u32[]{:S(2)}, u32[]{:S(2)}) collective-permute-start(bf16[4,16,1280]{2,1,0:T(8,128)(2,1)S(1)} %pad_maximum_fusion.3.refs_0_), channel_id=1, source_target_pairs={{0,1},{1,0},{2,3},{3,2},{4,5},{5,4},{6,7},{7,6},{8,9},{9,8},{10,11... | collective-permute-start | bytes 491528 | tf_op jit(solution)/shard_map/ppermute | solution.py:1035
  222.8 13.4 %collective-permute-start.41 = (bf16[4,16,1280]{2,1,0:T(8,128)(2,1)S(1)}, bf16[4,16,1280]{2,1,0:T(8,128)(2,1)S(1)}, u32[]{:S(2)}, u32[]{:S(2)}) collective-permute-start(bf16[4,16,1280]{2,1,0:T(8,128)(2,1)S(1)} %collective-permute-done.36.refs_2_), channel_id=1, source_target_pairs={{0,1},{1,0},{2,3},{3,2},{4,5},{5,4},{6,7},{7,6},{8,9},{9,8},{10,11... | collective-permute-start | bytes 491528 | tf_op jit(solution)/shard_map/ppermute | solution.py:1035
  242.8 12.1 %collective-permute-start.43 = (bf16[16,192,384]{2,1,0:T(8,128)(2,1)}, bf16[16,192,384]{2,1,0:T(8,128)(2,1)S(1)}, u32[]{:S(2)}, u32[]{:S(2)}) collective-permute-start(bf16[16,192,384]{2,1,0:T(8,128)(2,1)} %shard_map.134), channel_id=1, source_target_pairs={{0,1},{1,0},{2,3},{3,2},{4,5},{5,4},{6,7},{7,6},{8,9},{9,8},{10,11... | collective-permute-start | bytes 7077896 | tf_op jit(solution)/shard_map/ppermute | solution.py:1035
  244.9 9.9 %collective-permute-start.42 = (bf16[4,192,384]{2,1,0:T(8,128)(2,1)S(1)}, bf16[4,192,384]{2,1,0:T(8,128)(2,1)S(1)}, u32[]{:S(2)}, u32[]{:S(2)}) collective-permute-start(bf16[4,192,384]{2,1,0:T(8,128)(2,1)S(1)} %shard_map.136), channel_id=1, source_target_pairs={{0,2},{1,17},{2,0},{3,19},{4,6},{5,21},{6,4},{7,23},{8,10},{9,25},... | collective-permute-start | bytes 1769480 | tf_op jit(solution)/shard_map/ppermute | solution.py:1035
  246.0 7.4 %collective-permute-start.44 = (bf16[4,16,1280]{2,1,0:T(8,128)(2,1)S(1)}, bf16[4,16,1280]{2,1,0:T(8,128)(2,1)S(1)}, u32[]{:S(2)}, u32[]{:S(2)}) collective-permute-start(bf16[4,16,1280]{2,1,0:T(8,128)(2,1)S(1)} %collective-permute-done.38.refs_3_), channel_id=1, source_target_pairs={{0,1},{1,0},{2,3},{3,2},{4,5},{5,4},{6,7},{7,6},{8,9},{9,8},{10,11... | collective-permute-start | bytes 491528 | tf_op jit(solution)/shard_map/ppermute | solution.py:1035
  257.2 16.3 %collective-permute-start.45 = (bf16[8,192,384]{2,1,0:T(8,128)(2,1)S(1)}, bf16[8,192,384]{2,1,0:T(8,128)(2,1)S(1)}, u32[]{:S(2)}, u32[]{:S(2)}) collective-permute-start(bf16[8,192,384]{2,1,0:T(8,128)(2,1)S(1)} %shard_map.139), channel_id=1, source_target_pairs={{0,16},{1,3},{2,18},{3,1},{4,20},{5,7},{6,22},{7,5},{8,24},{9,11},... | collective-permute-start | bytes 3538952 | tf_op jit(solution)/shard_map/ppermute | solution.py:1035
  259.0 14.4 %collective-permute-start.46 = (bf16[192,384]{1,0:T(8,128)(2,1)S(1)}, bf16[192,384]{1,0:T(8,128)(2,1)S(1)}, u32[]{:S(2)}, u32[]{:S(2)}) collective-permute-start(bf16[192,384]{1,0:T(8,128)(2,1)S(1)} %get-tuple-element.257), channel_id=1, source_target_pairs={{0,4},{1,5},{2,6},{3,7},{4,0},{5,1},{6,2},{7,3},{8,12},{9,13},{10,... | collective-permute-start | bytes 442376 | tf_op jit(solution)/shard_map/ppermute | solution.py:1035
  259.0 14.4 %collective-permute-start.47 = (bf16[192,384]{1,0:T(8,128)(2,1)S(1)}, bf16[192,384]{1,0:T(8,128)(2,1)S(1)}, u32[]{:S(2)}, u32[]{:S(2)}) collective-permute-start(bf16[192,384]{1,0:T(8,128)(2,1)S(1)} %get-tuple-element.258), channel_id=1, source_target_pairs={{0,8},{1,9},{2,10},{3,11},{4,12},{5,13},{6,14},{7,15},{8,0},{9,1},... | collective-permute-start | bytes 442376 | tf_op jit(solution)/shard_map/ppermute | solution.py:1035
  261.4 12.0 %collective-permute-start.48 = (bf16[192,384]{1,0:T(8,128)(2,1)S(1)}, bf16[192,384]{1,0:T(8,128)(2,1)S(1)}, u32[]{:S(2)}, u32[]{:S(2)}) collective-permute-start(bf16[192,384]{1,0:T(8,128)(2,1)S(1)} %get-tuple-element.259), channel_id=1, source_target_pairs={{0,12},{1,13},{2,14},{3,15},{4,8},{5,9},{6,10},{7,11},{8,4},{9,5},... | collective-permute-start | bytes 442376 | tf_op jit(solution)/shard_map/ppermute | solution.py:1035
  275.7 9.9 %collective-permute-start.51 = (bf16[4,192,384]{2,1,0:T(8,128)(2,1)S(1)}, bf16[4,192,384]{2,1,0:T(8,128)(2,1)S(1)}, u32[]{:S(2)}, u32[]{:S(2)}) collective-permute-start(bf16[4,192,384]{2,1,0:T(8,128)(2,1)S(1)} %shard_map.143), channel_id=1, source_target_pairs={{0,2},{1,17},{2,0},{3,19},{4,6},{5,21},{6,4},{7,23},{8,10},{9,25},... | collective-permute-start | bytes 1769480 | tf_op jit(solution)/shard_map/ppermute | solution.py:1035
  285.6 16.0 %collective-permute-start.52 = (bf16[192,384]{1,0:T(8,128)(2,1)S(1)}, bf16[192,384]{1,0:T(8,128)(2,1)S(1)}, u32[]{:S(2)}, u32[]{:S(2)}) collective-permute-start(bf16[192,384]{1,0:T(8,128)(2,1)S(1)} %bitcast.44), channel_id=1, source_target_pairs={{0,1},{1,0},{2,3},{3,2},{4,5},{5,4},{6,7},{7,6},{8,9},{9,8},{10,11... | collective-permute-start | bytes 442376 | tf_op jit(solution)/shard_map/ppermute | solution.py:1035
  286.3 15.4 %collective-permute-start.55 = (bf16[192,384]{1,0:T(8,128)(2,1)S(1)}, bf16[192,384]{1,0:T(8,128)(2,1)S(1)}, u32[]{:S(2)}, u32[]{:S(2)}) collective-permute-start(bf16[192,384]{1,0:T(8,128)(2,1)S(1)} %get-tuple-element.274), channel_id=1, source_target_pairs={{0,4},{1,5},{2,6},{3,7},{4,0},{5,1},{6,2},{7,3},{8,12},{9,13},{10,... | collective-permute-start | bytes 442376 | tf_op jit(solution)/shard_map/ppermute | solution.py:1035
  288.1 14.0 %collective-permute-start.56 = (bf16[192,384]{1,0:T(8,128)(2,1)S(1)}, bf16[192,384]{1,0:T(8,128)(2,1)S(1)}, u32[]{:S(2)}, u32[]{:S(2)}) collective-permute-start(bf16[192,384]{1,0:T(8,128)(2,1)S(1)} %get-tuple-element.275), channel_id=1, source_target_pairs={{0,8},{1,9},{2,10},{3,11},{4,12},{5,13},{6,14},{7,15},{8,0},{9,1},... | collective-permute-start | bytes 442376 | tf_op jit(solution)/shard_map/ppermute | solution.py:1035
  288.7 13.4 %collective-permute-start.57 = (bf16[192,384]{1,0:T(8,128)(2,1)S(1)}, bf16[192,384]{1,0:T(8,128)(2,1)S(1)}, u32[]{:S(2)}, u32[]{:S(2)}) collective-permute-start(bf16[192,384]{1,0:T(8,128)(2,1)S(1)} %get-tuple-element.276), channel_id=1, source_target_pairs={{0,12},{1,13},{2,14},{3,15},{4,8},{5,9},{6,10},{7,11},{8,4},{9,5},... | collective-permute-start | bytes 442376 | tf_op jit(solution)/shard_map/ppermute | solution.py:1035
  307.5 25.2 %all-to-all-start.2 = ((bf16[8,8,16,384]{3,2,1,0:T(8,128)(2,1)}), bf16[8,8,16,384]{3,2,1,0:T(8,128)(2,1)S(1)}, u32[]{:S(2)}, u32[]{:S(2)}) async-start(bf16[8,8,16,384]{3,2,1,0:T(8,128)(2,1)} %bitcast.33), calls=%async_computation.2 | async-start | bytes 1572864 | tf_op jit(solution)/shard_map/all_to_all | solution.py:1151
  (71 other events, 646.4 us)

commit v4 on v3

--- a/solution.py
+++ b/solution.py
@@ -53,7 +53,7 @@
 )
 CHUNK_AT = ((0, 0), (1, 0), (1, 3), (2, 0), (2, 12))
 SLABS = (10, 15, 15)
-SAME_CORE = [[i * 2 + c for i in range(8)] for c in range(2)]
+CHIPS = [(dz, dy) for dz in range(4) for dy in range(2)]
 
 
 def nn(a, b):
@@ -187,7 +187,7 @@
     return jnp.sum(x, axis=0, keepdims=True)
 
 
-def qkv_block(j, me):
+def third(j, me):
     return jnp.where(me[CORE] == 0, j, 2 - j)
 
 
@@ -222,7 +222,7 @@
     def _():
         weight.wait(me_ref, pieces, w_ref, sems, 1, 2)
 
-    j = qkv_block(j, me_ref)
+    j = third(j, me_ref)
     bias = jnp.where(j == 0, vec_ref[4:5, :], jnp.where(j == 2, vec_ref[5:6, :], 0.0))
     scale = jnp.where(j == 0, f32(HEAD**-0.5), f32(1.0))
     w = w_ref[pl.ds(6 * j, 6)].reshape(D, D)
@@ -236,7 +236,7 @@
         (sds((n, D), bf16), sds((n, 3 * D), bf16), sds((16, D), f32)),
         (me, *weight.arrays, x, vec),
         weight.specs + [whole((n, D)), whole((16, D))],
-        [whole((n, D)), pl.BlockSpec((n, D), lambda j, me: (0, qkv_block(j, me))), whole((16, D))],
+        [whole((n, D)), pl.BlockSpec((n, D), lambda j, me: (0, third(j, me))), whole((16, D))],
         grid=(3,),
         out_hbm=(0,),
         scratch=weight.scratch + [pltpu.VMEM((2, 16, 384), bf16), pltpu.SemaphoreType.DMA((16,))],
@@ -310,13 +310,9 @@
 
 
 def gelu_parts(u):
-    size = jnp.abs(u)
-    t = 1.0 / (1.0 + 0.23164189 * size)
-    poly = t * (0.127414796 + t * (-0.142248368 + t * (0.7107068705 + t * (-0.7265760135 + t * 0.5307027145))))
-    e = jnp.exp2(u * u * -0.7213475204444817)
-    act = jnp.maximum(u, 0.0) - size * (poly * e)
-    w = e * (poly - 0.3989422804014327 * size)
-    return act, jnp.where(u >= 0.0, 1.0 - w, w)
+    phi = 0.5 + 0.5 * lax.erf(u * 0.7071067811865476)
+    density = jnp.exp2(u * u * -0.7213475204444817) * 0.3989422804014327
+    return u * phi, phi + u * density
 
 
 def own_block(j, me):
@@ -355,6 +351,7 @@
         weight.specs + [whole((n, D)), pl.BlockSpec((1, 1, D), lambda j, me: (own_block(j, me), 0, 0))],
         [cols, cols],
         grid=(FF // D,),
+        vmem_out=(0,),
         out_hbm=(1,),
         scratch=weight.scratch,
         flops=2 * n * D * FF,
@@ -384,44 +381,35 @@
 
 def down_kernel(images, weight, me_ref, *refs):
     count = len(weight.arrays)
-    act_ref, h_ref, vec_ref, sel_ref, inv_ref, out_ref, pooled_ref, w_ref, sems, sum_ref, y_ref = refs[count:]
-    k = pl.program_id(0)
-    quarters = FF // D
-
-    @pl.when(k == 0)
+    act_ref, h_ref, vec_ref, sel_ref, inv_ref, out_ref, pooled_ref, w_ref, sems = refs[count:]
+    j = pl.program_id(0)
+
+    @pl.when(j == 0)
     def _():
         weight.start(me_ref, refs[:count], w_ref, sems)
-
-    for part in range(quarters):
-
-        @pl.when(k == part)
-        def _():
-            weight.wait(me_ref, refs[:count], w_ref, sems, part, quarters)
-
-    @pl.when(k < quarters)
-    def _():
-        cols = pl.ds(pl.multiple_of((me_ref[Z] ^ k) * D, 128), D)
-        accumulate(k, y_ref, nt(act_ref[...], w_ref[:, :, cols].reshape(D, D)))
-
-    @pl.when(k >= quarters)
-    def _():
-        i = k - quarters
-        y = y_ref[pl.ds(pl.multiple_of(i * ROWS, 16), ROWS), :] + vec_ref[11:12, :]
-        out = (h_ref[...] + y).astype(bf16)
-        out_ref[0] = out[0:PATCHES, :]
-        accumulate(i, sum_ref, nn(sel_ref[i], out))
-        pooled_ref[...] = (sum_ref[...] * inv_ref[:, 0:1]).astype(bf16)
+        weight.wait(me_ref, refs[:count], w_ref, sems, 0, 2)
+
+    @pl.when(j == 1)
+    def _():
+        weight.wait(me_ref, refs[:count], w_ref, sems, 1, 2)
+
+    tiles = DOWN_TILES // 3
+    w = w_ref[pl.ds(tiles * third(j, me_ref), tiles)].reshape(D // 3, FF)
+    y = nt(act_ref[...], w)
+    total = jnp.zeros((16, D // 3), f32)
+    for i in range(images):
+        rows = slice(i * ROWS, i * ROWS + ROWS)
+        out = (h_ref[rows, :] + (y[rows] + vec_ref[11:12, :])).astype(bf16)
+        out_ref[i] = out[0:PATCHES, :]
+        total += nn(sel_ref[i], out)
+    pooled_ref[...] = (total * inv_ref[:, 0:1]).astype(bf16)
 
 
 def down_forward(images, act, weight, h, vec, sel, inv_count, me):
     n = images * ROWS
-    quarters = FF // D
-
-    def image(k):
-        return jnp.maximum(k - quarters, 0)
-
-    def quarter(k, me):
-        return me[Z] ^ jnp.minimum(k, quarters - 1)
+
+    def cols(rows):
+        return pl.BlockSpec((rows, D // 3), lambda j, me: (0, third(j, me)))
 
     return call(
         functools.partial(down_kernel, images, weight),
@@ -430,18 +418,16 @@
         weight.specs[:-1]
         + [
             pl.BlockSpec(memory_space=pl.ANY),
-            pl.BlockSpec((n, D), lambda k, me: (0, quarter(k, me))),
-            pl.BlockSpec((ROWS, D), lambda k, me: (image(k), 0)),
-            whole((16, D)),
+            pl.BlockSpec(memory_space=pltpu.VMEM),
+            cols(n),
+            cols(16),
             whole((images, 16, ROWS)),
             whole((16, 128)),
         ],
-        [
-            pl.BlockSpec((1, PATCHES, D), lambda k, me: (image(k), 0, 0)),
-            whole((16, D)),
-        ],
-        grid=(quarters + images,),
-        scratch=weight.scratch + [pltpu.VMEM((16, D), f32), pltpu.VMEM((n, D), f32)],
+        [pl.BlockSpec((images, PATCHES, D // 3), lambda j, me: (0, 0, third(j, me))), cols(16)],
+        grid=(3,),
+        vmem_in=(1 + len(weight.arrays),),
+        scratch=weight.scratch,
         flops=2 * n * D * FF,
         prefetch=1,
     )
@@ -552,7 +538,7 @@
     return (j // 2 + 1 - me[CORE]) % 2 * 2 + j % 2
 
 
-SPLIT = 528
+DM_COLS = 256
 
 
 def up_back_kernel(images, weight, me_ref, *refs):
@@ -576,7 +562,7 @@
             du_ref[at, cols] = du
             total += column_sum(du.astype(f32))
         db_ref[...] = jnp.broadcast_to(total, db_ref.shape)
-        dw = tn(du_ref[pl.ds(0, images * ROWS), cols], m_ref[...]).astype(bf16)
+        dw = tn(du_ref[:, cols], m_ref[...]).astype(bf16)
         if not weight.pieces:
             refs[count + 6][...] = dw
             return
@@ -596,14 +582,17 @@
 
     @pl.when(j >= blocks)
     def _():
-        rows = pl.ds(pl.multiple_of((j - blocks) * SPLIT, 16), SPLIT)
-        dm_ref[...] = nn(du_ref[rows, :], w_ref[...].reshape(FF, D))
+        for k in range(D // DM_COLS):
+
+            @pl.when(j == blocks + k)
+            def _():
+                dm_ref[...] = nn(du_ref[...], w_ref[:, :, k * DM_COLS : (k + 1) * DM_COLS].reshape(FF, DM_COLS))
 
 
 def up_backward(images, slope, m, weight, hidden, col, me):
     n = images * ROWS
     blocks = FF // D
-    steps = -(-n // SPLIT)
+    steps = D // DM_COLS
 
     def block(j, me):
         return half_block(jnp.minimum(j, blocks - 1), me)
@@ -625,10 +614,10 @@
         (sds((n, D), f32), sds((8, FF), f32)) + shapes,
         (me, *weight.arrays, slope, m, hidden, col),
         weight.specs + [cols(n), whole((n, D)), cols(16), whole((n, 128))],
-        [pl.BlockSpec((SPLIT, D), lambda j, me: (jnp.maximum(j - blocks, 0), 0)), cols(8)] + specs,
+        [pl.BlockSpec((n, DM_COLS), lambda j, me: (0, jnp.maximum(j - blocks, 0))), cols(8)] + specs,
         grid=(blocks + steps,),
         vmem=40,
-        scratch=weight.scratch + [pltpu.VMEM((steps * SPLIT, FF), bf16)],
+        scratch=weight.scratch + [pltpu.VMEM((n, FF), bf16)],
         flops=4 * n * D * FF,
         prefetch=1,
     )
@@ -872,9 +861,10 @@
 SUMMED, DOWN, PROJ, NONE, VEC = 0, 1, 2, 3, 4
 
 
-def adam_kernel(part_rows, fast, each, kind_ref, row_ref, *refs):
-    master_ref, first_ref, second_ref, summed_ref, down_ref, proj_ref, vec_ref = refs[:7]
-    new_master_ref, new_first_ref, new_second_ref, grad_ref, woven_ref = refs[7:]
+def adam_kernel(part_rows, fast, each, kind_ref, row_ref, me_ref, *refs):
+    master_ref, first_ref, second_ref, down_ref, proj_ref, vec_ref = refs[:6]
+    summed_refs = refs[6:-5]
+    new_master_ref, new_first_ref, new_second_ref, grad_ref, woven_ref = refs[-5:]
     wide = FF // D
     for k in range(each):
         slot = pl.program_id(0) * each + k
@@ -883,11 +873,12 @@
         @pl.when(kind == SUMMED)
         def _():
             if fast:
-                for z in range(4):
-                    for y in range(2):
-                        grad_ref[16 * z : 16 * z + 16, 384 * y : 384 * y + 384] = summed_ref[2 * z + y, k].astype(f32)
+                for summed_ref, (dz, dy) in zip(summed_refs, CHIPS, strict=True):
+                    rows = pl.ds(pl.multiple_of((me_ref[Z] ^ dz) * 16, 16), 16)
+                    cols = pl.ds(pl.multiple_of((me_ref[Y] ^ dy) * 384, 128), 384)
+                    grad_ref[rows, cols] = summed_ref[k].astype(f32)
             else:
-                grad_ref[...] = summed_ref[k].astype(f32)
+                grad_ref[...] = summed_refs[0][k].astype(f32)
 
         @pl.when(kind == VEC)
         def _():
@@ -922,33 +913,30 @@
         new_master_ref[0, k] = master - learn_rate * (direction / size + decay_rate * master)
 
 
-def adam(kind, row, master, first, second, summed, down, proj, vec, fast):
+def adam(kind, row, me, master, first, second, summed, down, proj, vec):
     slots, part_rows = master.shape[1:3]
     each = slots // 2
     block = pl.BlockSpec((1, each, part_rows, D), lambda s, *_: (0, s, 0, 0))
-    if fast:
-        summed_spec = pl.BlockSpec((8, each, 16, 384), lambda s, *_: (0, s, 0, 0))
-    else:
-        summed_spec = pl.BlockSpec((each, part_rows, D), lambda s, *_: (s, 0, 0))
+    fast = len(summed) > 1
     return call(
         functools.partial(adam_kernel, part_rows, fast, each),
         (sds(master.shape, f32),) * 3,
-        (kind, row, master, first, second, summed, down, proj, vec),
+        (kind, row, me, master, first, second, down, proj, vec, *summed),
         [
             block,
             block,
             block,
-            summed_spec,
             pl.BlockSpec((each,) + down.shape[1:], lambda s, *_: (s, 0, 0)),
             whole(proj.shape),
             whole(vec.shape),
-        ],
+        ]
+        + [pl.BlockSpec((each,) + a.shape[1:], lambda s, *_: (s, 0, 0)) for a in summed],
         [block] * 3,
         grid=(slots // each,),
         scratch=[pltpu.VMEM((part_rows, D), f32), pltpu.VMEM((D // 128, part_rows, 128), f32)],
         flops=20 * slots * part_rows * D,
-        in_hbm=(2, 3, 4, 6, 7),
-        prefetch=2,
+        in_hbm=(3, 4, 5, 6, 7),
+        prefetch=3,
     )
 
 
@@ -1125,30 +1113,30 @@
 
 
 def place_kernel(index_ref, *refs):
-    out_ref = refs[-1]
-    for k in range(out_ref.shape[0]):
+    for k in range(64):
         at = index_ref[k]
+        out_ref = refs[4 + k // 8]
         for q in range(4):
 
             @pl.when((at >= 12 * q) & (at < 12 * q + 12))
             def _():
-                out_ref[k] = refs[q][pl.ds(pl.multiple_of((at - 12 * q) * 16, 16), 16), :]
+                out_ref[k % 8] = refs[q][pl.ds(pl.multiple_of((at - 12 * q) * 16, 16), 16), :]
 
         @pl.when(at >= 48)
         def _():
-            out_ref[k] = jnp.zeros((16, 384), bf16)
+            out_ref[k % 8] = jnp.zeros((16, 384), bf16)
 
 
 def return_to_owners(sums, place):
     placed = call(
         place_kernel,
-        (sds((64, 16, 384), bf16),),
+        (sds((8, 16, 384), bf16),) * 8,
         (place, *sums),
         [whole((192, 384))] * 4,
-        [whole((64, 16, 384))],
+        [whole((8, 16, 384))] * 8,
         prefetch=1,
-    )[0]
-    return lax.all_to_all(placed.reshape(8, 8, 16, 384), "rep", 0, 0, axis_index_groups=SAME_CORE)
+    )
+    return exchange(placed)
 
 
 def plan_kernel(owner_ref, me_ref, pick_ref, place_ref, kind_ref, row_ref, counts, placed, tile_of):
@@ -1174,7 +1162,8 @@
     def slab(t):
         at = placed[t]
         owner = at // 8
-        return jnp.where(owner % 2 == c, 0, 64) + owner // 2 * 8 + at % 8
+        chip = (owner // 4 ^ me_ref[Z]) * 2 + (owner // 2 % 2 ^ me_ref[Y])
+        return jnp.where(owner % 2 == c, 0, 64) + chip * 8 + at % 8
 
     def fill(first, count, tile):
         @pl.loop(0, count)
@@ -1189,7 +1178,9 @@
 
     @pl.loop(0, 64)
     def _(k):
-        t = tile_of[k // 8 * 16 + c * 8 + k % 8]
+        chip = k // 8
+        owner = (chip // 2 ^ me_ref[Z]) * 4 + (chip % 2 ^ me_ref[Y]) * 2 + c
+        t = tile_of[owner * 8 + k % 8]
         u = t - QKV_TILES
         v = u - OUT_TILES
         half = jnp.where(t < QKV_TILES, t // 9, jnp.where(u < OUT_TILES, u // 3, v // 12))
@@ -1220,7 +1211,8 @@
     )(owner_list, me)
 
 
-def prepare_kernel(owner_ref, me_ref, master_ref, out_ref, lanes_ref, tile_ref):
+def prepare_kernel(owner_ref, me_ref, master_ref, *refs):
+    out_refs, (lanes_ref, tile_ref) = refs[:8], refs[8:]
     rep = me_ref[Z] * 4 + me_ref[Y] * 2 + me_ref[CORE]
     for s in range(9):
         tile_ref[s] = 0
@@ -1240,18 +1232,19 @@
 
         @pl.when(jnp.logical_not(down))
         def _():
-            for z in range(4):
-                for y in range(2):
-                    out_ref[2 * z + y, s] = master_ref[0, s, 16 * z : 16 * z + 16, 384 * y : 384 * y + 384].astype(bf16)
+            for k, (dz, dy) in enumerate(CHIPS):
+                rows = pl.ds(pl.multiple_of((me_ref[Z] ^ dz) * 16, 16), 16)
+                cols = pl.ds(pl.multiple_of((me_ref[Y] ^ dy) * 384, 128), 384)
+                out_refs[k][s] = master_ref[0, s, rows, cols].astype(bf16)
 
         @pl.when(down)
         def _():
             for k in range(6):
                 lanes_ref[k] = master_ref[0, s, :, 128 * k : 128 * k + 128]
-            for z in range(4):
-                for k in range(6):
-                    part = lanes_ref[k, pl.ds(z, 16, stride=4), :]
-                    out_ref[2 * z + k // 3, s, :, k % 3 * 128 : k % 3 * 128 + 128] = part.astype(bf16)
+            for k, (dz, dy) in enumerate(CHIPS):
+                for q in range(3):
+                    part = lanes_ref[(me_ref[Y] ^ dy) * 3 + q, pl.ds(me_ref[Z] ^ dz, 16, stride=4), :]
+                    out_refs[k][s, :, 128 * q : 128 * q + 128] = part.astype(bf16)
 
 
 def pick_kernel(index_ref, mine_ref, theirs_ref, text_ref, one_ref, two_ref, three_ref):
@@ -1281,11 +1274,12 @@
 
 
 class Spread:
-    def __init__(self, block):
-        self.parts = [block] + [send(block, move) for move in ACROSS_Z]
-
-    def cross_one(self):
-        self.ring = jnp.stack(self.parts)
+    def __init__(self, block=None):
+        if block is not None:
+            self.parts = [block] + [send(block, move) for move in ACROSS_Z]
+
+    def cross_one(self, ring=None):
+        self.ring = jnp.stack(self.parts) if ring is None else ring
         self.one = send(self.ring, CROSS_ONE)
         self.two = None
         self.near = []
@@ -1320,20 +1314,27 @@
             yield c, me[X] + flip_x - 2 * me[X] * flip_x, me[Y] + flip_y - 2 * me[Y] * flip_y
 
 
+def exchange(blocks):
+    return [blocks[0]] + [
+        send(blocks[k], pairs(lambda x, z, y, c, k=k: (x, z ^ CHIPS[k][0], y ^ CHIPS[k][1], c))) for k in range(1, 8)
+    ]
+
+
 def pick_slabs(master, text_emb, owner_list, me, *others):
     prepared = call(
         prepare_kernel,
-        (sds((8, 8, 16, 384), bf16),),
+        (sds((8, 16, 384), bf16),) * 8,
         (owner_list, me, master),
         [whole(master.shape)],
-        [whole((8, 8, 16, 384))],
+        [whole((8, 16, 384))] * 8,
         scratch=[pltpu.VMEM((6, 64, 128), f32), pltpu.SMEM((16,), jnp.int32)],
         in_hbm=(2,),
         prefetch=2,
-    )[0]
+    )
     pick, place, kind, row = plan(owner_list, me)
-    mine = lax.all_to_all(prepared, "rep", 0, 0, axis_index_groups=SAME_CORE).reshape(64, 16, 384)
-    mine, pick, *others = meet(mine, pick, *others)
+    *mine, pick = meet(*exchange(prepared), pick)
+    mine = jnp.concatenate(mine)
+    mine, *others = meet(mine, *others)
     blocks = call(
         pick_kernel,
         tuple(sds((slabs, 16, 384), bf16) for slabs in SLABS),
@@ -1445,55 +1446,64 @@
     both = jnp.concatenate([rank[:images], act_sum[:images]], axis=1)
     if fast:
         packed = jnp.concatenate([both[:, at * PACK : (at + 1) * PACK] for at in range(3)], axis=0)
-        ranks = Spread(jnp.pad(packed, ((0, 16 - 3 * images), (0, 0))))
+        ranks = Spread()
+        packed = jnp.pad(packed, ((0, 16 - 3 * images), (0, 0)))
+        beside = send(packed, SWAP_Z)
         dm, g_bias_up, other, mine = up_backward(images, slope, m, w_up, hidden, col, me)
-        dm, other, mine, *ranks.parts = meet(dm, other, mine, *ranks.parts)
+        dm, other, mine, packed, beside = meet(dm, other, mine, packed, beside)
         up_sum = PieceSum(other, me)
-        ranks.cross_one()
+        pair = jnp.stack([packed, beside])
+        far = send(pair, SWAP_ZZ)
+        dh, do, g_out, g_two = middle_backward(images, h, dm, col, spread, o, w_out, vec, me)
+        dh, do, up_sum.mine, up_sum.one, pair, far = meet(dh, do, mine, up_sum.one, pair, far)
+        up_sum.cross_one()
+        dqkv, g_bias = attention_backward(images, qkv, do, probabilities)
+        dqkv, up_sum.two, pair, far = meet(dqkv, up_sum.two, pair, far)
+        up_sum.cross_two()
+        ranks.cross_one(jnp.concatenate([pair, far]))
         ranks.two = send(ranks.ring, CROSS_TWO)
-        dh, do, g_out, g_two = middle_backward(images, h, dm, col, spread, o, w_out, vec, me)
-        dh, do, up_sum.mine, up_sum.one, ranks.ring, ranks.one, ranks.two = meet(
-            dh, do, mine, up_sum.one, ranks.ring, ranks.one, ranks.two
-        )
-        up_sum.cross_one()
-        ranks.cross_two()
-        ranks.send_near(0, 1, 2)
-        dqkv, g_bias = attention_backward(images, qkv, do, probabilities)
-        dqkv, up_sum.two, ranks.both, *ranks.near = meet(dqkv, up_sum.two, ranks.both, *ranks.near)
-        ranks.finish()
-        up_sum.cross_two()
         other = qkv_weight_grad_fast(images, dqkv, a, g_out, me, True)
         other, dqkv = meet(other, dqkv)
         qkv_sum = PieceSum(other, me)
         mine = qkv_weight_grad_fast(images, dqkv, a, g_out, me, False)
         up_sum.partial()
-        dqkv, up_sum.sums, up_sum.three, qkv_sum.mine, qkv_sum.one, ranks.near[3] = meet(
-            dqkv, up_sum.sums, up_sum.three, mine, qkv_sum.one, ranks.near[3]
+        dqkv, up_sum.sums, up_sum.three, qkv_sum.mine, qkv_sum.one, ranks.ring, ranks.one, ranks.two = meet(
+            dqkv, up_sum.sums, up_sum.three, mine, qkv_sum.one, ranks.ring, ranks.one, ranks.two
         )
         qkv_sum.cross_one()
         up_sum.cross_z()
+        ranks.cross_two()
         input_grad, vec_sum = input_backward(images, x, dqkv, w_qkv, dh, vec, g_two, g_bias, g_bias_up, me)
-        vec_sum, qkv_sum.two, *up_sum.last = meet(vec_sum, qkv_sum.two, *up_sum.last)
+        vec_sum, qkv_sum.two, ranks.ring, ranks.one, ranks.two, ranks.both, *up_sum.last = meet(
+            vec_sum, qkv_sum.two, ranks.ring, ranks.one, ranks.two, ranks.both, *up_sum.last
+        )
         qkv_sum.cross_two()
         near_vec = send(vec_sum, SWAP_CORE)
+        ranks.send_near(0, 1)
         up_total = up_sum.total()
         vec_sum, near_vec, up_total = meet(vec_sum, near_vec, up_total)
         vec_sum += near_vec
         vec_sum += send(vec_sum, SWAP_ZZ)
         qkv_sum.partial()
-        vec_sum, qkv_sum.sums, qkv_sum.three, up_total = meet(vec_sum, qkv_sum.sums, qkv_sum.three, up_total)
+        vec_sum, qkv_sum.sums, qkv_sum.three, up_total, ranks.two, ranks.both, *ranks.near = meet(
+            vec_sum, qkv_sum.sums, qkv_sum.three, up_total, ranks.two, ranks.both, *ranks.near
+        )
         qkv_sum.cross_z()
         near_up = send(up_total, SWAP_CORE)
         vec_sum += send(vec_sum, SWAP_Y)
         vec_sum += send(vec_sum, SWAP_Z)
-        near_up, vec_sum, *qkv_sum.last = meet(near_up, vec_sum, *qkv_sum.last)
+        near_up, vec_sum, ranks.two, ranks.both, *qkv_sum.last = meet(
+            near_up, vec_sum, ranks.two, ranks.both, *qkv_sum.last
+        )
         qkv_total = qkv_sum.total()
         near_qkv = send(qkv_total, SWAP_CORE)
-        near_qkv, vec_sum = meet(near_qkv, vec_sum)
+        ranks.finish()
+        across = send(vec_sum, SWAP_X)
+        near_qkv, across, *ranks.near = meet(near_qkv, across, *ranks.near)
+        vec_total = vec_sum + across
         summed = return_to_owners((qkv_total, up_total, near_qkv, near_up), place)
-        vec_total = vec_sum + send(vec_sum, SWAP_X)
         g_down, g_proj = rank_grads(images, kind, row, ranks.arrays(), dz_all, pooled_all)
-        summed, g_down, g_proj, vec_total = meet(summed, g_down.reshape(8, 16, FF), g_proj, vec_total)
+        g_down, g_proj, vec_total, *summed = meet(g_down.reshape(8, 16, FF), g_proj, vec_total, *summed)
     else:
         both_all = lax.all_gather(both, AXES, axis=0, tiled=True)
         dm, g_bias_up, g_up = up_backward(images, slope, m, w_up, hidden, col, me)
@@ -1517,9 +1527,9 @@
         last = jnp.pad(vec_total, ((0, TR - 16), (0, 0))).astype(bf16)
         tiles = jnp.concatenate([g_qkv, g_out, g_up, last], axis=0).reshape(-1, TR, D)
         index = jnp.where(tile_of_slot == VEC_TILE, DOWN_FIRST, jnp.where(tile_of_slot < DOWN_FIRST, tile_of_slot, 1 << 20))
-        summed = scatter_grads(tiles, index, slots, part_rows)
+        summed = [scatter_grads(tiles, index, slots, part_rows)]
     new_master, new_first, new_second = adam(
-        kind, row, master, first_moment, second_moment, summed, g_down, g_proj, vec_total, fast
+        kind, row, me, master, first_moment, second_moment, summed, g_down, g_proj, vec_total
     )
     return block_out, input_grad, new_master, new_first, new_second
 

time: 343 us -> 336 us (0.980)
  starting transfers between devices: 69.8 us -> 86 us
  waiting for transfers between devices: 84.6 us -> 69.4 us
  Pallas kernels: 171 us -> 162 us
    all_to_all x2 -> x0, waiting for transfers between devices: 26.7 us -> none  [the longest x1 14.8 us: return_to_owners(): lax.all_to_all(placed.reshape(8, 8, 16, 384), 'rep', 0, 0, axis_index_gro...]
    ppermute x60 -> x73, starting transfers between devices: 53.7 us -> 79.3 us  [send(): return lax.ppermute(value, AXES, permutation)]
    all_to_all x2 -> x0, starting transfers between devices: 12 us -> none  [the longest x1 7.28 us: pick_slabs(): lax.all_to_all(prepared, 'rep', 0, 0, axis_index_groups=SAME_CORE)]
    ppermute x60 -> x73, waiting for transfers between devices: 54.8 us -> 66.4 us  [send(): return lax.ppermute(value, AXES, permutation)]
    pallas_call x29, Pallas kernels: 165 us -> 154 us  [call(): pl.pallas_call(kernel, out_shape=tuple(outs), grid_spec=pltpu.PrefetchSca...]
    unnamed x112 -> x116, local copies, waits for them, and re-layouts: 8.09 us -> 8.36 us
  transfers between devices with their start and end apart: 63 -> 74, of which waited for: 26 -> 28; matrix products, arithmetic and copies ran while one was open for 1% -> 1% of each run, Pallas kernels for 37% -> 37%
where the time goes in v4:
time: 336 us; the launch traced here: 331 us
  Pallas kernels  162 us (48%)
  starting transfers between devices  86 us (26%)
  waiting for transfers between devices  69.4 us (21%)
  local copies, waits for them, and re-layouts  11.1 us (3%)
    pallas_call x29, Pallas kernels, call(): pl.pallas_call(kernel, out_shape=tuple(outs), grid_spec=pltpu.PrefetchSca...  154 us
    ppermute x73, starting transfers between devices, send(): return lax.ppermute(value, AXES, permutation)  79.3 us
    ppermute x73, waiting for transfers between devices, send(): return lax.ppermute(value, AXES, permutation)  66.4 us
    unnamed x116, local copies, waits for them, and re-layouts  8.36 us
    pallas_call x1, Pallas kernels, plan(): pl.pallas_call(plan_kernel, out_shape=tuple((sds((size,), jnp.int32) for...  7.15 us
  transfers between devices with their start and end apart: 74, of which 28 were waited for; matrix products, arithmetic and copies ran while one was open for 1% of the time, Pallas kernels for 37%

profile of v4, /device:TPU:0, one launch (start us, length us, event | category | flops | bytes accessed | tf_op | source)
XLA Modules:
  0.0 330.8 jit_solution(2119741039130438319)
XLA Ops:
  1.4 2.2 shard_map.119
  3.6 3.1 collective-permute-start
  8.2 3.0 collective-permute-start.3
  12.8 3.7 %collective-permute-start.5 = (bf16[8,16,384]{2,1,0:T(8,128)(2,1)S(1)}, bf16[8,16,384]{2,1,0:T(8,128)(2,1)S(1)}, u32[]{:S(2)}, u32[]{:S(2)}) collective-permute-start(bf16[8,16,384]{2,1,0:T(8,128)(2,1)S(1)} %get-tuple-element.200), channel_id=1, source_target_pairs={{0,12},{1,13},{2,14},{3,15},{4,8},{5,9},{6,10},{7,11},{8,4},{9,5},... | collective-permute-start | bytes 294920 | tf_op jit(solution)/shard_map/ppermute | solution.py:1023
  16.4 7.1 %shard_map.120 = (s32[39]{0:T(128)}, s32[64]{0:T(128)}, s32[8]{0:T(128)}, s32[8]{0:T(128)}) custom-call(s32[77]{0:T(128)} %owner_ref.3, s32[4]{0:T(128)} %copy-done.17), custom_call_target="tpu_custom_call" | custom-call | tf_op jit(solution)/shard_map/pallas_call | solution.py:1205
  27.1 2.3 collective-permute-done.7.theirs_ref
  30.5 4.0 %collective-permute-start.8 = (bf16[10,16,384]{2,1,0:T(8,128)(2,1)S(1)}, bf16[10,16,384]{2,1,0:T(8,128)(2,1)S(1)}, u32[]{:S(2)}, u32[]{:S(2)}) collective-permute-start(bf16[10,16,384]{2,1,0:T(8,128)(2,1)S(1)} %get-tuple-element.215), channel_id=1, source_target_pairs={{0,4},{1,5},{2,6},{3,7},{4,0},{5,1},{6,2},{7,3},{8,12},{9,13},{10,... | collective-permute-start | bytes 368648 | tf_op jit(solution)/shard_map/ppermute | solution.py:1023
  37.2 2.7 collective-permute-done.8
  39.8 7.0 %collective-permute-done.9 = bf16[10,16,384]{2,1,0:T(8,128)(2,1)S(1)} collective-permute-done((bf16[10,16,384]{2,1,0:T(8,128)(2,1)S(1)}, bf16[10,16,384]{2,1,0:T(8,128)(2,1)S(1)}, u32[]{:S(2)}, u32[]{:S(2)}) %collective-permute-start.9) | collective-permute-done | bytes 122912 | tf_op jit(solution)/shard_map/ppermute | solution.py:1023
  53.7 4.9 %collective-permute-done.11.refs_1_ = bf16[4,10,16,384]{3,2,1,0:T(8,128)(2,1)S(1)} collective-permute-done((bf16[4,10,16,384]{3,2,1,0:T(8,128)(2,1)S(1)}, bf16[4,10,16,384]{3,2,1,0:T(8,128)(2,1)S(1)}, u32[]{:S(2)}, u32[]{:S(2)}) %collective-permute-start.11) | collective-permute-done | bytes 491552 | tf_op jit(solution)/shard_map/ppermute | solution.py:1023
  60.2 6.5 %collective-permute-done.14 = bf16[15,16,384]{2,1,0:T(8,128)(2,1)S(1)} collective-permute-done((bf16[15,16,384]{2,1,0:T(8,128)(2,1)S(1)}, bf16[15,16,384]{2,1,0:T(8,128)(2,1)S(1)}, u32[]{:S(2)}, u32[]{:S(2)}) %collective-permute-start.14) | collective-permute-done | bytes 184352 | tf_op jit(solution)/shard_map/ppermute | solution.py:1023
  73.0 9.1 %shard_map.122 = (bf16[1040,768]{1,0:T(8,128)(2,1)}, bf16[1040,2304]{1,0:T(8,128)(2,1)S(1)}, f32[16,768]{1,0:T(8,128)S(1)}) custom-call(s32[4]{0:T(128)S(1)} %copy-done.18, bf16[4,10,16,384]{3,2,1,0:T(8,128)(2,1)} %copy-done.34, bf16[4,10,16,384]{3,2,1,0:T(8,128)(2,1)} %copy-done.41, bf16[4,10,16,384]{3,2,1,0:T(8,128)(2,1)} %copy-done.42, ...), custom_call_target="tpu_custom_call" | custom-call | flops 1 | bytes 1 | tf_op jit(solution)/shard_map/pallas_call | solution.py:84
  84.2 2.1 collective-permute-start.25
  89.2 9.0 %shard_map.123 = (bf16[1040,768]{1,0:T(8,128)(2,1)S(1)}, f32[5,16,208]{2,1,0:T(8,128)S(1)}) custom-call(bf16[1040,2304]{1,0:T(8,128)(2,1)S(1)} %get-tuple-element.235.qkv_ref, f32[5,1,208]{2,1,0:T(1,128)S(1)} %broadcast_in_dim.84.mask_ref), custom_call_target="tpu_custom_call" | custom-call | flops 1 | bytes 1 | tf_op jit(solution)/shard_map/pallas_call | solution.py:84
  98.3 4.4 %collective-permute-done.26 = bf16[15,16,384]{2,1,0:T(8,128)(2,1)S(1)} collective-permute-done((bf16[15,16,384]{2,1,0:T(8,128)(2,1)S(1)}, bf16[15,16,384]{2,1,0:T(8,128)(2,1)S(1)}, u32[]{:S(2)}, u32[]{:S(2)}) %collective-permute-start.26) | collective-permute-done | bytes 184352 | tf_op jit(solution)/shard_map/ppermute | solution.py:1023
  106.9 6.2 %shard_map.124 = (f32[1040,768]{1,0:T(8,128)S(1)}, bf16[1040,768]{1,0:T(8,128)(2,1)S(1)}) custom-call(s32[4]{0:T(128)S(1)} %copy-done.18, bf16[4,15,16,384]{3,2,1,0:T(8,128)(2,1)} %copy-done.25, bf16[4,15,16,384]{3,2,1,0:T(8,128)(2,1)} %copy-done.26, bf16[4,15,16,384]{3,2,1,0:T(8,128)(2,1)} %copy-done.28, bf16[4,15,16,384]{3,2,1,0:T(8,128)(2,1)} %copy-done.29, ...), custom_call_target="tpu_custom_call" | custom-call | flops 1 | bytes 1 | tf_op jit(solution)/shard_map/pallas_call | solution.py:84
  117.5 13.3 %shard_map.125 = (bf16[1040,3072]{1,0:T(8,128)(2,1)S(1)}, bf16[1040,3072]{1,0:T(8,128)(2,1)}) custom-call(s32[4]{0:T(128)S(1)} %copy-done.18, bf16[4,15,16,384]{3,2,1,0:T(8,128)(2,1)} %copy-done.25, bf16[4,15,16,384]{3,2,1,0:T(8,128)(2,1)} %copy-done.26, bf16[4,15,16,384]{3,2,1,0:T(8,128)(2,1)} %copy-done.28, bf16[4,15,16,384]{3,2,1,0:T(8,128)(2,1)} %copy-done.29, ...), custom_call_target="tpu_custom_call" | custom-call | flops 1 | bytes 1 | tf_op jit(solution)/shard_map/pallas_call | solution.py:84
  130.9 3.4 %collective-permute-done.33.refs_3_ = bf16[4,15,16,384]{3,2,1,0:T(8,128)(2,1)S(1)} collective-permute-done((bf16[4,15,16,384]{3,2,1,0:T(8,128)(2,1)S(1)}, bf16[4,15,16,384]{3,2,1,0:T(8,128)(2,1)S(1)}, u32[]{:S(2)}, u32[]{:S(2)}) %collective-permute-start.33) | collective-permute-done | bytes 737312 | tf_op jit(solution)/shard_map/ppermute | solution.py:1023
  137.7 10.0 %shard_map.126 = (bf16[5,196,768]{2,1,0:T(8,128)(2,1)}, bf16[16,768]{1,0:T(8,128)(2,1)S(1)}) custom-call(s32[4]{0:T(128)S(1)} %copy-done.18, bf16[4,15,16,384]{3,2,1,0:T(8,128)(2,1)} %copy-done.33, bf16[4,15,16,384]{3,2,1,0:T(8,128)(2,1)} %copy-done.35, bf16[4,15,16,384]{3,2,1,0:T(8,128)(2,1)} %copy-done.36, bf16[4,15,16,384]{3,2,1,0:T(8,128)(2,1)} %copy-done.37, ...), custom_call_target="tpu_custom_call" | custom-call | flops 1 | bytes 1 | tf_op jit(solution)/shard_map/pallas_call | solution.py:84
  148.5 6.7 %all-to-all-start = ((bf16[32,5,768]{2,1,0:T(8,128)(2,1)}), bf16[32,5,768]{2,1,0:T(8,128)(2,1)S(1)}, u32[]{:S(2)}, u32[]{:S(2)}) async-start(bf16[32,5,768]{2,1,0:T(8,128)(2,1)} %broadcast_in_dim.95), calls=%async_computation | async-start | bytes 786432 | tf_op jit(solution)/shard_map/all_to_all | solution.py:1437
  155.2 2.3 copy-done.6
  157.6 3.2 shard_map.128.p_ref
  160.8 2.7 copy-done.7
  165.3 3.0 all-to-all-done.refs_9_
  168.3 5.1 %shard_map.129 = (bf16[160,512]{1,0:T(8,128)(2,1)S(1)}, bf16[16,768]{1,0:T(8,128)(2,1)S(1)}, f32[16,768]{1,0:T(8,128)S(1)}, f32[16,3072]{1,0:T(8,128)S(1)}, bf16[160,768]{1,0:T(8,128)(2,1)S(1)}) custom-call(s32[4]{0:T(128)S(1)} %copy-done.18, s32[1]{0:T(128)} %bitcast.5.first_ref, bf16[4,15,16,384]{3,2,1,0:T(8,128)(2,1)} %copy-done.33, ...), custom_call_target="tpu_custom_call" | custom-call | flops 1 | bytes 1 | tf_op jit(solution)/shard_map/pallas_call | solution.py:84
  174.4 19.9 %shard_map.130 = (f32[1040,768]{1,0:T(8,128)S(1)}, f32[8,3072]{1,0:T(8,128)S(1)}, bf16[16,192,384]{2,1,0:T(8,128)(2,1)S(1)}, bf16[16,192,384]{2,1,0:T(8,128)(2,1)S(1)}) custom-call(s32[4]{0:T(128)S(1)} %copy-done.18, bf16[4,15,16,384]{3,2,1,0:T(8,128)(2,1)} %copy-done.25, bf16[4,15,16,384]{3,2,1,0:T(8,128)(2,1)} %copy-done.26, ...), custom_call_target="tpu_custom_call" | custom-call | flops 1 | bytes 1 | tf_op jit(solution)/shard_map/pallas_call | solution.py:84
  196.2 10.5 %shard_map.131 = (f32[1040,768]{1,0:T(8,128)S(1)}, bf16[1040,768]{1,0:T(8,128)(2,1)S(1)}, bf16[2,16,48,384]{3,2,1,0:T(8,128)(2,1)S(1)}, f32[8,768]{1,0:T(8,128)S(1)}) custom-call(s32[4]{0:T(128)S(1)} %copy-done.18, bf16[4,15,16,384]{3,2,1,0:T(8,128)(2,1)} %copy-done.25, bf16[4,15,16,384]{3,2,1,0:T(8,128)(2,1)} %copy-done.26, ...), custom_call_target="tpu_custom_call" | custom-call | flops 1 | bytes 1 | tf_op jit(solution)/shard_map/pallas_call | solution.py:84
  206.7 3.2 shard_map.133
  211.5 13.2 %shard_map.132 = (bf16[1040,2304]{1,0:T(8,128)(2,1)S(1)}, f32[16,2304]{1,0:T(8,128)S(1)}) custom-call(bf16[1040,2304]{1,0:T(8,128)(2,1)S(1)} %bitcast.32, bf16[1040,768]{1,0:T(8,128)(2,1)S(1)} %get-tuple-element.284.do_ref, bf16[5,12,208,208]{3,2,1,0:T(8,128)(2,1)S(1)} %bitcast.37), custom_call_target="tpu_custom_call" | custom-call | flops 1 | bytes 1 | tf_op jit(solution)/shard_map/pallas_call | solution.py:84
  226.3 4.9 %shard_map.134 = bf16[16,192,384]{2,1,0:T(8,128)(2,1)} custom-call(s32[4]{0:T(128)S(1)} %copy-done.18, bf16[1040,2304]{1,0:T(8,128)(2,1)S(1)} %get-tuple-element.299.dqkv_ref.refs_9_, bf16[1040,768]{1,0:T(8,128)(2,1)S(1)} %copy-done.11, bf16[2,16,48,384]{3,2,1,0:T(8,128)(2,1)S(1)} %get-tuple-element.293.out_ref), custom_call_target="tpu_custom_call" | custom-call | flops 1 | bytes 1 | tf_op jit(solution)/shard_map/pallas_call | solution.py:84
  236.0 2.3 shard_map.135.refs_0_.refs_2_.refs_4_.refs_6_
  238.2 4.9 %shard_map.137.refs_0_.refs_2_.refs_4_.refs_6_.refs_3_.refs_9_ = bf16[16,192,384]{2,1,0:T(8,128)(2,1)} custom-call(s32[4]{0:T(128)S(1)} %copy-done.18, bf16[1040,2304]{1,0:T(8,128)(2,1)S(1)} %get-tuple-element.299.dqkv_ref.refs_9_, bf16[1040,768]{1,0:T(8,128)(2,1)S(1)} %copy-done.11, bf16[2,16,48,384]{3,2,1,0:T(8,128)(2,1)S(1)} %get-tuple-element.293.out_ref), custom_call_target="tpu_custom_call" | custom-call | flops 1 | bytes 1 | tf_op jit(solution)/shard_map/pallas_call | solution.py:84
  243.2 3.4 %collective-permute-done.45.refs_2_ = bf16[4,16,1280]{2,1,0:T(8,128)(2,1)S(1)} collective-permute-done((bf16[4,16,1280]{2,1,0:T(8,128)(2,1)S(1)}, bf16[4,16,1280]{2,1,0:T(8,128)(2,1)S(1)}, u32[]{:S(2)}, u32[]{:S(2)}) %collective-permute-start.45) | collective-permute-done | bytes 163872 | tf_op jit(solution)/shard_map/ppermute | solution.py:1023
  246.6 2.4 shard_map.139
  252.2 2.2 collective-permute-start.49
  256.1 9.8 %shard_map.138 = (f32[5,196,768]{2,1,0:T(8,128)}, f32[16,768]{1,0:T(8,128)S(1)}) custom-call(s32[4]{0:T(128)S(1)} %copy-done.18, bf16[4,10,16,384]{3,2,1,0:T(8,128)(2,1)} %copy-done.34, bf16[4,10,16,384]{3,2,1,0:T(8,128)(2,1)} %copy-done.41, bf16[4,10,16,384]{3,2,1,0:T(8,128)(2,1)} %copy-done.42, bf16[4,10,16,384]{3,2,1,0:T(8,128)(2,1)} %copy-done.43, ...), custom_call_target="tpu_custom_call" | custom-call | flops 1 | bytes 1 | tf_op jit(solution)/shard_map/pallas_call | solution.py:84
  271.5 2.3 collective-permute-start.52
  273.8 2.3 shard_map.142.refs_0_.refs_2_.refs_4_.refs_6_
  284.7 2.6 collective-permute-done.57
  288.2 6.0 %collective-permute-done.58 = f32[16,768]{1,0:T(8,128)S(1)} collective-permute-done((f32[16,768]{1,0:T(8,128)S(1)}, f32[16,768]{1,0:T(8,128)S(1)}, u32[]{:S(2)}, u32[]{:S(2)}) %collective-permute-start.58) | collective-permute-done | bytes 49184 | tf_op jit(solution)/shard_map/ppermute | solution.py:1023
  297.1 2.8 collective-permute-done.63
  299.9 2.4 shard_map.147
  303.5 2.7 collective-permute-start.67
  306.9 2.6 collective-permute-start.69
  310.4 2.4 collective-permute-start.71
  314.5 4.3 %shard_map.146 = (f32[128,3072]{1,0:T(8,128)}, f32[512,768]{1,0:T(8,128)}) custom-call(s32[8]{0:T(128)S(1)} %copy-done.20, s32[8]{0:T(128)S(1)} %copy-done.21, bf16[4,16,1280]{2,1,0:T(8,128)(2,1)S(1)} %constant_dynamic-update-slice_fusion.8.refs_0_, bf16[4,16,1280]{2,1,0:T(8,128)(2,1)S(1)} %collective-permute-done.44.refs_1_, ...), custom_call_target="tpu_custom_call" | custom-call | flops 1 | bytes 1 | tf_op jit(solution)/shard_map/pallas_call | solution.py:84
  318.9 5.0 %collective-permute-done.70.refs_11_ = bf16[8,16,384]{2,1,0:T(8,128)(2,1)S(1)} collective-permute-done((bf16[8,16,384]{2,1,0:T(8,128)(2,1)S(1)}, bf16[8,16,384]{2,1,0:T(8,128)(2,1)S(1)}, u32[]{:S(2)}, u32[]{:S(2)}) %collective-permute-start.70) | collective-permute-done | bytes 98336 | tf_op jit(solution)/shard_map/ppermute | solution.py:1023
  323.9 6.7 %shard_map.148 = (f32[1,8,64,768]{3,2,1,0:T(8,128)}, f32[1,8,64,768]{3,2,1,0:T(8,128)}, f32[1,8,64,768]{3,2,1,0:T(8,128)}) custom-call(s32[8]{0:T(128)S(1)} %copy-done.20, s32[8]{0:T(128)S(1)} %copy-done.21, s32[4]{0:T(128)S(1)} %copy-done.18, f32[1,8,64,768]{3,2,1,0:T(8,128)} %refs_0_.1, f32[1,8,64,768]{3,2,1,0:T(8,128)} %refs_1_.1, ...), custom_call_target="tpu_custom_call" | custom-call | flops 1 | bytes 1 | tf_op jit(solution)/shard_map/pallas_call | solution.py:84
  (283 shorter events, 83.2 us)
Async XLA Ops:
  8.2 17.0 %collective-permute-start.2 = (bf16[8,16,384]{2,1,0:T(8,128)(2,1)S(1)}, bf16[8,16,384]{2,1,0:T(8,128)(2,1)S(1)}, u32[]{:S(2)}, u32[]{:S(2)}) collective-permute-start(bf16[8,16,384]{2,1,0:T(8,128)(2,1)S(1)} %get-tuple-element.197), channel_id=1, source_target_pairs={{0,6},{1,7},{2,4},{3,5},{4,2},{5,3},{6,0},{7,1},{8,14},{9,15},{10,... | collective-permute-start | bytes 294920 | tf_op jit(solution)/shard_map/ppermute | solution.py:1023
  8.2 17.0 %collective-permute-start.3 = (bf16[8,16,384]{2,1,0:T(8,128)(2,1)S(1)}, bf16[8,16,384]{2,1,0:T(8,128)(2,1)S(1)}, u32[]{:S(2)}, u32[]{:S(2)}) collective-permute-start(bf16[8,16,384]{2,1,0:T(8,128)(2,1)S(1)} %get-tuple-element.198), channel_id=1, source_target_pairs={{0,8},{1,9},{2,10},{3,11},{4,12},{5,13},{6,14},{7,15},{8,0},{9,1},... | collective-permute-start | bytes 294920 | tf_op jit(solution)/shard_map/ppermute | solution.py:1023
  11.2 15.2 %collective-permute-start.4 = (bf16[8,16,384]{2,1,0:T(8,128)(2,1)S(1)}, bf16[8,16,384]{2,1,0:T(8,128)(2,1)S(1)}, u32[]{:S(2)}, u32[]{:S(2)}) collective-permute-start(bf16[8,16,384]{2,1,0:T(8,128)(2,1)S(1)} %get-tuple-element.199), channel_id=1, source_target_pairs={{0,10},{1,11},{2,8},{3,9},{4,14},{5,15},{6,12},{7,13},{8,2},{9,3},... | collective-permute-start | bytes 294920 | tf_op jit(solution)/shard_map/ppermute | solution.py:1023
  12.8 13.7 %collective-permute-start.5 = (bf16[8,16,384]{2,1,0:T(8,128)(2,1)S(1)}, bf16[8,16,384]{2,1,0:T(8,128)(2,1)S(1)}, u32[]{:S(2)}, u32[]{:S(2)}) collective-permute-start(bf16[8,16,384]{2,1,0:T(8,128)(2,1)S(1)} %get-tuple-element.200), channel_id=1, source_target_pairs={{0,12},{1,13},{2,14},{3,15},{4,8},{5,9},{6,10},{7,11},{8,4},{9,5},... | collective-permute-start | bytes 294920 | tf_op jit(solution)/shard_map/ppermute | solution.py:1023
  16.4 10.0 %collective-permute-start.6 = (bf16[8,16,384]{2,1,0:T(8,128)(2,1)S(1)}, bf16[8,16,384]{2,1,0:T(8,128)(2,1)S(1)}, u32[]{:S(2)}, u32[]{:S(2)}) collective-permute-start(bf16[8,16,384]{2,1,0:T(8,128)(2,1)S(1)} %get-tuple-element.201), channel_id=1, source_target_pairs={{0,14},{1,15},{2,12},{3,13},{4,10},{5,11},{6,8},{7,9},{8,6},{9,7},... | collective-permute-start | bytes 294920 | tf_op jit(solution)/shard_map/ppermute | solution.py:1023
  34.5 12.4 %collective-permute-start.9 = (bf16[10,16,384]{2,1,0:T(8,128)(2,1)S(1)}, bf16[10,16,384]{2,1,0:T(8,128)(2,1)S(1)}, u32[]{:S(2)}, u32[]{:S(2)}) collective-permute-start(bf16[10,16,384]{2,1,0:T(8,128)(2,1)S(1)} %get-tuple-element.215), channel_id=1, source_target_pairs={{0,8},{1,9},{2,10},{3,11},{4,12},{5,13},{6,14},{7,15},{8,0},{9,1},... | collective-permute-start | bytes 368648 | tf_op jit(solution)/shard_map/ppermute | solution.py:1023
  35.8 11.1 %collective-permute-start.10 = (bf16[10,16,384]{2,1,0:T(8,128)(2,1)S(1)}, bf16[10,16,384]{2,1,0:T(8,128)(2,1)S(1)}, u32[]{:S(2)}, u32[]{:S(2)}) collective-permute-start(bf16[10,16,384]{2,1,0:T(8,128)(2,1)S(1)} %get-tuple-element.215), channel_id=1, source_target_pairs={{0,12},{1,13},{2,14},{3,15},{4,8},{5,9},{6,10},{7,11},{8,4},{9,5},... | collective-permute-start | bytes 368648 | tf_op jit(solution)/shard_map/ppermute | solution.py:1023
  47.0 11.6 %collective-permute-start.11 = (bf16[4,10,16,384]{3,2,1,0:T(8,128)(2,1)S(1)}, bf16[4,10,16,384]{3,2,1,0:T(8,128)(2,1)S(1)}, u32[]{:S(2)}, u32[]{:S(2)}) collective-permute-start(bf16[4,10,16,384]{3,2,1,0:T(8,128)(2,1)S(1)} %pad_maximum_fusion.2.refs_0_), channel_id=1, source_target_pairs={{0,16},{1,3},{2,18},{3,1},{4,20},{5,7},{6,22},{7,5},{8,24},{9,11},... | collective-permute-start | bytes 1474568 | tf_op jit(solution)/shard_map/ppermute | solution.py:1023
  48.5 10.1 %collective-permute-start.12 = (bf16[4,10,16,384]{3,2,1,0:T(8,128)(2,1)S(1)}, bf16[4,10,16,384]{3,2,1,0:T(8,128)(2,1)S(1)}, u32[]{:S(2)}, u32[]{:S(2)}) collective-permute-start(bf16[4,10,16,384]{3,2,1,0:T(8,128)(2,1)S(1)} %pad_maximum_fusion.2.refs_0_), channel_id=1, source_target_pairs={{0,2},{1,17},{2,0},{3,19},{4,6},{5,21},{6,4},{7,23},{8,10},{9,25},... | collective-permute-start | bytes 1474568 | tf_op jit(solution)/shard_map/ppermute | solution.py:1023
  49.0 11.2 %collective-permute-start.13 = (bf16[15,16,384]{2,1,0:T(8,128)(2,1)S(1)}, bf16[15,16,384]{2,1,0:T(8,128)(2,1)S(1)}, u32[]{:S(2)}, u32[]{:S(2)}) collective-permute-start(bf16[15,16,384]{2,1,0:T(8,128)(2,1)S(1)} %get-tuple-element.228), channel_id=1, source_target_pairs={{0,4},{1,5},{2,6},{3,7},{4,0},{5,1},{6,2},{7,3},{8,12},{9,13},{10,... | collective-permute-start | bytes 552968 | tf_op jit(solution)/shard_map/ppermute | solution.py:1023
  51.2 15.6 %collective-permute-start.14 = (bf16[15,16,384]{2,1,0:T(8,128)(2,1)S(1)}, bf16[15,16,384]{2,1,0:T(8,128)(2,1)S(1)}, u32[]{:S(2)}, u32[]{:S(2)}) collective-permute-start(bf16[15,16,384]{2,1,0:T(8,128)(2,1)S(1)} %get-tuple-element.228), channel_id=1, source_target_pairs={{0,8},{1,9},{2,10},{3,11},{4,12},{5,13},{6,14},{7,15},{8,0},{9,1},... | collective-permute-start | bytes 552968 | tf_op jit(solution)/shard_map/ppermute | solution.py:1023
  52.3 14.4 %collective-permute-start.15 = (bf16[15,16,384]{2,1,0:T(8,128)(2,1)S(1)}, bf16[15,16,384]{2,1,0:T(8,128)(2,1)S(1)}, u32[]{:S(2)}, u32[]{:S(2)}) collective-permute-start(bf16[15,16,384]{2,1,0:T(8,128)(2,1)S(1)} %get-tuple-element.228), channel_id=1, source_target_pairs={{0,12},{1,13},{2,14},{3,15},{4,8},{5,9},{6,10},{7,11},{8,4},{9,5},... | collective-permute-start | bytes 552968 | tf_op jit(solution)/shard_map/ppermute | solution.py:1023
  58.6 11.0 %collective-permute-start.16 = (bf16[4,10,16,384]{3,2,1,0:T(8,128)(2,1)S(1)}, bf16[4,10,16,384]{3,2,1,0:T(8,128)(2,1)S(1)}, u32[]{:S(2)}, u32[]{:S(2)}) collective-permute-start(bf16[4,10,16,384]{3,2,1,0:T(8,128)(2,1)S(1)} %collective-permute-done.11.refs_1_), channel_id=1, source_target_pairs={{0,2},{1,17},{2,0},{3,19},{4,6},{5,21},{6,4},{7,23},{8,10},{9,25},... | collective-permute-start | bytes 1474568 | tf_op jit(solution)/shard_map/ppermute | solution.py:1023
  66.9 15.2 %collective-permute-start.21 = (bf16[4,15,16,384]{3,2,1,0:T(8,128)(2,1)S(1)}, bf16[4,15,16,384]{3,2,1,0:T(8,128)(2,1)S(1)}, u32[]{:S(2)}, u32[]{:S(2)}) collective-permute-start(bf16[4,15,16,384]{3,2,1,0:T(8,128)(2,1)S(1)} %pad_maximum_fusion.refs_0_), channel_id=1, source_target_pairs={{0,16},{1,3},{2,18},{3,1},{4,20},{5,7},{6,22},{7,5},{8,24},{9,11},... | collective-permute-start | bytes 2211848 | tf_op jit(solution)/shard_map/ppermute | solution.py:1023
  67.5 14.6 %collective-permute-start.22 = (bf16[4,15,16,384]{3,2,1,0:T(8,128)(2,1)S(1)}, bf16[4,15,16,384]{3,2,1,0:T(8,128)(2,1)S(1)}, u32[]{:S(2)}, u32[]{:S(2)}) collective-permute-start(bf16[4,15,16,384]{3,2,1,0:T(8,128)(2,1)S(1)} %pad_maximum_fusion.refs_0_), channel_id=1, source_target_pairs={{0,1},{1,0},{2,3},{3,2},{4,5},{5,4},{6,7},{7,6},{8,9},{9,8},{10,11... | collective-permute-start | bytes 2211848 | tf_op jit(solution)/shard_map/ppermute | solution.py:1023
  82.1 20.6 %collective-permute-start.23 = (bf16[4,15,16,384]{3,2,1,0:T(8,128)(2,1)S(1)}, bf16[4,15,16,384]{3,2,1,0:T(8,128)(2,1)S(1)}, u32[]{:S(2)}, u32[]{:S(2)}) collective-permute-start(bf16[4,15,16,384]{3,2,1,0:T(8,128)(2,1)S(1)} %pad_maximum_fusion.refs_0_), channel_id=1, source_target_pairs={{0,2},{1,17},{2,0},{3,19},{4,6},{5,21},{6,4},{7,23},{8,10},{9,25},... | collective-permute-start | bytes 2211848 | tf_op jit(solution)/shard_map/ppermute | solution.py:1023
  83.7 19.0 %collective-permute-start.24 = (bf16[4,15,16,384]{3,2,1,0:T(8,128)(2,1)S(1)}, bf16[4,15,16,384]{3,2,1,0:T(8,128)(2,1)S(1)}, u32[]{:S(2)}, u32[]{:S(2)}) collective-permute-start(bf16[4,15,16,384]{3,2,1,0:T(8,128)(2,1)S(1)} %collective-permute-done.21.refs_1_), channel_id=1, source_target_pairs={{0,2},{1,17},{2,0},{3,19},{4,6},{5,21},{6,4},{7,23},{8,10},{9,25},... | collective-permute-start | bytes 2211848 | tf_op jit(solution)/shard_map/ppermute | solution.py:1023
  84.2 14.0 %collective-permute-start.25 = (bf16[15,16,384]{2,1,0:T(8,128)(2,1)S(1)}, bf16[15,16,384]{2,1,0:T(8,128)(2,1)S(1)}, u32[]{:S(2)}, u32[]{:S(2)}) collective-permute-start(bf16[15,16,384]{2,1,0:T(8,128)(2,1)S(1)} %get-tuple-element.246), channel_id=1, source_target_pairs={{0,4},{1,5},{2,6},{3,7},{4,0},{5,1},{6,2},{7,3},{8,12},{9,13},{10,... | collective-permute-start | bytes 552968 | tf_op jit(solution)/shard_map/ppermute | solution.py:1023
  86.3 16.4 %collective-permute-start.26 = (bf16[15,16,384]{2,1,0:T(8,128)(2,1)S(1)}, bf16[15,16,384]{2,1,0:T(8,128)(2,1)S(1)}, u32[]{:S(2)}, u32[]{:S(2)}) collective-permute-start(bf16[15,16,384]{2,1,0:T(8,128)(2,1)S(1)} %get-tuple-element.246), channel_id=1, source_target_pairs={{0,8},{1,9},{2,10},{3,11},{4,12},{5,13},{6,14},{7,15},{8,0},{9,1},... | collective-permute-start | bytes 552968 | tf_op jit(solution)/shard_map/ppermute | solution.py:1023
  87.7 15.0 %collective-permute-start.27 = (bf16[15,16,384]{2,1,0:T(8,128)(2,1)S(1)}, bf16[15,16,384]{2,1,0:T(8,128)(2,1)S(1)}, u32[]{:S(2)}, u32[]{:S(2)}) collective-permute-start(bf16[15,16,384]{2,1,0:T(8,128)(2,1)S(1)} %get-tuple-element.246), channel_id=1, source_target_pairs={{0,12},{1,13},{2,14},{3,15},{4,8},{5,9},{6,10},{7,11},{8,4},{9,5},... | collective-permute-start | bytes 552968 | tf_op jit(solution)/shard_map/ppermute | solution.py:1023
  103.4 11.5 %collective-permute-start.31 = (bf16[4,15,16,384]{3,2,1,0:T(8,128)(2,1)S(1)}, bf16[4,15,16,384]{3,2,1,0:T(8,128)(2,1)S(1)}, u32[]{:S(2)}, u32[]{:S(2)}) collective-permute-start(bf16[4,15,16,384]{3,2,1,0:T(8,128)(2,1)S(1)} %pad_maximum_fusion.1.refs_0_), channel_id=1, source_target_pairs={{0,16},{1,3},{2,18},{3,1},{4,20},{5,7},{6,22},{7,5},{8,24},{9,11},... | collective-permute-start | bytes 2211848 | tf_op jit(solution)/shard_map/ppermute | solution.py:1023
  115.0 15.9 %collective-permute-start.32 = (bf16[4,15,16,384]{3,2,1,0:T(8,128)(2,1)S(1)}, bf16[4,15,16,384]{3,2,1,0:T(8,128)(2,1)S(1)}, u32[]{:S(2)}, u32[]{:S(2)}) collective-permute-start(bf16[4,15,16,384]{3,2,1,0:T(8,128)(2,1)S(1)} %pad_maximum_fusion.1.refs_0_), channel_id=1, source_target_pairs={{0,2},{1,17},{2,0},{3,19},{4,6},{5,21},{6,4},{7,23},{8,10},{9,25},... | collective-permute-start | bytes 2211848 | tf_op jit(solution)/shard_map/ppermute | solution.py:1023
  116.5 17.9 %collective-permute-start.33 = (bf16[4,15,16,384]{3,2,1,0:T(8,128)(2,1)S(1)}, bf16[4,15,16,384]{3,2,1,0:T(8,128)(2,1)S(1)}, u32[]{:S(2)}, u32[]{:S(2)}) collective-permute-start(bf16[4,15,16,384]{3,2,1,0:T(8,128)(2,1)S(1)} %collective-permute-done.31.refs_1_), channel_id=1, source_target_pairs={{0,2},{1,17},{2,0},{3,19},{4,6},{5,21},{6,4},{7,23},{8,10},{9,25},... | collective-permute-start | bytes 2211848 | tf_op jit(solution)/shard_map/ppermute | solution.py:1023
  117.0 17.3 %collective-permute-start.34 = (bf16[4,15,16,384]{3,2,1,0:T(8,128)(2,1)S(1)}, bf16[4,15,16,384]{3,2,1,0:T(8,128)(2,1)S(1)}, u32[]{:S(2)}, u32[]{:S(2)}) collective-permute-start(bf16[4,15,16,384]{3,2,1,0:T(8,128)(2,1)S(1)} %pad_maximum_fusion.1.refs_0_), channel_id=1, source_target_pairs={{0,1},{1,0},{2,3},{3,2},{4,5},{5,4},{6,7},{7,6},{8,9},{9,8},{10,11... | collective-permute-start | bytes 2211848 | tf_op jit(solution)/shard_map/ppermute | solution.py:1023
  117.0 17.3 %collective-permute-start.35 = (bf16[4,15,16,384]{3,2,1,0:T(8,128)(2,1)S(1)}, bf16[4,15,16,384]{3,2,1,0:T(8,128)(2,1)S(1)}, u32[]{:S(2)}, u32[]{:S(2)}) collective-permute-start(bf16[4,15,16,384]{3,2,1,0:T(8,128)(2,1)S(1)} %collective-permute-done.31.refs_1_), channel_id=1, source_target_pairs={{0,1},{1,0},{2,3},{3,2},{4,5},{5,4},{6,7},{7,6},{8,9},{9,8},{10,11... | collective-permute-start | bytes 2211848 | tf_op jit(solution)/shard_map/ppermute | solution.py:1023
  148.5 19.8 %all-to-all-start = ((bf16[32,5,768]{2,1,0:T(8,128)(2,1)}), bf16[32,5,768]{2,1,0:T(8,128)(2,1)S(1)}, u32[]{:S(2)}, u32[]{:S(2)}) async-start(bf16[32,5,768]{2,1,0:T(8,128)(2,1)} %broadcast_in_dim.95), calls=%async_computation | async-start | bytes 786432 | tf_op jit(solution)/shard_map/all_to_all | solution.py:1437
  173.5 20.9 %collective-permute-start.38 = (bf16[16,1280]{1,0:T(8,128)(2,1)S(1)}, bf16[16,1280]{1,0:T(8,128)(2,1)S(1)}, u32[]{:S(2)}, u32[]{:S(2)}) collective-permute-start(bf16[16,1280]{1,0:T(8,128)(2,1)S(1)} %fusion.6), channel_id=1, source_target_pairs={{0,4},{1,5},{2,6},{3,7},{4,0},{5,1},{6,2},{7,3},{8,12},{9,13},{10,... | collective-permute-start | bytes 122888 | tf_op jit(solution)/shard_map/ppermute | solution.py:1023
  194.4 12.3 %collective-permute-start.39 = (bf16[16,192,384]{2,1,0:T(8,128)(2,1)S(1)}, bf16[16,192,384]{2,1,0:T(8,128)(2,1)S(1)}, u32[]{:S(2)}, u32[]{:S(2)}) collective-permute-start(bf16[16,192,384]{2,1,0:T(8,128)(2,1)S(1)} %get-tuple-element.281), channel_id=1, source_target_pairs={{0,1},{1,0},{2,3},{3,2},{4,5},{5,4},{6,7},{7,6},{8,9},{9,8},{10,11... | collective-permute-start | bytes 7077896 | tf_op jit(solution)/shard_map/ppermute | solution.py:1023
  194.5 12.2 %collective-permute-start.40 = (bf16[2,16,1280]{2,1,0:T(8,128)(2,1)S(1)}, bf16[2,16,1280]{2,1,0:T(8,128)(2,1)S(1)}, u32[]{:S(2)}, u32[]{:S(2)}) collective-permute-start(bf16[2,16,1280]{2,1,0:T(8,128)(2,1)S(1)} %pad_maximum_fusion.3), channel_id=1, source_target_pairs={{0,8},{1,9},{2,10},{3,11},{4,12},{5,13},{6,14},{7,15},{8,0},{9,1},... | collective-permute-start | bytes 245768 | tf_op jit(solution)/shard_map/ppermute | solution.py:1023
  210.0 16.3 %collective-permute-start.41 = (bf16[8,192,384]{2,1,0:T(8,128)(2,1)S(1)}, bf16[8,192,384]{2,1,0:T(8,128)(2,1)S(1)}, u32[]{:S(2)}, u32[]{:S(2)}) collective-permute-start(bf16[8,192,384]{2,1,0:T(8,128)(2,1)S(1)} %shard_map.133), channel_id=1, source_target_pairs={{0,16},{1,3},{2,18},{3,1},{4,20},{5,7},{6,22},{7,5},{8,24},{9,11},... | collective-permute-start | bytes 3538952 | tf_op jit(solution)/shard_map/ppermute | solution.py:1023
  231.1 15.5 %collective-permute-start.43 = (bf16[16,192,384]{2,1,0:T(8,128)(2,1)}, bf16[16,192,384]{2,1,0:T(8,128)(2,1)S(1)}, u32[]{:S(2)}, u32[]{:S(2)}) collective-permute-start(bf16[16,192,384]{2,1,0:T(8,128)(2,1)} %shard_map.134), channel_id=1, source_target_pairs={{0,1},{1,0},{2,3},{3,2},{4,5},{5,4},{6,7},{7,6},{8,9},{9,8},{10,11... | collective-permute-start | bytes 7077896 | tf_op jit(solution)/shard_map/ppermute | solution.py:1023
  233.2 13.4 %collective-permute-start.42 = (bf16[4,192,384]{2,1,0:T(8,128)(2,1)S(1)}, bf16[4,192,384]{2,1,0:T(8,128)(2,1)S(1)}, u32[]{:S(2)}, u32[]{:S(2)}) collective-permute-start(bf16[4,192,384]{2,1,0:T(8,128)(2,1)S(1)} %shard_map.136), channel_id=1, source_target_pairs={{0,2},{1,17},{2,0},{3,19},{4,6},{5,21},{6,4},{7,23},{8,10},{9,25},... | collective-permute-start | bytes 1769480 | tf_op jit(solution)/shard_map/ppermute | solution.py:1023
  235.2 11.4 %collective-permute-start.45 = (bf16[4,16,1280]{2,1,0:T(8,128)(2,1)S(1)}, bf16[4,16,1280]{2,1,0:T(8,128)(2,1)S(1)}, u32[]{:S(2)}, u32[]{:S(2)}) collective-permute-start(bf16[4,16,1280]{2,1,0:T(8,128)(2,1)S(1)} %constant_dynamic-update-slice_fusion.8.refs_0_), channel_id=1, source_target_pairs={{0,2},{1,17},{2,0},{3,19},{4,6},{5,21},{6,4},{7,23},{8,10},{9,25},... | collective-permute-start | bytes 491528 | tf_op jit(solution)/shard_map/ppermute | solution.py:1023
  249.0 17.1 %collective-permute-start.46 = (bf16[8,192,384]{2,1,0:T(8,128)(2,1)S(1)}, bf16[8,192,384]{2,1,0:T(8,128)(2,1)S(1)}, u32[]{:S(2)}, u32[]{:S(2)}) collective-permute-start(bf16[8,192,384]{2,1,0:T(8,128)(2,1)S(1)} %shard_map.139), channel_id=1, source_target_pairs={{0,16},{1,3},{2,18},{3,1},{4,20},{5,7},{6,22},{7,5},{8,24},{9,11},... | collective-permute-start | bytes 3538952 | tf_op jit(solution)/shard_map/ppermute | solution.py:1023
  249.7 16.2 %collective-permute-start.47 = (bf16[4,16,1280]{2,1,0:T(8,128)(2,1)S(1)}, bf16[4,16,1280]{2,1,0:T(8,128)(2,1)S(1)}, u32[]{:S(2)}, u32[]{:S(2)}) collective-permute-start(bf16[4,16,1280]{2,1,0:T(8,128)(2,1)S(1)} %collective-permute-done.44.refs_1_), channel_id=1, source_target_pairs={{0,2},{1,17},{2,0},{3,19},{4,6},{5,21},{6,4},{7,23},{8,10},{9,25},... | collective-permute-start | bytes 491528 | tf_op jit(solution)/shard_map/ppermute | solution.py:1023
  251.6 14.3 %collective-permute-start.48 = (bf16[192,384]{1,0:T(8,128)(2,1)S(1)}, bf16[192,384]{1,0:T(8,128)(2,1)S(1)}, u32[]{:S(2)}, u32[]{:S(2)}) collective-permute-start(bf16[192,384]{1,0:T(8,128)(2,1)S(1)} %get-tuple-element.315), channel_id=1, source_target_pairs={{0,4},{1,5},{2,6},{3,7},{4,0},{5,1},{6,2},{7,3},{8,12},{9,13},{10,... | collective-permute-start | bytes 442376 | tf_op jit(solution)/shard_map/ppermute | solution.py:1023
  252.2 13.7 %collective-permute-start.49 = (bf16[192,384]{1,0:T(8,128)(2,1)S(1)}, bf16[192,384]{1,0:T(8,128)(2,1)S(1)}, u32[]{:S(2)}, u32[]{:S(2)}) collective-permute-start(bf16[192,384]{1,0:T(8,128)(2,1)S(1)} %get-tuple-element.316), channel_id=1, source_target_pairs={{0,8},{1,9},{2,10},{3,11},{4,12},{5,13},{6,14},{7,15},{8,0},{9,1},... | collective-permute-start | bytes 442376 | tf_op jit(solution)/shard_map/ppermute | solution.py:1023
  254.4 11.6 %collective-permute-start.50 = (bf16[192,384]{1,0:T(8,128)(2,1)S(1)}, bf16[192,384]{1,0:T(8,128)(2,1)S(1)}, u32[]{:S(2)}, u32[]{:S(2)}) collective-permute-start(bf16[192,384]{1,0:T(8,128)(2,1)S(1)} %get-tuple-element.317), channel_id=1, source_target_pairs={{0,12},{1,13},{2,14},{3,15},{4,8},{5,9},{6,10},{7,11},{8,4},{9,5},... | collective-permute-start | bytes 442376 | tf_op jit(solution)/shard_map/ppermute | solution.py:1023
  268.2 9.9 %collective-permute-start.53 = (bf16[4,192,384]{2,1,0:T(8,128)(2,1)S(1)}, bf16[4,192,384]{2,1,0:T(8,128)(2,1)S(1)}, u32[]{:S(2)}, u32[]{:S(2)}) collective-permute-start(bf16[4,192,384]{2,1,0:T(8,128)(2,1)S(1)} %shard_map.143), channel_id=1, source_target_pairs={{0,2},{1,17},{2,0},{3,19},{4,6},{5,21},{6,4},{7,23},{8,10},{9,25},... | collective-permute-start | bytes 1769480 | tf_op jit(solution)/shard_map/ppermute | solution.py:1023
  278.2 16.0 %collective-permute-start.56 = (bf16[192,384]{1,0:T(8,128)(2,1)S(1)}, bf16[192,384]{1,0:T(8,128)(2,1)S(1)}, u32[]{:S(2)}, u32[]{:S(2)}) collective-permute-start(bf16[192,384]{1,0:T(8,128)(2,1)S(1)} %bitcast.38), channel_id=1, source_target_pairs={{0,1},{1,0},{2,3},{3,2},{4,5},{5,4},{6,7},{7,6},{8,9},{9,8},{10,11... | collective-permute-start | bytes 442376 | tf_op jit(solution)/shard_map/ppermute | solution.py:1023
  278.8 15.4 %collective-permute-start.59 = (bf16[192,384]{1,0:T(8,128)(2,1)S(1)}, bf16[192,384]{1,0:T(8,128)(2,1)S(1)}, u32[]{:S(2)}, u32[]{:S(2)}) collective-permute-start(bf16[192,384]{1,0:T(8,128)(2,1)S(1)} %get-tuple-element.337), channel_id=1, source_target_pairs={{0,4},{1,5},{2,6},{3,7},{4,0},{5,1},{6,2},{7,3},{8,12},{9,13},{10,... | collective-permute-start | bytes 442376 | tf_op jit(solution)/shard_map/ppermute | solution.py:1023
  280.5 14.0 %collective-permute-start.60 = (bf16[192,384]{1,0:T(8,128)(2,1)S(1)}, bf16[192,384]{1,0:T(8,128)(2,1)S(1)}, u32[]{:S(2)}, u32[]{:S(2)}) collective-permute-start(bf16[192,384]{1,0:T(8,128)(2,1)S(1)} %get-tuple-element.338), channel_id=1, source_target_pairs={{0,8},{1,9},{2,10},{3,11},{4,12},{5,13},{6,14},{7,15},{8,0},{9,1},... | collective-permute-start | bytes 442376 | tf_op jit(solution)/shard_map/ppermute | solution.py:1023
  282.3 12.2 %collective-permute-start.61 = (bf16[192,384]{1,0:T(8,128)(2,1)S(1)}, bf16[192,384]{1,0:T(8,128)(2,1)S(1)}, u32[]{:S(2)}, u32[]{:S(2)}) collective-permute-start(bf16[192,384]{1,0:T(8,128)(2,1)S(1)} %get-tuple-element.339), channel_id=1, source_target_pairs={{0,12},{1,13},{2,14},{3,15},{4,8},{5,9},{6,10},{7,11},{8,4},{9,5},... | collective-permute-start | bytes 442376 | tf_op jit(solution)/shard_map/ppermute | solution.py:1023
  306.2 12.6 %collective-permute-start.68 = (bf16[8,16,384]{2,1,0:T(8,128)(2,1)S(1)}, bf16[8,16,384]{2,1,0:T(8,128)(2,1)S(1)}, u32[]{:S(2)}, u32[]{:S(2)}) collective-permute-start(bf16[8,16,384]{2,1,0:T(8,128)(2,1)S(1)} %get-tuple-element.364), channel_id=1, source_target_pairs={{0,6},{1,7},{2,4},{3,5},{4,2},{5,3},{6,0},{7,1},{8,14},{9,15},{10,... | collective-permute-start | bytes 294920 | tf_op jit(solution)/shard_map/ppermute | solution.py:1023
  306.9 12.0 %collective-permute-start.69 = (bf16[8,16,384]{2,1,0:T(8,128)(2,1)S(1)}, bf16[8,16,384]{2,1,0:T(8,128)(2,1)S(1)}, u32[]{:S(2)}, u32[]{:S(2)}) collective-permute-start(bf16[8,16,384]{2,1,0:T(8,128)(2,1)S(1)} %get-tuple-element.365), channel_id=1, source_target_pairs={{0,8},{1,9},{2,10},{3,11},{4,12},{5,13},{6,14},{7,15},{8,0},{9,1},... | collective-permute-start | bytes 294920 | tf_op jit(solution)/shard_map/ppermute | solution.py:1023
  309.4 14.5 %collective-permute-start.70 = (bf16[8,16,384]{2,1,0:T(8,128)(2,1)S(1)}, bf16[8,16,384]{2,1,0:T(8,128)(2,1)S(1)}, u32[]{:S(2)}, u32[]{:S(2)}) collective-permute-start(bf16[8,16,384]{2,1,0:T(8,128)(2,1)S(1)} %get-tuple-element.366), channel_id=1, source_target_pairs={{0,10},{1,11},{2,8},{3,9},{4,14},{5,15},{6,12},{7,13},{8,2},{9,3},... | collective-permute-start | bytes 294920 | tf_op jit(solution)/shard_map/ppermute | solution.py:1023
  310.4 13.5 %collective-permute-start.71 = (bf16[8,16,384]{2,1,0:T(8,128)(2,1)S(1)}, bf16[8,16,384]{2,1,0:T(8,128)(2,1)S(1)}, u32[]{:S(2)}, u32[]{:S(2)}) collective-permute-start(bf16[8,16,384]{2,1,0:T(8,128)(2,1)S(1)} %get-tuple-element.367), channel_id=1, source_target_pairs={{0,12},{1,13},{2,14},{3,15},{4,8},{5,9},{6,10},{7,11},{8,4},{9,5},... | collective-permute-start | bytes 294920 | tf_op jit(solution)/shard_map/ppermute | solution.py:1023
  312.8 11.2 %collective-permute-start.72 = (bf16[8,16,384]{2,1,0:T(8,128)(2,1)S(1)}, bf16[8,16,384]{2,1,0:T(8,128)(2,1)S(1)}, u32[]{:S(2)}, u32[]{:S(2)}) collective-permute-start(bf16[8,16,384]{2,1,0:T(8,128)(2,1)S(1)} %get-tuple-element.368), channel_id=1, source_target_pairs={{0,14},{1,15},{2,12},{3,13},{4,10},{5,11},{6,8},{7,9},{8,6},{9,7},... | collective-permute-start | bytes 294920 | tf_op jit(solution)/shard_map/ppermute | solution.py:1023
  (80 other events, 731.5 us)

commit v5 on v4

--- a/solution.py
+++ b/solution.py
@@ -1383,20 +1383,20 @@
         two = Spread(block_two)
         one.ring, one.one, one.two = meet(one.ring, one.one, one.two)
         one.cross_two()
-        one.send_near(0, 1)
-        one.two, *two.parts = meet(one.two, *two.parts)
-        one.send_near(2)
+        one.ring, one.one, one.two, *two.parts = meet(one.ring, one.one, one.two, *two.parts)
+        one.send_near(0, 1, 2)
         one.both, block_three = meet(one.both, block_three)
         one.finish()
         two.cross_one()
-        two.send_near(0)
+        two.two = send(two.ring, CROSS_TWO)
+        three = Spread(block_three)
         w_qkv = Weight(one.arrays(), QKV_TILES)
         a, qkv, vec = qkv_forward(images, x, jnp.zeros((16, D), f32), w_qkv, me)
-        qkv, two.ring, two.one, two.near[0], block_three = meet(qkv, two.ring, two.one, two.near[0], block_three)
+        qkv, two.ring, two.one, two.two, *three.parts = meet(qkv, two.ring, two.one, two.two, *three.parts)
         two.cross_two()
-        three = Spread(block_three)
+        two.send_near(0, 1, 2)
         o, lse = attention_forward(images, qkv, mask_row)
-        o, two.two, two.both, *three.parts = meet(o, two.two, two.both, *three.parts)
+        o, two.both, *two.near = meet(o, two.both, *two.near)
         two.finish()
         three.cross_one()
         w_out = Weight(two.arrays(), OUT_TILES)

time: 336 us -> 334 us (level)
  transfers between devices with their start and end apart: 74 -> 74, of which waited for: 28 -> 26; matrix products, arithmetic and copies ran while one was open for 1% -> 1% of each run, Pallas kernels for 37% -> 37%
where the time goes in v5:
time: 334 us; the launch traced here: 329 us
  Pallas kernels  162 us (49%)
  starting transfers between devices  85.9 us (26%)
  waiting for transfers between devices  68.1 us (20%)
  local copies, waits for them, and re-layouts  10.4 us (3%)
    pallas_call x29, Pallas kernels, call(): pl.pallas_call(kernel, out_shape=tuple(outs), grid_spec=pltpu.PrefetchSca...  154 us
    ppermute x73, starting transfers between devices, send(): return lax.ppermute(value, AXES, permutation)  79.4 us
    ppermute x73, waiting for transfers between devices, send(): return lax.ppermute(value, AXES, permutation)  65.1 us
    unnamed x116, local copies, waits for them, and re-layouts  7.66 us
    pallas_call x1, Pallas kernels, plan(): pl.pallas_call(plan_kernel, out_shape=tuple((sds((size,), jnp.int32) for...  7.15 us
  transfers between devices with their start and end apart: 74, of which 26 were waited for; matrix products, arithmetic and copies ran while one was open for 1% of the time, Pallas kernels for 37%

profile of v5, /device:TPU:0, one launch (start us, length us, event | category | flops | bytes accessed | tf_op | source)
XLA Modules:
  0.0 328.6 jit_solution(18283443422114081935)
XLA Ops:
  3.6 3.0 collective-permute-start
  8.2 3.0 collective-permute-start.3
  12.7 3.7 %collective-permute-start.5 = (bf16[8,16,384]{2,1,0:T(8,128)(2,1)S(1)}, bf16[8,16,384]{2,1,0:T(8,128)(2,1)S(1)}, u32[]{:S(2)}, u32[]{:S(2)}) collective-permute-start(bf16[8,16,384]{2,1,0:T(8,128)(2,1)S(1)} %get-tuple-element.203), channel_id=1, source_target_pairs={{0,12},{1,13},{2,14},{3,15},{4,8},{5,9},{6,10},{7,11},{8,4},{9,5},... | collective-permute-start | bytes 294920 | tf_op jit(solution)/shard_map/ppermute | solution.py:1023
  16.5 7.2 %shard_map.120 = (s32[39]{0:T(128)}, s32[64]{0:T(128)}, s32[8]{0:T(128)}, s32[8]{0:T(128)}) custom-call(s32[77]{0:T(128)} %owner_ref.3, s32[4]{0:T(128)} %copy-done.17), custom_call_target="tpu_custom_call" | custom-call | tf_op jit(solution)/shard_map/pallas_call | solution.py:1205
  27.1 2.3 collective-permute-done.7.theirs_ref
  30.5 4.0 %collective-permute-start.8 = (bf16[10,16,384]{2,1,0:T(8,128)(2,1)S(1)}, bf16[10,16,384]{2,1,0:T(8,128)(2,1)S(1)}, u32[]{:S(2)}, u32[]{:S(2)}) collective-permute-start(bf16[10,16,384]{2,1,0:T(8,128)(2,1)S(1)} %get-tuple-element.218), channel_id=1, source_target_pairs={{0,4},{1,5},{2,6},{3,7},{4,0},{5,1},{6,2},{7,3},{8,12},{9,13},{10,... | collective-permute-start | bytes 368648 | tf_op jit(solution)/shard_map/ppermute | solution.py:1023
  37.1 2.7 collective-permute-done.8
  39.8 7.0 %collective-permute-done.9 = bf16[10,16,384]{2,1,0:T(8,128)(2,1)S(1)} collective-permute-done((bf16[10,16,384]{2,1,0:T(8,128)(2,1)S(1)}, bf16[10,16,384]{2,1,0:T(8,128)(2,1)S(1)}, u32[]{:S(2)}, u32[]{:S(2)}) %collective-permute-start.9) | collective-permute-done | bytes 122912 | tf_op jit(solution)/shard_map/ppermute | solution.py:1023
  53.8 4.9 %collective-permute-done.11.refs_1_ = bf16[4,10,16,384]{3,2,1,0:T(8,128)(2,1)S(1)} collective-permute-done((bf16[4,10,16,384]{3,2,1,0:T(8,128)(2,1)S(1)}, bf16[4,10,16,384]{3,2,1,0:T(8,128)(2,1)S(1)}, u32[]{:S(2)}, u32[]{:S(2)}) %collective-permute-start.11) | collective-permute-done | bytes 491552 | tf_op jit(solution)/shard_map/ppermute | solution.py:1023
  60.2 6.5 %collective-permute-done.14 = bf16[15,16,384]{2,1,0:T(8,128)(2,1)S(1)} collective-permute-done((bf16[15,16,384]{2,1,0:T(8,128)(2,1)S(1)}, bf16[15,16,384]{2,1,0:T(8,128)(2,1)S(1)}, u32[]{:S(2)}, u32[]{:S(2)}) %collective-permute-start.14) | collective-permute-done | bytes 184352 | tf_op jit(solution)/shard_map/ppermute | solution.py:1023
  70.8 2.5 collective-permute-start.23
  76.5 9.1 %shard_map.122 = (bf16[1040,768]{1,0:T(8,128)(2,1)}, bf16[1040,2304]{1,0:T(8,128)(2,1)S(1)}, f32[16,768]{1,0:T(8,128)S(1)}) custom-call(s32[4]{0:T(128)S(1)} %copy-done.18, bf16[4,10,16,384]{3,2,1,0:T(8,128)(2,1)} %copy-done.34, bf16[4,10,16,384]{3,2,1,0:T(8,128)(2,1)} %copy-done.41, bf16[4,10,16,384]{3,2,1,0:T(8,128)(2,1)} %copy-done.42, ...), custom_call_target="tpu_custom_call" | custom-call | flops 1 | bytes 1 | tf_op jit(solution)/shard_map/pallas_call | solution.py:84
  85.6 4.1 %collective-permute-done.24 = bf16[15,16,384]{2,1,0:T(8,128)(2,1)S(1)} collective-permute-done((bf16[15,16,384]{2,1,0:T(8,128)(2,1)S(1)}, bf16[15,16,384]{2,1,0:T(8,128)(2,1)S(1)}, u32[]{:S(2)}, u32[]{:S(2)}) %collective-permute-start.24) | collective-permute-done | bytes 184352 | tf_op jit(solution)/shard_map/ppermute | solution.py:1023
  90.8 9.0 %shard_map.123 = (bf16[1040,768]{1,0:T(8,128)(2,1)S(1)}, f32[5,16,208]{2,1,0:T(8,128)S(1)}) custom-call(bf16[1040,2304]{1,0:T(8,128)(2,1)S(1)} %get-tuple-element.241.qkv_ref, f32[5,1,208]{2,1,0:T(1,128)S(1)} %broadcast_in_dim.84.mask_ref), custom_call_target="tpu_custom_call" | custom-call | flops 1 | bytes 1 | tf_op jit(solution)/shard_map/pallas_call | solution.py:84
  104.4 6.2 %shard_map.124 = (f32[1040,768]{1,0:T(8,128)S(1)}, bf16[1040,768]{1,0:T(8,128)(2,1)S(1)}) custom-call(s32[4]{0:T(128)S(1)} %copy-done.18, bf16[4,15,16,384]{3,2,1,0:T(8,128)(2,1)} %copy-done.25, bf16[4,15,16,384]{3,2,1,0:T(8,128)(2,1)} %copy-done.26, bf16[4,15,16,384]{3,2,1,0:T(8,128)(2,1)} %copy-done.27, bf16[4,15,16,384]{3,2,1,0:T(8,128)(2,1)} %copy-done.28, ...), custom_call_target="tpu_custom_call" | custom-call | flops 1 | bytes 1 | tf_op jit(solution)/shard_map/pallas_call | solution.py:84
  110.6 2.4 collective-permute-done.31.refs_1_
  115.6 13.3 %shard_map.125 = (bf16[1040,3072]{1,0:T(8,128)(2,1)S(1)}, bf16[1040,3072]{1,0:T(8,128)(2,1)}) custom-call(s32[4]{0:T(128)S(1)} %copy-done.18, bf16[4,15,16,384]{3,2,1,0:T(8,128)(2,1)} %copy-done.25, bf16[4,15,16,384]{3,2,1,0:T(8,128)(2,1)} %copy-done.26, bf16[4,15,16,384]{3,2,1,0:T(8,128)(2,1)} %copy-done.27, bf16[4,15,16,384]{3,2,1,0:T(8,128)(2,1)} %copy-done.28, ...), custom_call_target="tpu_custom_call" | custom-call | flops 1 | bytes 1 | tf_op jit(solution)/shard_map/pallas_call | solution.py:84
  128.9 3.5 %collective-permute-done.33.refs_3_ = bf16[4,15,16,384]{3,2,1,0:T(8,128)(2,1)S(1)} collective-permute-done((bf16[4,15,16,384]{3,2,1,0:T(8,128)(2,1)S(1)}, bf16[4,15,16,384]{3,2,1,0:T(8,128)(2,1)S(1)}, u32[]{:S(2)}, u32[]{:S(2)}) %collective-permute-start.33) | collective-permute-done | bytes 737312 | tf_op jit(solution)/shard_map/ppermute | solution.py:1023
  135.8 10.0 %shard_map.126 = (bf16[5,196,768]{2,1,0:T(8,128)(2,1)}, bf16[16,768]{1,0:T(8,128)(2,1)S(1)}) custom-call(s32[4]{0:T(128)S(1)} %copy-done.18, bf16[4,15,16,384]{3,2,1,0:T(8,128)(2,1)} %copy-done.33, bf16[4,15,16,384]{3,2,1,0:T(8,128)(2,1)} %copy-done.35, bf16[4,15,16,384]{3,2,1,0:T(8,128)(2,1)} %copy-done.36, bf16[4,15,16,384]{3,2,1,0:T(8,128)(2,1)} %copy-done.37, ...), custom_call_target="tpu_custom_call" | custom-call | flops 1 | bytes 1 | tf_op jit(solution)/shard_map/pallas_call | solution.py:84
  146.6 6.4 %all-to-all-start = ((bf16[32,5,768]{2,1,0:T(8,128)(2,1)}), bf16[32,5,768]{2,1,0:T(8,128)(2,1)S(1)}, u32[]{:S(2)}, u32[]{:S(2)}) async-start(bf16[32,5,768]{2,1,0:T(8,128)(2,1)} %broadcast_in_dim.95), calls=%async_computation | async-start | bytes 786432 | tf_op jit(solution)/shard_map/all_to_all | solution.py:1437
  153.1 2.3 copy-done.6
  155.4 3.2 shard_map.128.p_ref
  158.7 2.7 copy-done.7
  163.2 3.0 all-to-all-done.refs_9_
  166.2 5.1 %shard_map.129 = (bf16[160,512]{1,0:T(8,128)(2,1)S(1)}, bf16[16,768]{1,0:T(8,128)(2,1)S(1)}, f32[16,768]{1,0:T(8,128)S(1)}, f32[16,3072]{1,0:T(8,128)S(1)}, bf16[160,768]{1,0:T(8,128)(2,1)S(1)}) custom-call(s32[4]{0:T(128)S(1)} %copy-done.18, s32[1]{0:T(128)} %bitcast.5.first_ref, bf16[4,15,16,384]{3,2,1,0:T(8,128)(2,1)} %copy-done.33, ...), custom_call_target="tpu_custom_call" | custom-call | flops 1 | bytes 1 | tf_op jit(solution)/shard_map/pallas_call | solution.py:84
  172.3 19.9 %shard_map.130 = (f32[1040,768]{1,0:T(8,128)S(1)}, f32[8,3072]{1,0:T(8,128)S(1)}, bf16[16,192,384]{2,1,0:T(8,128)(2,1)S(1)}, bf16[16,192,384]{2,1,0:T(8,128)(2,1)S(1)}) custom-call(s32[4]{0:T(128)S(1)} %copy-done.18, bf16[4,15,16,384]{3,2,1,0:T(8,128)(2,1)} %copy-done.25, bf16[4,15,16,384]{3,2,1,0:T(8,128)(2,1)} %copy-done.26, ...), custom_call_target="tpu_custom_call" | custom-call | flops 1 | bytes 1 | tf_op jit(solution)/shard_map/pallas_call | solution.py:84
  194.0 10.5 %shard_map.131 = (f32[1040,768]{1,0:T(8,128)S(1)}, bf16[1040,768]{1,0:T(8,128)(2,1)S(1)}, bf16[2,16,48,384]{3,2,1,0:T(8,128)(2,1)S(1)}, f32[8,768]{1,0:T(8,128)S(1)}) custom-call(s32[4]{0:T(128)S(1)} %copy-done.18, bf16[4,15,16,384]{3,2,1,0:T(8,128)(2,1)} %copy-done.25, bf16[4,15,16,384]{3,2,1,0:T(8,128)(2,1)} %copy-done.26, ...), custom_call_target="tpu_custom_call" | custom-call | flops 1 | bytes 1 | tf_op jit(solution)/shard_map/pallas_call | solution.py:84
  204.6 3.2 shard_map.133
  209.3 13.2 %shard_map.132 = (bf16[1040,2304]{1,0:T(8,128)(2,1)S(1)}, f32[16,2304]{1,0:T(8,128)S(1)}) custom-call(bf16[1040,2304]{1,0:T(8,128)(2,1)S(1)} %bitcast.32, bf16[1040,768]{1,0:T(8,128)(2,1)S(1)} %get-tuple-element.290.do_ref, bf16[5,12,208,208]{3,2,1,0:T(8,128)(2,1)S(1)} %bitcast.37), custom_call_target="tpu_custom_call" | custom-call | flops 1 | bytes 1 | tf_op jit(solution)/shard_map/pallas_call | solution.py:84
  224.1 4.9 %shard_map.134 = bf16[16,192,384]{2,1,0:T(8,128)(2,1)} custom-call(s32[4]{0:T(128)S(1)} %copy-done.18, bf16[1040,2304]{1,0:T(8,128)(2,1)S(1)} %get-tuple-element.305.dqkv_ref.refs_9_, bf16[1040,768]{1,0:T(8,128)(2,1)S(1)} %copy-done.11, bf16[2,16,48,384]{3,2,1,0:T(8,128)(2,1)S(1)} %get-tuple-element.299.out_ref), custom_call_target="tpu_custom_call" | custom-call | flops 1 | bytes 1 | tf_op jit(solution)/shard_map/pallas_call | solution.py:84
  233.8 2.3 shard_map.135.refs_0_.refs_2_.refs_4_.refs_6_
  236.1 4.9 %shard_map.137.refs_0_.refs_2_.refs_4_.refs_6_.refs_3_.refs_9_ = bf16[16,192,384]{2,1,0:T(8,128)(2,1)} custom-call(s32[4]{0:T(128)S(1)} %copy-done.18, bf16[1040,2304]{1,0:T(8,128)(2,1)S(1)} %get-tuple-element.305.dqkv_ref.refs_9_, bf16[1040,768]{1,0:T(8,128)(2,1)S(1)} %copy-done.11, bf16[2,16,48,384]{3,2,1,0:T(8,128)(2,1)S(1)} %get-tuple-element.299.out_ref), custom_call_target="tpu_custom_call" | custom-call | flops 1 | bytes 1 | tf_op jit(solution)/shard_map/pallas_call | solution.py:84
  241.0 3.4 %collective-permute-done.45.refs_2_ = bf16[4,16,1280]{2,1,0:T(8,128)(2,1)S(1)} collective-permute-done((bf16[4,16,1280]{2,1,0:T(8,128)(2,1)S(1)}, bf16[4,16,1280]{2,1,0:T(8,128)(2,1)S(1)}, u32[]{:S(2)}, u32[]{:S(2)}) %collective-permute-start.45) | collective-permute-done | bytes 163872 | tf_op jit(solution)/shard_map/ppermute | solution.py:1023
  244.5 2.4 shard_map.139
  250.0 2.2 collective-permute-start.49
  253.9 9.8 %shard_map.138 = (f32[5,196,768]{2,1,0:T(8,128)}, f32[16,768]{1,0:T(8,128)S(1)}) custom-call(s32[4]{0:T(128)S(1)} %copy-done.18, bf16[4,10,16,384]{3,2,1,0:T(8,128)(2,1)} %copy-done.34, bf16[4,10,16,384]{3,2,1,0:T(8,128)(2,1)} %copy-done.41, bf16[4,10,16,384]{3,2,1,0:T(8,128)(2,1)} %copy-done.42, bf16[4,10,16,384]{3,2,1,0:T(8,128)(2,1)} %copy-done.43, ...), custom_call_target="tpu_custom_call" | custom-call | flops 1 | bytes 1 | tf_op jit(solution)/shard_map/pallas_call | solution.py:84
  269.3 2.3 collective-permute-start.52
  271.6 2.3 shard_map.142.refs_0_.refs_2_.refs_4_.refs_6_
  282.6 2.6 collective-permute-done.57
  286.0 6.0 %collective-permute-done.58 = f32[16,768]{1,0:T(8,128)S(1)} collective-permute-done((f32[16,768]{1,0:T(8,128)S(1)}, f32[16,768]{1,0:T(8,128)S(1)}, u32[]{:S(2)}, u32[]{:S(2)}) %collective-permute-start.58) | collective-permute-done | bytes 49184 | tf_op jit(solution)/shard_map/ppermute | solution.py:1023
  294.9 2.8 collective-permute-done.63
  297.7 2.4 shard_map.147
  301.3 2.7 collective-permute-start.67
  304.7 2.6 collective-permute-start.69
  308.2 2.4 collective-permute-start.71
  312.4 4.3 %shard_map.146 = (f32[128,3072]{1,0:T(8,128)}, f32[512,768]{1,0:T(8,128)}) custom-call(s32[8]{0:T(128)S(1)} %copy-done.20, s32[8]{0:T(128)S(1)} %copy-done.21, bf16[4,16,1280]{2,1,0:T(8,128)(2,1)S(1)} %constant_dynamic-update-slice_fusion.8.refs_0_, bf16[4,16,1280]{2,1,0:T(8,128)(2,1)S(1)} %collective-permute-done.44.refs_1_, ...), custom_call_target="tpu_custom_call" | custom-call | flops 1 | bytes 1 | tf_op jit(solution)/shard_map/pallas_call | solution.py:84
  316.7 5.0 %collective-permute-done.70.refs_11_ = bf16[8,16,384]{2,1,0:T(8,128)(2,1)S(1)} collective-permute-done((bf16[8,16,384]{2,1,0:T(8,128)(2,1)S(1)}, bf16[8,16,384]{2,1,0:T(8,128)(2,1)S(1)}, u32[]{:S(2)}, u32[]{:S(2)}) %collective-permute-start.70) | collective-permute-done | bytes 98336 | tf_op jit(solution)/shard_map/ppermute | solution.py:1023
  321.7 6.7 %shard_map.148 = (f32[1,8,64,768]{3,2,1,0:T(8,128)}, f32[1,8,64,768]{3,2,1,0:T(8,128)}, f32[1,8,64,768]{3,2,1,0:T(8,128)}) custom-call(s32[8]{0:T(128)S(1)} %copy-done.20, s32[8]{0:T(128)S(1)} %copy-done.21, s32[4]{0:T(128)S(1)} %copy-done.18, f32[1,8,64,768]{3,2,1,0:T(8,128)} %refs_0_.1, f32[1,8,64,768]{3,2,1,0:T(8,128)} %refs_1_.1, ...), custom_call_target="tpu_custom_call" | custom-call | flops 1 | bytes 1 | tf_op jit(solution)/shard_map/pallas_call | solution.py:84
  (283 shorter events, 80.9 us)
Async XLA Ops:
  8.2 17.0 %collective-permute-start.2 = (bf16[8,16,384]{2,1,0:T(8,128)(2,1)S(1)}, bf16[8,16,384]{2,1,0:T(8,128)(2,1)S(1)}, u32[]{:S(2)}, u32[]{:S(2)}) collective-permute-start(bf16[8,16,384]{2,1,0:T(8,128)(2,1)S(1)} %get-tuple-element.200), channel_id=1, source_target_pairs={{0,6},{1,7},{2,4},{3,5},{4,2},{5,3},{6,0},{7,1},{8,14},{9,15},{10,... | collective-permute-start | bytes 294920 | tf_op jit(solution)/shard_map/ppermute | solution.py:1023
  8.2 17.1 %collective-permute-start.3 = (bf16[8,16,384]{2,1,0:T(8,128)(2,1)S(1)}, bf16[8,16,384]{2,1,0:T(8,128)(2,1)S(1)}, u32[]{:S(2)}, u32[]{:S(2)}) collective-permute-start(bf16[8,16,384]{2,1,0:T(8,128)(2,1)S(1)} %get-tuple-element.201), channel_id=1, source_target_pairs={{0,8},{1,9},{2,10},{3,11},{4,12},{5,13},{6,14},{7,15},{8,0},{9,1},... | collective-permute-start | bytes 294920 | tf_op jit(solution)/shard_map/ppermute | solution.py:1023
  11.2 15.2 %collective-permute-start.4 = (bf16[8,16,384]{2,1,0:T(8,128)(2,1)S(1)}, bf16[8,16,384]{2,1,0:T(8,128)(2,1)S(1)}, u32[]{:S(2)}, u32[]{:S(2)}) collective-permute-start(bf16[8,16,384]{2,1,0:T(8,128)(2,1)S(1)} %get-tuple-element.202), channel_id=1, source_target_pairs={{0,10},{1,11},{2,8},{3,9},{4,14},{5,15},{6,12},{7,13},{8,2},{9,3},... | collective-permute-start | bytes 294920 | tf_op jit(solution)/shard_map/ppermute | solution.py:1023
  12.7 13.7 %collective-permute-start.5 = (bf16[8,16,384]{2,1,0:T(8,128)(2,1)S(1)}, bf16[8,16,384]{2,1,0:T(8,128)(2,1)S(1)}, u32[]{:S(2)}, u32[]{:S(2)}) collective-permute-start(bf16[8,16,384]{2,1,0:T(8,128)(2,1)S(1)} %get-tuple-element.203), channel_id=1, source_target_pairs={{0,12},{1,13},{2,14},{3,15},{4,8},{5,9},{6,10},{7,11},{8,4},{9,5},... | collective-permute-start | bytes 294920 | tf_op jit(solution)/shard_map/ppermute | solution.py:1023
  34.5 12.4 %collective-permute-start.9 = (bf16[10,16,384]{2,1,0:T(8,128)(2,1)S(1)}, bf16[10,16,384]{2,1,0:T(8,128)(2,1)S(1)}, u32[]{:S(2)}, u32[]{:S(2)}) collective-permute-start(bf16[10,16,384]{2,1,0:T(8,128)(2,1)S(1)} %get-tuple-element.218), channel_id=1, source_target_pairs={{0,8},{1,9},{2,10},{3,11},{4,12},{5,13},{6,14},{7,15},{8,0},{9,1},... | collective-permute-start | bytes 368648 | tf_op jit(solution)/shard_map/ppermute | solution.py:1023
  35.8 11.1 %collective-permute-start.10 = (bf16[10,16,384]{2,1,0:T(8,128)(2,1)S(1)}, bf16[10,16,384]{2,1,0:T(8,128)(2,1)S(1)}, u32[]{:S(2)}, u32[]{:S(2)}) collective-permute-start(bf16[10,16,384]{2,1,0:T(8,128)(2,1)S(1)} %get-tuple-element.218), channel_id=1, source_target_pairs={{0,12},{1,13},{2,14},{3,15},{4,8},{5,9},{6,10},{7,11},{8,4},{9,5},... | collective-permute-start | bytes 368648 | tf_op jit(solution)/shard_map/ppermute | solution.py:1023
  46.9 11.7 %collective-permute-start.11 = (bf16[4,10,16,384]{3,2,1,0:T(8,128)(2,1)S(1)}, bf16[4,10,16,384]{3,2,1,0:T(8,128)(2,1)S(1)}, u32[]{:S(2)}, u32[]{:S(2)}) collective-permute-start(bf16[4,10,16,384]{3,2,1,0:T(8,128)(2,1)S(1)} %pad_maximum_fusion.2.refs_0_), channel_id=1, source_target_pairs={{0,16},{1,3},{2,18},{3,1},{4,20},{5,7},{6,22},{7,5},{8,24},{9,11},... | collective-permute-start | bytes 1474568 | tf_op jit(solution)/shard_map/ppermute | solution.py:1023
  48.5 10.2 %collective-permute-start.12 = (bf16[4,10,16,384]{3,2,1,0:T(8,128)(2,1)S(1)}, bf16[4,10,16,384]{3,2,1,0:T(8,128)(2,1)S(1)}, u32[]{:S(2)}, u32[]{:S(2)}) collective-permute-start(bf16[4,10,16,384]{3,2,1,0:T(8,128)(2,1)S(1)} %pad_maximum_fusion.2.refs_0_), channel_id=1, source_target_pairs={{0,2},{1,17},{2,0},{3,19},{4,6},{5,21},{6,4},{7,23},{8,10},{9,25},... | collective-permute-start | bytes 1474568 | tf_op jit(solution)/shard_map/ppermute | solution.py:1023
  49.0 11.2 %collective-permute-start.13 = (bf16[15,16,384]{2,1,0:T(8,128)(2,1)S(1)}, bf16[15,16,384]{2,1,0:T(8,128)(2,1)S(1)}, u32[]{:S(2)}, u32[]{:S(2)}) collective-permute-start(bf16[15,16,384]{2,1,0:T(8,128)(2,1)S(1)} %get-tuple-element.233), channel_id=1, source_target_pairs={{0,4},{1,5},{2,6},{3,7},{4,0},{5,1},{6,2},{7,3},{8,12},{9,13},{10,... | collective-permute-start | bytes 552968 | tf_op jit(solution)/shard_map/ppermute | solution.py:1023
  51.2 15.6 %collective-permute-start.14 = (bf16[15,16,384]{2,1,0:T(8,128)(2,1)S(1)}, bf16[15,16,384]{2,1,0:T(8,128)(2,1)S(1)}, u32[]{:S(2)}, u32[]{:S(2)}) collective-permute-start(bf16[15,16,384]{2,1,0:T(8,128)(2,1)S(1)} %get-tuple-element.233), channel_id=1, source_target_pairs={{0,8},{1,9},{2,10},{3,11},{4,12},{5,13},{6,14},{7,15},{8,0},{9,1},... | collective-permute-start | bytes 552968 | tf_op jit(solution)/shard_map/ppermute | solution.py:1023
  52.3 14.4 %collective-permute-start.15 = (bf16[15,16,384]{2,1,0:T(8,128)(2,1)S(1)}, bf16[15,16,384]{2,1,0:T(8,128)(2,1)S(1)}, u32[]{:S(2)}, u32[]{:S(2)}) collective-permute-start(bf16[15,16,384]{2,1,0:T(8,128)(2,1)S(1)} %get-tuple-element.233), channel_id=1, source_target_pairs={{0,12},{1,13},{2,14},{3,15},{4,8},{5,9},{6,10},{7,11},{8,4},{9,5},... | collective-permute-start | bytes 552968 | tf_op jit(solution)/shard_map/ppermute | solution.py:1023
  58.6 10.3 %collective-permute-start.16 = (bf16[4,10,16,384]{3,2,1,0:T(8,128)(2,1)S(1)}, bf16[4,10,16,384]{3,2,1,0:T(8,128)(2,1)S(1)}, u32[]{:S(2)}, u32[]{:S(2)}) collective-permute-start(bf16[4,10,16,384]{3,2,1,0:T(8,128)(2,1)S(1)} %collective-permute-done.11.refs_1_), channel_id=1, source_target_pairs={{0,2},{1,17},{2,0},{3,19},{4,6},{5,21},{6,4},{7,23},{8,10},{9,25},... | collective-permute-start | bytes 1474568 | tf_op jit(solution)/shard_map/ppermute | solution.py:1023
  66.9 22.8 %collective-permute-start.21 = (bf16[4,15,16,384]{3,2,1,0:T(8,128)(2,1)S(1)}, bf16[4,15,16,384]{3,2,1,0:T(8,128)(2,1)S(1)}, u32[]{:S(2)}, u32[]{:S(2)}) collective-permute-start(bf16[4,15,16,384]{3,2,1,0:T(8,128)(2,1)S(1)} %pad_maximum_fusion.refs_0_), channel_id=1, source_target_pairs={{0,16},{1,3},{2,18},{3,1},{4,20},{5,7},{6,22},{7,5},{8,24},{9,11},... | collective-permute-start | bytes 2211848 | tf_op jit(solution)/shard_map/ppermute | solution.py:1023
  67.5 22.2 %collective-permute-start.22 = (bf16[4,15,16,384]{3,2,1,0:T(8,128)(2,1)S(1)}, bf16[4,15,16,384]{3,2,1,0:T(8,128)(2,1)S(1)}, u32[]{:S(2)}, u32[]{:S(2)}) collective-permute-start(bf16[4,15,16,384]{3,2,1,0:T(8,128)(2,1)S(1)} %pad_maximum_fusion.refs_0_), channel_id=1, source_target_pairs={{0,2},{1,17},{2,0},{3,19},{4,6},{5,21},{6,4},{7,23},{8,10},{9,25},... | collective-permute-start | bytes 2211848 | tf_op jit(solution)/shard_map/ppermute | solution.py:1023
  70.8 14.8 %collective-permute-start.23 = (bf16[15,16,384]{2,1,0:T(8,128)(2,1)S(1)}, bf16[15,16,384]{2,1,0:T(8,128)(2,1)S(1)}, u32[]{:S(2)}, u32[]{:S(2)}) collective-permute-start(bf16[15,16,384]{2,1,0:T(8,128)(2,1)S(1)} %get-tuple-element.252), channel_id=1, source_target_pairs={{0,4},{1,5},{2,6},{3,7},{4,0},{5,1},{6,2},{7,3},{8,12},{9,13},{10,... | collective-permute-start | bytes 552968 | tf_op jit(solution)/shard_map/ppermute | solution.py:1023
  73.3 16.3 %collective-permute-start.24 = (bf16[15,16,384]{2,1,0:T(8,128)(2,1)S(1)}, bf16[15,16,384]{2,1,0:T(8,128)(2,1)S(1)}, u32[]{:S(2)}, u32[]{:S(2)}) collective-permute-start(bf16[15,16,384]{2,1,0:T(8,128)(2,1)S(1)} %get-tuple-element.252), channel_id=1, source_target_pairs={{0,8},{1,9},{2,10},{3,11},{4,12},{5,13},{6,14},{7,15},{8,0},{9,1},... | collective-permute-start | bytes 552968 | tf_op jit(solution)/shard_map/ppermute | solution.py:1023
  75.5 14.2 %collective-permute-start.25 = (bf16[15,16,384]{2,1,0:T(8,128)(2,1)S(1)}, bf16[15,16,384]{2,1,0:T(8,128)(2,1)S(1)}, u32[]{:S(2)}, u32[]{:S(2)}) collective-permute-start(bf16[15,16,384]{2,1,0:T(8,128)(2,1)S(1)} %get-tuple-element.252), channel_id=1, source_target_pairs={{0,12},{1,13},{2,14},{3,15},{4,8},{5,9},{6,10},{7,11},{8,4},{9,5},... | collective-permute-start | bytes 552968 | tf_op jit(solution)/shard_map/ppermute | solution.py:1023
  89.7 11.5 %collective-permute-start.26 = (bf16[4,15,16,384]{3,2,1,0:T(8,128)(2,1)S(1)}, bf16[4,15,16,384]{3,2,1,0:T(8,128)(2,1)S(1)}, u32[]{:S(2)}, u32[]{:S(2)}) collective-permute-start(bf16[4,15,16,384]{3,2,1,0:T(8,128)(2,1)S(1)} %collective-permute-done.21.refs_1_), channel_id=1, source_target_pairs={{0,2},{1,17},{2,0},{3,19},{4,6},{5,21},{6,4},{7,23},{8,10},{9,25},... | collective-permute-start | bytes 2211848 | tf_op jit(solution)/shard_map/ppermute | solution.py:1023
  90.3 10.9 %collective-permute-start.28 = (bf16[4,15,16,384]{3,2,1,0:T(8,128)(2,1)S(1)}, bf16[4,15,16,384]{3,2,1,0:T(8,128)(2,1)S(1)}, u32[]{:S(2)}, u32[]{:S(2)}) collective-permute-start(bf16[4,15,16,384]{3,2,1,0:T(8,128)(2,1)S(1)} %collective-permute-done.21.refs_1_), channel_id=1, source_target_pairs={{0,1},{1,0},{2,3},{3,2},{4,5},{5,4},{6,7},{7,6},{8,9},{9,8},{10,11... | collective-permute-start | bytes 2211848 | tf_op jit(solution)/shard_map/ppermute | solution.py:1023
  90.3 10.9 %collective-permute-start.27 = (bf16[4,15,16,384]{3,2,1,0:T(8,128)(2,1)S(1)}, bf16[4,15,16,384]{3,2,1,0:T(8,128)(2,1)S(1)}, u32[]{:S(2)}, u32[]{:S(2)}) collective-permute-start(bf16[4,15,16,384]{3,2,1,0:T(8,128)(2,1)S(1)} %pad_maximum_fusion.refs_0_), channel_id=1, source_target_pairs={{0,1},{1,0},{2,3},{3,2},{4,5},{5,4},{6,7},{7,6},{8,9},{9,8},{10,11... | collective-permute-start | bytes 2211848 | tf_op jit(solution)/shard_map/ppermute | solution.py:1023
  90.8 10.4 %collective-permute-start.29 = (bf16[4,15,16,384]{3,2,1,0:T(8,128)(2,1)S(1)}, bf16[4,15,16,384]{3,2,1,0:T(8,128)(2,1)S(1)}, u32[]{:S(2)}, u32[]{:S(2)}) collective-permute-start(bf16[4,15,16,384]{3,2,1,0:T(8,128)(2,1)S(1)} %collective-permute-done.22.refs_2_), channel_id=1, source_target_pairs={{0,1},{1,0},{2,3},{3,2},{4,5},{5,4},{6,7},{7,6},{8,9},{9,8},{10,11... | collective-permute-start | bytes 2211848 | tf_op jit(solution)/shard_map/ppermute | solution.py:1023
  101.5 11.5 %collective-permute-start.31 = (bf16[4,15,16,384]{3,2,1,0:T(8,128)(2,1)S(1)}, bf16[4,15,16,384]{3,2,1,0:T(8,128)(2,1)S(1)}, u32[]{:S(2)}, u32[]{:S(2)}) collective-permute-start(bf16[4,15,16,384]{3,2,1,0:T(8,128)(2,1)S(1)} %pad_maximum_fusion.1.refs_0_), channel_id=1, source_target_pairs={{0,16},{1,3},{2,18},{3,1},{4,20},{5,7},{6,22},{7,5},{8,24},{9,11},... | collective-permute-start | bytes 2211848 | tf_op jit(solution)/shard_map/ppermute | solution.py:1023
  113.0 15.9 %collective-permute-start.32 = (bf16[4,15,16,384]{3,2,1,0:T(8,128)(2,1)S(1)}, bf16[4,15,16,384]{3,2,1,0:T(8,128)(2,1)S(1)}, u32[]{:S(2)}, u32[]{:S(2)}) collective-permute-start(bf16[4,15,16,384]{3,2,1,0:T(8,128)(2,1)S(1)} %pad_maximum_fusion.1.refs_0_), channel_id=1, source_target_pairs={{0,2},{1,17},{2,0},{3,19},{4,6},{5,21},{6,4},{7,23},{8,10},{9,25},... | collective-permute-start | bytes 2211848 | tf_op jit(solution)/shard_map/ppermute | solution.py:1023
  113.7 18.7 %collective-permute-start.33 = (bf16[4,15,16,384]{3,2,1,0:T(8,128)(2,1)S(1)}, bf16[4,15,16,384]{3,2,1,0:T(8,128)(2,1)S(1)}, u32[]{:S(2)}, u32[]{:S(2)}) collective-permute-start(bf16[4,15,16,384]{3,2,1,0:T(8,128)(2,1)S(1)} %collective-permute-done.31.refs_1_), channel_id=1, source_target_pairs={{0,2},{1,17},{2,0},{3,19},{4,6},{5,21},{6,4},{7,23},{8,10},{9,25},... | collective-permute-start | bytes 2211848 | tf_op jit(solution)/shard_map/ppermute | solution.py:1023
  115.0 17.3 %collective-permute-start.34 = (bf16[4,15,16,384]{3,2,1,0:T(8,128)(2,1)S(1)}, bf16[4,15,16,384]{3,2,1,0:T(8,128)(2,1)S(1)}, u32[]{:S(2)}, u32[]{:S(2)}) collective-permute-start(bf16[4,15,16,384]{3,2,1,0:T(8,128)(2,1)S(1)} %pad_maximum_fusion.1.refs_0_), channel_id=1, source_target_pairs={{0,1},{1,0},{2,3},{3,2},{4,5},{5,4},{6,7},{7,6},{8,9},{9,8},{10,11... | collective-permute-start | bytes 2211848 | tf_op jit(solution)/shard_map/ppermute | solution.py:1023
  115.1 17.3 %collective-permute-start.35 = (bf16[4,15,16,384]{3,2,1,0:T(8,128)(2,1)S(1)}, bf16[4,15,16,384]{3,2,1,0:T(8,128)(2,1)S(1)}, u32[]{:S(2)}, u32[]{:S(2)}) collective-permute-start(bf16[4,15,16,384]{3,2,1,0:T(8,128)(2,1)S(1)} %collective-permute-done.31.refs_1_), channel_id=1, source_target_pairs={{0,1},{1,0},{2,3},{3,2},{4,5},{5,4},{6,7},{7,6},{8,9},{9,8},{10,11... | collective-permute-start | bytes 2211848 | tf_op jit(solution)/shard_map/ppermute | solution.py:1023
  146.6 19.5 %all-to-all-start = ((bf16[32,5,768]{2,1,0:T(8,128)(2,1)}), bf16[32,5,768]{2,1,0:T(8,128)(2,1)S(1)}, u32[]{:S(2)}, u32[]{:S(2)}) async-start(bf16[32,5,768]{2,1,0:T(8,128)(2,1)} %broadcast_in_dim.95), calls=%async_computation | async-start | bytes 786432 | tf_op jit(solution)/shard_map/all_to_all | solution.py:1437
  171.3 20.9 %collective-permute-start.38 = (bf16[16,1280]{1,0:T(8,128)(2,1)S(1)}, bf16[16,1280]{1,0:T(8,128)(2,1)S(1)}, u32[]{:S(2)}, u32[]{:S(2)}) collective-permute-start(bf16[16,1280]{1,0:T(8,128)(2,1)S(1)} %fusion.6), channel_id=1, source_target_pairs={{0,4},{1,5},{2,6},{3,7},{4,0},{5,1},{6,2},{7,3},{8,12},{9,13},{10,... | collective-permute-start | bytes 122888 | tf_op jit(solution)/shard_map/ppermute | solution.py:1023
  192.2 12.3 %collective-permute-start.39 = (bf16[16,192,384]{2,1,0:T(8,128)(2,1)S(1)}, bf16[16,192,384]{2,1,0:T(8,128)(2,1)S(1)}, u32[]{:S(2)}, u32[]{:S(2)}) collective-permute-start(bf16[16,192,384]{2,1,0:T(8,128)(2,1)S(1)} %get-tuple-element.287), channel_id=1, source_target_pairs={{0,1},{1,0},{2,3},{3,2},{4,5},{5,4},{6,7},{7,6},{8,9},{9,8},{10,11... | collective-permute-start | bytes 7077896 | tf_op jit(solution)/shard_map/ppermute | solution.py:1023
  192.3 12.2 %collective-permute-start.40 = (bf16[2,16,1280]{2,1,0:T(8,128)(2,1)S(1)}, bf16[2,16,1280]{2,1,0:T(8,128)(2,1)S(1)}, u32[]{:S(2)}, u32[]{:S(2)}) collective-permute-start(bf16[2,16,1280]{2,1,0:T(8,128)(2,1)S(1)} %pad_maximum_fusion.3), channel_id=1, source_target_pairs={{0,8},{1,9},{2,10},{3,11},{4,12},{5,13},{6,14},{7,15},{8,0},{9,1},... | collective-permute-start | bytes 245768 | tf_op jit(solution)/shard_map/ppermute | solution.py:1023
  207.8 16.3 %collective-permute-start.41 = (bf16[8,192,384]{2,1,0:T(8,128)(2,1)S(1)}, bf16[8,192,384]{2,1,0:T(8,128)(2,1)S(1)}, u32[]{:S(2)}, u32[]{:S(2)}) collective-permute-start(bf16[8,192,384]{2,1,0:T(8,128)(2,1)S(1)} %shard_map.133), channel_id=1, source_target_pairs={{0,16},{1,3},{2,18},{3,1},{4,20},{5,7},{6,22},{7,5},{8,24},{9,11},... | collective-permute-start | bytes 3538952 | tf_op jit(solution)/shard_map/ppermute | solution.py:1023
  229.0 15.5 %collective-permute-start.43 = (bf16[16,192,384]{2,1,0:T(8,128)(2,1)}, bf16[16,192,384]{2,1,0:T(8,128)(2,1)S(1)}, u32[]{:S(2)}, u32[]{:S(2)}) collective-permute-start(bf16[16,192,384]{2,1,0:T(8,128)(2,1)} %shard_map.134), channel_id=1, source_target_pairs={{0,1},{1,0},{2,3},{3,2},{4,5},{5,4},{6,7},{7,6},{8,9},{9,8},{10,11... | collective-permute-start | bytes 7077896 | tf_op jit(solution)/shard_map/ppermute | solution.py:1023
  231.1 13.4 %collective-permute-start.42 = (bf16[4,192,384]{2,1,0:T(8,128)(2,1)S(1)}, bf16[4,192,384]{2,1,0:T(8,128)(2,1)S(1)}, u32[]{:S(2)}, u32[]{:S(2)}) collective-permute-start(bf16[4,192,384]{2,1,0:T(8,128)(2,1)S(1)} %shard_map.136), channel_id=1, source_target_pairs={{0,2},{1,17},{2,0},{3,19},{4,6},{5,21},{6,4},{7,23},{8,10},{9,25},... | collective-permute-start | bytes 1769480 | tf_op jit(solution)/shard_map/ppermute | solution.py:1023
  233.0 11.4 %collective-permute-start.45 = (bf16[4,16,1280]{2,1,0:T(8,128)(2,1)S(1)}, bf16[4,16,1280]{2,1,0:T(8,128)(2,1)S(1)}, u32[]{:S(2)}, u32[]{:S(2)}) collective-permute-start(bf16[4,16,1280]{2,1,0:T(8,128)(2,1)S(1)} %constant_dynamic-update-slice_fusion.8.refs_0_), channel_id=1, source_target_pairs={{0,2},{1,17},{2,0},{3,19},{4,6},{5,21},{6,4},{7,23},{8,10},{9,25},... | collective-permute-start | bytes 491528 | tf_op jit(solution)/shard_map/ppermute | solution.py:1023
  246.8 17.1 %collective-permute-start.46 = (bf16[8,192,384]{2,1,0:T(8,128)(2,1)S(1)}, bf16[8,192,384]{2,1,0:T(8,128)(2,1)S(1)}, u32[]{:S(2)}, u32[]{:S(2)}) collective-permute-start(bf16[8,192,384]{2,1,0:T(8,128)(2,1)S(1)} %shard_map.139), channel_id=1, source_target_pairs={{0,16},{1,3},{2,18},{3,1},{4,20},{5,7},{6,22},{7,5},{8,24},{9,11},... | collective-permute-start | bytes 3538952 | tf_op jit(solution)/shard_map/ppermute | solution.py:1023
  247.6 16.2 %collective-permute-start.47 = (bf16[4,16,1280]{2,1,0:T(8,128)(2,1)S(1)}, bf16[4,16,1280]{2,1,0:T(8,128)(2,1)S(1)}, u32[]{:S(2)}, u32[]{:S(2)}) collective-permute-start(bf16[4,16,1280]{2,1,0:T(8,128)(2,1)S(1)} %collective-permute-done.44.refs_1_), channel_id=1, source_target_pairs={{0,2},{1,17},{2,0},{3,19},{4,6},{5,21},{6,4},{7,23},{8,10},{9,25},... | collective-permute-start | bytes 491528 | tf_op jit(solution)/shard_map/ppermute | solution.py:1023
  249.4 14.3 %collective-permute-start.48 = (bf16[192,384]{1,0:T(8,128)(2,1)S(1)}, bf16[192,384]{1,0:T(8,128)(2,1)S(1)}, u32[]{:S(2)}, u32[]{:S(2)}) collective-permute-start(bf16[192,384]{1,0:T(8,128)(2,1)S(1)} %get-tuple-element.321), channel_id=1, source_target_pairs={{0,4},{1,5},{2,6},{3,7},{4,0},{5,1},{6,2},{7,3},{8,12},{9,13},{10,... | collective-permute-start | bytes 442376 | tf_op jit(solution)/shard_map/ppermute | solution.py:1023
  250.0 13.7 %collective-permute-start.49 = (bf16[192,384]{1,0:T(8,128)(2,1)S(1)}, bf16[192,384]{1,0:T(8,128)(2,1)S(1)}, u32[]{:S(2)}, u32[]{:S(2)}) collective-permute-start(bf16[192,384]{1,0:T(8,128)(2,1)S(1)} %get-tuple-element.322), channel_id=1, source_target_pairs={{0,8},{1,9},{2,10},{3,11},{4,12},{5,13},{6,14},{7,15},{8,0},{9,1},... | collective-permute-start | bytes 442376 | tf_op jit(solution)/shard_map/ppermute | solution.py:1023
  252.2 11.6 %collective-permute-start.50 = (bf16[192,384]{1,0:T(8,128)(2,1)S(1)}, bf16[192,384]{1,0:T(8,128)(2,1)S(1)}, u32[]{:S(2)}, u32[]{:S(2)}) collective-permute-start(bf16[192,384]{1,0:T(8,128)(2,1)S(1)} %get-tuple-element.323), channel_id=1, source_target_pairs={{0,12},{1,13},{2,14},{3,15},{4,8},{5,9},{6,10},{7,11},{8,4},{9,5},... | collective-permute-start | bytes 442376 | tf_op jit(solution)/shard_map/ppermute | solution.py:1023
  276.0 16.0 %collective-permute-start.56 = (bf16[192,384]{1,0:T(8,128)(2,1)S(1)}, bf16[192,384]{1,0:T(8,128)(2,1)S(1)}, u32[]{:S(2)}, u32[]{:S(2)}) collective-permute-start(bf16[192,384]{1,0:T(8,128)(2,1)S(1)} %bitcast.38), channel_id=1, source_target_pairs={{0,1},{1,0},{2,3},{3,2},{4,5},{5,4},{6,7},{7,6},{8,9},{9,8},{10,11... | collective-permute-start | bytes 442376 | tf_op jit(solution)/shard_map/ppermute | solution.py:1023
  276.7 15.4 %collective-permute-start.59 = (bf16[192,384]{1,0:T(8,128)(2,1)S(1)}, bf16[192,384]{1,0:T(8,128)(2,1)S(1)}, u32[]{:S(2)}, u32[]{:S(2)}) collective-permute-start(bf16[192,384]{1,0:T(8,128)(2,1)S(1)} %get-tuple-element.343), channel_id=1, source_target_pairs={{0,4},{1,5},{2,6},{3,7},{4,0},{5,1},{6,2},{7,3},{8,12},{9,13},{10,... | collective-permute-start | bytes 442376 | tf_op jit(solution)/shard_map/ppermute | solution.py:1023
  278.4 14.0 %collective-permute-start.60 = (bf16[192,384]{1,0:T(8,128)(2,1)S(1)}, bf16[192,384]{1,0:T(8,128)(2,1)S(1)}, u32[]{:S(2)}, u32[]{:S(2)}) collective-permute-start(bf16[192,384]{1,0:T(8,128)(2,1)S(1)} %get-tuple-element.344), channel_id=1, source_target_pairs={{0,8},{1,9},{2,10},{3,11},{4,12},{5,13},{6,14},{7,15},{8,0},{9,1},... | collective-permute-start | bytes 442376 | tf_op jit(solution)/shard_map/ppermute | solution.py:1023
  280.1 12.2 %collective-permute-start.61 = (bf16[192,384]{1,0:T(8,128)(2,1)S(1)}, bf16[192,384]{1,0:T(8,128)(2,1)S(1)}, u32[]{:S(2)}, u32[]{:S(2)}) collective-permute-start(bf16[192,384]{1,0:T(8,128)(2,1)S(1)} %get-tuple-element.345), channel_id=1, source_target_pairs={{0,12},{1,13},{2,14},{3,15},{4,8},{5,9},{6,10},{7,11},{8,4},{9,5},... | collective-permute-start | bytes 442376 | tf_op jit(solution)/shard_map/ppermute | solution.py:1023
  304.0 12.6 %collective-permute-start.68 = (bf16[8,16,384]{2,1,0:T(8,128)(2,1)S(1)}, bf16[8,16,384]{2,1,0:T(8,128)(2,1)S(1)}, u32[]{:S(2)}, u32[]{:S(2)}) collective-permute-start(bf16[8,16,384]{2,1,0:T(8,128)(2,1)S(1)} %get-tuple-element.370), channel_id=1, source_target_pairs={{0,6},{1,7},{2,4},{3,5},{4,2},{5,3},{6,0},{7,1},{8,14},{9,15},{10,... | collective-permute-start | bytes 294920 | tf_op jit(solution)/shard_map/ppermute | solution.py:1023
  304.7 12.0 %collective-permute-start.69 = (bf16[8,16,384]{2,1,0:T(8,128)(2,1)S(1)}, bf16[8,16,384]{2,1,0:T(8,128)(2,1)S(1)}, u32[]{:S(2)}, u32[]{:S(2)}) collective-permute-start(bf16[8,16,384]{2,1,0:T(8,128)(2,1)S(1)} %get-tuple-element.371), channel_id=1, source_target_pairs={{0,8},{1,9},{2,10},{3,11},{4,12},{5,13},{6,14},{7,15},{8,0},{9,1},... | collective-permute-start | bytes 294920 | tf_op jit(solution)/shard_map/ppermute | solution.py:1023
  307.3 14.5 %collective-permute-start.70 = (bf16[8,16,384]{2,1,0:T(8,128)(2,1)S(1)}, bf16[8,16,384]{2,1,0:T(8,128)(2,1)S(1)}, u32[]{:S(2)}, u32[]{:S(2)}) collective-permute-start(bf16[8,16,384]{2,1,0:T(8,128)(2,1)S(1)} %get-tuple-element.372), channel_id=1, source_target_pairs={{0,10},{1,11},{2,8},{3,9},{4,14},{5,15},{6,12},{7,13},{8,2},{9,3},... | collective-permute-start | bytes 294920 | tf_op jit(solution)/shard_map/ppermute | solution.py:1023
  308.2 13.5 %collective-permute-start.71 = (bf16[8,16,384]{2,1,0:T(8,128)(2,1)S(1)}, bf16[8,16,384]{2,1,0:T(8,128)(2,1)S(1)}, u32[]{:S(2)}, u32[]{:S(2)}) collective-permute-start(bf16[8,16,384]{2,1,0:T(8,128)(2,1)S(1)} %get-tuple-element.373), channel_id=1, source_target_pairs={{0,12},{1,13},{2,14},{3,15},{4,8},{5,9},{6,10},{7,11},{8,4},{9,5},... | collective-permute-start | bytes 294920 | tf_op jit(solution)/shard_map/ppermute | solution.py:1023
  310.6 11.2 %collective-permute-start.72 = (bf16[8,16,384]{2,1,0:T(8,128)(2,1)S(1)}, bf16[8,16,384]{2,1,0:T(8,128)(2,1)S(1)}, u32[]{:S(2)}, u32[]{:S(2)}) collective-permute-start(bf16[8,16,384]{2,1,0:T(8,128)(2,1)S(1)} %get-tuple-element.374), channel_id=1, source_target_pairs={{0,14},{1,15},{2,12},{3,13},{4,10},{5,11},{6,8},{7,9},{8,6},{9,7},... | collective-permute-start | bytes 294920 | tf_op jit(solution)/shard_map/ppermute | solution.py:1023
  (80 other events, 754.7 us)

commit v6 on v5

--- a/solution.py
+++ b/solution.py
@@ -935,7 +935,8 @@
         grid=(slots // each,),
         scratch=[pltpu.VMEM((part_rows, D), f32), pltpu.VMEM((D // 128, part_rows, 128), f32)],
         flops=20 * slots * part_rows * D,
-        in_hbm=(3, 4, 5, 6, 7),
+        in_hbm=(3, 4, 5),
+        vmem_in=(6, 7) if fast else (),
         prefetch=3,
     )
 
@@ -958,7 +959,7 @@
         here = (row - col == segment * images) & (row // 16 == col // 16) & (col % 16 < images)
         rank = nn(jnp.where(here, 1.0, 0.0).astype(bf16), mine).astype(bf16)
         part = held[:, D:PACK] if segment == 0 else held
-        down_ref[:, first : first + part.shape[1]] = tn(rank, part)
+        down_ref[:, :, first : first + part.shape[1]] = tn(rank, part).reshape(8, 16, part.shape[1])
         first += part.shape[1]
     proj_ref[...] = tn(dz_ref[...], pooled_ref[...])
 
@@ -966,11 +967,11 @@
 def rank_grads(images, kind, row, arrays, dz, pooled):
     return call(
         functools.partial(rank_grad_kernel, images),
-        (sds((128, FF), f32), sds((EMB, D), f32)),
+        (sds((8, 16, FF), f32), sds((EMB, D), f32)),
         (kind, row, *arrays, dz, pooled),
         [whole(a.shape) for a in arrays] + [whole(dz.shape), whole(pooled.shape)],
-        [whole((128, FF)), whole((EMB, D))],
-        out_hbm=(0, 1),
+        [whole((8, 16, FF)), whole((EMB, D))],
+        vmem_out=(0, 1),
         flops=256 * D * FF,
         prefetch=2,
     )
@@ -1090,7 +1091,8 @@
             return self.kept(self.second_send(i, me), me)
 
         parts = [(self.mine, own), (self.one, own), (self.two, self.second_send)]
-        self.three = send(add_pieces(parts, self.me, 4, near=(2,)), CROSS_TWO)
+        self.part = add_pieces(parts, self.me, 4, near=(2,))
+        self.three = send(self.part, CROSS_TWO)
 
     def partial(self):
         def crossed(i, me):
@@ -1461,24 +1463,25 @@
         dqkv, up_sum.two, pair, far = meet(dqkv, up_sum.two, pair, far)
         up_sum.cross_two()
         ranks.cross_one(jnp.concatenate([pair, far]))
-        ranks.two = send(ranks.ring, CROSS_TWO)
+        dqkv, _ = meet(dqkv, up_sum.part)
         other = qkv_weight_grad_fast(images, dqkv, a, g_out, me, True)
         other, dqkv = meet(other, dqkv)
         qkv_sum = PieceSum(other, me)
         mine = qkv_weight_grad_fast(images, dqkv, a, g_out, me, False)
         up_sum.partial()
-        dqkv, up_sum.sums, up_sum.three, qkv_sum.mine, qkv_sum.one, ranks.ring, ranks.one, ranks.two = meet(
-            dqkv, up_sum.sums, up_sum.three, mine, qkv_sum.one, ranks.ring, ranks.one, ranks.two
+        dqkv, up_sum.sums, up_sum.three, qkv_sum.mine, qkv_sum.one, ranks.ring, ranks.one = meet(
+            dqkv, up_sum.sums, up_sum.three, mine, qkv_sum.one, ranks.ring, ranks.one
         )
         qkv_sum.cross_one()
         up_sum.cross_z()
-        ranks.cross_two()
+        ranks.both = send(ranks.one, CROSS_TWO)
         input_grad, vec_sum = input_backward(images, x, dqkv, w_qkv, dh, vec, g_two, g_bias, g_bias_up, me)
-        vec_sum, qkv_sum.two, ranks.ring, ranks.one, ranks.two, ranks.both, *up_sum.last = meet(
-            vec_sum, qkv_sum.two, ranks.ring, ranks.one, ranks.two, ranks.both, *up_sum.last
+        vec_sum, qkv_sum.two, ranks.ring, ranks.one, ranks.both, *up_sum.last = meet(
+            vec_sum, qkv_sum.two, ranks.ring, ranks.one, ranks.both, *up_sum.last
         )
         qkv_sum.cross_two()
         near_vec = send(vec_sum, SWAP_CORE)
+        ranks.two = send(ranks.ring, CROSS_TWO)
         ranks.send_near(0, 1)
         up_total = up_sum.total()
         vec_sum, near_vec, up_total = meet(vec_sum, near_vec, up_total)
@@ -1503,7 +1506,7 @@
         vec_total = vec_sum + across
         summed = return_to_owners((qkv_total, up_total, near_qkv, near_up), place)
         g_down, g_proj = rank_grads(images, kind, row, ranks.arrays(), dz_all, pooled_all)
-        g_down, g_proj, vec_total, *summed = meet(g_down.reshape(8, 16, FF), g_proj, vec_total, *summed)
+        g_down, g_proj, vec_total, *summed = meet(g_down, g_proj, vec_total, *summed)
     else:
         both_all = lax.all_gather(both, AXES, axis=0, tiled=True)
         dm, g_bias_up, g_up = up_backward(images, slope, m, w_up, hidden, col, me)

time: 334 us -> 333 us (level)
  transfers between devices with their start and end apart: 74 -> 74, of which waited for: 26 -> 26; matrix products, arithmetic and copies ran while one was open for 1% -> 1% of each run, Pallas kernels for 37% -> 36%
where the time goes in v6:
time: 333 us; the launch traced here: 328 us
  Pallas kernels  160 us (48%)
  starting transfers between devices  85.4 us (26%)
  waiting for transfers between devices  69.7 us (21%)
  local copies, waits for them, and re-layouts  10.5 us (3%)
    pallas_call x29, Pallas kernels, call(): pl.pallas_call(kernel, out_shape=tuple(outs), grid_spec=pltpu.PrefetchSca...  153 us
    ppermute x73, starting transfers between devices, send(): return lax.ppermute(value, AXES, permutation)  79 us
    ppermute x73, waiting for transfers between devices, send(): return lax.ppermute(value, AXES, permutation)  66.7 us
    unnamed x116, local copies, waits for them, and re-layouts  7.67 us
    pallas_call x1, Pallas kernels, plan(): pl.pallas_call(plan_kernel, out_shape=tuple((sds((size,), jnp.int32) for...  7.15 us
  transfers between devices with their start and end apart: 74, of which 26 were waited for; matrix products, arithmetic and copies ran while one was open for 1% of the time, Pallas kernels for 36%

profile of v6, /device:TPU:0, one launch (start us, length us, event | category | flops | bytes accessed | tf_op | source)
XLA Modules:
  0.0 327.9 jit_solution(16057758223572017415)
XLA Ops:
  3.7 3.0 collective-permute-start
  8.3 3.0 collective-permute-start.3
  12.7 3.7 %collective-permute-start.5 = (bf16[8,16,384]{2,1,0:T(8,128)(2,1)S(1)}, bf16[8,16,384]{2,1,0:T(8,128)(2,1)S(1)}, u32[]{:S(2)}, u32[]{:S(2)}) collective-permute-start(bf16[8,16,384]{2,1,0:T(8,128)(2,1)S(1)} %get-tuple-element.202), channel_id=1, source_target_pairs={{0,12},{1,13},{2,14},{3,15},{4,8},{5,9},{6,10},{7,11},{8,4},{9,5},... | collective-permute-start | bytes 294920 | tf_op jit(solution)/shard_map/ppermute | solution.py:1024
  16.5 7.1 %shard_map.120 = (s32[39]{0:T(128)}, s32[64]{0:T(128)}, s32[8]{0:T(128)}, s32[8]{0:T(128)}) custom-call(s32[77]{0:T(128)} %owner_ref.3, s32[4]{0:T(128)} %copy-done.17), custom_call_target="tpu_custom_call" | custom-call | tf_op jit(solution)/shard_map/pallas_call | solution.py:1207
  27.1 2.3 collective-permute-done.7.theirs_ref
  30.5 4.0 %collective-permute-start.8 = (bf16[10,16,384]{2,1,0:T(8,128)(2,1)S(1)}, bf16[10,16,384]{2,1,0:T(8,128)(2,1)S(1)}, u32[]{:S(2)}, u32[]{:S(2)}) collective-permute-start(bf16[10,16,384]{2,1,0:T(8,128)(2,1)S(1)} %get-tuple-element.217), channel_id=1, source_target_pairs={{0,4},{1,5},{2,6},{3,7},{4,0},{5,1},{6,2},{7,3},{8,12},{9,13},{10,... | collective-permute-start | bytes 368648 | tf_op jit(solution)/shard_map/ppermute | solution.py:1024
  37.1 2.7 collective-permute-done.8
  39.8 7.1 %collective-permute-done.9 = bf16[10,16,384]{2,1,0:T(8,128)(2,1)S(1)} collective-permute-done((bf16[10,16,384]{2,1,0:T(8,128)(2,1)S(1)}, bf16[10,16,384]{2,1,0:T(8,128)(2,1)S(1)}, u32[]{:S(2)}, u32[]{:S(2)}) %collective-permute-start.9) | collective-permute-done | bytes 122912 | tf_op jit(solution)/shard_map/ppermute | solution.py:1024
  53.8 4.9 %collective-permute-done.11.refs_1_ = bf16[4,10,16,384]{3,2,1,0:T(8,128)(2,1)S(1)} collective-permute-done((bf16[4,10,16,384]{3,2,1,0:T(8,128)(2,1)S(1)}, bf16[4,10,16,384]{3,2,1,0:T(8,128)(2,1)S(1)}, u32[]{:S(2)}, u32[]{:S(2)}) %collective-permute-start.11) | collective-permute-done | bytes 491552 | tf_op jit(solution)/shard_map/ppermute | solution.py:1024
  60.2 6.5 %collective-permute-done.14 = bf16[15,16,384]{2,1,0:T(8,128)(2,1)S(1)} collective-permute-done((bf16[15,16,384]{2,1,0:T(8,128)(2,1)S(1)}, bf16[15,16,384]{2,1,0:T(8,128)(2,1)S(1)}, u32[]{:S(2)}, u32[]{:S(2)}) %collective-permute-start.14) | collective-permute-done | bytes 184352 | tf_op jit(solution)/shard_map/ppermute | solution.py:1024
  70.8 2.5 collective-permute-start.23
  76.5 9.1 %shard_map.122 = (bf16[1040,768]{1,0:T(8,128)(2,1)}, bf16[1040,2304]{1,0:T(8,128)(2,1)S(1)}, f32[16,768]{1,0:T(8,128)S(1)}) custom-call(s32[4]{0:T(128)S(1)} %copy-done.18, bf16[4,10,16,384]{3,2,1,0:T(8,128)(2,1)} %copy-done.34, bf16[4,10,16,384]{3,2,1,0:T(8,128)(2,1)} %copy-done.41, bf16[4,10,16,384]{3,2,1,0:T(8,128)(2,1)} %copy-done.42, ...), custom_call_target="tpu_custom_call" | custom-call | flops 1 | bytes 1 | tf_op jit(solution)/shard_map/pallas_call | solution.py:84
  85.6 4.0 %collective-permute-done.24 = bf16[15,16,384]{2,1,0:T(8,128)(2,1)S(1)} collective-permute-done((bf16[15,16,384]{2,1,0:T(8,128)(2,1)S(1)}, bf16[15,16,384]{2,1,0:T(8,128)(2,1)S(1)}, u32[]{:S(2)}, u32[]{:S(2)}) %collective-permute-start.24) | collective-permute-done | bytes 184352 | tf_op jit(solution)/shard_map/ppermute | solution.py:1024
  90.8 9.0 %shard_map.123 = (bf16[1040,768]{1,0:T(8,128)(2,1)S(1)}, f32[5,16,208]{2,1,0:T(8,128)S(1)}) custom-call(bf16[1040,2304]{1,0:T(8,128)(2,1)S(1)} %get-tuple-element.240.qkv_ref, f32[5,1,208]{2,1,0:T(1,128)S(1)} %broadcast_in_dim.84.mask_ref), custom_call_target="tpu_custom_call" | custom-call | flops 1 | bytes 1 | tf_op jit(solution)/shard_map/pallas_call | solution.py:84
  104.4 6.1 %shard_map.124 = (f32[1040,768]{1,0:T(8,128)S(1)}, bf16[1040,768]{1,0:T(8,128)(2,1)S(1)}) custom-call(s32[4]{0:T(128)S(1)} %copy-done.18, bf16[4,15,16,384]{3,2,1,0:T(8,128)(2,1)} %copy-done.25, bf16[4,15,16,384]{3,2,1,0:T(8,128)(2,1)} %copy-done.26, bf16[4,15,16,384]{3,2,1,0:T(8,128)(2,1)} %copy-done.27, bf16[4,15,16,384]{3,2,1,0:T(8,128)(2,1)} %copy-done.28, ...), custom_call_target="tpu_custom_call" | custom-call | flops 1 | bytes 1 | tf_op jit(solution)/shard_map/pallas_call | solution.py:84
  110.6 2.4 collective-permute-done.31.refs_1_
  115.6 13.3 %shard_map.125 = (bf16[1040,3072]{1,0:T(8,128)(2,1)S(1)}, bf16[1040,3072]{1,0:T(8,128)(2,1)}) custom-call(s32[4]{0:T(128)S(1)} %copy-done.18, bf16[4,15,16,384]{3,2,1,0:T(8,128)(2,1)} %copy-done.25, bf16[4,15,16,384]{3,2,1,0:T(8,128)(2,1)} %copy-done.26, bf16[4,15,16,384]{3,2,1,0:T(8,128)(2,1)} %copy-done.27, bf16[4,15,16,384]{3,2,1,0:T(8,128)(2,1)} %copy-done.28, ...), custom_call_target="tpu_custom_call" | custom-call | flops 1 | bytes 1 | tf_op jit(solution)/shard_map/pallas_call | solution.py:84
  128.9 3.5 %collective-permute-done.33.refs_3_ = bf16[4,15,16,384]{3,2,1,0:T(8,128)(2,1)S(1)} collective-permute-done((bf16[4,15,16,384]{3,2,1,0:T(8,128)(2,1)S(1)}, bf16[4,15,16,384]{3,2,1,0:T(8,128)(2,1)S(1)}, u32[]{:S(2)}, u32[]{:S(2)}) %collective-permute-start.33) | collective-permute-done | bytes 737312 | tf_op jit(solution)/shard_map/ppermute | solution.py:1024
  135.8 10.0 %shard_map.126 = (bf16[5,196,768]{2,1,0:T(8,128)(2,1)}, bf16[16,768]{1,0:T(8,128)(2,1)S(1)}) custom-call(s32[4]{0:T(128)S(1)} %copy-done.18, bf16[4,15,16,384]{3,2,1,0:T(8,128)(2,1)} %copy-done.33, bf16[4,15,16,384]{3,2,1,0:T(8,128)(2,1)} %copy-done.35, bf16[4,15,16,384]{3,2,1,0:T(8,128)(2,1)} %copy-done.36, bf16[4,15,16,384]{3,2,1,0:T(8,128)(2,1)} %copy-done.37, ...), custom_call_target="tpu_custom_call" | custom-call | flops 1 | bytes 1 | tf_op jit(solution)/shard_map/pallas_call | solution.py:84
  146.6 6.4 %all-to-all-start = ((bf16[32,5,768]{2,1,0:T(8,128)(2,1)}), bf16[32,5,768]{2,1,0:T(8,128)(2,1)S(1)}, u32[]{:S(2)}, u32[]{:S(2)}) async-start(bf16[32,5,768]{2,1,0:T(8,128)(2,1)} %broadcast_in_dim.95), calls=%async_computation | async-start | bytes 786432 | tf_op jit(solution)/shard_map/all_to_all | solution.py:1439
  153.0 2.3 copy-done.6
  155.4 3.2 shard_map.128.p_ref
  158.6 2.7 copy-done.7
  163.1 3.0 all-to-all-done.refs_9_
  166.1 5.1 %shard_map.129 = (bf16[160,512]{1,0:T(8,128)(2,1)S(1)}, bf16[16,768]{1,0:T(8,128)(2,1)S(1)}, f32[16,768]{1,0:T(8,128)S(1)}, f32[16,3072]{1,0:T(8,128)S(1)}, bf16[160,768]{1,0:T(8,128)(2,1)S(1)}) custom-call(s32[4]{0:T(128)S(1)} %copy-done.18, s32[1]{0:T(128)} %bitcast.5.first_ref, bf16[4,15,16,384]{3,2,1,0:T(8,128)(2,1)} %copy-done.33, ...), custom_call_target="tpu_custom_call" | custom-call | flops 1 | bytes 1 | tf_op jit(solution)/shard_map/pallas_call | solution.py:84
  172.2 19.9 %shard_map.130 = (f32[1040,768]{1,0:T(8,128)S(1)}, f32[8,3072]{1,0:T(8,128)S(1)}, bf16[16,192,384]{2,1,0:T(8,128)(2,1)S(1)}, bf16[16,192,384]{2,1,0:T(8,128)(2,1)S(1)}) custom-call(s32[4]{0:T(128)S(1)} %copy-done.18, bf16[4,15,16,384]{3,2,1,0:T(8,128)(2,1)} %copy-done.25, bf16[4,15,16,384]{3,2,1,0:T(8,128)(2,1)} %copy-done.26, ...), custom_call_target="tpu_custom_call" | custom-call | flops 1 | bytes 1 | tf_op jit(solution)/shard_map/pallas_call | solution.py:84
  193.9 10.6 %shard_map.131 = (f32[1040,768]{1,0:T(8,128)S(1)}, bf16[1040,768]{1,0:T(8,128)(2,1)S(1)}, bf16[2,16,48,384]{3,2,1,0:T(8,128)(2,1)S(1)}, f32[8,768]{1,0:T(8,128)S(1)}) custom-call(s32[4]{0:T(128)S(1)} %copy-done.18, bf16[4,15,16,384]{3,2,1,0:T(8,128)(2,1)} %copy-done.25, bf16[4,15,16,384]{3,2,1,0:T(8,128)(2,1)} %copy-done.26, ...), custom_call_target="tpu_custom_call" | custom-call | flops 1 | bytes 1 | tf_op jit(solution)/shard_map/pallas_call | solution.py:84
  204.6 3.2 shard_map.133
  209.3 13.3 %shard_map.132 = (bf16[1040,2304]{1,0:T(8,128)(2,1)S(1)}, f32[16,2304]{1,0:T(8,128)S(1)}) custom-call(bf16[1040,2304]{1,0:T(8,128)(2,1)S(1)} %bitcast.31, bf16[1040,768]{1,0:T(8,128)(2,1)S(1)} %get-tuple-element.289.do_ref, bf16[5,12,208,208]{3,2,1,0:T(8,128)(2,1)S(1)} %bitcast.36), custom_call_target="tpu_custom_call" | custom-call | flops 1 | bytes 1 | tf_op jit(solution)/shard_map/pallas_call | solution.py:84
  224.1 2.5 shard_map.134
  226.6 4.9 %shard_map.135 = bf16[16,192,384]{2,1,0:T(8,128)(2,1)} custom-call(s32[4]{0:T(128)S(1)} %copy-done.18, bf16[1040,2304]{1,0:T(8,128)(2,1)S(1)} %get-tuple-element.305.dqkv_ref.refs_9_, bf16[1040,768]{1,0:T(8,128)(2,1)S(1)} %copy-done.11, bf16[2,16,48,384]{3,2,1,0:T(8,128)(2,1)S(1)} %get-tuple-element.300.out_ref), custom_call_target="tpu_custom_call" | custom-call | flops 1 | bytes 1 | tf_op jit(solution)/shard_map/pallas_call | solution.py:84
  233.4 2.3 shard_map.136.refs_0_.refs_2_.refs_4_.refs_6_
  235.6 4.9 %shard_map.137.refs_0_.refs_2_.refs_4_.refs_6_.refs_3_.refs_9_ = bf16[16,192,384]{2,1,0:T(8,128)(2,1)} custom-call(s32[4]{0:T(128)S(1)} %copy-done.18, bf16[1040,2304]{1,0:T(8,128)(2,1)S(1)} %get-tuple-element.305.dqkv_ref.refs_9_, bf16[1040,768]{1,0:T(8,128)(2,1)S(1)} %copy-done.11, bf16[2,16,48,384]{3,2,1,0:T(8,128)(2,1)S(1)} %get-tuple-element.300.out_ref), custom_call_target="tpu_custom_call" | custom-call | flops 1 | bytes 1 | tf_op jit(solution)/shard_map/pallas_call | solution.py:84
  240.6 2.5 collective-permute-done.42.refs_1_.refs_3_.refs_5_.refs_7_
  243.1 2.4 shard_map.139
  252.5 9.9 %shard_map.138 = (f32[5,196,768]{2,1,0:T(8,128)}, f32[16,768]{1,0:T(8,128)S(1)}) custom-call(s32[4]{0:T(128)S(1)} %copy-done.18, bf16[4,10,16,384]{3,2,1,0:T(8,128)(2,1)} %copy-done.34, bf16[4,10,16,384]{3,2,1,0:T(8,128)(2,1)} %copy-done.41, bf16[4,10,16,384]{3,2,1,0:T(8,128)(2,1)} %copy-done.42, bf16[4,10,16,384]{3,2,1,0:T(8,128)(2,1)} %copy-done.43, ...), custom_call_target="tpu_custom_call" | custom-call | flops 1 | bytes 1 | tf_op jit(solution)/shard_map/pallas_call | solution.py:84
  268.6 2.2 collective-permute-start.51
  270.8 2.3 shard_map.142.refs_0_.refs_2_.refs_4_.refs_6_
  283.1 2.6 collective-permute-done.57
  286.5 6.0 %collective-permute-done.58 = f32[16,768]{1,0:T(8,128)S(1)} collective-permute-done((f32[16,768]{1,0:T(8,128)S(1)}, f32[16,768]{1,0:T(8,128)S(1)}, u32[]{:S(2)}, u32[]{:S(2)}) %collective-permute-start.58) | collective-permute-done | bytes 49184 | tf_op jit(solution)/shard_map/ppermute | solution.py:1024
  295.4 2.8 collective-permute-done.63
  298.3 2.4 shard_map.147
  301.8 2.7 collective-permute-start.67
  305.2 2.6 collective-permute-start.69
  308.7 2.4 collective-permute-start.71
  312.9 2.9 shard_map.146
  315.8 6.5 %collective-permute-done.70.refs_11_ = bf16[8,16,384]{2,1,0:T(8,128)(2,1)S(1)} collective-permute-done((bf16[8,16,384]{2,1,0:T(8,128)(2,1)S(1)}, bf16[8,16,384]{2,1,0:T(8,128)(2,1)S(1)}, u32[]{:S(2)}, u32[]{:S(2)}) %collective-permute-start.70) | collective-permute-done | bytes 98336 | tf_op jit(solution)/shard_map/ppermute | solution.py:1024
  322.3 5.5 %shard_map.148 = (f32[1,8,64,768]{3,2,1,0:T(8,128)}, f32[1,8,64,768]{3,2,1,0:T(8,128)}, f32[1,8,64,768]{3,2,1,0:T(8,128)}) custom-call(s32[8]{0:T(128)S(1)} %copy-done.20, s32[8]{0:T(128)S(1)} %copy-done.21, s32[4]{0:T(128)S(1)} %copy-done.18, f32[1,8,64,768]{3,2,1,0:T(8,128)} %refs_0_.1, f32[1,8,64,768]{3,2,1,0:T(8,128)} %refs_1_.1, ...), custom_call_target="tpu_custom_call" | custom-call | flops 1 | bytes 1 | tf_op jit(solution)/shard_map/pallas_call | solution.py:84
  (283 shorter events, 81.9 us)
Async XLA Ops:
  8.3 17.0 %collective-permute-start.2 = (bf16[8,16,384]{2,1,0:T(8,128)(2,1)S(1)}, bf16[8,16,384]{2,1,0:T(8,128)(2,1)S(1)}, u32[]{:S(2)}, u32[]{:S(2)}) collective-permute-start(bf16[8,16,384]{2,1,0:T(8,128)(2,1)S(1)} %get-tuple-element.199), channel_id=1, source_target_pairs={{0,6},{1,7},{2,4},{3,5},{4,2},{5,3},{6,0},{7,1},{8,14},{9,15},{10,... | collective-permute-start | bytes 294920 | tf_op jit(solution)/shard_map/ppermute | solution.py:1024
  8.3 17.0 %collective-permute-start.3 = (bf16[8,16,384]{2,1,0:T(8,128)(2,1)S(1)}, bf16[8,16,384]{2,1,0:T(8,128)(2,1)S(1)}, u32[]{:S(2)}, u32[]{:S(2)}) collective-permute-start(bf16[8,16,384]{2,1,0:T(8,128)(2,1)S(1)} %get-tuple-element.200), channel_id=1, source_target_pairs={{0,8},{1,9},{2,10},{3,11},{4,12},{5,13},{6,14},{7,15},{8,0},{9,1},... | collective-permute-start | bytes 294920 | tf_op jit(solution)/shard_map/ppermute | solution.py:1024
  11.2 15.2 %collective-permute-start.4 = (bf16[8,16,384]{2,1,0:T(8,128)(2,1)S(1)}, bf16[8,16,384]{2,1,0:T(8,128)(2,1)S(1)}, u32[]{:S(2)}, u32[]{:S(2)}) collective-permute-start(bf16[8,16,384]{2,1,0:T(8,128)(2,1)S(1)} %get-tuple-element.201), channel_id=1, source_target_pairs={{0,10},{1,11},{2,8},{3,9},{4,14},{5,15},{6,12},{7,13},{8,2},{9,3},... | collective-permute-start | bytes 294920 | tf_op jit(solution)/shard_map/ppermute | solution.py:1024
  12.7 13.7 %collective-permute-start.5 = (bf16[8,16,384]{2,1,0:T(8,128)(2,1)S(1)}, bf16[8,16,384]{2,1,0:T(8,128)(2,1)S(1)}, u32[]{:S(2)}, u32[]{:S(2)}) collective-permute-start(bf16[8,16,384]{2,1,0:T(8,128)(2,1)S(1)} %get-tuple-element.202), channel_id=1, source_target_pairs={{0,12},{1,13},{2,14},{3,15},{4,8},{5,9},{6,10},{7,11},{8,4},{9,5},... | collective-permute-start | bytes 294920 | tf_op jit(solution)/shard_map/ppermute | solution.py:1024
  34.5 12.4 %collective-permute-start.9 = (bf16[10,16,384]{2,1,0:T(8,128)(2,1)S(1)}, bf16[10,16,384]{2,1,0:T(8,128)(2,1)S(1)}, u32[]{:S(2)}, u32[]{:S(2)}) collective-permute-start(bf16[10,16,384]{2,1,0:T(8,128)(2,1)S(1)} %get-tuple-element.217), channel_id=1, source_target_pairs={{0,8},{1,9},{2,10},{3,11},{4,12},{5,13},{6,14},{7,15},{8,0},{9,1},... | collective-permute-start | bytes 368648 | tf_op jit(solution)/shard_map/ppermute | solution.py:1024
  35.7 11.1 %collective-permute-start.10 = (bf16[10,16,384]{2,1,0:T(8,128)(2,1)S(1)}, bf16[10,16,384]{2,1,0:T(8,128)(2,1)S(1)}, u32[]{:S(2)}, u32[]{:S(2)}) collective-permute-start(bf16[10,16,384]{2,1,0:T(8,128)(2,1)S(1)} %get-tuple-element.217), channel_id=1, source_target_pairs={{0,12},{1,13},{2,14},{3,15},{4,8},{5,9},{6,10},{7,11},{8,4},{9,5},... | collective-permute-start | bytes 368648 | tf_op jit(solution)/shard_map/ppermute | solution.py:1024
  46.9 11.7 %collective-permute-start.11 = (bf16[4,10,16,384]{3,2,1,0:T(8,128)(2,1)S(1)}, bf16[4,10,16,384]{3,2,1,0:T(8,128)(2,1)S(1)}, u32[]{:S(2)}, u32[]{:S(2)}) collective-permute-start(bf16[4,10,16,384]{3,2,1,0:T(8,128)(2,1)S(1)} %pad_maximum_fusion.2.refs_0_), channel_id=1, source_target_pairs={{0,16},{1,3},{2,18},{3,1},{4,20},{5,7},{6,22},{7,5},{8,24},{9,11},... | collective-permute-start | bytes 1474568 | tf_op jit(solution)/shard_map/ppermute | solution.py:1024
  49.1 11.1 %collective-permute-start.13 = (bf16[15,16,384]{2,1,0:T(8,128)(2,1)S(1)}, bf16[15,16,384]{2,1,0:T(8,128)(2,1)S(1)}, u32[]{:S(2)}, u32[]{:S(2)}) collective-permute-start(bf16[15,16,384]{2,1,0:T(8,128)(2,1)S(1)} %get-tuple-element.232), channel_id=1, source_target_pairs={{0,4},{1,5},{2,6},{3,7},{4,0},{5,1},{6,2},{7,3},{8,12},{9,13},{10,... | collective-permute-start | bytes 552968 | tf_op jit(solution)/shard_map/ppermute | solution.py:1024
  51.2 15.6 %collective-permute-start.14 = (bf16[15,16,384]{2,1,0:T(8,128)(2,1)S(1)}, bf16[15,16,384]{2,1,0:T(8,128)(2,1)S(1)}, u32[]{:S(2)}, u32[]{:S(2)}) collective-permute-start(bf16[15,16,384]{2,1,0:T(8,128)(2,1)S(1)} %get-tuple-element.232), channel_id=1, source_target_pairs={{0,8},{1,9},{2,10},{3,11},{4,12},{5,13},{6,14},{7,15},{8,0},{9,1},... | collective-permute-start | bytes 552968 | tf_op jit(solution)/shard_map/ppermute | solution.py:1024
  52.3 14.4 %collective-permute-start.15 = (bf16[15,16,384]{2,1,0:T(8,128)(2,1)S(1)}, bf16[15,16,384]{2,1,0:T(8,128)(2,1)S(1)}, u32[]{:S(2)}, u32[]{:S(2)}) collective-permute-start(bf16[15,16,384]{2,1,0:T(8,128)(2,1)S(1)} %get-tuple-element.232), channel_id=1, source_target_pairs={{0,12},{1,13},{2,14},{3,15},{4,8},{5,9},{6,10},{7,11},{8,4},{9,5},... | collective-permute-start | bytes 552968 | tf_op jit(solution)/shard_map/ppermute | solution.py:1024
  58.6 10.3 %collective-permute-start.16 = (bf16[4,10,16,384]{3,2,1,0:T(8,128)(2,1)S(1)}, bf16[4,10,16,384]{3,2,1,0:T(8,128)(2,1)S(1)}, u32[]{:S(2)}, u32[]{:S(2)}) collective-permute-start(bf16[4,10,16,384]{3,2,1,0:T(8,128)(2,1)S(1)} %collective-permute-done.11.refs_1_), channel_id=1, source_target_pairs={{0,2},{1,17},{2,0},{3,19},{4,6},{5,21},{6,4},{7,23},{8,10},{9,25},... | collective-permute-start | bytes 1474568 | tf_op jit(solution)/shard_map/ppermute | solution.py:1024
  66.9 22.8 %collective-permute-start.21 = (bf16[4,15,16,384]{3,2,1,0:T(8,128)(2,1)S(1)}, bf16[4,15,16,384]{3,2,1,0:T(8,128)(2,1)S(1)}, u32[]{:S(2)}, u32[]{:S(2)}) collective-permute-start(bf16[4,15,16,384]{3,2,1,0:T(8,128)(2,1)S(1)} %pad_maximum_fusion.refs_0_), channel_id=1, source_target_pairs={{0,16},{1,3},{2,18},{3,1},{4,20},{5,7},{6,22},{7,5},{8,24},{9,11},... | collective-permute-start | bytes 2211848 | tf_op jit(solution)/shard_map/ppermute | solution.py:1024
  67.5 22.2 %collective-permute-start.22 = (bf16[4,15,16,384]{3,2,1,0:T(8,128)(2,1)S(1)}, bf16[4,15,16,384]{3,2,1,0:T(8,128)(2,1)S(1)}, u32[]{:S(2)}, u32[]{:S(2)}) collective-permute-start(bf16[4,15,16,384]{3,2,1,0:T(8,128)(2,1)S(1)} %pad_maximum_fusion.refs_0_), channel_id=1, source_target_pairs={{0,2},{1,17},{2,0},{3,19},{4,6},{5,21},{6,4},{7,23},{8,10},{9,25},... | collective-permute-start | bytes 2211848 | tf_op jit(solution)/shard_map/ppermute | solution.py:1024
  70.8 14.8 %collective-permute-start.23 = (bf16[15,16,384]{2,1,0:T(8,128)(2,1)S(1)}, bf16[15,16,384]{2,1,0:T(8,128)(2,1)S(1)}, u32[]{:S(2)}, u32[]{:S(2)}) collective-permute-start(bf16[15,16,384]{2,1,0:T(8,128)(2,1)S(1)} %get-tuple-element.251), channel_id=1, source_target_pairs={{0,4},{1,5},{2,6},{3,7},{4,0},{5,1},{6,2},{7,3},{8,12},{9,13},{10,... | collective-permute-start | bytes 552968 | tf_op jit(solution)/shard_map/ppermute | solution.py:1024
  73.3 16.3 %collective-permute-start.24 = (bf16[15,16,384]{2,1,0:T(8,128)(2,1)S(1)}, bf16[15,16,384]{2,1,0:T(8,128)(2,1)S(1)}, u32[]{:S(2)}, u32[]{:S(2)}) collective-permute-start(bf16[15,16,384]{2,1,0:T(8,128)(2,1)S(1)} %get-tuple-element.251), channel_id=1, source_target_pairs={{0,8},{1,9},{2,10},{3,11},{4,12},{5,13},{6,14},{7,15},{8,0},{9,1},... | collective-permute-start | bytes 552968 | tf_op jit(solution)/shard_map/ppermute | solution.py:1024
  75.5 14.2 %collective-permute-start.25 = (bf16[15,16,384]{2,1,0:T(8,128)(2,1)S(1)}, bf16[15,16,384]{2,1,0:T(8,128)(2,1)S(1)}, u32[]{:S(2)}, u32[]{:S(2)}) collective-permute-start(bf16[15,16,384]{2,1,0:T(8,128)(2,1)S(1)} %get-tuple-element.251), channel_id=1, source_target_pairs={{0,12},{1,13},{2,14},{3,15},{4,8},{5,9},{6,10},{7,11},{8,4},{9,5},... | collective-permute-start | bytes 552968 | tf_op jit(solution)/shard_map/ppermute | solution.py:1024
  89.7 11.5 %collective-permute-start.26 = (bf16[4,15,16,384]{3,2,1,0:T(8,128)(2,1)S(1)}, bf16[4,15,16,384]{3,2,1,0:T(8,128)(2,1)S(1)}, u32[]{:S(2)}, u32[]{:S(2)}) collective-permute-start(bf16[4,15,16,384]{3,2,1,0:T(8,128)(2,1)S(1)} %collective-permute-done.21.refs_1_), channel_id=1, source_target_pairs={{0,2},{1,17},{2,0},{3,19},{4,6},{5,21},{6,4},{7,23},{8,10},{9,25},... | collective-permute-start | bytes 2211848 | tf_op jit(solution)/shard_map/ppermute | solution.py:1024
  90.3 10.9 %collective-permute-start.28 = (bf16[4,15,16,384]{3,2,1,0:T(8,128)(2,1)S(1)}, bf16[4,15,16,384]{3,2,1,0:T(8,128)(2,1)S(1)}, u32[]{:S(2)}, u32[]{:S(2)}) collective-permute-start(bf16[4,15,16,384]{3,2,1,0:T(8,128)(2,1)S(1)} %collective-permute-done.21.refs_1_), channel_id=1, source_target_pairs={{0,1},{1,0},{2,3},{3,2},{4,5},{5,4},{6,7},{7,6},{8,9},{9,8},{10,11... | collective-permute-start | bytes 2211848 | tf_op jit(solution)/shard_map/ppermute | solution.py:1024
  90.3 10.9 %collective-permute-start.27 = (bf16[4,15,16,384]{3,2,1,0:T(8,128)(2,1)S(1)}, bf16[4,15,16,384]{3,2,1,0:T(8,128)(2,1)S(1)}, u32[]{:S(2)}, u32[]{:S(2)}) collective-permute-start(bf16[4,15,16,384]{3,2,1,0:T(8,128)(2,1)S(1)} %pad_maximum_fusion.refs_0_), channel_id=1, source_target_pairs={{0,1},{1,0},{2,3},{3,2},{4,5},{5,4},{6,7},{7,6},{8,9},{9,8},{10,11... | collective-permute-start | bytes 2211848 | tf_op jit(solution)/shard_map/ppermute | solution.py:1024
  90.8 10.4 %collective-permute-start.29 = (bf16[4,15,16,384]{3,2,1,0:T(8,128)(2,1)S(1)}, bf16[4,15,16,384]{3,2,1,0:T(8,128)(2,1)S(1)}, u32[]{:S(2)}, u32[]{:S(2)}) collective-permute-start(bf16[4,15,16,384]{3,2,1,0:T(8,128)(2,1)S(1)} %collective-permute-done.22.refs_2_), channel_id=1, source_target_pairs={{0,1},{1,0},{2,3},{3,2},{4,5},{5,4},{6,7},{7,6},{8,9},{9,8},{10,11... | collective-permute-start | bytes 2211848 | tf_op jit(solution)/shard_map/ppermute | solution.py:1024
  101.5 11.5 %collective-permute-start.31 = (bf16[4,15,16,384]{3,2,1,0:T(8,128)(2,1)S(1)}, bf16[4,15,16,384]{3,2,1,0:T(8,128)(2,1)S(1)}, u32[]{:S(2)}, u32[]{:S(2)}) collective-permute-start(bf16[4,15,16,384]{3,2,1,0:T(8,128)(2,1)S(1)} %pad_maximum_fusion.1.refs_0_), channel_id=1, source_target_pairs={{0,16},{1,3},{2,18},{3,1},{4,20},{5,7},{6,22},{7,5},{8,24},{9,11},... | collective-permute-start | bytes 2211848 | tf_op jit(solution)/shard_map/ppermute | solution.py:1024
  113.0 15.9 %collective-permute-start.32 = (bf16[4,15,16,384]{3,2,1,0:T(8,128)(2,1)S(1)}, bf16[4,15,16,384]{3,2,1,0:T(8,128)(2,1)S(1)}, u32[]{:S(2)}, u32[]{:S(2)}) collective-permute-start(bf16[4,15,16,384]{3,2,1,0:T(8,128)(2,1)S(1)} %pad_maximum_fusion.1.refs_0_), channel_id=1, source_target_pairs={{0,2},{1,17},{2,0},{3,19},{4,6},{5,21},{6,4},{7,23},{8,10},{9,25},... | collective-permute-start | bytes 2211848 | tf_op jit(solution)/shard_map/ppermute | solution.py:1024
  113.6 18.8 %collective-permute-start.33 = (bf16[4,15,16,384]{3,2,1,0:T(8,128)(2,1)S(1)}, bf16[4,15,16,384]{3,2,1,0:T(8,128)(2,1)S(1)}, u32[]{:S(2)}, u32[]{:S(2)}) collective-permute-start(bf16[4,15,16,384]{3,2,1,0:T(8,128)(2,1)S(1)} %collective-permute-done.31.refs_1_), channel_id=1, source_target_pairs={{0,2},{1,17},{2,0},{3,19},{4,6},{5,21},{6,4},{7,23},{8,10},{9,25},... | collective-permute-start | bytes 2211848 | tf_op jit(solution)/shard_map/ppermute | solution.py:1024
  115.0 17.3 %collective-permute-start.34 = (bf16[4,15,16,384]{3,2,1,0:T(8,128)(2,1)S(1)}, bf16[4,15,16,384]{3,2,1,0:T(8,128)(2,1)S(1)}, u32[]{:S(2)}, u32[]{:S(2)}) collective-permute-start(bf16[4,15,16,384]{3,2,1,0:T(8,128)(2,1)S(1)} %pad_maximum_fusion.1.refs_0_), channel_id=1, source_target_pairs={{0,1},{1,0},{2,3},{3,2},{4,5},{5,4},{6,7},{7,6},{8,9},{9,8},{10,11... | collective-permute-start | bytes 2211848 | tf_op jit(solution)/shard_map/ppermute | solution.py:1024
  115.0 17.3 %collective-permute-start.35 = (bf16[4,15,16,384]{3,2,1,0:T(8,128)(2,1)S(1)}, bf16[4,15,16,384]{3,2,1,0:T(8,128)(2,1)S(1)}, u32[]{:S(2)}, u32[]{:S(2)}) collective-permute-start(bf16[4,15,16,384]{3,2,1,0:T(8,128)(2,1)S(1)} %collective-permute-done.31.refs_1_), channel_id=1, source_target_pairs={{0,1},{1,0},{2,3},{3,2},{4,5},{5,4},{6,7},{7,6},{8,9},{9,8},{10,11... | collective-permute-start | bytes 2211848 | tf_op jit(solution)/shard_map/ppermute | solution.py:1024
  146.6 19.5 %all-to-all-start = ((bf16[32,5,768]{2,1,0:T(8,128)(2,1)}), bf16[32,5,768]{2,1,0:T(8,128)(2,1)S(1)}, u32[]{:S(2)}, u32[]{:S(2)}) async-start(bf16[32,5,768]{2,1,0:T(8,128)(2,1)} %broadcast_in_dim.95), calls=%async_computation | async-start | bytes 786432 | tf_op jit(solution)/shard_map/all_to_all | solution.py:1439
  171.3 20.9 %collective-permute-start.38 = (bf16[16,1280]{1,0:T(8,128)(2,1)S(1)}, bf16[16,1280]{1,0:T(8,128)(2,1)S(1)}, u32[]{:S(2)}, u32[]{:S(2)}) collective-permute-start(bf16[16,1280]{1,0:T(8,128)(2,1)S(1)} %fusion.6), channel_id=1, source_target_pairs={{0,4},{1,5},{2,6},{3,7},{4,0},{5,1},{6,2},{7,3},{8,12},{9,13},{10,... | collective-permute-start | bytes 122888 | tf_op jit(solution)/shard_map/ppermute | solution.py:1024
  192.2 12.4 %collective-permute-start.39 = (bf16[16,192,384]{2,1,0:T(8,128)(2,1)S(1)}, bf16[16,192,384]{2,1,0:T(8,128)(2,1)S(1)}, u32[]{:S(2)}, u32[]{:S(2)}) collective-permute-start(bf16[16,192,384]{2,1,0:T(8,128)(2,1)S(1)} %get-tuple-element.286), channel_id=1, source_target_pairs={{0,1},{1,0},{2,3},{3,2},{4,5},{5,4},{6,7},{7,6},{8,9},{9,8},{10,11... | collective-permute-start | bytes 7077896 | tf_op jit(solution)/shard_map/ppermute | solution.py:1024
  192.3 12.3 %collective-permute-start.40 = (bf16[2,16,1280]{2,1,0:T(8,128)(2,1)S(1)}, bf16[2,16,1280]{2,1,0:T(8,128)(2,1)S(1)}, u32[]{:S(2)}, u32[]{:S(2)}) collective-permute-start(bf16[2,16,1280]{2,1,0:T(8,128)(2,1)S(1)} %pad_maximum_fusion.3), channel_id=1, source_target_pairs={{0,8},{1,9},{2,10},{3,11},{4,12},{5,13},{6,14},{7,15},{8,0},{9,1},... | collective-permute-start | bytes 245768 | tf_op jit(solution)/shard_map/ppermute | solution.py:1024
  207.8 16.3 %collective-permute-start.41 = (bf16[8,192,384]{2,1,0:T(8,128)(2,1)S(1)}, bf16[8,192,384]{2,1,0:T(8,128)(2,1)S(1)}, u32[]{:S(2)}, u32[]{:S(2)}) collective-permute-start(bf16[8,192,384]{2,1,0:T(8,128)(2,1)S(1)} %shard_map.133), channel_id=1, source_target_pairs={{0,16},{1,3},{2,18},{3,1},{4,20},{5,7},{6,22},{7,5},{8,24},{9,11},... | collective-permute-start | bytes 3538952 | tf_op jit(solution)/shard_map/ppermute | solution.py:1024
  231.5 11.5 %collective-permute-start.43 = (bf16[16,192,384]{2,1,0:T(8,128)(2,1)}, bf16[16,192,384]{2,1,0:T(8,128)(2,1)S(1)}, u32[]{:S(2)}, u32[]{:S(2)}) collective-permute-start(bf16[16,192,384]{2,1,0:T(8,128)(2,1)} %shard_map.135), channel_id=1, source_target_pairs={{0,1},{1,0},{2,3},{3,2},{4,5},{5,4},{6,7},{7,6},{8,9},{9,8},{10,11... | collective-permute-start | bytes 7077896 | tf_op jit(solution)/shard_map/ppermute | solution.py:1024
  231.5 11.5 %collective-permute-start.42 = (bf16[4,192,384]{2,1,0:T(8,128)(2,1)S(1)}, bf16[4,192,384]{2,1,0:T(8,128)(2,1)S(1)}, u32[]{:S(2)}, u32[]{:S(2)}) collective-permute-start(bf16[4,192,384]{2,1,0:T(8,128)(2,1)S(1)} %shard_map.134), channel_id=1, source_target_pairs={{0,2},{1,17},{2,0},{3,19},{4,6},{5,21},{6,4},{7,23},{8,10},{9,25},... | collective-permute-start | bytes 1769480 | tf_op jit(solution)/shard_map/ppermute | solution.py:1024
  245.5 17.1 %collective-permute-start.45 = (bf16[8,192,384]{2,1,0:T(8,128)(2,1)S(1)}, bf16[8,192,384]{2,1,0:T(8,128)(2,1)S(1)}, u32[]{:S(2)}, u32[]{:S(2)}) collective-permute-start(bf16[8,192,384]{2,1,0:T(8,128)(2,1)S(1)} %shard_map.139), channel_id=1, source_target_pairs={{0,16},{1,3},{2,18},{3,1},{4,20},{5,7},{6,22},{7,5},{8,24},{9,11},... | collective-permute-start | bytes 3538952 | tf_op jit(solution)/shard_map/ppermute | solution.py:1024
  246.2 16.3 %collective-permute-start.46 = (bf16[4,16,1280]{2,1,0:T(8,128)(2,1)S(1)}, bf16[4,16,1280]{2,1,0:T(8,128)(2,1)S(1)}, u32[]{:S(2)}, u32[]{:S(2)}) collective-permute-start(bf16[4,16,1280]{2,1,0:T(8,128)(2,1)S(1)} %collective-permute-done.44.refs_1_), channel_id=1, source_target_pairs={{0,2},{1,17},{2,0},{3,19},{4,6},{5,21},{6,4},{7,23},{8,10},{9,25},... | collective-permute-start | bytes 491528 | tf_op jit(solution)/shard_map/ppermute | solution.py:1024
  248.1 14.4 %collective-permute-start.47 = (bf16[192,384]{1,0:T(8,128)(2,1)S(1)}, bf16[192,384]{1,0:T(8,128)(2,1)S(1)}, u32[]{:S(2)}, u32[]{:S(2)}) collective-permute-start(bf16[192,384]{1,0:T(8,128)(2,1)S(1)} %get-tuple-element.320), channel_id=1, source_target_pairs={{0,4},{1,5},{2,6},{3,7},{4,0},{5,1},{6,2},{7,3},{8,12},{9,13},{10,... | collective-permute-start | bytes 442376 | tf_op jit(solution)/shard_map/ppermute | solution.py:1024
  248.6 13.9 %collective-permute-start.48 = (bf16[192,384]{1,0:T(8,128)(2,1)S(1)}, bf16[192,384]{1,0:T(8,128)(2,1)S(1)}, u32[]{:S(2)}, u32[]{:S(2)}) collective-permute-start(bf16[192,384]{1,0:T(8,128)(2,1)S(1)} %get-tuple-element.321), channel_id=1, source_target_pairs={{0,8},{1,9},{2,10},{3,11},{4,12},{5,13},{6,14},{7,15},{8,0},{9,1},... | collective-permute-start | bytes 442376 | tf_op jit(solution)/shard_map/ppermute | solution.py:1024
  250.8 11.6 %collective-permute-start.49 = (bf16[192,384]{1,0:T(8,128)(2,1)S(1)}, bf16[192,384]{1,0:T(8,128)(2,1)S(1)}, u32[]{:S(2)}, u32[]{:S(2)}) collective-permute-start(bf16[192,384]{1,0:T(8,128)(2,1)S(1)} %get-tuple-element.322), channel_id=1, source_target_pairs={{0,12},{1,13},{2,14},{3,15},{4,8},{5,9},{6,10},{7,11},{8,4},{9,5},... | collective-permute-start | bytes 442376 | tf_op jit(solution)/shard_map/ppermute | solution.py:1024
  264.7 11.7 %collective-permute-start.52 = (bf16[4,192,384]{2,1,0:T(8,128)(2,1)S(1)}, bf16[4,192,384]{2,1,0:T(8,128)(2,1)S(1)}, u32[]{:S(2)}, u32[]{:S(2)}) collective-permute-start(bf16[4,192,384]{2,1,0:T(8,128)(2,1)S(1)} %shard_map.143), channel_id=1, source_target_pairs={{0,2},{1,17},{2,0},{3,19},{4,6},{5,21},{6,4},{7,23},{8,10},{9,25},... | collective-permute-start | bytes 1769480 | tf_op jit(solution)/shard_map/ppermute | solution.py:1024
  266.3 10.2 %collective-permute-start.53 = (bf16[4,16,1280]{2,1,0:T(8,128)(2,1)S(1)}, bf16[4,16,1280]{2,1,0:T(8,128)(2,1)S(1)}, u32[]{:S(2)}, u32[]{:S(2)}) collective-permute-start(bf16[4,16,1280]{2,1,0:T(8,128)(2,1)S(1)} %constant_dynamic-update-slice_fusion.8.refs_0_), channel_id=1, source_target_pairs={{0,2},{1,17},{2,0},{3,19},{4,6},{5,21},{6,4},{7,23},{8,10},{9,25},... | collective-permute-start | bytes 491528 | tf_op jit(solution)/shard_map/ppermute | solution.py:1024
  276.5 16.1 %collective-permute-start.56 = (bf16[192,384]{1,0:T(8,128)(2,1)S(1)}, bf16[192,384]{1,0:T(8,128)(2,1)S(1)}, u32[]{:S(2)}, u32[]{:S(2)}) collective-permute-start(bf16[192,384]{1,0:T(8,128)(2,1)S(1)} %bitcast.37), channel_id=1, source_target_pairs={{0,1},{1,0},{2,3},{3,2},{4,5},{5,4},{6,7},{7,6},{8,9},{9,8},{10,11... | collective-permute-start | bytes 442376 | tf_op jit(solution)/shard_map/ppermute | solution.py:1024
  277.2 15.4 %collective-permute-start.59 = (bf16[192,384]{1,0:T(8,128)(2,1)S(1)}, bf16[192,384]{1,0:T(8,128)(2,1)S(1)}, u32[]{:S(2)}, u32[]{:S(2)}) collective-permute-start(bf16[192,384]{1,0:T(8,128)(2,1)S(1)} %get-tuple-element.341), channel_id=1, source_target_pairs={{0,4},{1,5},{2,6},{3,7},{4,0},{5,1},{6,2},{7,3},{8,12},{9,13},{10,... | collective-permute-start | bytes 442376 | tf_op jit(solution)/shard_map/ppermute | solution.py:1024
  278.9 14.0 %collective-permute-start.60 = (bf16[192,384]{1,0:T(8,128)(2,1)S(1)}, bf16[192,384]{1,0:T(8,128)(2,1)S(1)}, u32[]{:S(2)}, u32[]{:S(2)}) collective-permute-start(bf16[192,384]{1,0:T(8,128)(2,1)S(1)} %get-tuple-element.342), channel_id=1, source_target_pairs={{0,8},{1,9},{2,10},{3,11},{4,12},{5,13},{6,14},{7,15},{8,0},{9,1},... | collective-permute-start | bytes 442376 | tf_op jit(solution)/shard_map/ppermute | solution.py:1024
  280.6 12.2 %collective-permute-start.61 = (bf16[192,384]{1,0:T(8,128)(2,1)S(1)}, bf16[192,384]{1,0:T(8,128)(2,1)S(1)}, u32[]{:S(2)}, u32[]{:S(2)}) collective-permute-start(bf16[192,384]{1,0:T(8,128)(2,1)S(1)} %get-tuple-element.343), channel_id=1, source_target_pairs={{0,12},{1,13},{2,14},{3,15},{4,8},{5,9},{6,10},{7,11},{8,4},{9,5},... | collective-permute-start | bytes 442376 | tf_op jit(solution)/shard_map/ppermute | solution.py:1024
  304.5 11.2 %collective-permute-start.68 = (bf16[8,16,384]{2,1,0:T(8,128)(2,1)S(1)}, bf16[8,16,384]{2,1,0:T(8,128)(2,1)S(1)}, u32[]{:S(2)}, u32[]{:S(2)}) collective-permute-start(bf16[8,16,384]{2,1,0:T(8,128)(2,1)S(1)} %get-tuple-element.368), channel_id=1, source_target_pairs={{0,6},{1,7},{2,4},{3,5},{4,2},{5,3},{6,0},{7,1},{8,14},{9,15},{10,... | collective-permute-start | bytes 294920 | tf_op jit(solution)/shard_map/ppermute | solution.py:1024
  305.2 10.6 %collective-permute-start.69 = (bf16[8,16,384]{2,1,0:T(8,128)(2,1)S(1)}, bf16[8,16,384]{2,1,0:T(8,128)(2,1)S(1)}, u32[]{:S(2)}, u32[]{:S(2)}) collective-permute-start(bf16[8,16,384]{2,1,0:T(8,128)(2,1)S(1)} %get-tuple-element.369), channel_id=1, source_target_pairs={{0,8},{1,9},{2,10},{3,11},{4,12},{5,13},{6,14},{7,15},{8,0},{9,1},... | collective-permute-start | bytes 294920 | tf_op jit(solution)/shard_map/ppermute | solution.py:1024
  307.8 14.5 %collective-permute-start.70 = (bf16[8,16,384]{2,1,0:T(8,128)(2,1)S(1)}, bf16[8,16,384]{2,1,0:T(8,128)(2,1)S(1)}, u32[]{:S(2)}, u32[]{:S(2)}) collective-permute-start(bf16[8,16,384]{2,1,0:T(8,128)(2,1)S(1)} %get-tuple-element.370), channel_id=1, source_target_pairs={{0,10},{1,11},{2,8},{3,9},{4,14},{5,15},{6,12},{7,13},{8,2},{9,3},... | collective-permute-start | bytes 294920 | tf_op jit(solution)/shard_map/ppermute | solution.py:1024
  308.7 13.5 %collective-permute-start.71 = (bf16[8,16,384]{2,1,0:T(8,128)(2,1)S(1)}, bf16[8,16,384]{2,1,0:T(8,128)(2,1)S(1)}, u32[]{:S(2)}, u32[]{:S(2)}) collective-permute-start(bf16[8,16,384]{2,1,0:T(8,128)(2,1)S(1)} %get-tuple-element.371), channel_id=1, source_target_pairs={{0,12},{1,13},{2,14},{3,15},{4,8},{5,9},{6,10},{7,11},{8,4},{9,5},... | collective-permute-start | bytes 294920 | tf_op jit(solution)/shard_map/ppermute | solution.py:1024
  311.1 11.2 %collective-permute-start.72 = (bf16[8,16,384]{2,1,0:T(8,128)(2,1)S(1)}, bf16[8,16,384]{2,1,0:T(8,128)(2,1)S(1)}, u32[]{:S(2)}, u32[]{:S(2)}) collective-permute-start(bf16[8,16,384]{2,1,0:T(8,128)(2,1)S(1)} %get-tuple-element.372), channel_id=1, source_target_pairs={{0,14},{1,15},{2,12},{3,13},{4,10},{5,11},{6,8},{7,9},{8,6},{9,7},... | collective-permute-start | bytes 294920 | tf_op jit(solution)/shard_map/ppermute | solution.py:1024
  (80 other events, 743.3 us)

commit v7 on v6

--- a/solution.py
+++ b/solution.py
@@ -616,7 +616,7 @@
         weight.specs + [cols(n), whole((n, D)), cols(16), whole((n, 128))],
         [pl.BlockSpec((n, DM_COLS), lambda j, me: (0, jnp.maximum(j - blocks, 0))), cols(8)] + specs,
         grid=(blocks + steps,),
-        vmem=40,
+        vmem=34,
         scratch=weight.scratch + [pltpu.VMEM((n, FF), bf16)],
         flops=4 * n * D * FF,
         prefetch=1,

time: 333 us -> 335 us (level)
    unnamed x116 -> x118, local copies, waits for them, and re-layouts: 7.67 us -> 10.5 us
  transfers between devices with their start and end apart: 74 -> 74, of which waited for: 26 -> 25; matrix products, arithmetic and copies ran while one was open for 1% -> 1% of each run, Pallas kernels for 36% -> 36%
where the time goes in v7:
time: 335 us; the launch traced here: 330 us
  Pallas kernels  159 us (47%)
  starting transfers between devices  85.5 us (26%)
  waiting for transfers between devices  69.6 us (21%)
  local copies, waits for them, and re-layouts  13.3 us (4%)
    pallas_call x29, Pallas kernels, call(): pl.pallas_call(kernel, out_shape=tuple(outs), grid_spec=pltpu.PrefetchSca...  152 us
    ppermute x73, starting transfers between devices, send(): return lax.ppermute(value, AXES, permutation)  79.1 us
    ppermute x73, waiting for transfers between devices, send(): return lax.ppermute(value, AXES, permutation)  66.6 us
    unnamed x118, local copies, waits for them, and re-layouts  10.5 us
    pallas_call x1, Pallas kernels, plan(): pl.pallas_call(plan_kernel, out_shape=tuple((sds((size,), jnp.int32) for...  7.15 us
  transfers between devices with their start and end apart: 74, of which 25 were waited for; matrix products, arithmetic and copies ran while one was open for 1% of the time, Pallas kernels for 36%

profile of v7, /device:TPU:0, one launch (start us, length us, event | category | flops | bytes accessed | tf_op | source)
XLA Modules:
  0.0 330.1 jit_solution(11951440759877685250)
XLA Ops:
  1.4 2.3 shard_map.119
  3.7 2.9 collective-permute-start
  8.2 3.0 collective-permute-start.3
  12.7 3.7 %collective-permute-start.5 = (bf16[8,16,384]{2,1,0:T(8,128)(2,1)S(1)}, bf16[8,16,384]{2,1,0:T(8,128)(2,1)S(1)}, u32[]{:S(2)}, u32[]{:S(2)}) collective-permute-start(bf16[8,16,384]{2,1,0:T(8,128)(2,1)S(1)} %get-tuple-element.202), channel_id=1, source_target_pairs={{0,12},{1,13},{2,14},{3,15},{4,8},{5,9},{6,10},{7,11},{8,4},{9,5},... | collective-permute-start | bytes 294920 | tf_op jit(solution)/shard_map/ppermute | solution.py:1024
  16.5 7.2 %shard_map.120 = (s32[39]{0:T(128)}, s32[64]{0:T(128)}, s32[8]{0:T(128)}, s32[8]{0:T(128)}) custom-call(s32[77]{0:T(128)} %owner_ref.3, s32[4]{0:T(128)} %copy-done.18), custom_call_target="tpu_custom_call" | custom-call | tf_op jit(solution)/shard_map/pallas_call | solution.py:1207
  27.0 2.3 collective-permute-done.7.theirs_ref
  30.4 4.0 %collective-permute-start.8 = (bf16[10,16,384]{2,1,0:T(8,128)(2,1)S(1)}, bf16[10,16,384]{2,1,0:T(8,128)(2,1)S(1)}, u32[]{:S(2)}, u32[]{:S(2)}) collective-permute-start(bf16[10,16,384]{2,1,0:T(8,128)(2,1)S(1)} %get-tuple-element.217), channel_id=1, source_target_pairs={{0,4},{1,5},{2,6},{3,7},{4,0},{5,1},{6,2},{7,3},{8,12},{9,13},{10,... | collective-permute-start | bytes 368648 | tf_op jit(solution)/shard_map/ppermute | solution.py:1024
  37.1 2.7 collective-permute-done.8
  39.8 7.0 %collective-permute-done.9 = bf16[10,16,384]{2,1,0:T(8,128)(2,1)S(1)} collective-permute-done((bf16[10,16,384]{2,1,0:T(8,128)(2,1)S(1)}, bf16[10,16,384]{2,1,0:T(8,128)(2,1)S(1)}, u32[]{:S(2)}, u32[]{:S(2)}) %collective-permute-start.9) | collective-permute-done | bytes 122912 | tf_op jit(solution)/shard_map/ppermute | solution.py:1024
  53.8 4.9 %collective-permute-done.11.refs_1_ = bf16[4,10,16,384]{3,2,1,0:T(8,128)(2,1)S(1)} collective-permute-done((bf16[4,10,16,384]{3,2,1,0:T(8,128)(2,1)S(1)}, bf16[4,10,16,384]{3,2,1,0:T(8,128)(2,1)S(1)}, u32[]{:S(2)}, u32[]{:S(2)}) %collective-permute-start.11) | collective-permute-done | bytes 491552 | tf_op jit(solution)/shard_map/ppermute | solution.py:1024
  60.2 6.6 %collective-permute-done.14 = bf16[15,16,384]{2,1,0:T(8,128)(2,1)S(1)} collective-permute-done((bf16[15,16,384]{2,1,0:T(8,128)(2,1)S(1)}, bf16[15,16,384]{2,1,0:T(8,128)(2,1)S(1)}, u32[]{:S(2)}, u32[]{:S(2)}) %collective-permute-start.14) | collective-permute-done | bytes 184352 | tf_op jit(solution)/shard_map/ppermute | solution.py:1024
  70.8 2.5 collective-permute-start.23
  76.5 9.1 %shard_map.122 = (bf16[1040,768]{1,0:T(8,128)(2,1)}, bf16[1040,2304]{1,0:T(8,128)(2,1)S(1)}, f32[16,768]{1,0:T(8,128)S(1)}) custom-call(s32[4]{0:T(128)S(1)} %copy-done.19, bf16[4,10,16,384]{3,2,1,0:T(8,128)(2,1)} %copy-done.35, bf16[4,10,16,384]{3,2,1,0:T(8,128)(2,1)} %copy-done.42, bf16[4,10,16,384]{3,2,1,0:T(8,128)(2,1)} %copy-done.43, ...), custom_call_target="tpu_custom_call" | custom-call | flops 1 | bytes 1 | tf_op jit(solution)/shard_map/pallas_call | solution.py:84
  85.6 4.0 %collective-permute-done.24 = bf16[15,16,384]{2,1,0:T(8,128)(2,1)S(1)} collective-permute-done((bf16[15,16,384]{2,1,0:T(8,128)(2,1)S(1)}, bf16[15,16,384]{2,1,0:T(8,128)(2,1)S(1)}, u32[]{:S(2)}, u32[]{:S(2)}) %collective-permute-start.24) | collective-permute-done | bytes 184352 | tf_op jit(solution)/shard_map/ppermute | solution.py:1024
  90.9 8.9 %shard_map.123 = (bf16[1040,768]{1,0:T(8,128)(2,1)S(1)}, f32[5,16,208]{2,1,0:T(8,128)S(1)}) custom-call(bf16[1040,2304]{1,0:T(8,128)(2,1)S(1)} %get-tuple-element.240.qkv_ref, f32[5,1,208]{2,1,0:T(1,128)S(1)} %broadcast_in_dim.84.mask_ref), custom_call_target="tpu_custom_call" | custom-call | flops 1 | bytes 1 | tf_op jit(solution)/shard_map/pallas_call | solution.py:84
  104.4 6.2 %shard_map.124 = (f32[1040,768]{1,0:T(8,128)S(1)}, bf16[1040,768]{1,0:T(8,128)(2,1)S(1)}) custom-call(s32[4]{0:T(128)S(1)} %copy-done.19, bf16[4,15,16,384]{3,2,1,0:T(8,128)(2,1)} %copy-done.26, bf16[4,15,16,384]{3,2,1,0:T(8,128)(2,1)} %copy-done.27, bf16[4,15,16,384]{3,2,1,0:T(8,128)(2,1)} %copy-done.28, bf16[4,15,16,384]{3,2,1,0:T(8,128)(2,1)} %copy-done.29, ...), custom_call_target="tpu_custom_call" | custom-call | flops 1 | bytes 1 | tf_op jit(solution)/shard_map/pallas_call | solution.py:84
  110.6 2.4 collective-permute-done.31.refs_1_
  115.6 13.3 %shard_map.125 = (bf16[1040,3072]{1,0:T(8,128)(2,1)S(1)}, bf16[1040,3072]{1,0:T(8,128)(2,1)}) custom-call(s32[4]{0:T(128)S(1)} %copy-done.19, bf16[4,15,16,384]{3,2,1,0:T(8,128)(2,1)} %copy-done.26, bf16[4,15,16,384]{3,2,1,0:T(8,128)(2,1)} %copy-done.27, bf16[4,15,16,384]{3,2,1,0:T(8,128)(2,1)} %copy-done.28, bf16[4,15,16,384]{3,2,1,0:T(8,128)(2,1)} %copy-done.29, ...), custom_call_target="tpu_custom_call" | custom-call | flops 1 | bytes 1 | tf_op jit(solution)/shard_map/pallas_call | solution.py:84
  129.0 3.4 %collective-permute-done.33.refs_3_ = bf16[4,15,16,384]{3,2,1,0:T(8,128)(2,1)S(1)} collective-permute-done((bf16[4,15,16,384]{3,2,1,0:T(8,128)(2,1)S(1)}, bf16[4,15,16,384]{3,2,1,0:T(8,128)(2,1)S(1)}, u32[]{:S(2)}, u32[]{:S(2)}) %collective-permute-start.33) | collective-permute-done | bytes 737312 | tf_op jit(solution)/shard_map/ppermute | solution.py:1024
  135.8 10.0 %shard_map.126 = (bf16[5,196,768]{2,1,0:T(8,128)(2,1)}, bf16[16,768]{1,0:T(8,128)(2,1)S(1)}) custom-call(s32[4]{0:T(128)S(1)} %copy-done.19, bf16[4,15,16,384]{3,2,1,0:T(8,128)(2,1)} %copy-done.34, bf16[4,15,16,384]{3,2,1,0:T(8,128)(2,1)} %copy-done.36, bf16[4,15,16,384]{3,2,1,0:T(8,128)(2,1)} %copy-done.37, bf16[4,15,16,384]{3,2,1,0:T(8,128)(2,1)} %copy-done.38, ...), custom_call_target="tpu_custom_call" | custom-call | flops 1 | bytes 1 | tf_op jit(solution)/shard_map/pallas_call | solution.py:84
  146.6 6.4 %all-to-all-start = ((bf16[32,5,768]{2,1,0:T(8,128)(2,1)}), bf16[32,5,768]{2,1,0:T(8,128)(2,1)S(1)}, u32[]{:S(2)}, u32[]{:S(2)}) async-start(bf16[32,5,768]{2,1,0:T(8,128)(2,1)} %broadcast_in_dim.95), calls=%async_computation | async-start | bytes 786432 | tf_op jit(solution)/shard_map/all_to_all | solution.py:1439
  153.1 2.3 copy-done.6
  155.4 3.2 shard_map.128.p_ref
  158.7 2.7 copy-done.7
  163.2 3.0 all-to-all-done.refs_9_
  166.2 5.1 %shard_map.129 = (bf16[160,512]{1,0:T(8,128)(2,1)S(1)}, bf16[16,768]{1,0:T(8,128)(2,1)S(1)}, f32[16,768]{1,0:T(8,128)S(1)}, f32[16,3072]{1,0:T(8,128)S(1)}, bf16[160,768]{1,0:T(8,128)(2,1)S(1)}) custom-call(s32[4]{0:T(128)S(1)} %copy-done.19, s32[1]{0:T(128)} %bitcast.5.first_ref, bf16[4,15,16,384]{3,2,1,0:T(8,128)(2,1)} %copy-done.34, ...), custom_call_target="tpu_custom_call" | custom-call | flops 1 | bytes 1 | tf_op jit(solution)/shard_map/pallas_call | solution.py:84
  172.3 2.8 copy-done.16
  175.1 19.1 %shard_map.130 = (f32[1040,768]{1,0:T(8,128)S(1)}, f32[8,3072]{1,0:T(8,128)S(1)}, bf16[16,192,384]{2,1,0:T(8,128)(2,1)S(1)}, bf16[16,192,384]{2,1,0:T(8,128)(2,1)S(1)}) custom-call(s32[4]{0:T(128)S(1)} %copy-done.19, bf16[4,15,16,384]{3,2,1,0:T(8,128)(2,1)} %copy-done.26, bf16[4,15,16,384]{3,2,1,0:T(8,128)(2,1)} %copy-done.27, ...), custom_call_target="tpu_custom_call" | custom-call | flops 1 | bytes 1 | tf_op jit(solution)/shard_map/pallas_call | solution.py:84
  196.0 10.6 %shard_map.131 = (f32[1040,768]{1,0:T(8,128)S(1)}, bf16[1040,768]{1,0:T(8,128)(2,1)S(1)}, bf16[2,16,48,384]{3,2,1,0:T(8,128)(2,1)S(1)}, f32[8,768]{1,0:T(8,128)S(1)}) custom-call(s32[4]{0:T(128)S(1)} %copy-done.19, bf16[4,15,16,384]{3,2,1,0:T(8,128)(2,1)} %copy-done.26, bf16[4,15,16,384]{3,2,1,0:T(8,128)(2,1)} %copy-done.27, ...), custom_call_target="tpu_custom_call" | custom-call | flops 1 | bytes 1 | tf_op jit(solution)/shard_map/pallas_call | solution.py:84
  206.6 3.2 shard_map.133
  211.4 13.2 %shard_map.132 = (bf16[1040,2304]{1,0:T(8,128)(2,1)S(1)}, f32[16,2304]{1,0:T(8,128)S(1)}) custom-call(bf16[1040,2304]{1,0:T(8,128)(2,1)S(1)} %bitcast.31, bf16[1040,768]{1,0:T(8,128)(2,1)S(1)} %get-tuple-element.289.do_ref, bf16[5,12,208,208]{3,2,1,0:T(8,128)(2,1)S(1)} %bitcast.36), custom_call_target="tpu_custom_call" | custom-call | flops 1 | bytes 1 | tf_op jit(solution)/shard_map/pallas_call | solution.py:84
  226.2 2.5 shard_map.134
  228.7 4.9 %shard_map.135 = bf16[16,192,384]{2,1,0:T(8,128)(2,1)} custom-call(s32[4]{0:T(128)S(1)} %copy-done.19, bf16[1040,2304]{1,0:T(8,128)(2,1)S(1)} %get-tuple-element.305.dqkv_ref.refs_9_, bf16[1040,768]{1,0:T(8,128)(2,1)S(1)} %copy-done.11, bf16[2,16,48,384]{3,2,1,0:T(8,128)(2,1)S(1)} %get-tuple-element.300.out_ref), custom_call_target="tpu_custom_call" | custom-call | flops 1 | bytes 1 | tf_op jit(solution)/shard_map/pallas_call | solution.py:84
  237.7 4.9 %shard_map.137.refs_0_.refs_2_.refs_4_.refs_6_.refs_3_.refs_9_ = bf16[16,192,384]{2,1,0:T(8,128)(2,1)} custom-call(s32[4]{0:T(128)S(1)} %copy-done.19, bf16[1040,2304]{1,0:T(8,128)(2,1)S(1)} %get-tuple-element.305.dqkv_ref.refs_9_, bf16[1040,768]{1,0:T(8,128)(2,1)S(1)} %copy-done.11, bf16[2,16,48,384]{3,2,1,0:T(8,128)(2,1)S(1)} %get-tuple-element.300.out_ref), custom_call_target="tpu_custom_call" | custom-call | flops 1 | bytes 1 | tf_op jit(solution)/shard_map/pallas_call | solution.py:84
  242.6 2.5 collective-permute-done.42.refs_1_.refs_3_.refs_5_.refs_7_
  245.1 2.4 shard_map.139
  254.6 9.9 %shard_map.138 = (f32[5,196,768]{2,1,0:T(8,128)}, f32[16,768]{1,0:T(8,128)S(1)}) custom-call(s32[4]{0:T(128)S(1)} %copy-done.19, bf16[4,10,16,384]{3,2,1,0:T(8,128)(2,1)} %copy-done.35, bf16[4,10,16,384]{3,2,1,0:T(8,128)(2,1)} %copy-done.42, bf16[4,10,16,384]{3,2,1,0:T(8,128)(2,1)} %copy-done.43, bf16[4,10,16,384]{3,2,1,0:T(8,128)(2,1)} %copy-done.44, ...), custom_call_target="tpu_custom_call" | custom-call | flops 1 | bytes 1 | tf_op jit(solution)/shard_map/pallas_call | solution.py:84
  276.2 2.3 collective-permute-done.53.refs_2_
  285.2 2.6 collective-permute-done.57
  288.6 6.0 %collective-permute-done.58 = f32[16,768]{1,0:T(8,128)S(1)} collective-permute-done((f32[16,768]{1,0:T(8,128)S(1)}, f32[16,768]{1,0:T(8,128)S(1)}, u32[]{:S(2)}, u32[]{:S(2)}) %collective-permute-start.58) | collective-permute-done | bytes 49184 | tf_op jit(solution)/shard_map/ppermute | solution.py:1024
  297.5 2.8 collective-permute-done.63
  300.3 2.4 shard_map.147
  304.0 2.7 collective-permute-start.67
  307.3 2.6 collective-permute-start.69
  310.8 2.4 collective-permute-start.71
  315.0 2.9 shard_map.146
  317.9 6.4 %collective-permute-done.70.refs_11_ = bf16[8,16,384]{2,1,0:T(8,128)(2,1)S(1)} collective-permute-done((bf16[8,16,384]{2,1,0:T(8,128)(2,1)S(1)}, bf16[8,16,384]{2,1,0:T(8,128)(2,1)S(1)}, u32[]{:S(2)}, u32[]{:S(2)}) %collective-permute-start.70) | collective-permute-done | bytes 98336 | tf_op jit(solution)/shard_map/ppermute | solution.py:1024
  324.4 5.5 %shard_map.148 = (f32[1,8,64,768]{3,2,1,0:T(8,128)}, f32[1,8,64,768]{3,2,1,0:T(8,128)}, f32[1,8,64,768]{3,2,1,0:T(8,128)}) custom-call(s32[8]{0:T(128)S(1)} %copy-done.21, s32[8]{0:T(128)S(1)} %copy-done.22, s32[4]{0:T(128)S(1)} %copy-done.19, f32[1,8,64,768]{3,2,1,0:T(8,128)} %refs_0_.1, f32[1,8,64,768]{3,2,1,0:T(8,128)} %refs_1_.1, ...), custom_call_target="tpu_custom_call" | custom-call | flops 1 | bytes 1 | tf_op jit(solution)/shard_map/pallas_call | solution.py:84
  (285 shorter events, 84.3 us)
Async XLA Ops:
  8.2 17.0 %collective-permute-start.2 = (bf16[8,16,384]{2,1,0:T(8,128)(2,1)S(1)}, bf16[8,16,384]{2,1,0:T(8,128)(2,1)S(1)}, u32[]{:S(2)}, u32[]{:S(2)}) collective-permute-start(bf16[8,16,384]{2,1,0:T(8,128)(2,1)S(1)} %get-tuple-element.199), channel_id=1, source_target_pairs={{0,6},{1,7},{2,4},{3,5},{4,2},{5,3},{6,0},{7,1},{8,14},{9,15},{10,... | collective-permute-start | bytes 294920 | tf_op jit(solution)/shard_map/ppermute | solution.py:1024
  8.2 17.1 %collective-permute-start.3 = (bf16[8,16,384]{2,1,0:T(8,128)(2,1)S(1)}, bf16[8,16,384]{2,1,0:T(8,128)(2,1)S(1)}, u32[]{:S(2)}, u32[]{:S(2)}) collective-permute-start(bf16[8,16,384]{2,1,0:T(8,128)(2,1)S(1)} %get-tuple-element.200), channel_id=1, source_target_pairs={{0,8},{1,9},{2,10},{3,11},{4,12},{5,13},{6,14},{7,15},{8,0},{9,1},... | collective-permute-start | bytes 294920 | tf_op jit(solution)/shard_map/ppermute | solution.py:1024
  11.2 15.2 %collective-permute-start.4 = (bf16[8,16,384]{2,1,0:T(8,128)(2,1)S(1)}, bf16[8,16,384]{2,1,0:T(8,128)(2,1)S(1)}, u32[]{:S(2)}, u32[]{:S(2)}) collective-permute-start(bf16[8,16,384]{2,1,0:T(8,128)(2,1)S(1)} %get-tuple-element.201), channel_id=1, source_target_pairs={{0,10},{1,11},{2,8},{3,9},{4,14},{5,15},{6,12},{7,13},{8,2},{9,3},... | collective-permute-start | bytes 294920 | tf_op jit(solution)/shard_map/ppermute | solution.py:1024
  12.7 13.7 %collective-permute-start.5 = (bf16[8,16,384]{2,1,0:T(8,128)(2,1)S(1)}, bf16[8,16,384]{2,1,0:T(8,128)(2,1)S(1)}, u32[]{:S(2)}, u32[]{:S(2)}) collective-permute-start(bf16[8,16,384]{2,1,0:T(8,128)(2,1)S(1)} %get-tuple-element.202), channel_id=1, source_target_pairs={{0,12},{1,13},{2,14},{3,15},{4,8},{5,9},{6,10},{7,11},{8,4},{9,5},... | collective-permute-start | bytes 294920 | tf_op jit(solution)/shard_map/ppermute | solution.py:1024
  34.5 12.4 %collective-permute-start.9 = (bf16[10,16,384]{2,1,0:T(8,128)(2,1)S(1)}, bf16[10,16,384]{2,1,0:T(8,128)(2,1)S(1)}, u32[]{:S(2)}, u32[]{:S(2)}) collective-permute-start(bf16[10,16,384]{2,1,0:T(8,128)(2,1)S(1)} %get-tuple-element.217), channel_id=1, source_target_pairs={{0,8},{1,9},{2,10},{3,11},{4,12},{5,13},{6,14},{7,15},{8,0},{9,1},... | collective-permute-start | bytes 368648 | tf_op jit(solution)/shard_map/ppermute | solution.py:1024
  35.8 11.1 %collective-permute-start.10 = (bf16[10,16,384]{2,1,0:T(8,128)(2,1)S(1)}, bf16[10,16,384]{2,1,0:T(8,128)(2,1)S(1)}, u32[]{:S(2)}, u32[]{:S(2)}) collective-permute-start(bf16[10,16,384]{2,1,0:T(8,128)(2,1)S(1)} %get-tuple-element.217), channel_id=1, source_target_pairs={{0,12},{1,13},{2,14},{3,15},{4,8},{5,9},{6,10},{7,11},{8,4},{9,5},... | collective-permute-start | bytes 368648 | tf_op jit(solution)/shard_map/ppermute | solution.py:1024
  46.9 11.7 %collective-permute-start.11 = (bf16[4,10,16,384]{3,2,1,0:T(8,128)(2,1)S(1)}, bf16[4,10,16,384]{3,2,1,0:T(8,128)(2,1)S(1)}, u32[]{:S(2)}, u32[]{:S(2)}) collective-permute-start(bf16[4,10,16,384]{3,2,1,0:T(8,128)(2,1)S(1)} %pad_maximum_fusion.2.refs_0_), channel_id=1, source_target_pairs={{0,16},{1,3},{2,18},{3,1},{4,20},{5,7},{6,22},{7,5},{8,24},{9,11},... | collective-permute-start | bytes 1474568 | tf_op jit(solution)/shard_map/ppermute | solution.py:1024
  49.1 11.1 %collective-permute-start.13 = (bf16[15,16,384]{2,1,0:T(8,128)(2,1)S(1)}, bf16[15,16,384]{2,1,0:T(8,128)(2,1)S(1)}, u32[]{:S(2)}, u32[]{:S(2)}) collective-permute-start(bf16[15,16,384]{2,1,0:T(8,128)(2,1)S(1)} %get-tuple-element.232), channel_id=1, source_target_pairs={{0,4},{1,5},{2,6},{3,7},{4,0},{5,1},{6,2},{7,3},{8,12},{9,13},{10,... | collective-permute-start | bytes 552968 | tf_op jit(solution)/shard_map/ppermute | solution.py:1024
  51.2 15.6 %collective-permute-start.14 = (bf16[15,16,384]{2,1,0:T(8,128)(2,1)S(1)}, bf16[15,16,384]{2,1,0:T(8,128)(2,1)S(1)}, u32[]{:S(2)}, u32[]{:S(2)}) collective-permute-start(bf16[15,16,384]{2,1,0:T(8,128)(2,1)S(1)} %get-tuple-element.232), channel_id=1, source_target_pairs={{0,8},{1,9},{2,10},{3,11},{4,12},{5,13},{6,14},{7,15},{8,0},{9,1},... | collective-permute-start | bytes 552968 | tf_op jit(solution)/shard_map/ppermute | solution.py:1024
  52.3 14.4 %collective-permute-start.15 = (bf16[15,16,384]{2,1,0:T(8,128)(2,1)S(1)}, bf16[15,16,384]{2,1,0:T(8,128)(2,1)S(1)}, u32[]{:S(2)}, u32[]{:S(2)}) collective-permute-start(bf16[15,16,384]{2,1,0:T(8,128)(2,1)S(1)} %get-tuple-element.232), channel_id=1, source_target_pairs={{0,12},{1,13},{2,14},{3,15},{4,8},{5,9},{6,10},{7,11},{8,4},{9,5},... | collective-permute-start | bytes 552968 | tf_op jit(solution)/shard_map/ppermute | solution.py:1024
  58.7 10.3 %collective-permute-start.16 = (bf16[4,10,16,384]{3,2,1,0:T(8,128)(2,1)S(1)}, bf16[4,10,16,384]{3,2,1,0:T(8,128)(2,1)S(1)}, u32[]{:S(2)}, u32[]{:S(2)}) collective-permute-start(bf16[4,10,16,384]{3,2,1,0:T(8,128)(2,1)S(1)} %collective-permute-done.11.refs_1_), channel_id=1, source_target_pairs={{0,2},{1,17},{2,0},{3,19},{4,6},{5,21},{6,4},{7,23},{8,10},{9,25},... | collective-permute-start | bytes 1474568 | tf_op jit(solution)/shard_map/ppermute | solution.py:1024
  66.9 22.7 %collective-permute-start.21 = (bf16[4,15,16,384]{3,2,1,0:T(8,128)(2,1)S(1)}, bf16[4,15,16,384]{3,2,1,0:T(8,128)(2,1)S(1)}, u32[]{:S(2)}, u32[]{:S(2)}) collective-permute-start(bf16[4,15,16,384]{3,2,1,0:T(8,128)(2,1)S(1)} %pad_maximum_fusion.refs_0_), channel_id=1, source_target_pairs={{0,16},{1,3},{2,18},{3,1},{4,20},{5,7},{6,22},{7,5},{8,24},{9,11},... | collective-permute-start | bytes 2211848 | tf_op jit(solution)/shard_map/ppermute | solution.py:1024
  67.5 22.1 %collective-permute-start.22 = (bf16[4,15,16,384]{3,2,1,0:T(8,128)(2,1)S(1)}, bf16[4,15,16,384]{3,2,1,0:T(8,128)(2,1)S(1)}, u32[]{:S(2)}, u32[]{:S(2)}) collective-permute-start(bf16[4,15,16,384]{3,2,1,0:T(8,128)(2,1)S(1)} %pad_maximum_fusion.refs_0_), channel_id=1, source_target_pairs={{0,2},{1,17},{2,0},{3,19},{4,6},{5,21},{6,4},{7,23},{8,10},{9,25},... | collective-permute-start | bytes 2211848 | tf_op jit(solution)/shard_map/ppermute | solution.py:1024
  70.8 14.8 %collective-permute-start.23 = (bf16[15,16,384]{2,1,0:T(8,128)(2,1)S(1)}, bf16[15,16,384]{2,1,0:T(8,128)(2,1)S(1)}, u32[]{:S(2)}, u32[]{:S(2)}) collective-permute-start(bf16[15,16,384]{2,1,0:T(8,128)(2,1)S(1)} %get-tuple-element.251), channel_id=1, source_target_pairs={{0,4},{1,5},{2,6},{3,7},{4,0},{5,1},{6,2},{7,3},{8,12},{9,13},{10,... | collective-permute-start | bytes 552968 | tf_op jit(solution)/shard_map/ppermute | solution.py:1024
  73.3 16.3 %collective-permute-start.24 = (bf16[15,16,384]{2,1,0:T(8,128)(2,1)S(1)}, bf16[15,16,384]{2,1,0:T(8,128)(2,1)S(1)}, u32[]{:S(2)}, u32[]{:S(2)}) collective-permute-start(bf16[15,16,384]{2,1,0:T(8,128)(2,1)S(1)} %get-tuple-element.251), channel_id=1, source_target_pairs={{0,8},{1,9},{2,10},{3,11},{4,12},{5,13},{6,14},{7,15},{8,0},{9,1},... | collective-permute-start | bytes 552968 | tf_op jit(solution)/shard_map/ppermute | solution.py:1024
  75.5 14.1 %collective-permute-start.25 = (bf16[15,16,384]{2,1,0:T(8,128)(2,1)S(1)}, bf16[15,16,384]{2,1,0:T(8,128)(2,1)S(1)}, u32[]{:S(2)}, u32[]{:S(2)}) collective-permute-start(bf16[15,16,384]{2,1,0:T(8,128)(2,1)S(1)} %get-tuple-element.251), channel_id=1, source_target_pairs={{0,12},{1,13},{2,14},{3,15},{4,8},{5,9},{6,10},{7,11},{8,4},{9,5},... | collective-permute-start | bytes 552968 | tf_op jit(solution)/shard_map/ppermute | solution.py:1024
  89.7 11.5 %collective-permute-start.26 = (bf16[4,15,16,384]{3,2,1,0:T(8,128)(2,1)S(1)}, bf16[4,15,16,384]{3,2,1,0:T(8,128)(2,1)S(1)}, u32[]{:S(2)}, u32[]{:S(2)}) collective-permute-start(bf16[4,15,16,384]{3,2,1,0:T(8,128)(2,1)S(1)} %collective-permute-done.21.refs_1_), channel_id=1, source_target_pairs={{0,2},{1,17},{2,0},{3,19},{4,6},{5,21},{6,4},{7,23},{8,10},{9,25},... | collective-permute-start | bytes 2211848 | tf_op jit(solution)/shard_map/ppermute | solution.py:1024
  90.4 10.9 %collective-permute-start.28 = (bf16[4,15,16,384]{3,2,1,0:T(8,128)(2,1)S(1)}, bf16[4,15,16,384]{3,2,1,0:T(8,128)(2,1)S(1)}, u32[]{:S(2)}, u32[]{:S(2)}) collective-permute-start(bf16[4,15,16,384]{3,2,1,0:T(8,128)(2,1)S(1)} %collective-permute-done.21.refs_1_), channel_id=1, source_target_pairs={{0,1},{1,0},{2,3},{3,2},{4,5},{5,4},{6,7},{7,6},{8,9},{9,8},{10,11... | collective-permute-start | bytes 2211848 | tf_op jit(solution)/shard_map/ppermute | solution.py:1024
  90.4 10.8 %collective-permute-start.27 = (bf16[4,15,16,384]{3,2,1,0:T(8,128)(2,1)S(1)}, bf16[4,15,16,384]{3,2,1,0:T(8,128)(2,1)S(1)}, u32[]{:S(2)}, u32[]{:S(2)}) collective-permute-start(bf16[4,15,16,384]{3,2,1,0:T(8,128)(2,1)S(1)} %pad_maximum_fusion.refs_0_), channel_id=1, source_target_pairs={{0,1},{1,0},{2,3},{3,2},{4,5},{5,4},{6,7},{7,6},{8,9},{9,8},{10,11... | collective-permute-start | bytes 2211848 | tf_op jit(solution)/shard_map/ppermute | solution.py:1024
  90.9 10.4 %collective-permute-start.29 = (bf16[4,15,16,384]{3,2,1,0:T(8,128)(2,1)S(1)}, bf16[4,15,16,384]{3,2,1,0:T(8,128)(2,1)S(1)}, u32[]{:S(2)}, u32[]{:S(2)}) collective-permute-start(bf16[4,15,16,384]{3,2,1,0:T(8,128)(2,1)S(1)} %collective-permute-done.22.refs_2_), channel_id=1, source_target_pairs={{0,1},{1,0},{2,3},{3,2},{4,5},{5,4},{6,7},{7,6},{8,9},{9,8},{10,11... | collective-permute-start | bytes 2211848 | tf_op jit(solution)/shard_map/ppermute | solution.py:1024
  101.5 11.5 %collective-permute-start.31 = (bf16[4,15,16,384]{3,2,1,0:T(8,128)(2,1)S(1)}, bf16[4,15,16,384]{3,2,1,0:T(8,128)(2,1)S(1)}, u32[]{:S(2)}, u32[]{:S(2)}) collective-permute-start(bf16[4,15,16,384]{3,2,1,0:T(8,128)(2,1)S(1)} %pad_maximum_fusion.1.refs_0_), channel_id=1, source_target_pairs={{0,16},{1,3},{2,18},{3,1},{4,20},{5,7},{6,22},{7,5},{8,24},{9,11},... | collective-permute-start | bytes 2211848 | tf_op jit(solution)/shard_map/ppermute | solution.py:1024
  113.0 15.9 %collective-permute-start.32 = (bf16[4,15,16,384]{3,2,1,0:T(8,128)(2,1)S(1)}, bf16[4,15,16,384]{3,2,1,0:T(8,128)(2,1)S(1)}, u32[]{:S(2)}, u32[]{:S(2)}) collective-permute-start(bf16[4,15,16,384]{3,2,1,0:T(8,128)(2,1)S(1)} %pad_maximum_fusion.1.refs_0_), channel_id=1, source_target_pairs={{0,2},{1,17},{2,0},{3,19},{4,6},{5,21},{6,4},{7,23},{8,10},{9,25},... | collective-permute-start | bytes 2211848 | tf_op jit(solution)/shard_map/ppermute | solution.py:1024
  113.6 18.7 %collective-permute-start.33 = (bf16[4,15,16,384]{3,2,1,0:T(8,128)(2,1)S(1)}, bf16[4,15,16,384]{3,2,1,0:T(8,128)(2,1)S(1)}, u32[]{:S(2)}, u32[]{:S(2)}) collective-permute-start(bf16[4,15,16,384]{3,2,1,0:T(8,128)(2,1)S(1)} %collective-permute-done.31.refs_1_), channel_id=1, source_target_pairs={{0,2},{1,17},{2,0},{3,19},{4,6},{5,21},{6,4},{7,23},{8,10},{9,25},... | collective-permute-start | bytes 2211848 | tf_op jit(solution)/shard_map/ppermute | solution.py:1024
  115.0 17.3 %collective-permute-start.34 = (bf16[4,15,16,384]{3,2,1,0:T(8,128)(2,1)S(1)}, bf16[4,15,16,384]{3,2,1,0:T(8,128)(2,1)S(1)}, u32[]{:S(2)}, u32[]{:S(2)}) collective-permute-start(bf16[4,15,16,384]{3,2,1,0:T(8,128)(2,1)S(1)} %pad_maximum_fusion.1.refs_0_), channel_id=1, source_target_pairs={{0,1},{1,0},{2,3},{3,2},{4,5},{5,4},{6,7},{7,6},{8,9},{9,8},{10,11... | collective-permute-start | bytes 2211848 | tf_op jit(solution)/shard_map/ppermute | solution.py:1024
  115.0 17.3 %collective-permute-start.35 = (bf16[4,15,16,384]{3,2,1,0:T(8,128)(2,1)S(1)}, bf16[4,15,16,384]{3,2,1,0:T(8,128)(2,1)S(1)}, u32[]{:S(2)}, u32[]{:S(2)}) collective-permute-start(bf16[4,15,16,384]{3,2,1,0:T(8,128)(2,1)S(1)} %collective-permute-done.31.refs_1_), channel_id=1, source_target_pairs={{0,1},{1,0},{2,3},{3,2},{4,5},{5,4},{6,7},{7,6},{8,9},{9,8},{10,11... | collective-permute-start | bytes 2211848 | tf_op jit(solution)/shard_map/ppermute | solution.py:1024
  146.6 19.5 %all-to-all-start = ((bf16[32,5,768]{2,1,0:T(8,128)(2,1)}), bf16[32,5,768]{2,1,0:T(8,128)(2,1)S(1)}, u32[]{:S(2)}, u32[]{:S(2)}) async-start(bf16[32,5,768]{2,1,0:T(8,128)(2,1)} %broadcast_in_dim.95), calls=%async_computation | async-start | bytes 786432 | tf_op jit(solution)/shard_map/all_to_all | solution.py:1439
  171.3 22.9 %collective-permute-start.38 = (bf16[16,1280]{1,0:T(8,128)(2,1)S(1)}, bf16[16,1280]{1,0:T(8,128)(2,1)S(1)}, u32[]{:S(2)}, u32[]{:S(2)}) collective-permute-start(bf16[16,1280]{1,0:T(8,128)(2,1)S(1)} %fusion.6), channel_id=1, source_target_pairs={{0,4},{1,5},{2,6},{3,7},{4,0},{5,1},{6,2},{7,3},{8,12},{9,13},{10,... | collective-permute-start | bytes 122888 | tf_op jit(solution)/shard_map/ppermute | solution.py:1024
  194.2 12.4 %collective-permute-start.39 = (bf16[16,192,384]{2,1,0:T(8,128)(2,1)S(1)}, bf16[16,192,384]{2,1,0:T(8,128)(2,1)S(1)}, u32[]{:S(2)}, u32[]{:S(2)}) collective-permute-start(bf16[16,192,384]{2,1,0:T(8,128)(2,1)S(1)} %get-tuple-element.286), channel_id=1, source_target_pairs={{0,1},{1,0},{2,3},{3,2},{4,5},{5,4},{6,7},{7,6},{8,9},{9,8},{10,11... | collective-permute-start | bytes 7077896 | tf_op jit(solution)/shard_map/ppermute | solution.py:1024
  194.3 12.3 %collective-permute-start.40 = (bf16[2,16,1280]{2,1,0:T(8,128)(2,1)S(1)}, bf16[2,16,1280]{2,1,0:T(8,128)(2,1)S(1)}, u32[]{:S(2)}, u32[]{:S(2)}) collective-permute-start(bf16[2,16,1280]{2,1,0:T(8,128)(2,1)S(1)} %pad_maximum_fusion.3), channel_id=1, source_target_pairs={{0,8},{1,9},{2,10},{3,11},{4,12},{5,13},{6,14},{7,15},{8,0},{9,1},... | collective-permute-start | bytes 245768 | tf_op jit(solution)/shard_map/ppermute | solution.py:1024
  209.9 16.3 %collective-permute-start.41 = (bf16[8,192,384]{2,1,0:T(8,128)(2,1)S(1)}, bf16[8,192,384]{2,1,0:T(8,128)(2,1)S(1)}, u32[]{:S(2)}, u32[]{:S(2)}) collective-permute-start(bf16[8,192,384]{2,1,0:T(8,128)(2,1)S(1)} %shard_map.133), channel_id=1, source_target_pairs={{0,16},{1,3},{2,18},{3,1},{4,20},{5,7},{6,22},{7,5},{8,24},{9,11},... | collective-permute-start | bytes 3538952 | tf_op jit(solution)/shard_map/ppermute | solution.py:1024
  233.6 11.5 %collective-permute-start.43 = (bf16[16,192,384]{2,1,0:T(8,128)(2,1)}, bf16[16,192,384]{2,1,0:T(8,128)(2,1)S(1)}, u32[]{:S(2)}, u32[]{:S(2)}) collective-permute-start(bf16[16,192,384]{2,1,0:T(8,128)(2,1)} %shard_map.135), channel_id=1, source_target_pairs={{0,1},{1,0},{2,3},{3,2},{4,5},{5,4},{6,7},{7,6},{8,9},{9,8},{10,11... | collective-permute-start | bytes 7077896 | tf_op jit(solution)/shard_map/ppermute | solution.py:1024
  233.6 11.5 %collective-permute-start.42 = (bf16[4,192,384]{2,1,0:T(8,128)(2,1)S(1)}, bf16[4,192,384]{2,1,0:T(8,128)(2,1)S(1)}, u32[]{:S(2)}, u32[]{:S(2)}) collective-permute-start(bf16[4,192,384]{2,1,0:T(8,128)(2,1)S(1)} %shard_map.134), channel_id=1, source_target_pairs={{0,2},{1,17},{2,0},{3,19},{4,6},{5,21},{6,4},{7,23},{8,10},{9,25},... | collective-permute-start | bytes 1769480 | tf_op jit(solution)/shard_map/ppermute | solution.py:1024
  247.5 17.1 %collective-permute-start.45 = (bf16[8,192,384]{2,1,0:T(8,128)(2,1)S(1)}, bf16[8,192,384]{2,1,0:T(8,128)(2,1)S(1)}, u32[]{:S(2)}, u32[]{:S(2)}) collective-permute-start(bf16[8,192,384]{2,1,0:T(8,128)(2,1)S(1)} %shard_map.139), channel_id=1, source_target_pairs={{0,16},{1,3},{2,18},{3,1},{4,20},{5,7},{6,22},{7,5},{8,24},{9,11},... | collective-permute-start | bytes 3538952 | tf_op jit(solution)/shard_map/ppermute | solution.py:1024
  248.3 16.3 %collective-permute-start.46 = (bf16[4,16,1280]{2,1,0:T(8,128)(2,1)S(1)}, bf16[4,16,1280]{2,1,0:T(8,128)(2,1)S(1)}, u32[]{:S(2)}, u32[]{:S(2)}) collective-permute-start(bf16[4,16,1280]{2,1,0:T(8,128)(2,1)S(1)} %collective-permute-done.44.refs_1_), channel_id=1, source_target_pairs={{0,2},{1,17},{2,0},{3,19},{4,6},{5,21},{6,4},{7,23},{8,10},{9,25},... | collective-permute-start | bytes 491528 | tf_op jit(solution)/shard_map/ppermute | solution.py:1024
  250.1 14.4 %collective-permute-start.47 = (bf16[192,384]{1,0:T(8,128)(2,1)S(1)}, bf16[192,384]{1,0:T(8,128)(2,1)S(1)}, u32[]{:S(2)}, u32[]{:S(2)}) collective-permute-start(bf16[192,384]{1,0:T(8,128)(2,1)S(1)} %get-tuple-element.320), channel_id=1, source_target_pairs={{0,4},{1,5},{2,6},{3,7},{4,0},{5,1},{6,2},{7,3},{8,12},{9,13},{10,... | collective-permute-start | bytes 442376 | tf_op jit(solution)/shard_map/ppermute | solution.py:1024
  250.7 13.8 %collective-permute-start.48 = (bf16[192,384]{1,0:T(8,128)(2,1)S(1)}, bf16[192,384]{1,0:T(8,128)(2,1)S(1)}, u32[]{:S(2)}, u32[]{:S(2)}) collective-permute-start(bf16[192,384]{1,0:T(8,128)(2,1)S(1)} %get-tuple-element.321), channel_id=1, source_target_pairs={{0,8},{1,9},{2,10},{3,11},{4,12},{5,13},{6,14},{7,15},{8,0},{9,1},... | collective-permute-start | bytes 442376 | tf_op jit(solution)/shard_map/ppermute | solution.py:1024
  252.9 11.6 %collective-permute-start.49 = (bf16[192,384]{1,0:T(8,128)(2,1)S(1)}, bf16[192,384]{1,0:T(8,128)(2,1)S(1)}, u32[]{:S(2)}, u32[]{:S(2)}) collective-permute-start(bf16[192,384]{1,0:T(8,128)(2,1)S(1)} %get-tuple-element.322), channel_id=1, source_target_pairs={{0,12},{1,13},{2,14},{3,15},{4,8},{5,9},{6,10},{7,11},{8,4},{9,5},... | collective-permute-start | bytes 442376 | tf_op jit(solution)/shard_map/ppermute | solution.py:1024
  266.8 11.7 %collective-permute-start.52 = (bf16[4,192,384]{2,1,0:T(8,128)(2,1)S(1)}, bf16[4,192,384]{2,1,0:T(8,128)(2,1)S(1)}, u32[]{:S(2)}, u32[]{:S(2)}) collective-permute-start(bf16[4,192,384]{2,1,0:T(8,128)(2,1)S(1)} %shard_map.143), channel_id=1, source_target_pairs={{0,2},{1,17},{2,0},{3,19},{4,6},{5,21},{6,4},{7,23},{8,10},{9,25},... | collective-permute-start | bytes 1769480 | tf_op jit(solution)/shard_map/ppermute | solution.py:1024
  268.3 10.2 %collective-permute-start.53 = (bf16[4,16,1280]{2,1,0:T(8,128)(2,1)S(1)}, bf16[4,16,1280]{2,1,0:T(8,128)(2,1)S(1)}, u32[]{:S(2)}, u32[]{:S(2)}) collective-permute-start(bf16[4,16,1280]{2,1,0:T(8,128)(2,1)S(1)} %constant_dynamic-update-slice_fusion.8.refs_0_), channel_id=1, source_target_pairs={{0,2},{1,17},{2,0},{3,19},{4,6},{5,21},{6,4},{7,23},{8,10},{9,25},... | collective-permute-start | bytes 491528 | tf_op jit(solution)/shard_map/ppermute | solution.py:1024
  278.5 16.1 %collective-permute-start.56 = (bf16[192,384]{1,0:T(8,128)(2,1)S(1)}, bf16[192,384]{1,0:T(8,128)(2,1)S(1)}, u32[]{:S(2)}, u32[]{:S(2)}) collective-permute-start(bf16[192,384]{1,0:T(8,128)(2,1)S(1)} %bitcast.37), channel_id=1, source_target_pairs={{0,1},{1,0},{2,3},{3,2},{4,5},{5,4},{6,7},{7,6},{8,9},{9,8},{10,11... | collective-permute-start | bytes 442376 | tf_op jit(solution)/shard_map/ppermute | solution.py:1024
  279.3 15.4 %collective-permute-start.59 = (bf16[192,384]{1,0:T(8,128)(2,1)S(1)}, bf16[192,384]{1,0:T(8,128)(2,1)S(1)}, u32[]{:S(2)}, u32[]{:S(2)}) collective-permute-start(bf16[192,384]{1,0:T(8,128)(2,1)S(1)} %get-tuple-element.341), channel_id=1, source_target_pairs={{0,4},{1,5},{2,6},{3,7},{4,0},{5,1},{6,2},{7,3},{8,12},{9,13},{10,... | collective-permute-start | bytes 442376 | tf_op jit(solution)/shard_map/ppermute | solution.py:1024
  281.0 14.0 %collective-permute-start.60 = (bf16[192,384]{1,0:T(8,128)(2,1)S(1)}, bf16[192,384]{1,0:T(8,128)(2,1)S(1)}, u32[]{:S(2)}, u32[]{:S(2)}) collective-permute-start(bf16[192,384]{1,0:T(8,128)(2,1)S(1)} %get-tuple-element.342), channel_id=1, source_target_pairs={{0,8},{1,9},{2,10},{3,11},{4,12},{5,13},{6,14},{7,15},{8,0},{9,1},... | collective-permute-start | bytes 442376 | tf_op jit(solution)/shard_map/ppermute | solution.py:1024
  282.7 12.3 %collective-permute-start.61 = (bf16[192,384]{1,0:T(8,128)(2,1)S(1)}, bf16[192,384]{1,0:T(8,128)(2,1)S(1)}, u32[]{:S(2)}, u32[]{:S(2)}) collective-permute-start(bf16[192,384]{1,0:T(8,128)(2,1)S(1)} %get-tuple-element.343), channel_id=1, source_target_pairs={{0,12},{1,13},{2,14},{3,15},{4,8},{5,9},{6,10},{7,11},{8,4},{9,5},... | collective-permute-start | bytes 442376 | tf_op jit(solution)/shard_map/ppermute | solution.py:1024
  306.7 11.2 %collective-permute-start.68 = (bf16[8,16,384]{2,1,0:T(8,128)(2,1)S(1)}, bf16[8,16,384]{2,1,0:T(8,128)(2,1)S(1)}, u32[]{:S(2)}, u32[]{:S(2)}) collective-permute-start(bf16[8,16,384]{2,1,0:T(8,128)(2,1)S(1)} %get-tuple-element.368), channel_id=1, source_target_pairs={{0,6},{1,7},{2,4},{3,5},{4,2},{5,3},{6,0},{7,1},{8,14},{9,15},{10,... | collective-permute-start | bytes 294920 | tf_op jit(solution)/shard_map/ppermute | solution.py:1024
  307.3 10.6 %collective-permute-start.69 = (bf16[8,16,384]{2,1,0:T(8,128)(2,1)S(1)}, bf16[8,16,384]{2,1,0:T(8,128)(2,1)S(1)}, u32[]{:S(2)}, u32[]{:S(2)}) collective-permute-start(bf16[8,16,384]{2,1,0:T(8,128)(2,1)S(1)} %get-tuple-element.369), channel_id=1, source_target_pairs={{0,8},{1,9},{2,10},{3,11},{4,12},{5,13},{6,14},{7,15},{8,0},{9,1},... | collective-permute-start | bytes 294920 | tf_op jit(solution)/shard_map/ppermute | solution.py:1024
  309.9 14.5 %collective-permute-start.70 = (bf16[8,16,384]{2,1,0:T(8,128)(2,1)S(1)}, bf16[8,16,384]{2,1,0:T(8,128)(2,1)S(1)}, u32[]{:S(2)}, u32[]{:S(2)}) collective-permute-start(bf16[8,16,384]{2,1,0:T(8,128)(2,1)S(1)} %get-tuple-element.370), channel_id=1, source_target_pairs={{0,10},{1,11},{2,8},{3,9},{4,14},{5,15},{6,12},{7,13},{8,2},{9,3},... | collective-permute-start | bytes 294920 | tf_op jit(solution)/shard_map/ppermute | solution.py:1024
  310.8 13.5 %collective-permute-start.71 = (bf16[8,16,384]{2,1,0:T(8,128)(2,1)S(1)}, bf16[8,16,384]{2,1,0:T(8,128)(2,1)S(1)}, u32[]{:S(2)}, u32[]{:S(2)}) collective-permute-start(bf16[8,16,384]{2,1,0:T(8,128)(2,1)S(1)} %get-tuple-element.371), channel_id=1, source_target_pairs={{0,12},{1,13},{2,14},{3,15},{4,8},{5,9},{6,10},{7,11},{8,4},{9,5},... | collective-permute-start | bytes 294920 | tf_op jit(solution)/shard_map/ppermute | solution.py:1024
  313.2 11.2 %collective-permute-start.72 = (bf16[8,16,384]{2,1,0:T(8,128)(2,1)S(1)}, bf16[8,16,384]{2,1,0:T(8,128)(2,1)S(1)}, u32[]{:S(2)}, u32[]{:S(2)}) collective-permute-start(bf16[8,16,384]{2,1,0:T(8,128)(2,1)S(1)} %get-tuple-element.372), channel_id=1, source_target_pairs={{0,14},{1,15},{2,12},{3,13},{4,10},{5,11},{6,8},{7,9},{8,6},{9,7},... | collective-permute-start | bytes 294920 | tf_op jit(solution)/shard_map/ppermute | solution.py:1024
  (81 other events, 745.2 us)
